TPU v7x, 32 devices: a whole 2x2x4 slice. The times are simulated.
32 devices in a mesh: row: 4 (over y, core), col: 8 (over z, x).
Axes of the slice: x: 2, y: 2, z: 4, core: 2. Of those that a mesh axis runs over, the one named last changes fastest.
Arguments:
- probes: bfloat16 [4, 8192, 256], P(None, ('row', 'col')), may hold values from -6 to 6
- points: bfloat16 [16, 4, 8192], P(None, None, ('row', 'col')), may hold values from -8 to 8
- leaf_skeleton: int32 [64, 64], P(('row', 'col')), may hold values from 0 to 127, as said below
- skeleton_one: int32 [32, 64], P(('row', 'col')), may hold values from 0 to 127, as said below
- skeleton_two: int32 [16, 64], P('row'), may hold values from 0 to 127, as said below
- skeleton_three: int32 [8, 64], P('row'), may hold values from 0 to 127, as said below
Outputs:
- leaf_interp: float32 [64, 128, 64], P(('row', 'col'))
- upper_interp: float32 [3, 32, 128, 64], P(None, ('row', 'col'))
- top_state: float32 [2, 32, 64, 256], P(None, ('row', 'col'))
Inputs may be any that keep to these rules, and one draw needn't show every extreme that they name: `leaf_skeleton`: each row names 64 different rows of its leaf, in ascending order. `skeleton_one`: each row names 64 different rows of the node's stacked child skeletons, in ascending order. `skeleton_two`: each row names 64 different rows of the node's stacked child skeletons, in ascending order. `skeleton_three`: each row names 64 different rows of the node's stacked child skeletons, in ascending order.
All inputs are finite; a program needn't handle non-finite values.
Results may differ from a plain program's by a relative error of at most 0.0059.
Values may be sent and summed in bfloat16 or wider, within the bound.
No kernel may reach another device: no remote copies, remote signals or barrier semaphores. Data moves between devices by JAX's collectives and lax.ppermute only.
A program may use at most 64 MiB of HBM per device.

v0:
```python
import math

import jax
import jax.numpy as jnp
from jax import lax
from jax.experimental import pallas as pl
from jax.experimental.pallas import tpu as pltpu
from jax.sharding import PartitionSpec as P

LEAF = 128
F32 = jnp.float32
BF16 = jnp.bfloat16
DOUBLINGS = 9
VMEM = pl.BlockSpec(memory_space=pltpu.VMEM)
SMEM = pl.BlockSpec(memory_space=pltpu.SMEM)
COST = pl.CostEstimate(flops=0, bytes_accessed=0, transcendentals=0)
PARAMS = pltpu.CompilerParams(vmem_limit_bytes=40 << 20)


def chebyshev_constants():
    taus = [1282.0 / 1280.0]
    for _ in range(DOUBLINGS):
        taus.append(2.0 * taus[-1] * taus[-1] - 1.0)
    front = 2.0**DOUBLINGS * math.prod(taus[:-1]) / taus[-1]
    return taus[:-1], front


TAUS, FRONT = chebyshev_constants()


def over(first, second, first_dim, second_dim):
    return lax.dot_general(
        first,
        second,
        (((first_dim,), (second_dim,)), ((), ())),
        preferred_element_type=F32,
    )


def split(value):
    high = value.astype(BF16)
    rest = value - high.astype(F32)
    middle = rest.astype(BF16)
    return high, middle, (rest - middle.astype(F32)).astype(BF16)


def norm_rows(norm, first, width):
    parts = [part.astype(F32) for part in split(norm)]
    place = lax.broadcasted_iota(jnp.int32, (16, width), 0)
    extra = jnp.where(place < 6, 1.0, 0.0)
    for pos in range(3):
        extra = jnp.where(place == pos + first, parts[pos], extra)
    return extra


def row_features(feats, gain):
    feats = feats.astype(F32)
    depth, width = feats.shape
    unit = math.log2(math.e) / (2.0 * depth)
    norm = jnp.sum(feats * feats, axis=0, keepdims=True) * -unit + math.log2(gain)
    parts = [part.astype(F32) for part in split(feats * (2.0 * unit))]
    return jnp.concatenate([*parts, norm_rows(norm, 0, width)], axis=0)


def col_features(feats):
    feats = feats.astype(F32)
    depth, width = feats.shape
    unit = math.log2(math.e) / (2.0 * depth)
    norm = jnp.sum(feats * feats, axis=0, keepdims=True) * -unit
    return jnp.concatenate([feats, feats, feats, norm_rows(norm, 3, width)], axis=0).astype(BF16)


def pack_body(probes_ref, points_ref, packed_ref, own_ref, held_ref, sem):
    quarters, span, _ = probes_ref.shape
    copies = [pltpu.make_async_copy(points_ref, held_ref, sem.at[quarters])]
    copies += [
        pltpu.make_async_copy(
            probes_ref.at[quarter], packed_ref.at[pl.ds(quarter * span, span)], sem.at[quarter]
        )
        for quarter in range(quarters)
    ]
    for copy in copies:
        copy.start()
    copies[0].wait()
    points = held_ref[...].astype(F32)
    for quarter in range(quarters):
        feats = points[:, quarter, :].astype(BF16)
        packed_ref[pl.ds(quarters * span + 16 * quarter, 16), :] = feats
        if quarter == 0:
            own_ref[...] = feats
    for copy in copies[1:]:
        copy.wait()


def pack(probes, points):
    quarters, span, samples = probes.shape
    return pl.pallas_call(
        pack_body,
        out_shape=(
            jax.ShapeDtypeStruct((quarters * (span + 16), samples), BF16),
            jax.ShapeDtypeStruct((16, span), BF16),
        ),
        in_specs=[pl.BlockSpec(memory_space=pl.ANY)] * 2,
        scratch_shapes=[
            pltpu.VMEM(points.shape, BF16),
            pltpu.SemaphoreType.DMA((quarters + 1,)),
        ],
        compiler_params=pltpu.CompilerParams(vmem_limit_bytes=60 << 20),
        name="pack",
    )(probes, points)


def masked(entries):
    shape = entries.shape
    row_leaf = lax.broadcasted_iota(jnp.int32, shape, 0) // LEAF
    col_leaf = lax.broadcasted_iota(jnp.int32, shape, 1) // LEAF
    return jnp.where(row_leaf == col_leaf, 0.0, entries)


def add_source(source_ref, row_refs, cols_ref, put, span, own):
    quarters = source_ref.shape[0] // (span + 16)
    columns = quarters * span
    for quarter in range(quarters):
        feats = source_ref[pl.ds(columns + 16 * quarter, 16), :]
        cols_ref[:, pl.ds(quarter * span, span)] = col_features(feats)
    for half, rows_ref in enumerate(row_refs):
        for start in range(0, rows_ref.shape[0], span):
            feats = rows_ref[pl.ds(start, span), :]
            entries = jnp.exp2(over(feats, cols_ref[:, :columns], 1, 0))
            if own and half == 0 and start == 0:
                entries = jnp.concatenate([masked(entries[:, :span]), entries[:, span:]], axis=1)
            randoms = source_ref[pl.ds(0, columns), :]
            put(half, start, over(entries.astype(BF16), randoms, 1, 0))


def product_body(gain, span, first, source_count, half_count, *refs):
    refs = list(refs)
    cols_ref = refs.pop()
    take = lambda count: [refs.pop(0) for _ in range(count)]
    sources = take(source_count)
    if first:
        point_refs, row_refs = take(half_count), take(half_count)
        for points_ref, rows_ref in zip(point_refs, row_refs):
            for start in range(0, points_ref.shape[1], span):
                feats = points_ref[:, pl.ds(start, span)]
                rows_ref[pl.ds(start, span), :] = row_features(feats, gain).T.astype(BF16)
    else:
        row_refs, old_refs = take(half_count), take(half_count)
    total_refs = take(half_count)
    for number, source in enumerate(sources):

        def put(half, start, value):
            place = pl.ds(start, span)
            if number > 0:
                total_refs[half][place, :] += value
            elif first:
                total_refs[half][place, :] = value
            else:
                total_refs[half][place, :] = old_refs[half][place, :] + value

        add_source(source, row_refs, cols_ref, put, span, first and number == 0)


def product(sources, rows, span, totals=None, gain=None):
    samples = sources[0].shape[1]
    first = totals is None
    halves = len(rows)
    counts = [half.shape[1] if first else half.shape[0] for half in rows]
    columns = max(s.shape[0] // (span + 16) * span for s in sources)
    out = [jax.ShapeDtypeStruct((count, samples), F32) for count in counts]
    if first:
        out = [jax.ShapeDtypeStruct((count, 64), BF16) for count in counts] + out
    out = pl.pallas_call(
        lambda *refs: product_body(gain, span, first, len(sources), halves, *refs),
        out_shape=out,
        scratch_shapes=[pltpu.VMEM((64, columns), BF16)],
        cost_estimate=COST,
        compiler_params=PARAMS,
        name="product",
    )(*sources, *rows, *([] if first else totals))
    return (out[:halves], out[halves:]) if first else out


def combine_body(span, mine_ref, theirs_ref, own_ref, *sent_refs):
    own_ref[...] = mine_ref[pl.ds(0, span), :] + theirs_ref[pl.ds(0, span), :]
    for number, sent_ref in enumerate(sent_refs):
        place = pl.ds((number + 1) * span, span)
        sent_ref[...] = (mine_ref[place, :] + theirs_ref[place, :]).astype(BF16)


def combine(mine, theirs, span):
    rows, samples = mine.shape
    return pl.pallas_call(
        lambda *refs: combine_body(span, *refs),
        out_shape=[jax.ShapeDtypeStruct((span, samples), F32)]
        + [jax.ShapeDtypeStruct((span, samples), BF16)] * (rows // span - 1),
        compiler_params=PARAMS,
        name="combine",
    )(mine, theirs)


def wide_product(first, second, second_dim):
    high, middle, low = split(first)
    other_high, other_middle, other_low = split(second)
    return over(
        jnp.concatenate([high, high, middle, middle, low, high], axis=1),
        jnp.concatenate(
            [other_high, other_middle, other_high, other_middle, other_high, other_low],
            axis=second_dim,
        ),
        1,
        second_dim,
    )


def exact_product(first, second):
    second = second.astype(BF16)
    return over(
        jnp.concatenate(split(first), axis=1), jnp.concatenate([second] * 3, axis=0), 1, 0
    )


def twice_product(twice_parts, parts):
    high, middle, low = twice_parts
    other_high, other_middle, other_low = parts
    left = lax.broadcasted_iota(jnp.int32, high.shape, 1) < high.shape[1] // 2
    last = jnp.where(left, low.astype(F32), high.astype(F32)).astype(BF16)
    return over(
        jnp.concatenate([high, middle, last], axis=1),
        jnp.concatenate(
            [other_high, other_middle, other_high, other_middle, other_high, other_low], axis=0
        ),
        1,
        0,
    )


def select_rows(picks, value):
    return over(
        jnp.concatenate([picks] * 3, axis=1), jnp.concatenate(split(value), axis=0), 1, 0
    )


def interpolate(stacks, picks_list, early=None):
    rank, pool = picks_list[0].shape
    place = lax.broadcasted_iota(jnp.int32, (rank, 2 * rank), 0)
    other = lax.broadcasted_iota(jnp.int32, (rank, 2 * rank), 1)
    eyes = jnp.where((other == place) | (other == place + rank), 1.0, 0.0)
    skeletons = [select_rows(picks, stack) for picks, stack in zip(picks_list, stacks)]
    if early is not None:
        early(*skeletons)
    states = []
    for skeleton, stack in zip(skeletons, stacks):
        products = wide_product(skeleton, jnp.concatenate([stack, skeleton, skeleton], axis=0), 1)
        ridge = 0.05 * jnp.sum(skeleton * skeleton, keepdims=True) / rank + 1e-05
        inverse = 1.0 / (640.0 * ridge)
        states.append((products[:, :pool], eyes - products[:, pool:] * inverse, inverse))
    for number, tau in enumerate(TAUS):
        last = number == DOUBLINGS - 1
        later = []
        for solved, power, inverse in states:
            power_parts = split(power)
            parts = split(solved)
            if not last:
                parts = [jnp.concatenate(pair, axis=1) for pair in zip(parts, power_parts)]
            both = twice_product(power_parts, parts)
            solved = solved + both[:, :pool] * (1.0 / tau)
            later.append((solved, None if last else 2.0 * both[:, pool:] - eyes, inverse))
        states = later
    return [
        (solved * (inverse * FRONT), skeleton)
        for (solved, _, inverse), skeleton in zip(states, skeletons)
    ]


def merge(first, second, couplings_ref, picks, early=None):
    first_samples, first_reduced = first
    second_samples, second_reduced = second
    first_parts, second_parts = split(first_reduced), split(second_reduced)
    stacked = jnp.concatenate(
        [
            first_samples - twice_product(split(couplings_ref[0]), second_parts),
            second_samples - twice_product(split(couplings_ref[1]), first_parts),
        ],
        axis=0,
    )
    ((interp, skeleton),) = interpolate([stacked], [picks], early)
    reduced = wide_product(interp, jnp.concatenate([first_reduced, second_reduced], axis=0), 0)
    return interp, skeleton, reduced


def leaves_body(received, *refs):
    own_ref, *others = refs[: received + 1]
    source_ref, picks_ref, couplings_ref = refs[received + 1 : received + 4]
    leaf_ref, upper_ref, state_ref, held_ref, sem = refs[-5:]
    rank = picks_ref.shape[1]
    total = own_ref[...]
    for other in others:
        total = total + other[...].astype(F32)
    count = total.shape[0] // LEAF
    stacks = [total[leaf * LEAF : (leaf + 1) * LEAF] for leaf in range(count)]
    children = []
    for leaf, (interp, skeleton) in enumerate(
        interpolate(stacks, [picks_ref[leaf] for leaf in range(count)])
    ):
        held_ref[leaf] = interp
        randoms = source_ref[pl.ds(leaf * LEAF, LEAF), :]
        children.append((skeleton, exact_product(interp, randoms)))
    copy = pltpu.make_async_copy(held_ref, leaf_ref, sem)
    copy.start()
    interp, skeleton, reduced = merge(*children, couplings_ref, picks_ref[count])
    upper_ref[...] = interp
    state_ref[pl.ds(0, rank), :] = skeleton
    state_ref[pl.ds(rank, rank), :] = reduced
    copy.wait()


def leaves(own, others, source, picks, couplings, upper_couplings, leaf_count):
    samples = own.shape[1]
    rank, pool = picks.shape[1:]
    return pl.pallas_call(
        lambda *refs: leaves_body(len(others), *refs),
        out_shape=(
            jax.ShapeDtypeStruct((leaf_count, rank, LEAF), F32),
            jax.ShapeDtypeStruct((rank, pool), F32),
            jax.ShapeDtypeStruct((2 * rank, samples), F32),
        ),
        out_specs=(pl.BlockSpec(memory_space=pl.ANY), VMEM, VMEM),
        scratch_shapes=[pltpu.VMEM((leaf_count, rank, LEAF), F32), pltpu.SemaphoreType.DMA],
        cost_estimate=COST,
        compiler_params=PARAMS,
        name="leaves",
    )(own, *others, source, picks, couplings, *upper_couplings)


def level_body(number, place_ref, mine_ref, theirs_ref, picks_ref, couplings_ref, *refs):
    rank = picks_ref.shape[1]
    if number == 2:
        upper_ref, state_ref = refs
    else:
        one_ref, two_ref, upper_out, top_out, upper_ref, state_ref, sem = refs
        places = [
            (one_ref, upper_out.at[0, 0]),
            (two_ref, upper_out.at[1, 0]),
            (state_ref.at[pl.ds(0, rank)], top_out.at[0, 0]),
            (state_ref.at[pl.ds(rank, rank)], top_out.at[1, 0]),
            (upper_ref, upper_out.at[2, 0]),
        ]
        copies = [
            pltpu.make_async_copy(source, target, sem.at[pos])
            for pos, (source, target) in enumerate(places)
        ]
        copies[0].start()
        copies[1].start()

    def early(skeleton):
        state_ref[pl.ds(0, rank), :] = skeleton
        if number > 2:
            copies[2].start()

    mine_first = place_ref[number - 2] == 0
    mine, theirs = mine_ref[...], theirs_ref[...]
    first = jnp.where(mine_first, mine, theirs)
    second = jnp.where(mine_first, theirs, mine)
    interp, _, reduced = merge(
        (first[:rank], first[rank:]),
        (second[:rank], second[rank:]),
        couplings_ref,
        picks_ref[picks_ref.shape[0] + number - 4],
        early,
    )
    upper_ref[...] = interp
    state_ref[pl.ds(rank, rank), :] = reduced
    if number > 2:
        copies[3].start()
        copies[4].start()
        for copy in copies:
            copy.wait()


def level(number, place, mine, theirs, picks, couplings, below=()):
    rank, pool = picks.shape[1:]
    samples = mine.shape[1]
    out_shape = (
        jax.ShapeDtypeStruct((rank, pool), F32),
        jax.ShapeDtypeStruct(mine.shape, F32),
    )
    out_specs = (VMEM, VMEM)
    scratch = []
    if below:
        scratch = [pltpu.VMEM(out.shape, F32) for out in out_shape]
        scratch.append(pltpu.SemaphoreType.DMA((5,)))
        out_shape = (
            jax.ShapeDtypeStruct((3, 1, rank, pool), F32),
            jax.ShapeDtypeStruct((2, 1, rank, samples), F32),
        )
        out_specs = (pl.BlockSpec(memory_space=pl.ANY),) * 2
    return pl.pallas_call(
        lambda *refs: level_body(number, *refs),
        out_shape=out_shape,
        in_specs=[SMEM] + [VMEM] * (4 + len(below)),
        out_specs=out_specs,
        scratch_shapes=scratch,
        cost_estimate=COST,
        compiler_params=PARAMS,
        name="level",
    )(place, mine, theirs, picks, couplings, *below)


def one_hot(chosen, pool):
    place = lax.broadcasted_iota(jnp.int32, (pool, chosen.shape[1]), 0)
    return jnp.where(place == chosen, 1.0, 0.0).astype(F32)


def couple(first, second, picks, gain, couplings_ref, points_ref):
    for number, (left, right) in enumerate(((first, second), (second, first))):
        twice = jnp.concatenate([right, right], axis=1)
        rows = row_features(left, gain).astype(BF16)
        couplings_ref[number] = jnp.exp2(over(rows, col_features(twice), 0, 0))
    if points_ref is not None:
        rank = first.shape[1]
        points = over(first, picks[:rank], 1, 0) + over(second, picks[rank:], 1, 0)
        points_ref[...] = points.astype(BF16)


def skeletons_body(gain, place_ref, own_ref, leaf_ref, one_ref, two_ref, three_ref, *refs):
    picks_ref, couplings_ref, points_ref = refs
    count, rank = leaf_ref.shape
    rows = [leaf_ref[leaf : leaf + 1, :] for leaf in range(count)]
    rows.append(one_ref[...])
    rows.append(two_ref[pl.ds(place_ref[2], 1), :])
    rows.append(three_ref[pl.ds(place_ref[3], 1), :])
    hots = [one_hot(row, picks_ref.shape[2]) for row in rows]
    for number, hot in enumerate(hots):
        picks_ref[number] = hot.T.astype(BF16)
    children = [
        over(own_ref[:, pl.ds(leaf * LEAF, LEAF)], hots[leaf].astype(BF16), 1, 0)
        for leaf in range(count)
    ]
    couple(*children, hots[count], gain, couplings_ref, points_ref)


def skeletons(place, own_points, tables, gain):
    leaf_count, rank = tables[0].shape
    return pl.pallas_call(
        lambda *refs: skeletons_body(gain, *refs),
        out_shape=(
            jax.ShapeDtypeStruct((leaf_count + 3, rank, LEAF), BF16),
            jax.ShapeDtypeStruct((2, rank, 2 * rank), F32),
            jax.ShapeDtypeStruct((16, rank), BF16),
        ),
        in_specs=[SMEM] + [VMEM] * 5,
        compiler_params=PARAMS,
        name="skeletons",
    )(place, own_points, *tables)


def couplings_body(gain, number, place_ref, mine_ref, theirs_ref, picks_ref, couplings_ref, *refs):
    mine_first = place_ref[number - 2] == 0
    mine, theirs = mine_ref[...].astype(F32), theirs_ref[...].astype(F32)
    first = jnp.where(mine_first, mine, theirs)
    second = jnp.where(mine_first, theirs, mine)
    picks = picks_ref[picks_ref.shape[0] + number - 4].astype(F32).T
    couple(first, second, picks, gain, couplings_ref, refs[0] if refs else None)


def couplings(number, place, mine, theirs, picks, gain):
    rank = picks.shape[1]
    out_shape = [jax.ShapeDtypeStruct((2, rank, 2 * rank), F32)]
    if number == 2:
        out_shape.append(jax.ShapeDtypeStruct(mine.shape, BF16))
    return pl.pallas_call(
        lambda *refs: couplings_body(gain, number, *refs),
        out_shape=out_shape,
        in_specs=[SMEM] + [VMEM] * 3,
        compiler_params=PARAMS,
        name="couplings",
    )(place, mine, theirs, picks)


def local(probes, points, leaf_skeleton, skeleton_one, skeleton_two, skeleton_three):
    span = probes.shape[1]
    row_count = lax.axis_size("row")
    col_count = lax.axis_size("col")
    col_pos = lax.axis_index("col")
    gain = 16.0 / math.sqrt(4 * span * row_count * col_count)
    place = jnp.stack([col_pos & 1, col_pos >> 1 & 1, col_pos >> 1, col_pos >> 2])

    def swap(value, row_bits, col_bits):
        pairs = [
            (r * col_count + c, (r ^ row_bits) * col_count + (c ^ col_bits))
            for r in range(row_count)
            for c in range(col_count)
        ]
        return lax.ppermute(value, ("row", "col"), pairs)

    packed, own_points = pack(probes, points)
    beside = swap(packed, 0, 1)
    across = swap(packed, 2, 0)
    line_points = [own_points]
    for offset in range(1, col_count // 2):
        line_points.append(swap(own_points, 0, 2 * offset))
    line_points = jnp.concatenate(line_points, axis=1)
    row_points = [line_points, swap(line_points, 1, 0)]

    row_feats, totals = product([packed], row_points, span, gain=gain)
    beside, across, *totals = lax.optimization_barrier((beside, across, *totals))
    pieces = [packed, beside, across]
    random_rows, half = 4 * span, 2 * span

    def part(value, number):
        return jnp.concatenate(
            [
                value[number * half : (number + 1) * half],
                value[random_rows + 32 * number : random_rows + 32 * (number + 1)],
            ],
            axis=0,
        )

    diagonal = [swap(part(beside, 0), 2, 0), swap(part(across, 1), 0, 1)]
    totals = product([beside], row_feats, span, totals)
    totals = product([across], row_feats, span, totals)
    pieces += diagonal
    for bit in range(2, row_count.bit_length() - 1):
        more = [swap(value, 1 << bit, 0) for value in pieces]
        totals = product(more, row_feats, span, totals)
        pieces += more
    (theirs,) = product(diagonal, row_feats[1:], span, totals[1:])
    from_sibling = swap(theirs, 1, 0)
    (mine,) = product(diagonal, row_feats[:1], span, totals[:1])
    kept, *sent = combine(mine, from_sibling, span)
    received = [swap(value, 0, 2 * (number + 1)) for number, value in enumerate(sent)]

    own_points, kept = lax.optimization_barrier((own_points, kept))
    tables = (leaf_skeleton, skeleton_one, skeleton_two, skeleton_three)
    picks, couplings_one, points_one = skeletons(place, own_points, tables, gain)
    couplings_two, points_two = couplings(
        2, place, points_one, swap(points_one, 0, 1), picks, gain
    )
    (couplings_three,) = couplings(3, place, points_two, swap(points_two, 0, 2), picks, gain)

    leaf_count = leaf_skeleton.shape[0]
    leaf_interp, interp_one, state = leaves(
        kept, received, packed, picks, couplings_one, (couplings_two, couplings_three), leaf_count
    )
    interp_two, state_two = level(2, place, state, swap(state, 0, 1), picks, couplings_two)
    upper_interp, top_state = level(
        3,
        place,
        state_two,
        swap(state_two, 0, 2),
        picks,
        couplings_three,
        (interp_one, interp_two),
    )
    return jnp.swapaxes(leaf_interp, 1, 2), jnp.swapaxes(upper_interp, 2, 3), top_state


def solution(mesh):
    placed = (
        P(None, ("row", "col"), None),
        P(None, None, ("row", "col")),
        P(("row", "col"), None),
        P(("row", "col"), None),
        P("row", None),
        P("row", None),
    )
    return jax.shard_map(
        local,
        mesh=mesh,
        in_specs=placed,
        out_specs=(
            P(("row", "col"), None, None),
            P(None, ("row", "col"), None, None),
            P(None, ("row", "col"), None, None),
        ),
        check_vma=False,
    )
```

profile of v0, /device:TPU:0, one launch (start us, length us, event | category | flops | bytes accessed | tf_op | source)
XLA Modules:
  0.0 73.8 jit_solution(18410925383724142604)
XLA Ops:
  0.6 2.0 %pack.1 = (bf16[1088,256]{1,0:T(8,128)(2,1)}, bf16[16,256]{1,0:T(8,128)(2,1)}) custom-call(bf16[4,256,256]{2,1,0:T(8,128)(2,1)} %probes_ref.1, bf16[16,4,256]{2,1,0:T(4,128)(2,1)} %points_ref.1), custom_call_target="tpu_custom_call" | custom-call | tf_op jit(solution)/shard_map/pack/pallas_call | solution.py:97
  2.6 3.0 %collective-permute-start = (bf16[1088,256]{1,0:T(8,128)(2,1)}, bf16[1088,256]{1,0:T(8,128)(2,1)S(1)}, u32[]{:S(2)}, u32[]{:S(2)}) collective-permute-start(bf16[1088,256]{1,0:T(8,128)(2,1)} %get-tuple-element.36.refs_0_.refs_4_), channel_id=1, source_target_pairs={{0,1},{1,0},{2,3},{3,2},{4,5},{5,4},{6,7},{7,6},{8,9},{9,8},{10,11... | collective-permute-start | bytes 1671176 | tf_op jit(solution)/shard_map/ppermute | solution.py:495
  5.6 1.5 %collective-permute-start.1 = (bf16[1088,256]{1,0:T(8,128)(2,1)}, bf16[1088,256]{1,0:T(8,128)(2,1)S(1)}, u32[]{:S(2)}, u32[]{:S(2)}) collective-permute-start(bf16[1088,256]{1,0:T(8,128)(2,1)} %get-tuple-element.36.refs_0_.refs_4_), channel_id=1, source_target_pairs={{0,16},{1,17},{2,18},{3,19},{4,20},{5,21},{6,22},{7,23},{8,24},{9,... | collective-permute-start | bytes 1671176 | tf_op jit(solution)/shard_map/ppermute | solution.py:495
  7.1 1.6 %collective-permute-start.2 = (bf16[16,256]{1,0:T(8,128)(2,1)}, bf16[16,256]{1,0:T(8,128)(2,1)S(1)}, u32[]{:S(2)}, u32[]{:S(2)}) collective-permute-start(bf16[16,256]{1,0:T(8,128)(2,1)} %get-tuple-element.54.refs_1_), channel_id=1, source_target_pairs={{0,2},{1,3},{2,0},{3,1},{4,6},{5,7},{6,4},{7,5},{8,10},{9,11},{10,... | collective-permute-start | bytes 24584 | tf_op jit(solution)/shard_map/ppermute | solution.py:495
  8.7 2.6 %collective-permute-start.3 = (bf16[16,256]{1,0:T(8,128)(2,1)}, bf16[16,256]{1,0:T(8,128)(2,1)S(1)}, u32[]{:S(2)}, u32[]{:S(2)}) collective-permute-start(bf16[16,256]{1,0:T(8,128)(2,1)} %get-tuple-element.54.refs_1_), channel_id=1, source_target_pairs={{0,4},{1,5},{2,6},{3,7},{4,0},{5,1},{6,2},{7,3},{8,12},{9,13},{10,... | collective-permute-start | bytes 24584 | tf_op jit(solution)/shard_map/ppermute | solution.py:495
  11.3 0.2 collective-permute-start.4
  11.5 0.7 constant_dynamic-update-slice_fusion.3
  12.2 0.0 collective-permute-done.2
  12.2 1.2 %collective-permute-done.3 = bf16[16,256]{1,0:T(8,128)(2,1)S(1)} collective-permute-done((bf16[16,256]{1,0:T(8,128)(2,1)}, bf16[16,256]{1,0:T(8,128)(2,1)S(1)}, u32[]{:S(2)}, u32[]{:S(2)}) %collective-permute-start.3) | collective-permute-done | bytes 8224 | tf_op jit(solution)/shard_map/ppermute | solution.py:495
  13.5 3.5 %collective-permute-done.4 = bf16[16,256]{1,0:T(8,128)(2,1)S(1)} collective-permute-done((bf16[16,256]{1,0:T(8,128)(2,1)}, bf16[16,256]{1,0:T(8,128)(2,1)S(1)}, u32[]{:S(2)}, u32[]{:S(2)}) %collective-permute-start.4) | collective-permute-done | bytes 8224 | tf_op jit(solution)/shard_map/ppermute | solution.py:495
  17.0 0.0 collective-permute-start.5
  17.0 1.2 %collective-permute-done.5.refs_2_ = bf16[16,1024]{1,0:T(8,128)(2,1)S(1)} collective-permute-done((bf16[16,1024]{1,0:T(8,128)(2,1)S(1)}, bf16[16,1024]{1,0:T(8,128)(2,1)S(1)}, u32[]{:S(2)}, u32[]{:S(2)}) %collective-permute-start.5) | collective-permute-done | bytes 32800 | tf_op jit(solution)/shard_map/ppermute | solution.py:495
  18.2 0.0 copy-start
  18.2 1.1 %copy-done = bf16[1088,256]{1,0:T(8,128)(2,1)S(1)} copy-done((bf16[1088,256]{1,0:T(8,128)(2,1)S(1)}, bf16[1088,256]{1,0:T(8,128)(2,1)}, u32[]{:S(2)}) %copy-start) | copy-done | bytes 557080
  19.2 2.5 %product.5 = (bf16[1024,64]{1,0:T(8,128)(2,1)S(1)}, bf16[1024,64]{1,0:T(8,128)(2,1)S(1)}, f32[1024,256]{1,0:T(8,128)S(1)}, f32[1024,256]{1,0:T(8,128)S(1)}) custom-call(bf16[1088,256]{1,0:T(8,128)(2,1)S(1)} %copy-done, bf16[16,1024]{1,0:T(8,128)(2,1)S(1)} %constant_dynamic-update-slice_fusion.refs_1_, bf16[16,1024]{1,0:T(8,128)(2,1)S(1)} %collective-permute-done.5.refs_2_), custom_call_target="tpu_custom_call" | custom-call | tf_op jit(solution)/shard_map/product/pallas_call | solution.py:173
  21.7 0.0 collective-permute-done.refs_0_
  21.8 0.0 copy-start.2
  21.8 0.0 collective-permute-done.1.refs_0_
  21.8 0.8 %copy-done.2 = bf16[1088,256]{1,0:T(8,128)(2,1)} copy-done((bf16[1088,256]{1,0:T(8,128)(2,1)}, bf16[1088,256]{1,0:T(8,128)(2,1)S(1)}, u32[]{:S(2)}) %copy-start.2) | copy-done | bytes 557080
  22.6 0.0 slice-start
  22.6 0.0 slice-start.1
  22.6 0.0 copy-start.3
  22.6 0.6 collective-permute-start.7
  23.2 0.3 slice-done
  23.6 0.0 slice-done.1
  23.6 0.6 collective-permute-start.6
  24.2 0.0 copy-done.3
  24.2 2.5 %product.6 = (f32[1024,256]{1,0:T(8,128)S(1)}, f32[1024,256]{1,0:T(8,128)S(1)}) custom-call(bf16[1088,256]{1,0:T(8,128)(2,1)S(1)} %copy-done.3, bf16[1024,64]{1,0:T(8,128)(2,1)S(1)} %get-tuple-element.41.refs_1_.refs_2_, bf16[1024,64]{1,0:T(8,128)(2,1)S(1)} %get-tuple-element.42.refs_2_, f32[1024,256]{1,0:T(8,128)S(1)} %get-tuple-element.43.refs_3_, ...), custom_call_target="tpu_custom_call" | custom-call | tf_op jit(solution)/shard_map/product/pallas_call | solution.py:173
  26.6 2.5 %product.7 = (f32[1024,256]{1,0:T(8,128)S(1)}, f32[1024,256]{1,0:T(8,128)S(1)}) custom-call(bf16[1088,256]{1,0:T(8,128)(2,1)S(1)} %collective-permute-done.1.refs_0_, bf16[1024,64]{1,0:T(8,128)(2,1)S(1)} %get-tuple-element.41.refs_1_.refs_2_, bf16[1024,64]{1,0:T(8,128)(2,1)S(1)} %get-tuple-element.42.refs_2_, f32[1024,256]{1,0:T(8,128)S(1)} %get-tuple-element.45.refs_3_, ...), custom_call_target="tpu_custom_call" | custom-call | tf_op jit(solution)/shard_map/product/pallas_call | solution.py:173
  29.1 2.3 %collective-permute-done.7.refs_1_ = bf16[544,256]{1,0:T(8,128)(2,1)S(1)} collective-permute-done((bf16[544,256]{1,0:T(8,128)(2,1)S(1)}, bf16[544,256]{1,0:T(8,128)(2,1)S(1)}, u32[]{:S(2)}, u32[]{:S(2)}) %collective-permute-start.7) | collective-permute-done | bytes 278560 | tf_op jit(solution)/shard_map/ppermute | solution.py:495
  31.4 0.9 %collective-permute-done.6.refs_0_ = bf16[544,256]{1,0:T(8,128)(2,1)S(1)} collective-permute-done((bf16[544,256]{1,0:T(8,128)(2,1)S(1)}, bf16[544,256]{1,0:T(8,128)(2,1)S(1)}, u32[]{:S(2)}, u32[]{:S(2)}) %collective-permute-start.6) | collective-permute-done | bytes 278560 | tf_op jit(solution)/shard_map/ppermute | solution.py:495
  32.4 1.4 %product.9 = f32[1024,256]{1,0:T(8,128)S(1)} custom-call(bf16[544,256]{1,0:T(8,128)(2,1)S(1)} %collective-permute-done.6.refs_0_, bf16[544,256]{1,0:T(8,128)(2,1)S(1)} %collective-permute-done.7.refs_1_, bf16[1024,64]{1,0:T(8,128)(2,1)S(1)} %get-tuple-element.42.refs_2_, f32[1024,256]{1,0:T(8,128)S(1)} %get-tuple-element.48.refs_3_), custom_call_target="tpu_custom_call" | custom-call | tf_op jit(solution)/shard_map/product/pallas_call | solution.py:173
  33.8 0.1 collective-permute-start.8
  33.9 1.4 %product.8.refs_0_ = f32[1024,256]{1,0:T(8,128)S(1)} custom-call(bf16[544,256]{1,0:T(8,128)(2,1)S(1)} %collective-permute-done.6.refs_0_, bf16[544,256]{1,0:T(8,128)(2,1)S(1)} %collective-permute-done.7.refs_1_, bf16[1024,64]{1,0:T(8,128)(2,1)S(1)} %get-tuple-element.41.refs_1_.refs_2_, f32[1024,256]{1,0:T(8,128)S(1)} %get-tuple-element.47.refs_3_), custom_call_target="tpu_custom_call" | custom-call | tf_op jit(solution)/shard_map/product/pallas_call | solution.py:173
  35.3 1.2 %collective-permute-done.8.refs_1_ = f32[1024,256]{1,0:T(8,128)S(1)} collective-permute-done((f32[1024,256]{1,0:T(8,128)S(1)}, f32[1024,256]{1,0:T(8,128)S(1)}, u32[]{:S(2)}, u32[]{:S(2)}) %collective-permute-start.8) | collective-permute-done | bytes 1048608 | tf_op jit(solution)/shard_map/ppermute | solution.py:495
  36.5 0.0 copy-start.7
  36.5 0.1 combine.1
  36.6 0.1 collective-permute-start.10
  36.7 1.0 %collective-permute-start.11 = (bf16[256,256]{1,0:T(8,128)(2,1)S(1)}, bf16[256,256]{1,0:T(8,128)(2,1)S(1)}, u32[]{:S(2)}, u32[]{:S(2)}) collective-permute-start(bf16[256,256]{1,0:T(8,128)(2,1)S(1)} %get-tuple-element.53), channel_id=1, source_target_pairs={{0,6},{1,7},{2,4},{3,5},{4,2},{5,3},{6,0},{7,1},{8,14},{9,15},{10,... | collective-permute-start | bytes 393224 | tf_op jit(solution)/shard_map/ppermute | solution.py:495
  37.7 2.5 %collective-permute-start.9 = (bf16[256,256]{1,0:T(8,128)(2,1)S(1)}, bf16[256,256]{1,0:T(8,128)(2,1)S(1)}, u32[]{:S(2)}, u32[]{:S(2)}) collective-permute-start(bf16[256,256]{1,0:T(8,128)(2,1)S(1)} %get-tuple-element.51), channel_id=1, source_target_pairs={{0,2},{1,3},{2,0},{3,1},{4,6},{5,7},{6,4},{7,5},{8,10},{9,11},{10,... | collective-permute-start | bytes 393224 | tf_op jit(solution)/shard_map/ppermute | solution.py:495
  40.2 0.1 pad_add_fusion.refs_0_
  40.3 0.0 copy-done.7
  40.3 0.6 copy-done.4
  40.9 0.0 copy-done.5
  40.9 0.1 copy-done.6
  41.0 0.0 copy-done.8
  41.0 0.9 %skeletons.1 = (bf16[5,64,128]{2,1,0:T(8,128)(2,1)S(1)}, f32[2,64,128]{2,1,0:T(8,128)S(1)}, bf16[16,64]{1,0:T(8,128)(2,1)S(1)}) custom-call(s32[4]{0:T(128)S(1)} %pad_add_fusion.refs_0_, bf16[16,256]{1,0:T(8,128)(2,1)S(1)} %copy-done.4, s32[2,64]{1,0:T(2,128)S(1)} %copy-done.6, s32[1,64]{1,0:T(1,128)S(1)} %copy-done.8, s32[4,64]{1,0:T(4,128)S(1)} %copy-done.5, ...), custom_call_target="tpu_custom_call" | custom-call | tf_op jit(solution)/shard_map/skeletons/pallas_call | solution.py:445
  41.9 1.0 %collective-permute-start.12 = (bf16[16,64]{1,0:T(8,128)(2,1)S(1)}, bf16[16,64]{1,0:T(8,128)(2,1)S(1)}, u32[]{:S(2)}, u32[]{:S(2)}) collective-permute-start(bf16[16,64]{1,0:T(8,128)(2,1)S(1)} %get-tuple-element.57.refs_1_), channel_id=1, source_target_pairs={{0,1},{1,0},{2,3},{3,2},{4,5},{5,4},{6,7},{7,6},{8,9},{9,8},{10,11... | collective-permute-start | bytes 6152 | tf_op jit(solution)/shard_map/ppermute | solution.py:495
  42.8 2.7 %collective-permute-done.12.refs_2_ = bf16[16,64]{1,0:T(8,128)(2,1)S(1)} collective-permute-done((bf16[16,64]{1,0:T(8,128)(2,1)S(1)}, bf16[16,64]{1,0:T(8,128)(2,1)S(1)}, u32[]{:S(2)}, u32[]{:S(2)}) %collective-permute-start.12) | collective-permute-done | bytes 2080 | tf_op jit(solution)/shard_map/ppermute | solution.py:495
  45.5 0.8 %couplings.2 = (f32[2,64,128]{2,1,0:T(8,128)S(1)}, bf16[16,64]{1,0:T(8,128)(2,1)S(1)}) custom-call(s32[4]{0:T(128)S(1)} %pad_add_fusion.refs_0_, bf16[16,64]{1,0:T(8,128)(2,1)S(1)} %get-tuple-element.57.refs_1_, bf16[16,64]{1,0:T(8,128)(2,1)S(1)} %collective-permute-done.12.refs_2_, bf16[5,64,128]{2,1,0:T(8,128)(2,1)S(1)} %get-tuple-element.55.refs_3_.refs_5_), custom_call_target="tpu_custom_call" | custom-call | tf_op jit(solution)/shard_map/couplings/pallas_call | solution.py:472
  46.3 0.1 collective-permute-start.13
  46.4 3.6 %collective-permute-done.13.refs_2_ = bf16[16,64]{1,0:T(8,128)(2,1)S(1)} collective-permute-done((bf16[16,64]{1,0:T(8,128)(2,1)S(1)}, bf16[16,64]{1,0:T(8,128)(2,1)S(1)}, u32[]{:S(2)}, u32[]{:S(2)}) %collective-permute-start.13) | collective-permute-done | bytes 2080 | tf_op jit(solution)/shard_map/ppermute | solution.py:495
  50.0 0.8 %couplings.3.refs_8_.refs_4_ = f32[2,64,128]{2,1,0:T(8,128)S(1)} custom-call(s32[4]{0:T(128)S(1)} %pad_add_fusion.refs_0_, bf16[16,64]{1,0:T(8,128)(2,1)S(1)} %get-tuple-element.59.refs_1_, bf16[16,64]{1,0:T(8,128)(2,1)S(1)} %collective-permute-done.13.refs_2_, bf16[5,64,128]{2,1,0:T(8,128)(2,1)S(1)} %get-tuple-element.55.refs_3_.refs_5_), custom_call_target="tpu_custom_call" | custom-call | tf_op jit(solution)/shard_map/couplings/pallas_call | solution.py:472
  50.7 0.0 collective-permute-done.10.refs_2_
  50.7 0.0 collective-permute-done.11.refs_3_
  50.8 0.0 collective-permute-done.9.refs_1_
  50.8 0.0 copy-done.1
  50.8 5.7 %leaves.1 = (f32[2,64,128]{2,1,0:T(8,128)}, f32[64,128]{1,0:T(8,128)S(1)}, f32[128,256]{1,0:T(8,128)S(1)}) custom-call(f32[256,256]{1,0:T(8,128)S(1)} %get-tuple-element.50.refs_0_, bf16[256,256]{1,0:T(8,128)(2,1)S(1)} %collective-permute-done.9.refs_1_, bf16[256,256]{1,0:T(8,128)(2,1)S(1)} %collective-permute-done.10.refs_2_, ...), custom_call_target="tpu_custom_call" | custom-call | tf_op jit(solution)/shard_map/leaves/pallas_call | solution.py:321
  56.5 1.0 %collective-permute-start.14 = (f32[128,256]{1,0:T(8,128)S(1)}, f32[128,256]{1,0:T(8,128)S(1)}, u32[]{:S(2)}, u32[]{:S(2)}) collective-permute-start(f32[128,256]{1,0:T(8,128)S(1)} %get-tuple-element.61.refs_1_), channel_id=1, source_target_pairs={{0,1},{1,0},{2,3},{3,2},{4,5},{5,4},{6,7},{7,6},{8,9},{9,8},{10,11... | collective-permute-start | bytes 393224 | tf_op jit(solution)/shard_map/ppermute | solution.py:495
  57.5 4.1 %collective-permute-done.14.refs_2_ = f32[128,256]{1,0:T(8,128)S(1)} collective-permute-done((f32[128,256]{1,0:T(8,128)S(1)}, f32[128,256]{1,0:T(8,128)S(1)}, u32[]{:S(2)}, u32[]{:S(2)}) %collective-permute-start.14) | collective-permute-done | bytes 131104 | tf_op jit(solution)/shard_map/ppermute | solution.py:495
  61.5 3.2 %level.2 = (f32[64,128]{1,0:T(8,128)S(1)}, f32[128,256]{1,0:T(8,128)S(1)}) custom-call(s32[4]{0:T(128)S(1)} %pad_add_fusion.refs_0_, f32[128,256]{1,0:T(8,128)S(1)} %get-tuple-element.61.refs_1_, f32[128,256]{1,0:T(8,128)S(1)} %collective-permute-done.14.refs_2_, bf16[5,64,128]{2,1,0:T(8,128)(2,1)S(1)} %get-tuple-element.55.refs_3_.refs_5_, ...), custom_call_target="tpu_custom_call" | custom-call | tf_op jit(solution)/shard_map/level/pallas_call | solution.py:398
  64.7 0.1 collective-permute-start.15
  64.8 5.0 %collective-permute-done.15.refs_2_ = f32[128,256]{1,0:T(8,128)S(1)} collective-permute-done((f32[128,256]{1,0:T(8,128)S(1)}, f32[128,256]{1,0:T(8,128)S(1)}, u32[]{:S(2)}, u32[]{:S(2)}) %collective-permute-start.15) | collective-permute-done | bytes 131104 | tf_op jit(solution)/shard_map/ppermute | solution.py:495
  69.8 3.9 %level.3 = (f32[3,1,64,128]{3,2,1,0:T(8,128)}, f32[2,1,64,256]{3,2,1,0:T(8,128)}) custom-call(s32[4]{0:T(128)S(1)} %pad_add_fusion.refs_0_, f32[128,256]{1,0:T(8,128)S(1)} %get-tuple-element.62.refs_1_, f32[128,256]{1,0:T(8,128)S(1)} %collective-permute-done.15.refs_2_, bf16[5,64,128]{2,1,0:T(8,128)(2,1)S(1)} %get-tuple-element.55.refs_3_.refs_5_, ...), custom_call_target="tpu_custom_call" | custom-call | tf_op jit(solution)/shard_map/level/pallas_call | solution.py:398
  (12 shorter events, 0.1 us)
Async XLA Ops:
  2.6 19.2 %collective-permute-start = (bf16[1088,256]{1,0:T(8,128)(2,1)}, bf16[1088,256]{1,0:T(8,128)(2,1)S(1)}, u32[]{:S(2)}, u32[]{:S(2)}) collective-permute-start(bf16[1088,256]{1,0:T(8,128)(2,1)} %get-tuple-element.36.refs_0_.refs_4_), channel_id=1, source_target_pairs={{0,1},{1,0},{2,3},{3,2},{4,5},{5,4},{6,7},{7,6},{8,9},{9,8},{10,11... | collective-permute-start | bytes 1671176 | tf_op jit(solution)/shard_map/ppermute | solution.py:495
  5.6 16.2 %collective-permute-start.1 = (bf16[1088,256]{1,0:T(8,128)(2,1)}, bf16[1088,256]{1,0:T(8,128)(2,1)S(1)}, u32[]{:S(2)}, u32[]{:S(2)}) collective-permute-start(bf16[1088,256]{1,0:T(8,128)(2,1)} %get-tuple-element.36.refs_0_.refs_4_), channel_id=1, source_target_pairs={{0,16},{1,17},{2,18},{3,19},{4,20},{5,21},{6,22},{7,23},{8,24},{9,... | collective-permute-start | bytes 1671176 | tf_op jit(solution)/shard_map/ppermute | solution.py:495
  7.1 5.1 %collective-permute-start.2 = (bf16[16,256]{1,0:T(8,128)(2,1)}, bf16[16,256]{1,0:T(8,128)(2,1)S(1)}, u32[]{:S(2)}, u32[]{:S(2)}) collective-permute-start(bf16[16,256]{1,0:T(8,128)(2,1)} %get-tuple-element.54.refs_1_), channel_id=1, source_target_pairs={{0,2},{1,3},{2,0},{3,1},{4,6},{5,7},{6,4},{7,5},{8,10},{9,11},{10,... | collective-permute-start | bytes 24584 | tf_op jit(solution)/shard_map/ppermute | solution.py:495
  8.7 4.8 %collective-permute-start.3 = (bf16[16,256]{1,0:T(8,128)(2,1)}, bf16[16,256]{1,0:T(8,128)(2,1)S(1)}, u32[]{:S(2)}, u32[]{:S(2)}) collective-permute-start(bf16[16,256]{1,0:T(8,128)(2,1)} %get-tuple-element.54.refs_1_), channel_id=1, source_target_pairs={{0,4},{1,5},{2,6},{3,7},{4,0},{5,1},{6,2},{7,3},{8,12},{9,13},{10,... | collective-permute-start | bytes 24584 | tf_op jit(solution)/shard_map/ppermute | solution.py:495
  11.3 5.7 %collective-permute-start.4 = (bf16[16,256]{1,0:T(8,128)(2,1)}, bf16[16,256]{1,0:T(8,128)(2,1)S(1)}, u32[]{:S(2)}, u32[]{:S(2)}) collective-permute-start(bf16[16,256]{1,0:T(8,128)(2,1)} %get-tuple-element.54.refs_1_), channel_id=1, source_target_pairs={{0,6},{1,7},{2,4},{3,5},{4,2},{5,3},{6,0},{7,1},{8,14},{9,15},{10,... | collective-permute-start | bytes 24584 | tf_op jit(solution)/shard_map/ppermute | solution.py:495
  17.0 1.2 %collective-permute-start.5 = (bf16[16,1024]{1,0:T(8,128)(2,1)S(1)}, bf16[16,1024]{1,0:T(8,128)(2,1)S(1)}, u32[]{:S(2)}, u32[]{:S(2)}) collective-permute-start(bf16[16,1024]{1,0:T(8,128)(2,1)S(1)} %constant_dynamic-update-slice_fusion.refs_1_), channel_id=1, source_target_pairs={{0,8},{1,9},{2,10},{3,11},{4,12},{5,13},{6,14},{7,15},{8,0},{9,1},... | collective-permute-start | bytes 98312 | tf_op jit(solution)/shard_map/ppermute | solution.py:495
  18.2 1.1 %copy-start = (bf16[1088,256]{1,0:T(8,128)(2,1)S(1)}, bf16[1088,256]{1,0:T(8,128)(2,1)}, u32[]{:S(2)}) copy-start(bf16[1088,256]{1,0:T(8,128)(2,1)} %get-tuple-element.36.refs_0_.refs_4_) | copy-start | bytes 1671172
  21.8 0.8 %copy-start.2 = (bf16[1088,256]{1,0:T(8,128)(2,1)}, bf16[1088,256]{1,0:T(8,128)(2,1)S(1)}, u32[]{:S(2)}) copy-start(bf16[1088,256]{1,0:T(8,128)(2,1)S(1)} %collective-permute-done.refs_0_) | copy-start | bytes 1671172
  22.6 0.9 %slice-start = ((bf16[1088,256]{1,0:T(8,128)(2,1)}), bf16[512,256]{1,0:T(8,128)(2,1)S(1)}, s32[]{:S(2)}) async-start(bf16[1088,256]{1,0:T(8,128)(2,1)} %copy-done.2), calls=%async_computation | async-start | bytes 524288 | tf_op jit(solution)/shard_map/slice | solution.py:514
  22.6 1.0 %slice-start.1 = ((bf16[1088,256]{1,0:T(8,128)(2,1)}), bf16[32,256]{1,0:T(8,128)(2,1)S(1)}, s32[]{:S(2)}) async-start(bf16[1088,256]{1,0:T(8,128)(2,1)} %copy-done.2), calls=%async_computation.1 | async-start | bytes 32768 | tf_op jit(solution)/shard_map/slice | solution.py:515
  22.6 1.5 %copy-start.3 = (bf16[1088,256]{1,0:T(8,128)(2,1)S(1)}, bf16[1088,256]{1,0:T(8,128)(2,1)}, u32[]{:S(2)}) copy-start(bf16[1088,256]{1,0:T(8,128)(2,1)} %copy-done.2) | copy-start | bytes 1671172
  22.6 8.8 %collective-permute-start.7 = (bf16[544,256]{1,0:T(8,128)(2,1)S(1)}, bf16[544,256]{1,0:T(8,128)(2,1)S(1)}, u32[]{:S(2)}, u32[]{:S(2)}) collective-permute-start(bf16[544,256]{1,0:T(8,128)(2,1)S(1)} %pad_maximum_fusion.1), channel_id=1, source_target_pairs={{0,1},{1,0},{2,3},{3,2},{4,5},{5,4},{6,7},{7,6},{8,9},{9,8},{10,11... | collective-permute-start | bytes 835592 | tf_op jit(solution)/shard_map/ppermute | solution.py:495
  23.6 8.8 %collective-permute-start.6 = (bf16[544,256]{1,0:T(8,128)(2,1)S(1)}, bf16[544,256]{1,0:T(8,128)(2,1)S(1)}, u32[]{:S(2)}, u32[]{:S(2)}) collective-permute-start(bf16[544,256]{1,0:T(8,128)(2,1)S(1)} %pad_maximum_fusion), channel_id=1, source_target_pairs={{0,16},{1,17},{2,18},{3,19},{4,20},{5,21},{6,22},{7,23},{8,24},{9,... | collective-permute-start | bytes 835592 | tf_op jit(solution)/shard_map/ppermute | solution.py:495
  33.8 2.7 %collective-permute-start.8 = (f32[1024,256]{1,0:T(8,128)S(1)}, f32[1024,256]{1,0:T(8,128)S(1)}, u32[]{:S(2)}, u32[]{:S(2)}) collective-permute-start(f32[1024,256]{1,0:T(8,128)S(1)} %product.9), channel_id=1, source_target_pairs={{0,8},{1,9},{2,10},{3,11},{4,12},{5,13},{6,14},{7,15},{8,0},{9,1},... | collective-permute-start | bytes 3145736 | tf_op jit(solution)/shard_map/ppermute | solution.py:495
  36.5 3.7 %copy-start.7 = (s32[2,64]{1,0:T(2,128)S(1)}, s32[2,64]{1,0:T(2,128)}, u32[]{:S(2)}) copy-start(s32[2,64]{1,0:T(2,128)} %refs_5_.1) | copy-start | bytes 1540
  36.5 14.2 %copy-start.1 = (bf16[1088,256]{1,0:T(8,128)(2,1)S(1)}, bf16[1088,256]{1,0:T(8,128)(2,1)}, u32[]{:S(2)}) copy-start(bf16[1088,256]{1,0:T(8,128)(2,1)} %get-tuple-element.36.refs_0_.refs_4_) | copy-start | bytes 1671172
  36.6 14.1 %collective-permute-start.10 = (bf16[256,256]{1,0:T(8,128)(2,1)S(1)}, bf16[256,256]{1,0:T(8,128)(2,1)S(1)}, u32[]{:S(2)}, u32[]{:S(2)}) collective-permute-start(bf16[256,256]{1,0:T(8,128)(2,1)S(1)} %get-tuple-element.52), channel_id=1, source_target_pairs={{0,4},{1,5},{2,6},{3,7},{4,0},{5,1},{6,2},{7,3},{8,12},{9,13},{10,... | collective-permute-start | bytes 393224 | tf_op jit(solution)/shard_map/ppermute | solution.py:495
  36.7 14.0 %collective-permute-start.11 = (bf16[256,256]{1,0:T(8,128)(2,1)S(1)}, bf16[256,256]{1,0:T(8,128)(2,1)S(1)}, u32[]{:S(2)}, u32[]{:S(2)}) collective-permute-start(bf16[256,256]{1,0:T(8,128)(2,1)S(1)} %get-tuple-element.53), channel_id=1, source_target_pairs={{0,6},{1,7},{2,4},{3,5},{4,2},{5,3},{6,0},{7,1},{8,14},{9,15},{10,... | collective-permute-start | bytes 393224 | tf_op jit(solution)/shard_map/ppermute | solution.py:495
  37.7 13.0 %collective-permute-start.9 = (bf16[256,256]{1,0:T(8,128)(2,1)S(1)}, bf16[256,256]{1,0:T(8,128)(2,1)S(1)}, u32[]{:S(2)}, u32[]{:S(2)}) collective-permute-start(bf16[256,256]{1,0:T(8,128)(2,1)S(1)} %get-tuple-element.51), channel_id=1, source_target_pairs={{0,2},{1,3},{2,0},{3,1},{4,6},{5,7},{6,4},{7,5},{8,10},{9,11},{10,... | collective-permute-start | bytes 393224 | tf_op jit(solution)/shard_map/ppermute | solution.py:495
  40.2 0.7 copy-start.4
  40.2 0.7 copy-start.5
  40.3 0.7 copy-start.6
  40.3 0.7 copy-start.8
  41.9 3.7 %collective-permute-start.12 = (bf16[16,64]{1,0:T(8,128)(2,1)S(1)}, bf16[16,64]{1,0:T(8,128)(2,1)S(1)}, u32[]{:S(2)}, u32[]{:S(2)}) collective-permute-start(bf16[16,64]{1,0:T(8,128)(2,1)S(1)} %get-tuple-element.57.refs_1_), channel_id=1, source_target_pairs={{0,1},{1,0},{2,3},{3,2},{4,5},{5,4},{6,7},{7,6},{8,9},{9,8},{10,11... | collective-permute-start | bytes 6152 | tf_op jit(solution)/shard_map/ppermute | solution.py:495
  46.3 3.7 %collective-permute-start.13 = (bf16[16,64]{1,0:T(8,128)(2,1)S(1)}, bf16[16,64]{1,0:T(8,128)(2,1)S(1)}, u32[]{:S(2)}, u32[]{:S(2)}) collective-permute-start(bf16[16,64]{1,0:T(8,128)(2,1)S(1)} %get-tuple-element.59.refs_1_), channel_id=1, source_target_pairs={{0,2},{1,3},{2,0},{3,1},{4,6},{5,7},{6,4},{7,5},{8,10},{9,11},{10,... | collective-permute-start | bytes 6152 | tf_op jit(solution)/shard_map/ppermute | solution.py:495
  56.5 5.0 %collective-permute-start.14 = (f32[128,256]{1,0:T(8,128)S(1)}, f32[128,256]{1,0:T(8,128)S(1)}, u32[]{:S(2)}, u32[]{:S(2)}) collective-permute-start(f32[128,256]{1,0:T(8,128)S(1)} %get-tuple-element.61.refs_1_), channel_id=1, source_target_pairs={{0,1},{1,0},{2,3},{3,2},{4,5},{5,4},{6,7},{7,6},{8,9},{9,8},{10,11... | collective-permute-start | bytes 393224 | tf_op jit(solution)/shard_map/ppermute | solution.py:495
  64.7 5.0 %collective-permute-start.15 = (f32[128,256]{1,0:T(8,128)S(1)}, f32[128,256]{1,0:T(8,128)S(1)}, u32[]{:S(2)}, u32[]{:S(2)}) collective-permute-start(f32[128,256]{1,0:T(8,128)S(1)} %get-tuple-element.62.refs_1_), channel_id=1, source_target_pairs={{0,2},{1,3},{2,0},{3,1},{4,6},{5,7},{6,4},{7,5},{8,10},{9,11},{10,... | collective-permute-start | bytes 393224 | tf_op jit(solution)/shard_map/ppermute | solution.py:495
where the time goes:
time: 74.1 us; the launch traced here: 73.8 us
  Pallas kernels  27.6 us (37%)
  waiting for transfers between devices  25.7 us (35%)
  starting transfers between devices  15.8 us (21%)
  local copies, waits for them, and re-layouts  3.62 us (5%)
  between operations  1 us (1%)
    ppermute x16, waiting for transfers between devices, swap(): return lax.ppermute(value, ('row', 'col'), pairs)  25.7 us
    ppermute x16, starting transfers between devices, swap(): return lax.ppermute(value, ('row', 'col'), pairs)  15.8 us
    pallas_call x5, Pallas kernels, product(): pl.pallas_call(lambda *refs: product_body(gain, span, first, len(sources)...  10.3 us
    pallas_call x2, Pallas kernels, level(): pl.pallas_call(lambda *refs: level_body(number, *refs), out_shape=out_sha...  7.06 us
    pallas_call x1, Pallas kernels, leaves(): pl.pallas_call(lambda *refs: leaves_body(len(others), *refs), out_shape=(...  5.72 us
    unnamed x21, local copies, waits for them, and re-layouts  3.27 us
    pallas_call x1, Pallas kernels, pack(): pl.pallas_call(pack_body, out_shape=(jax.ShapeDtypeStruct((quarters * (sp...  1.96 us
    pallas_call x2, Pallas kernels, couplings(): pl.pallas_call(lambda *refs: couplings_body(gain, number, *refs), out_sha...  1.53 us
  transfers between devices with their start and end apart: 16, of which 10 were waited for; matrix products, arithmetic and copies ran while one was open for 1% of the time, Pallas kernels for 15%

commit v1 on v0

--- a/solution.py
+++ b/solution.py
@@ -14,7 +14,7 @@
 VMEM = pl.BlockSpec(memory_space=pltpu.VMEM)
 SMEM = pl.BlockSpec(memory_space=pltpu.SMEM)
 COST = pl.CostEstimate(flops=0, bytes_accessed=0, transcendentals=0)
-PARAMS = pltpu.CompilerParams(vmem_limit_bytes=40 << 20)
+PARAMS = pltpu.CompilerParams(vmem_limit_bytes=16 << 20)
 
 
 def chebyshev_constants():
@@ -100,12 +100,13 @@
             jax.ShapeDtypeStruct((quarters * (span + 16), samples), BF16),
             jax.ShapeDtypeStruct((16, span), BF16),
         ),
-        in_specs=[pl.BlockSpec(memory_space=pl.ANY)] * 2,
+        in_specs=[pl.BlockSpec(memory_space=pltpu.HBM)] * 2,
         scratch_shapes=[
             pltpu.VMEM(points.shape, BF16),
             pltpu.SemaphoreType.DMA((quarters + 1,)),
         ],
-        compiler_params=pltpu.CompilerParams(vmem_limit_bytes=60 << 20),
+        cost_estimate=COST,
+        compiler_params=pltpu.CompilerParams(vmem_limit_bytes=64512 << 10),
         name="pack",
     )(probes, points)
 
@@ -133,7 +134,7 @@
             put(half, start, over(entries.astype(BF16), randoms, 1, 0))
 
 
-def product_body(gain, span, first, source_count, half_count, *refs):
+def product_body(gain, span, first, own, source_count, half_count, *refs):
     refs = list(refs)
     cols_ref = refs.pop()
     take = lambda count: [refs.pop(0) for _ in range(count)]
@@ -158,27 +159,46 @@
             else:
                 total_refs[half][place, :] = old_refs[half][place, :] + value
 
-        add_source(source, row_refs, cols_ref, put, span, first and number == 0)
-
-
-def product(sources, rows, span, totals=None, gain=None):
+        add_source(source, row_refs, cols_ref, put, span, first and own and number == 0)
+
+
+def product(sources, rows, span, totals=None, gain=None, own=True):
     samples = sources[0].shape[1]
     first = totals is None
-    halves = len(rows)
+    count = len(rows)
     counts = [half.shape[1] if first else half.shape[0] for half in rows]
     columns = max(s.shape[0] // (span + 16) * span for s in sources)
     out = [jax.ShapeDtypeStruct((count, samples), F32) for count in counts]
     if first:
         out = [jax.ShapeDtypeStruct((count, 64), BF16) for count in counts] + out
     out = pl.pallas_call(
-        lambda *refs: product_body(gain, span, first, len(sources), halves, *refs),
+        lambda *refs: product_body(gain, span, first, own, len(sources), count, *refs),
         out_shape=out,
         scratch_shapes=[pltpu.VMEM((64, columns), BF16)],
         cost_estimate=COST,
         compiler_params=PARAMS,
         name="product",
     )(*sources, *rows, *([] if first else totals))
-    return (out[:halves], out[halves:]) if first else out
+    return (out[:count], out[count:]) if first else out
+
+
+def halves_body(quarters, span, *refs):
+    size = quarters * span // 2
+    for number, (source_ref, half_ref) in enumerate(zip(refs[:2], refs[2:])):
+        feats = quarters * span + 8 * quarters * number
+        half_ref[pl.ds(0, size), :] = source_ref[pl.ds(size * number, size), :]
+        half_ref[pl.ds(size, 8 * quarters), :] = source_ref[pl.ds(feats, 8 * quarters), :]
+
+
+def halves(first, second, span):
+    rows, samples = first.shape
+    return pl.pallas_call(
+        lambda *refs: halves_body(rows // (span + 16), span, *refs),
+        out_shape=[jax.ShapeDtypeStruct((rows // 2, samples), BF16)] * 2,
+        cost_estimate=COST,
+        compiler_params=PARAMS,
+        name="halves",
+    )(first, second)
 
 
 def combine_body(span, mine_ref, theirs_ref, own_ref, *sent_refs):
@@ -194,6 +214,7 @@
         lambda *refs: combine_body(span, *refs),
         out_shape=[jax.ShapeDtypeStruct((span, samples), F32)]
         + [jax.ShapeDtypeStruct((span, samples), BF16)] * (rows // span - 1),
+        cost_estimate=COST,
         compiler_params=PARAMS,
         name="combine",
     )(mine, theirs)
@@ -241,14 +262,11 @@
     )
 
 
-def interpolate(stacks, picks_list, early=None):
-    rank, pool = picks_list[0].shape
+def interpolate(stacks, skeletons):
+    rank, pool = skeletons[0].shape[0], stacks[0].shape[0]
     place = lax.broadcasted_iota(jnp.int32, (rank, 2 * rank), 0)
     other = lax.broadcasted_iota(jnp.int32, (rank, 2 * rank), 1)
     eyes = jnp.where((other == place) | (other == place + rank), 1.0, 0.0)
-    skeletons = [select_rows(picks, stack) for picks, stack in zip(picks_list, stacks)]
-    if early is not None:
-        early(*skeletons)
     states = []
     for skeleton, stack in zip(skeletons, stacks):
         products = wide_product(skeleton, jnp.concatenate([stack, skeleton, skeleton], axis=0), 1)
@@ -267,26 +285,21 @@
             solved = solved + both[:, :pool] * (1.0 / tau)
             later.append((solved, None if last else 2.0 * both[:, pool:] - eyes, inverse))
         states = later
-    return [
-        (solved * (inverse * FRONT), skeleton)
-        for (solved, _, inverse), skeleton in zip(states, skeletons)
-    ]
-
-
-def merge(first, second, couplings_ref, picks, early=None):
-    first_samples, first_reduced = first
-    second_samples, second_reduced = second
-    first_parts, second_parts = split(first_reduced), split(second_reduced)
-    stacked = jnp.concatenate(
-        [
-            first_samples - twice_product(split(couplings_ref[0]), second_parts),
-            second_samples - twice_product(split(couplings_ref[1]), first_parts),
-        ],
-        axis=0,
-    )
-    ((interp, skeleton),) = interpolate([stacked], [picks], early)
-    reduced = wide_product(interp, jnp.concatenate([first_reduced, second_reduced], axis=0), 0)
-    return interp, skeleton, reduced
+    return [solved * (inverse * FRONT) for solved, _, inverse in states]
+
+
+def merge(samples, reduced, coupling, picks, early=None):
+    pool = samples.shape[0]
+    high, middle, low = split(reduced)
+    coupled = over(
+        coupling, jnp.concatenate([high, middle, high, middle, high, low], axis=0), 1, 0
+    )
+    stacked = samples - coupled[:pool]
+    skeleton = select_rows(picks, samples) - coupled[pool:]
+    if early is not None:
+        early(skeleton)
+    (interp,) = interpolate([stacked], [skeleton])
+    return interp, skeleton, wide_product(interp, reduced, 0)
 
 
 def leaves_body(received, *refs):
@@ -299,16 +312,19 @@
         total = total + other[...].astype(F32)
     count = total.shape[0] // LEAF
     stacks = [total[leaf * LEAF : (leaf + 1) * LEAF] for leaf in range(count)]
-    children = []
-    for leaf, (interp, skeleton) in enumerate(
-        interpolate(stacks, [picks_ref[leaf] for leaf in range(count)])
-    ):
+    skeletons = [select_rows(picks_ref[leaf], stack) for leaf, stack in enumerate(stacks)]
+    reduced = []
+    for leaf, interp in enumerate(interpolate(stacks, skeletons)):
         held_ref[leaf] = interp
-        randoms = source_ref[pl.ds(leaf * LEAF, LEAF), :]
-        children.append((skeleton, exact_product(interp, randoms)))
+        reduced.append(exact_product(interp, source_ref[pl.ds(leaf * LEAF, LEAF), :]))
     copy = pltpu.make_async_copy(held_ref, leaf_ref, sem)
     copy.start()
-    interp, skeleton, reduced = merge(*children, couplings_ref, picks_ref[count])
+    interp, skeleton, reduced = merge(
+        jnp.concatenate(skeletons, axis=0),
+        jnp.concatenate(reduced, axis=0),
+        couplings_ref[...],
+        picks_ref[count],
+    )
     upper_ref[...] = interp
     state_ref[pl.ds(0, rank), :] = skeleton
     state_ref[pl.ds(rank, rank), :] = reduced
@@ -363,9 +379,9 @@
     first = jnp.where(mine_first, mine, theirs)
     second = jnp.where(mine_first, theirs, mine)
     interp, _, reduced = merge(
-        (first[:rank], first[rank:]),
-        (second[:rank], second[rank:]),
-        couplings_ref,
+        jnp.concatenate([first[:rank], second[:rank]], axis=0),
+        jnp.concatenate([first[rank:], second[rank:]], axis=0),
+        couplings_ref[...],
         picks_ref[picks_ref.shape[0] + number - 4],
         early,
     )
@@ -413,14 +429,21 @@
 
 
 def couple(first, second, picks, gain, couplings_ref, points_ref):
-    for number, (left, right) in enumerate(((first, second), (second, first))):
-        twice = jnp.concatenate([right, right], axis=1)
-        rows = row_features(left, gain).astype(BF16)
-        couplings_ref[number] = jnp.exp2(over(rows, col_features(twice), 0, 0))
+    rank = first.shape[1]
+    points = jnp.concatenate([first, second], axis=1)
+    entries = jnp.exp2(over(row_features(points, gain).astype(BF16), col_features(points), 0, 0))
+    left = lax.broadcasted_iota(jnp.int32, entries.shape, 1) < rank
+    upper = lax.broadcasted_iota(jnp.int32, entries.shape, 0) < rank
+    entries = jnp.where(left == upper, 0.0, entries)
+    chosen = select_rows(picks.T.astype(BF16), entries)
+    high, middle, low = split(jnp.concatenate([entries, chosen], axis=0))
+    couplings_ref[...] = jnp.concatenate([high, high, middle, middle, low, high], axis=1)
     if points_ref is not None:
-        rank = first.shape[1]
-        points = over(first, picks[:rank], 1, 0) + over(second, picks[rank:], 1, 0)
-        points_ref[...] = points.astype(BF16)
+        points_ref[...] = over(points, picks, 1, 0).astype(BF16)
+
+
+def coupling_shape(rank):
+    return jax.ShapeDtypeStruct((3 * rank, 12 * rank), BF16)
 
 
 def skeletons_body(gain, place_ref, own_ref, leaf_ref, one_ref, two_ref, three_ref, *refs):
@@ -446,10 +469,11 @@
         lambda *refs: skeletons_body(gain, *refs),
         out_shape=(
             jax.ShapeDtypeStruct((leaf_count + 3, rank, LEAF), BF16),
-            jax.ShapeDtypeStruct((2, rank, 2 * rank), F32),
+            coupling_shape(rank),
             jax.ShapeDtypeStruct((16, rank), BF16),
         ),
         in_specs=[SMEM] + [VMEM] * 5,
+        cost_estimate=COST,
         compiler_params=PARAMS,
         name="skeletons",
     )(place, own_points, *tables)
@@ -466,13 +490,14 @@
 
 def couplings(number, place, mine, theirs, picks, gain):
     rank = picks.shape[1]
-    out_shape = [jax.ShapeDtypeStruct((2, rank, 2 * rank), F32)]
+    out_shape = [coupling_shape(rank)]
     if number == 2:
         out_shape.append(jax.ShapeDtypeStruct(mine.shape, BF16))
     return pl.pallas_call(
         lambda *refs: couplings_body(gain, number, *refs),
         out_shape=out_shape,
         in_specs=[SMEM] + [VMEM] * 3,
+        cost_estimate=COST,
         compiler_params=PARAMS,
         name="couplings",
     )(place, mine, theirs, picks)
@@ -503,23 +528,18 @@
     line_points = jnp.concatenate(line_points, axis=1)
     row_points = [line_points, swap(line_points, 1, 0)]
 
-    row_feats, totals = product([packed], row_points, span, gain=gain)
+    row_feats, totals = product([packed], row_points[:1], span, gain=gain)
+    more_feats, more_totals = product([packed], row_points[1:], span, gain=gain, own=False)
+    row_feats, totals = row_feats + more_feats, totals + more_totals
     beside, across, *totals = lax.optimization_barrier((beside, across, *totals))
     pieces = [packed, beside, across]
-    random_rows, half = 4 * span, 2 * span
-
-    def part(value, number):
-        return jnp.concatenate(
-            [
-                value[number * half : (number + 1) * half],
-                value[random_rows + 32 * number : random_rows + 32 * (number + 1)],
-            ],
-            axis=0,
-        )
-
-    diagonal = [swap(part(beside, 0), 2, 0), swap(part(across, 1), 0, 1)]
+    relayed = halves(beside, across, span)
+    diagonal = [swap(relayed[0], 2, 0), swap(relayed[1], 0, 1)]
     totals = product([beside], row_feats, span, totals)
     totals = product([across], row_feats, span, totals)
+    tables = (leaf_skeleton, skeleton_one, skeleton_two, skeleton_three)
+    picks, couplings_one, points_one = skeletons(place, own_points, tables, gain)
+    points_one, *totals = lax.optimization_barrier((points_one, *totals))
     pieces += diagonal
     for bit in range(2, row_count.bit_length() - 1):
         more = [swap(value, 1 << bit, 0) for value in pieces]
@@ -531,9 +551,7 @@
     kept, *sent = combine(mine, from_sibling, span)
     received = [swap(value, 0, 2 * (number + 1)) for number, value in enumerate(sent)]
 
-    own_points, kept = lax.optimization_barrier((own_points, kept))
-    tables = (leaf_skeleton, skeleton_one, skeleton_two, skeleton_three)
-    picks, couplings_one, points_one = skeletons(place, own_points, tables, gain)
+    points_one, kept = lax.optimization_barrier((points_one, kept))
     couplings_two, points_two = couplings(
         2, place, points_one, swap(points_one, 0, 1), picks, gain
     )

time: 74.1 us -> 72.8 us (0.982)
  waiting for transfers between devices: 25.7 us -> 18 us
  starting transfers between devices: 15.8 us -> 19.9 us
  Pallas kernels: 27.6 us -> 29 us
  local copies, waits for them, and re-layouts: 3.62 us -> 4.63 us
    ppermute x16, waiting for transfers between devices: 25.7 us -> 18 us  [swap(): return lax.ppermute(value, ('row', 'col'), pairs)]
    ppermute x16, starting transfers between devices: 15.8 us -> 19.9 us  [swap(): return lax.ppermute(value, ('row', 'col'), pairs)]
    unnamed x21, local copies, waits for them, and re-layouts: 3.27 us -> 4.63 us
    pallas_call x5 -> x7, Pallas kernels: 10.3 us -> 11.4 us  [the longest x6 10.7 us: product(): pl.pallas_call(lambda *refs: product_body(gain, span, first, own, len(sou...]
  transfers between devices with their start and end apart: 16 -> 16, of which waited for: 10 -> 8; matrix products, arithmetic and copies ran while one was open for 1% -> 1% of each run, Pallas kernels for 15% -> 17%
where the time goes in v1:
time: 72.8 us; the launch traced here: 72.4 us
  Pallas kernels  29 us (40%)
  starting transfers between devices  19.9 us (27%)
  waiting for transfers between devices  18 us (25%)
  local copies, waits for them, and re-layouts  4.63 us (6%)
  between operations  0.96 us (1%)
    ppermute x16, starting transfers between devices, swap(): return lax.ppermute(value, ('row', 'col'), pairs)  19.9 us
    ppermute x16, waiting for transfers between devices, swap(): return lax.ppermute(value, ('row', 'col'), pairs)  18 us
    pallas_call x6, Pallas kernels, product(): pl.pallas_call(lambda *refs: product_body(gain, span, first, own, len(sou...  10.7 us
    pallas_call x2, Pallas kernels, level(): pl.pallas_call(lambda *refs: level_body(number, *refs), out_shape=out_sha...  6.83 us
    pallas_call x1, Pallas kernels, leaves(): pl.pallas_call(lambda *refs: leaves_body(len(others), *refs), out_shape=(...  5.61 us
    unnamed x21, local copies, waits for them, and re-layouts  4.63 us
    pallas_call x1, Pallas kernels, pack(): pl.pallas_call(pack_body, out_shape=(jax.ShapeDtypeStruct((quarters * (sp...  1.97 us
    pallas_call x2, Pallas kernels, couplings(): pl.pallas_call(lambda *refs: couplings_body(gain, number, *refs), out_sha...  1.93 us
  transfers between devices with their start and end apart: 16, of which 8 were waited for; matrix products, arithmetic and copies ran while one was open for 1% of the time, Pallas kernels for 17%

profile of v1, /device:TPU:0, one launch (start us, length us, event | category | flops | bytes accessed | tf_op | source)
XLA Modules:
  0.0 72.4 jit_solution(2109886261659007056)
XLA Ops:
  0.6 2.0 %pack.1 = (bf16[1088,256]{1,0:T(8,128)(2,1)}, bf16[16,256]{1,0:T(8,128)(2,1)}) custom-call(bf16[4,256,256]{2,1,0:T(8,128)(2,1)} %probes_ref.1, bf16[16,4,256]{2,1,0:T(4,128)(2,1)} %points_ref.1), custom_call_target="tpu_custom_call" | custom-call | tf_op jit(solution)/shard_map/pack/pallas_call | solution.py:97
  2.6 3.0 %collective-permute-start.1 = (bf16[1088,256]{1,0:T(8,128)(2,1)}, bf16[1088,256]{1,0:T(8,128)(2,1)S(1)}, u32[]{:S(2)}, u32[]{:S(2)}) collective-permute-start(bf16[1088,256]{1,0:T(8,128)(2,1)} %get-tuple-element.42.refs_0_.refs_4_), channel_id=1, source_target_pairs={{0,16},{1,17},{2,18},{3,19},{4,20},{5,21},{6,22},{7,23},{8,24},{9,... | collective-permute-start | bytes 1671176 | tf_op jit(solution)/shard_map/ppermute | solution.py:520
  5.6 1.5 %collective-permute-start = (bf16[1088,256]{1,0:T(8,128)(2,1)}, bf16[1088,256]{1,0:T(8,128)(2,1)S(1)}, u32[]{:S(2)}, u32[]{:S(2)}) collective-permute-start(bf16[1088,256]{1,0:T(8,128)(2,1)} %get-tuple-element.42.refs_0_.refs_4_), channel_id=1, source_target_pairs={{0,1},{1,0},{2,3},{3,2},{4,5},{5,4},{6,7},{7,6},{8,9},{9,8},{10,11... | collective-permute-start | bytes 1671176 | tf_op jit(solution)/shard_map/ppermute | solution.py:520
  7.1 3.6 %collective-permute-start.4 = (bf16[16,256]{1,0:T(8,128)(2,1)}, bf16[16,256]{1,0:T(8,128)(2,1)S(1)}, u32[]{:S(2)}, u32[]{:S(2)}) collective-permute-start(bf16[16,256]{1,0:T(8,128)(2,1)} %get-tuple-element.40.refs_1_), channel_id=1, source_target_pairs={{0,6},{1,7},{2,4},{3,5},{4,2},{5,3},{6,0},{7,1},{8,14},{9,15},{10,... | collective-permute-start | bytes 24584 | tf_op jit(solution)/shard_map/ppermute | solution.py:520
  10.7 0.0 collective-permute-start.3
  10.7 0.8 %collective-permute-start.2 = (bf16[16,256]{1,0:T(8,128)(2,1)}, bf16[16,256]{1,0:T(8,128)(2,1)S(1)}, u32[]{:S(2)}, u32[]{:S(2)}) collective-permute-start(bf16[16,256]{1,0:T(8,128)(2,1)} %get-tuple-element.40.refs_1_), channel_id=1, source_target_pairs={{0,2},{1,3},{2,0},{3,1},{4,6},{5,7},{6,4},{7,5},{8,10},{9,11},{10,... | collective-permute-start | bytes 24584 | tf_op jit(solution)/shard_map/ppermute | solution.py:520
  11.5 0.7 %constant_dynamic-update-slice_fusion.3 = bf16[16,1024]{1,0:T(8,128)(2,1)S(1)} fusion(bf16[16,256]{1,0:T(8,128)(2,1)} %get-tuple-element.40.refs_1_), kind=kLoop, calls=%fused_computation.3 | loop fusion | bytes 16384
  12.3 2.3 %collective-permute-done.2 = bf16[16,256]{1,0:T(8,128)(2,1)S(1)} collective-permute-done((bf16[16,256]{1,0:T(8,128)(2,1)}, bf16[16,256]{1,0:T(8,128)(2,1)S(1)}, u32[]{:S(2)}, u32[]{:S(2)}) %collective-permute-start.2) | collective-permute-done | bytes 8224 | tf_op jit(solution)/shard_map/ppermute | solution.py:520
  14.6 0.9 %collective-permute-done.3 = bf16[16,256]{1,0:T(8,128)(2,1)S(1)} collective-permute-done((bf16[16,256]{1,0:T(8,128)(2,1)}, bf16[16,256]{1,0:T(8,128)(2,1)S(1)}, u32[]{:S(2)}, u32[]{:S(2)}) %collective-permute-start.3) | collective-permute-done | bytes 8224 | tf_op jit(solution)/shard_map/ppermute | solution.py:520
  15.5 0.0 collective-permute-done.4
  15.5 0.1 collective-permute-start.5
  15.6 0.0 copy-start
  15.6 1.0 %copy-done = bf16[1088,256]{1,0:T(8,128)(2,1)S(1)} copy-done((bf16[1088,256]{1,0:T(8,128)(2,1)S(1)}, bf16[1088,256]{1,0:T(8,128)(2,1)}, u32[]{:S(2)}) %copy-start) | copy-done | bytes 557080
  16.6 1.4 %product.6 = (bf16[1024,64]{1,0:T(8,128)(2,1)S(1)}, f32[1024,256]{1,0:T(8,128)S(1)}) custom-call(bf16[1088,256]{1,0:T(8,128)(2,1)S(1)} %copy-done, bf16[16,1024]{1,0:T(8,128)(2,1)S(1)} %constant_dynamic-update-slice_fusion.refs_1_), custom_call_target="tpu_custom_call" | custom-call | tf_op jit(solution)/shard_map/product/pallas_call | solution.py:174
  18.1 0.0 collective-permute-done.5.refs_1_
  18.1 1.4 %product.7 = (bf16[1024,64]{1,0:T(8,128)(2,1)S(1)}, f32[1024,256]{1,0:T(8,128)S(1)}) custom-call(bf16[1088,256]{1,0:T(8,128)(2,1)S(1)} %copy-done, bf16[16,1024]{1,0:T(8,128)(2,1)S(1)} %collective-permute-done.5.refs_1_), custom_call_target="tpu_custom_call" | custom-call | tf_op jit(solution)/shard_map/product/pallas_call | solution.py:174
  19.5 0.0 copy-start.2
  19.6 1.0 %copy-done.2 = f32[1024,256]{1,0:T(8,128)} copy-done((f32[1024,256]{1,0:T(8,128)}, f32[1024,256]{1,0:T(8,128)S(1)}, u32[]{:S(2)}) %copy-start.2) | copy-done | bytes 1048600
  20.5 0.0 collective-permute-done.1.refs_0_.refs_1_
  20.5 0.0 collective-permute-done.refs_0_
  20.5 0.0 copy-start.8
  20.5 0.7 %halves.1 = (bf16[544,256]{1,0:T(8,128)(2,1)}, bf16[544,256]{1,0:T(8,128)(2,1)S(1)}) custom-call(bf16[1088,256]{1,0:T(8,128)(2,1)S(1)} %collective-permute-done.refs_0_, bf16[1088,256]{1,0:T(8,128)(2,1)S(1)} %collective-permute-done.1.refs_0_.refs_1_), custom_call_target="tpu_custom_call" | custom-call | tf_op jit(solution)/shard_map/halves/pallas_call | solution.py:195
  21.3 0.5 collective-permute-start.6
  21.8 0.9 %collective-permute-start.7 = (bf16[544,256]{1,0:T(8,128)(2,1)S(1)}, bf16[544,256]{1,0:T(8,128)(2,1)S(1)}, u32[]{:S(2)}, u32[]{:S(2)}) collective-permute-start(bf16[544,256]{1,0:T(8,128)(2,1)S(1)} %get-tuple-element.57), channel_id=1, source_target_pairs={{0,1},{1,0},{2,3},{3,2},{4,5},{5,4},{6,7},{7,6},{8,9},{9,8},{10,11... | collective-permute-start | bytes 835592 | tf_op jit(solution)/shard_map/ppermute | solution.py:520
  22.7 0.0 copy-start.4
  22.7 0.0 copy-start.5
  22.7 0.0 copy-start.6
  22.7 0.1 pad_add_fusion.refs_0_
  22.8 0.0 copy-done.8
  22.8 0.6 copy-done.4
  23.4 0.0 copy-done.5
  23.4 0.0 copy-done.6
  23.4 0.0 copy-done.7
  23.4 1.1 %skeletons.1 = (bf16[5,64,128]{2,1,0:T(8,128)(2,1)S(1)}, bf16[192,768]{1,0:T(8,128)(2,1)S(1)}, bf16[16,64]{1,0:T(8,128)(2,1)S(1)}) custom-call(s32[4]{0:T(128)S(1)} %pad_add_fusion.refs_0_, bf16[16,256]{1,0:T(8,128)(2,1)S(1)} %copy-done.4, s32[2,64]{1,0:T(2,128)S(1)} %copy-done.6, s32[1,64]{1,0:T(1,128)S(1)} %copy-done.8, s32[4,64]{1,0:T(4,128)S(1)} %copy-done.5, ...), custom_call_target="tpu_custom_call" | custom-call | tf_op jit(solution)/shard_map/skeletons/pallas_call | solution.py:468
  24.5 1.2 %copy-done.3 = f32[1024,256]{1,0:T(8,128)S(1)} copy-done((f32[1024,256]{1,0:T(8,128)S(1)}, f32[1024,256]{1,0:T(8,128)}, u32[]{:S(2)}) %copy-start.3) | copy-done | bytes 1048600
  25.7 2.5 %product.8 = (f32[1024,256]{1,0:T(8,128)S(1)}, f32[1024,256]{1,0:T(8,128)S(1)}) custom-call(bf16[1088,256]{1,0:T(8,128)(2,1)S(1)} %collective-permute-done.refs_0_, bf16[1024,64]{1,0:T(8,128)(2,1)S(1)} %get-tuple-element.46.refs_1_.refs_2_, bf16[1024,64]{1,0:T(8,128)(2,1)S(1)} %get-tuple-element.47.refs_2_, f32[1024,256]{1,0:T(8,128)S(1)} %get-tuple-element.49.refs_3_, ...), custom_call_target="tpu_custom_call" | custom-call | tf_op jit(solution)/shard_map/product/pallas_call | solution.py:174
  28.2 2.5 %product.9 = (f32[1024,256]{1,0:T(8,128)S(1)}, f32[1024,256]{1,0:T(8,128)S(1)}) custom-call(bf16[1088,256]{1,0:T(8,128)(2,1)S(1)} %collective-permute-done.1.refs_0_.refs_1_, bf16[1024,64]{1,0:T(8,128)(2,1)S(1)} %get-tuple-element.46.refs_1_.refs_2_, bf16[1024,64]{1,0:T(8,128)(2,1)S(1)} %get-tuple-element.47.refs_2_, ...), custom_call_target="tpu_custom_call" | custom-call | tf_op jit(solution)/shard_map/product/pallas_call | solution.py:174
  30.6 0.0 collective-permute-done.6.refs_0_
  30.7 0.0 collective-permute-done.7.refs_1_
  30.7 1.4 %product.11 = f32[1024,256]{1,0:T(8,128)S(1)} custom-call(bf16[544,256]{1,0:T(8,128)(2,1)S(1)} %collective-permute-done.6.refs_0_, bf16[544,256]{1,0:T(8,128)(2,1)S(1)} %collective-permute-done.7.refs_1_, bf16[1024,64]{1,0:T(8,128)(2,1)S(1)} %get-tuple-element.47.refs_2_, f32[1024,256]{1,0:T(8,128)S(1)} %get-tuple-element.59.refs_3_), custom_call_target="tpu_custom_call" | custom-call | tf_op jit(solution)/shard_map/product/pallas_call | solution.py:174
  32.1 0.1 collective-permute-start.8
  32.2 1.4 %product.10.refs_0_ = f32[1024,256]{1,0:T(8,128)S(1)} custom-call(bf16[544,256]{1,0:T(8,128)(2,1)S(1)} %collective-permute-done.6.refs_0_, bf16[544,256]{1,0:T(8,128)(2,1)S(1)} %collective-permute-done.7.refs_1_, bf16[1024,64]{1,0:T(8,128)(2,1)S(1)} %get-tuple-element.46.refs_1_.refs_2_, f32[1024,256]{1,0:T(8,128)S(1)} %get-tuple-element.58.refs_3_), custom_call_target="tpu_custom_call" | custom-call | tf_op jit(solution)/shard_map/product/pallas_call | solution.py:174
  33.6 1.2 %collective-permute-done.8.refs_1_ = f32[1024,256]{1,0:T(8,128)S(1)} collective-permute-done((f32[1024,256]{1,0:T(8,128)S(1)}, f32[1024,256]{1,0:T(8,128)S(1)}, u32[]{:S(2)}, u32[]{:S(2)}) %collective-permute-start.8) | collective-permute-done | bytes 1048608 | tf_op jit(solution)/shard_map/ppermute | solution.py:520
  34.8 0.1 combine.1
  34.9 1.6 %collective-permute-start.9 = (bf16[256,256]{1,0:T(8,128)(2,1)S(1)}, bf16[256,256]{1,0:T(8,128)(2,1)S(1)}, u32[]{:S(2)}, u32[]{:S(2)}) collective-permute-start(bf16[256,256]{1,0:T(8,128)(2,1)S(1)} %get-tuple-element.62), channel_id=1, source_target_pairs={{0,2},{1,3},{2,0},{3,1},{4,6},{5,7},{6,4},{7,5},{8,10},{9,11},{10,... | collective-permute-start | bytes 393224 | tf_op jit(solution)/shard_map/ppermute | solution.py:520
  36.6 2.6 %collective-permute-start.10 = (bf16[256,256]{1,0:T(8,128)(2,1)S(1)}, bf16[256,256]{1,0:T(8,128)(2,1)S(1)}, u32[]{:S(2)}, u32[]{:S(2)}) collective-permute-start(bf16[256,256]{1,0:T(8,128)(2,1)S(1)} %get-tuple-element.63), channel_id=1, source_target_pairs={{0,4},{1,5},{2,6},{3,7},{4,0},{5,1},{6,2},{7,3},{8,12},{9,13},{10,... | collective-permute-start | bytes 393224 | tf_op jit(solution)/shard_map/ppermute | solution.py:520
  39.2 0.2 collective-permute-start.11
  39.4 1.1 %collective-permute-start.12 = (bf16[16,64]{1,0:T(8,128)(2,1)S(1)}, bf16[16,64]{1,0:T(8,128)(2,1)S(1)}, u32[]{:S(2)}, u32[]{:S(2)}) collective-permute-start(bf16[16,64]{1,0:T(8,128)(2,1)S(1)} %get-tuple-element.67.refs_1_), channel_id=1, source_target_pairs={{0,1},{1,0},{2,3},{3,2},{4,5},{5,4},{6,7},{7,6},{8,9},{9,8},{10,11... | collective-permute-start | bytes 6152 | tf_op jit(solution)/shard_map/ppermute | solution.py:520
  40.5 2.5 %collective-permute-done.12.refs_2_ = bf16[16,64]{1,0:T(8,128)(2,1)S(1)} collective-permute-done((bf16[16,64]{1,0:T(8,128)(2,1)S(1)}, bf16[16,64]{1,0:T(8,128)(2,1)S(1)}, u32[]{:S(2)}, u32[]{:S(2)}) %collective-permute-start.12) | collective-permute-done | bytes 2080 | tf_op jit(solution)/shard_map/ppermute | solution.py:520
  43.0 1.0 %couplings.2 = (bf16[192,768]{1,0:T(8,128)(2,1)S(1)}, bf16[16,64]{1,0:T(8,128)(2,1)S(1)}) custom-call(s32[4]{0:T(128)S(1)} %pad_add_fusion.refs_0_, bf16[16,64]{1,0:T(8,128)(2,1)S(1)} %get-tuple-element.67.refs_1_, bf16[16,64]{1,0:T(8,128)(2,1)S(1)} %collective-permute-done.12.refs_2_, bf16[5,64,128]{2,1,0:T(8,128)(2,1)S(1)} %get-tuple-element.65.refs_3_.refs_5_), custom_call_target="tpu_custom_call" | custom-call | tf_op jit(solution)/shard_map/couplings/pallas_call | solution.py:496
  44.0 0.7 %collective-permute-start.13 = (bf16[16,64]{1,0:T(8,128)(2,1)S(1)}, bf16[16,64]{1,0:T(8,128)(2,1)S(1)}, u32[]{:S(2)}, u32[]{:S(2)}) collective-permute-start(bf16[16,64]{1,0:T(8,128)(2,1)S(1)} %get-tuple-element.69.refs_1_), channel_id=1, source_target_pairs={{0,2},{1,3},{2,0},{3,1},{4,6},{5,7},{6,4},{7,5},{8,10},{9,11},{10,... | collective-permute-start | bytes 6152 | tf_op jit(solution)/shard_map/ppermute | solution.py:520
  44.7 3.3 %collective-permute-done.13.refs_2_ = bf16[16,64]{1,0:T(8,128)(2,1)S(1)} collective-permute-done((bf16[16,64]{1,0:T(8,128)(2,1)S(1)}, bf16[16,64]{1,0:T(8,128)(2,1)S(1)}, u32[]{:S(2)}, u32[]{:S(2)}) %collective-permute-start.13) | collective-permute-done | bytes 2080 | tf_op jit(solution)/shard_map/ppermute | solution.py:520
  48.0 1.0 %couplings.3.refs_8_.refs_4_ = bf16[192,768]{1,0:T(8,128)(2,1)S(1)} custom-call(s32[4]{0:T(128)S(1)} %pad_add_fusion.refs_0_, bf16[16,64]{1,0:T(8,128)(2,1)S(1)} %get-tuple-element.69.refs_1_, bf16[16,64]{1,0:T(8,128)(2,1)S(1)} %collective-permute-done.13.refs_2_, bf16[5,64,128]{2,1,0:T(8,128)(2,1)S(1)} %get-tuple-element.65.refs_3_.refs_5_), custom_call_target="tpu_custom_call" | custom-call | tf_op jit(solution)/shard_map/couplings/pallas_call | solution.py:496
  49.0 0.0 collective-permute-done.9.refs_1_
  49.0 0.4 collective-permute-done.10.refs_2_
  49.5 0.0 collective-permute-done.11.refs_3_
  49.5 0.0 copy-done.1
  49.5 5.6 %leaves.1 = (f32[2,64,128]{2,1,0:T(8,128)}, f32[64,128]{1,0:T(8,128)S(1)}, f32[128,256]{1,0:T(8,128)S(1)}) custom-call(f32[256,256]{1,0:T(8,128)S(1)} %get-tuple-element.61.refs_0_, bf16[256,256]{1,0:T(8,128)(2,1)S(1)} %collective-permute-done.9.refs_1_, bf16[256,256]{1,0:T(8,128)(2,1)S(1)} %collective-permute-done.10.refs_2_, ...), custom_call_target="tpu_custom_call" | custom-call | tf_op jit(solution)/shard_map/leaves/pallas_call | solution.py:337
  55.1 0.7 %collective-permute-start.14 = (f32[128,256]{1,0:T(8,128)S(1)}, f32[128,256]{1,0:T(8,128)S(1)}, u32[]{:S(2)}, u32[]{:S(2)}) collective-permute-start(f32[128,256]{1,0:T(8,128)S(1)} %get-tuple-element.71.refs_1_), channel_id=1, source_target_pairs={{0,1},{1,0},{2,3},{3,2},{4,5},{5,4},{6,7},{7,6},{8,9},{9,8},{10,11... | collective-permute-start | bytes 393224 | tf_op jit(solution)/shard_map/ppermute | solution.py:520
  55.8 4.3 %collective-permute-done.14.refs_2_ = f32[128,256]{1,0:T(8,128)S(1)} collective-permute-done((f32[128,256]{1,0:T(8,128)S(1)}, f32[128,256]{1,0:T(8,128)S(1)}, u32[]{:S(2)}, u32[]{:S(2)}) %collective-permute-start.14) | collective-permute-done | bytes 131104 | tf_op jit(solution)/shard_map/ppermute | solution.py:520
  60.1 3.1 %level.2 = (f32[64,128]{1,0:T(8,128)S(1)}, f32[128,256]{1,0:T(8,128)S(1)}) custom-call(s32[4]{0:T(128)S(1)} %pad_add_fusion.refs_0_, f32[128,256]{1,0:T(8,128)S(1)} %get-tuple-element.71.refs_1_, f32[128,256]{1,0:T(8,128)S(1)} %collective-permute-done.14.refs_2_, bf16[5,64,128]{2,1,0:T(8,128)(2,1)S(1)} %get-tuple-element.65.refs_3_.refs_5_, ...), custom_call_target="tpu_custom_call" | custom-call | tf_op jit(solution)/shard_map/level/pallas_call | solution.py:414
  63.2 2.4 %collective-permute-start.15 = (f32[128,256]{1,0:T(8,128)S(1)}, f32[128,256]{1,0:T(8,128)S(1)}, u32[]{:S(2)}, u32[]{:S(2)}) collective-permute-start(f32[128,256]{1,0:T(8,128)S(1)} %get-tuple-element.72.refs_1_), channel_id=1, source_target_pairs={{0,2},{1,3},{2,0},{3,1},{4,6},{5,7},{6,4},{7,5},{8,10},{9,11},{10,... | collective-permute-start | bytes 393224 | tf_op jit(solution)/shard_map/ppermute | solution.py:520
  65.6 2.9 %collective-permute-done.15.refs_2_ = f32[128,256]{1,0:T(8,128)S(1)} collective-permute-done((f32[128,256]{1,0:T(8,128)S(1)}, f32[128,256]{1,0:T(8,128)S(1)}, u32[]{:S(2)}, u32[]{:S(2)}) %collective-permute-start.15) | collective-permute-done | bytes 131104 | tf_op jit(solution)/shard_map/ppermute | solution.py:520
  68.5 3.8 %level.3 = (f32[3,1,64,128]{3,2,1,0:T(8,128)}, f32[2,1,64,256]{3,2,1,0:T(8,128)}) custom-call(s32[4]{0:T(128)S(1)} %pad_add_fusion.refs_0_, f32[128,256]{1,0:T(8,128)S(1)} %get-tuple-element.72.refs_1_, f32[128,256]{1,0:T(8,128)S(1)} %collective-permute-done.15.refs_2_, bf16[5,64,128]{2,1,0:T(8,128)(2,1)S(1)} %get-tuple-element.65.refs_3_.refs_5_, ...), custom_call_target="tpu_custom_call" | custom-call | tf_op jit(solution)/shard_map/level/pallas_call | solution.py:414
  (6 shorter events, 0.0 us)
Async XLA Ops:
  2.6 17.9 %collective-permute-start.1 = (bf16[1088,256]{1,0:T(8,128)(2,1)}, bf16[1088,256]{1,0:T(8,128)(2,1)S(1)}, u32[]{:S(2)}, u32[]{:S(2)}) collective-permute-start(bf16[1088,256]{1,0:T(8,128)(2,1)} %get-tuple-element.42.refs_0_.refs_4_), channel_id=1, source_target_pairs={{0,16},{1,17},{2,18},{3,19},{4,20},{5,21},{6,22},{7,23},{8,24},{9,... | collective-permute-start | bytes 1671176 | tf_op jit(solution)/shard_map/ppermute | solution.py:520
  5.6 14.9 %collective-permute-start = (bf16[1088,256]{1,0:T(8,128)(2,1)}, bf16[1088,256]{1,0:T(8,128)(2,1)S(1)}, u32[]{:S(2)}, u32[]{:S(2)}) collective-permute-start(bf16[1088,256]{1,0:T(8,128)(2,1)} %get-tuple-element.42.refs_0_.refs_4_), channel_id=1, source_target_pairs={{0,1},{1,0},{2,3},{3,2},{4,5},{5,4},{6,7},{7,6},{8,9},{9,8},{10,11... | collective-permute-start | bytes 1671176 | tf_op jit(solution)/shard_map/ppermute | solution.py:520
  7.1 8.4 %collective-permute-start.4 = (bf16[16,256]{1,0:T(8,128)(2,1)}, bf16[16,256]{1,0:T(8,128)(2,1)S(1)}, u32[]{:S(2)}, u32[]{:S(2)}) collective-permute-start(bf16[16,256]{1,0:T(8,128)(2,1)} %get-tuple-element.40.refs_1_), channel_id=1, source_target_pairs={{0,6},{1,7},{2,4},{3,5},{4,2},{5,3},{6,0},{7,1},{8,14},{9,15},{10,... | collective-permute-start | bytes 24584 | tf_op jit(solution)/shard_map/ppermute | solution.py:520
  10.7 4.8 %collective-permute-start.3 = (bf16[16,256]{1,0:T(8,128)(2,1)}, bf16[16,256]{1,0:T(8,128)(2,1)S(1)}, u32[]{:S(2)}, u32[]{:S(2)}) collective-permute-start(bf16[16,256]{1,0:T(8,128)(2,1)} %get-tuple-element.40.refs_1_), channel_id=1, source_target_pairs={{0,4},{1,5},{2,6},{3,7},{4,0},{5,1},{6,2},{7,3},{8,12},{9,13},{10,... | collective-permute-start | bytes 24584 | tf_op jit(solution)/shard_map/ppermute | solution.py:520
  10.7 3.9 %collective-permute-start.2 = (bf16[16,256]{1,0:T(8,128)(2,1)}, bf16[16,256]{1,0:T(8,128)(2,1)S(1)}, u32[]{:S(2)}, u32[]{:S(2)}) collective-permute-start(bf16[16,256]{1,0:T(8,128)(2,1)} %get-tuple-element.40.refs_1_), channel_id=1, source_target_pairs={{0,2},{1,3},{2,0},{3,1},{4,6},{5,7},{6,4},{7,5},{8,10},{9,11},{10,... | collective-permute-start | bytes 24584 | tf_op jit(solution)/shard_map/ppermute | solution.py:520
  15.5 2.6 %collective-permute-start.5 = (bf16[16,1024]{1,0:T(8,128)(2,1)S(1)}, bf16[16,1024]{1,0:T(8,128)(2,1)S(1)}, u32[]{:S(2)}, u32[]{:S(2)}) collective-permute-start(bf16[16,1024]{1,0:T(8,128)(2,1)S(1)} %constant_dynamic-update-slice_fusion.refs_1_), channel_id=1, source_target_pairs={{0,8},{1,9},{2,10},{3,11},{4,12},{5,13},{6,14},{7,15},{8,0},{9,1},... | collective-permute-start | bytes 98312 | tf_op jit(solution)/shard_map/ppermute | solution.py:520
  15.6 1.1 %copy-start = (bf16[1088,256]{1,0:T(8,128)(2,1)S(1)}, bf16[1088,256]{1,0:T(8,128)(2,1)}, u32[]{:S(2)}) copy-start(bf16[1088,256]{1,0:T(8,128)(2,1)} %get-tuple-element.42.refs_0_.refs_4_) | copy-start | bytes 1671172
  19.5 1.0 %copy-start.2 = (f32[1024,256]{1,0:T(8,128)}, f32[1024,256]{1,0:T(8,128)S(1)}, u32[]{:S(2)}) copy-start(f32[1024,256]{1,0:T(8,128)S(1)} %get-tuple-element.50.refs_4_) | copy-start | bytes 3145732
  20.5 2.2 %copy-start.8 = (s32[1,64]{1,0:T(1,128)S(1)}, s32[1,64]{1,0:T(1,128)}, u32[]{:S(2)}) copy-start(s32[1,64]{1,0:T(1,128)} %refs_3_.1) | copy-start | bytes 772
  21.3 9.4 %collective-permute-start.6 = (bf16[544,256]{1,0:T(8,128)(2,1)}, bf16[544,256]{1,0:T(8,128)(2,1)S(1)}, u32[]{:S(2)}, u32[]{:S(2)}) collective-permute-start(bf16[544,256]{1,0:T(8,128)(2,1)} %get-tuple-element.56), channel_id=1, source_target_pairs={{0,16},{1,17},{2,18},{3,19},{4,20},{5,21},{6,22},{7,23},{8,24},{9,... | collective-permute-start | bytes 835592 | tf_op jit(solution)/shard_map/ppermute | solution.py:520
  21.8 8.9 %collective-permute-start.7 = (bf16[544,256]{1,0:T(8,128)(2,1)S(1)}, bf16[544,256]{1,0:T(8,128)(2,1)S(1)}, u32[]{:S(2)}, u32[]{:S(2)}) collective-permute-start(bf16[544,256]{1,0:T(8,128)(2,1)S(1)} %get-tuple-element.57), channel_id=1, source_target_pairs={{0,1},{1,0},{2,3},{3,2},{4,5},{5,4},{6,7},{7,6},{8,9},{9,8},{10,11... | collective-permute-start | bytes 835592 | tf_op jit(solution)/shard_map/ppermute | solution.py:520
  22.7 0.7 copy-start.4
  22.7 0.7 copy-start.5
  22.7 0.7 copy-start.6
  22.7 0.7 copy-start.7
  24.5 1.2 %copy-start.3 = (f32[1024,256]{1,0:T(8,128)S(1)}, f32[1024,256]{1,0:T(8,128)}, u32[]{:S(2)}) copy-start(f32[1024,256]{1,0:T(8,128)} %copy-done.2) | copy-start | bytes 3145732
  32.1 2.7 %collective-permute-start.8 = (f32[1024,256]{1,0:T(8,128)S(1)}, f32[1024,256]{1,0:T(8,128)S(1)}, u32[]{:S(2)}, u32[]{:S(2)}) collective-permute-start(f32[1024,256]{1,0:T(8,128)S(1)} %product.11), channel_id=1, source_target_pairs={{0,8},{1,9},{2,10},{3,11},{4,12},{5,13},{6,14},{7,15},{8,0},{9,1},... | collective-permute-start | bytes 3145736 | tf_op jit(solution)/shard_map/ppermute | solution.py:520
  34.8 14.6 %copy-start.1 = (bf16[1088,256]{1,0:T(8,128)(2,1)S(1)}, bf16[1088,256]{1,0:T(8,128)(2,1)}, u32[]{:S(2)}) copy-start(bf16[1088,256]{1,0:T(8,128)(2,1)} %get-tuple-element.42.refs_0_.refs_4_) | copy-start | bytes 1671172
  34.9 14.1 %collective-permute-start.9 = (bf16[256,256]{1,0:T(8,128)(2,1)S(1)}, bf16[256,256]{1,0:T(8,128)(2,1)S(1)}, u32[]{:S(2)}, u32[]{:S(2)}) collective-permute-start(bf16[256,256]{1,0:T(8,128)(2,1)S(1)} %get-tuple-element.62), channel_id=1, source_target_pairs={{0,2},{1,3},{2,0},{3,1},{4,6},{5,7},{6,4},{7,5},{8,10},{9,11},{10,... | collective-permute-start | bytes 393224 | tf_op jit(solution)/shard_map/ppermute | solution.py:520
  36.6 12.9 %collective-permute-start.10 = (bf16[256,256]{1,0:T(8,128)(2,1)S(1)}, bf16[256,256]{1,0:T(8,128)(2,1)S(1)}, u32[]{:S(2)}, u32[]{:S(2)}) collective-permute-start(bf16[256,256]{1,0:T(8,128)(2,1)S(1)} %get-tuple-element.63), channel_id=1, source_target_pairs={{0,4},{1,5},{2,6},{3,7},{4,0},{5,1},{6,2},{7,3},{8,12},{9,13},{10,... | collective-permute-start | bytes 393224 | tf_op jit(solution)/shard_map/ppermute | solution.py:520
  39.2 10.3 %collective-permute-start.11 = (bf16[256,256]{1,0:T(8,128)(2,1)S(1)}, bf16[256,256]{1,0:T(8,128)(2,1)S(1)}, u32[]{:S(2)}, u32[]{:S(2)}) collective-permute-start(bf16[256,256]{1,0:T(8,128)(2,1)S(1)} %get-tuple-element.64), channel_id=1, source_target_pairs={{0,6},{1,7},{2,4},{3,5},{4,2},{5,3},{6,0},{7,1},{8,14},{9,15},{10,... | collective-permute-start | bytes 393224 | tf_op jit(solution)/shard_map/ppermute | solution.py:520
  39.4 3.6 %collective-permute-start.12 = (bf16[16,64]{1,0:T(8,128)(2,1)S(1)}, bf16[16,64]{1,0:T(8,128)(2,1)S(1)}, u32[]{:S(2)}, u32[]{:S(2)}) collective-permute-start(bf16[16,64]{1,0:T(8,128)(2,1)S(1)} %get-tuple-element.67.refs_1_), channel_id=1, source_target_pairs={{0,1},{1,0},{2,3},{3,2},{4,5},{5,4},{6,7},{7,6},{8,9},{9,8},{10,11... | collective-permute-start | bytes 6152 | tf_op jit(solution)/shard_map/ppermute | solution.py:520
  44.0 4.1 %collective-permute-start.13 = (bf16[16,64]{1,0:T(8,128)(2,1)S(1)}, bf16[16,64]{1,0:T(8,128)(2,1)S(1)}, u32[]{:S(2)}, u32[]{:S(2)}) collective-permute-start(bf16[16,64]{1,0:T(8,128)(2,1)S(1)} %get-tuple-element.69.refs_1_), channel_id=1, source_target_pairs={{0,2},{1,3},{2,0},{3,1},{4,6},{5,7},{6,4},{7,5},{8,10},{9,11},{10,... | collective-permute-start | bytes 6152 | tf_op jit(solution)/shard_map/ppermute | solution.py:520
  55.1 5.0 %collective-permute-start.14 = (f32[128,256]{1,0:T(8,128)S(1)}, f32[128,256]{1,0:T(8,128)S(1)}, u32[]{:S(2)}, u32[]{:S(2)}) collective-permute-start(f32[128,256]{1,0:T(8,128)S(1)} %get-tuple-element.71.refs_1_), channel_id=1, source_target_pairs={{0,1},{1,0},{2,3},{3,2},{4,5},{5,4},{6,7},{7,6},{8,9},{9,8},{10,11... | collective-permute-start | bytes 393224 | tf_op jit(solution)/shard_map/ppermute | solution.py:520
  63.2 5.3 %collective-permute-start.15 = (f32[128,256]{1,0:T(8,128)S(1)}, f32[128,256]{1,0:T(8,128)S(1)}, u32[]{:S(2)}, u32[]{:S(2)}) collective-permute-start(f32[128,256]{1,0:T(8,128)S(1)} %get-tuple-element.72.refs_1_), channel_id=1, source_target_pairs={{0,2},{1,3},{2,0},{3,1},{4,6},{5,7},{6,4},{7,5},{8,10},{9,11},{10,... | collective-permute-start | bytes 393224 | tf_op jit(solution)/shard_map/ppermute | solution.py:520

commit v2 on v1

--- a/solution.py
+++ b/solution.py
@@ -13,6 +13,12 @@
 DOUBLINGS = 9
 VMEM = pl.BlockSpec(memory_space=pltpu.VMEM)
 SMEM = pl.BlockSpec(memory_space=pltpu.SMEM)
+
+
+def vmem(shape, kind=F32):
+    return pltpu.VMEM(tuple(shape), kind)
+
+
 COST = pl.CostEstimate(flops=0, bytes_accessed=0, transcendentals=0)
 PARAMS = pltpu.CompilerParams(vmem_limit_bytes=16 << 20)
 
@@ -72,20 +78,21 @@
 
 def pack_body(probes_ref, points_ref, packed_ref, own_ref, held_ref, sem):
     quarters, span, _ = probes_ref.shape
+    half = quarters // 2
+    rows = half * (span + 16)
     copies = [pltpu.make_async_copy(points_ref, held_ref, sem.at[quarters])]
-    copies += [
-        pltpu.make_async_copy(
-            probes_ref.at[quarter], packed_ref.at[pl.ds(quarter * span, span)], sem.at[quarter]
-        )
-        for quarter in range(quarters)
-    ]
+    for quarter in range(quarters):
+        start = quarter // half * rows + quarter % half * span
+        target = packed_ref.at[pl.ds(start, span)]
+        copies.append(pltpu.make_async_copy(probes_ref.at[quarter], target, sem.at[quarter]))
     for copy in copies:
         copy.start()
     copies[0].wait()
     points = held_ref[...].astype(F32)
     for quarter in range(quarters):
         feats = points[:, quarter, :].astype(BF16)
-        packed_ref[pl.ds(quarters * span + 16 * quarter, 16), :] = feats
+        start = quarter // half * rows + half * span + quarter % half * 16
+        packed_ref[pl.ds(start, 16), :] = feats
         if quarter == 0:
             own_ref[...] = feats
     for copy in copies[1:]:
@@ -97,8 +104,8 @@
     return pl.pallas_call(
         pack_body,
         out_shape=(
-            jax.ShapeDtypeStruct((quarters * (span + 16), samples), BF16),
-            jax.ShapeDtypeStruct((16, span), BF16),
+            vmem((quarters * (span + 16), samples), BF16),
+            vmem((16, span), BF16),
         ),
         in_specs=[pl.BlockSpec(memory_space=pltpu.HBM)] * 2,
         scratch_shapes=[
@@ -106,9 +113,9 @@
             pltpu.SemaphoreType.DMA((quarters + 1,)),
         ],
         cost_estimate=COST,
-        compiler_params=pltpu.CompilerParams(vmem_limit_bytes=64512 << 10),
+        compiler_params=PARAMS,
         name="pack",
-    )(probes, points)
+    )(*(pltpu.with_memory_space_constraint(value, pltpu.HBM) for value in (probes, points)))
 
 
 def masked(entries):
@@ -119,19 +126,21 @@
 
 
 def add_source(source_ref, row_refs, cols_ref, put, span, own):
-    quarters = source_ref.shape[0] // (span + 16)
-    columns = quarters * span
-    for quarter in range(quarters):
-        feats = source_ref[pl.ds(columns + 16 * quarter, 16), :]
-        cols_ref[:, pl.ds(quarter * span, span)] = col_features(feats)
+    size = 2 * (span + 16)
+    parts = range(0, source_ref.shape[0], size)
+    for number, part in enumerate(parts):
+        for quarter in range(2):
+            feats = source_ref[pl.ds(part + 2 * span + 16 * quarter, 16), :]
+            cols_ref[:, pl.ds((2 * number + quarter) * span, span)] = col_features(feats)
+    columns = 2 * span * len(parts)
     for half, rows_ref in enumerate(row_refs):
         for start in range(0, rows_ref.shape[0], span):
             feats = rows_ref[pl.ds(start, span), :]
             entries = jnp.exp2(over(feats, cols_ref[:, :columns], 1, 0))
             if own and half == 0 and start == 0:
                 entries = jnp.concatenate([masked(entries[:, :span]), entries[:, span:]], axis=1)
-            randoms = source_ref[pl.ds(0, columns), :]
-            put(half, start, over(entries.astype(BF16), randoms, 1, 0))
+            randoms = [source_ref[pl.ds(part, 2 * span), :] for part in parts]
+            put(half, start, over(entries.astype(BF16), jnp.concatenate(randoms, axis=0), 1, 0))
 
 
 def product_body(gain, span, first, own, source_count, half_count, *refs):
@@ -168,9 +177,9 @@
     count = len(rows)
     counts = [half.shape[1] if first else half.shape[0] for half in rows]
     columns = max(s.shape[0] // (span + 16) * span for s in sources)
-    out = [jax.ShapeDtypeStruct((count, samples), F32) for count in counts]
+    out = [vmem((count, samples), F32) for count in counts]
     if first:
-        out = [jax.ShapeDtypeStruct((count, 64), BF16) for count in counts] + out
+        out = [vmem((count, 64), BF16) for count in counts] + out
     out = pl.pallas_call(
         lambda *refs: product_body(gain, span, first, own, len(sources), count, *refs),
         out_shape=out,
@@ -180,25 +189,6 @@
         name="product",
     )(*sources, *rows, *([] if first else totals))
     return (out[:count], out[count:]) if first else out
-
-
-def halves_body(quarters, span, *refs):
-    size = quarters * span // 2
-    for number, (source_ref, half_ref) in enumerate(zip(refs[:2], refs[2:])):
-        feats = quarters * span + 8 * quarters * number
-        half_ref[pl.ds(0, size), :] = source_ref[pl.ds(size * number, size), :]
-        half_ref[pl.ds(size, 8 * quarters), :] = source_ref[pl.ds(feats, 8 * quarters), :]
-
-
-def halves(first, second, span):
-    rows, samples = first.shape
-    return pl.pallas_call(
-        lambda *refs: halves_body(rows // (span + 16), span, *refs),
-        out_shape=[jax.ShapeDtypeStruct((rows // 2, samples), BF16)] * 2,
-        cost_estimate=COST,
-        compiler_params=PARAMS,
-        name="halves",
-    )(first, second)
 
 
 def combine_body(span, mine_ref, theirs_ref, own_ref, *sent_refs):
@@ -212,8 +202,8 @@
     rows, samples = mine.shape
     return pl.pallas_call(
         lambda *refs: combine_body(span, *refs),
-        out_shape=[jax.ShapeDtypeStruct((span, samples), F32)]
-        + [jax.ShapeDtypeStruct((span, samples), BF16)] * (rows // span - 1),
+        out_shape=[vmem((span, samples), F32)]
+        + [vmem((span, samples), BF16)] * (rows // span - 1),
         cost_estimate=COST,
         compiler_params=PARAMS,
         name="combine",
@@ -338,8 +328,8 @@
         lambda *refs: leaves_body(len(others), *refs),
         out_shape=(
             jax.ShapeDtypeStruct((leaf_count, rank, LEAF), F32),
-            jax.ShapeDtypeStruct((rank, pool), F32),
-            jax.ShapeDtypeStruct((2 * rank, samples), F32),
+            vmem((rank, pool), F32),
+            vmem((2 * rank, samples), F32),
         ),
         out_specs=(pl.BlockSpec(memory_space=pl.ANY), VMEM, VMEM),
         scratch_shapes=[pltpu.VMEM((leaf_count, rank, LEAF), F32), pltpu.SemaphoreType.DMA],
@@ -398,8 +388,8 @@
     rank, pool = picks.shape[1:]
     samples = mine.shape[1]
     out_shape = (
-        jax.ShapeDtypeStruct((rank, pool), F32),
-        jax.ShapeDtypeStruct(mine.shape, F32),
+        vmem((rank, pool), F32),
+        vmem(mine.shape, F32),
     )
     out_specs = (VMEM, VMEM)
     scratch = []
@@ -443,7 +433,7 @@
 
 
 def coupling_shape(rank):
-    return jax.ShapeDtypeStruct((3 * rank, 12 * rank), BF16)
+    return vmem((3 * rank, 12 * rank), BF16)
 
 
 def skeletons_body(gain, place_ref, own_ref, leaf_ref, one_ref, two_ref, three_ref, *refs):
@@ -468,9 +458,9 @@
     return pl.pallas_call(
         lambda *refs: skeletons_body(gain, *refs),
         out_shape=(
-            jax.ShapeDtypeStruct((leaf_count + 3, rank, LEAF), BF16),
+            vmem((leaf_count + 3, rank, LEAF), BF16),
             coupling_shape(rank),
-            jax.ShapeDtypeStruct((16, rank), BF16),
+            vmem((16, rank), BF16),
         ),
         in_specs=[SMEM] + [VMEM] * 5,
         cost_estimate=COST,
@@ -492,7 +482,7 @@
     rank = picks.shape[1]
     out_shape = [coupling_shape(rank)]
     if number == 2:
-        out_shape.append(jax.ShapeDtypeStruct(mine.shape, BF16))
+        out_shape.append(vmem(mine.shape, BF16))
     return pl.pallas_call(
         lambda *refs: couplings_body(gain, number, *refs),
         out_shape=out_shape,
@@ -533,8 +523,8 @@
     row_feats, totals = row_feats + more_feats, totals + more_totals
     beside, across, *totals = lax.optimization_barrier((beside, across, *totals))
     pieces = [packed, beside, across]
-    relayed = halves(beside, across, span)
-    diagonal = [swap(relayed[0], 2, 0), swap(relayed[1], 0, 1)]
+    half = packed.shape[0] // 2
+    diagonal = [swap(beside[:half], 2, 0), swap(across[half:], 0, 1)]
     totals = product([beside], row_feats, span, totals)
     totals = product([across], row_feats, span, totals)
     tables = (leaf_skeleton, skeleton_one, skeleton_two, skeleton_three)

time: 72.8 us -> 73.2 us (level)
  waiting for transfers between devices: 18 us -> 19.5 us
  Pallas kernels: 29 us -> 27.6 us
    ppermute x16, waiting for transfers between devices: 18 us -> 19.5 us  [swap(): return lax.ppermute(value, ('row', 'col'), pairs)]
    pallas_call x4 -> x3, Pallas kernels: 3.9 us -> 2.35 us  [the longest x1 1.16 us: pack(): pl.pallas_call(pack_body, out_shape=(vmem((quarters * (span + 16), sample...]
    unnamed x21 -> x19, local copies, waits for them, and re-layouts: 4.63 us -> 5.03 us
  transfers between devices with their start and end apart: 16 -> 16, of which waited for: 8 -> 7; matrix products, arithmetic and copies ran while one was open for 1% -> 0% of each run, Pallas kernels for 17% -> 17%
where the time goes in v2:
time: 73.2 us; the launch traced here: 73 us
  Pallas kernels  27.6 us (38%)
  starting transfers between devices  19.8 us (27%)
  waiting for transfers between devices  19.5 us (27%)
  local copies, waits for them, and re-layouts  5.07 us (7%)
  between operations  0.96 us (1%)
    ppermute x16, starting transfers between devices, swap(): return lax.ppermute(value, ('row', 'col'), pairs)  19.8 us
    ppermute x16, waiting for transfers between devices, swap(): return lax.ppermute(value, ('row', 'col'), pairs)  19.5 us
    pallas_call x6, Pallas kernels, product(): pl.pallas_call(lambda *refs: product_body(gain, span, first, own, len(sou...  10.7 us
    pallas_call x2, Pallas kernels, level(): pl.pallas_call(lambda *refs: level_body(number, *refs), out_shape=out_sha...  6.84 us
    pallas_call x1, Pallas kernels, leaves(): pl.pallas_call(lambda *refs: leaves_body(len(others), *refs), out_shape=(...  5.78 us
    unnamed x19, local copies, waits for them, and re-layouts  5.03 us
    pallas_call x2, Pallas kernels, couplings(): pl.pallas_call(lambda *refs: couplings_body(gain, number, *refs), out_sha...  1.93 us
  transfers between devices with their start and end apart: 16, of which 7 were waited for; matrix products, arithmetic and copies ran while one was open for 0% of the time, Pallas kernels for 17%

profile of v2, /device:TPU:0, one launch (start us, length us, event | category | flops | bytes accessed | tf_op | source)
XLA Modules:
  0.0 73.0 jit_solution(15590344471312167965)
XLA Ops:
  0.6 1.2 %pack.1 = (bf16[1088,256]{1,0:T(8,128)(2,1)S(1)}, bf16[16,256]{1,0:T(8,128)(2,1)S(1)}) custom-call(bf16[4,256,256]{2,1,0:T(8,128)(2,1)} %probes_ref.1, bf16[16,4,256]{2,1,0:T(4,128)(2,1)} %points_ref.1), custom_call_target="tpu_custom_call" | custom-call | tf_op jit(solution)/shard_map/pack/pallas_call | solution.py:104
  1.8 3.0 %collective-permute-start = (bf16[1088,256]{1,0:T(8,128)(2,1)S(1)}, bf16[1088,256]{1,0:T(8,128)(2,1)S(1)}, u32[]{:S(2)}, u32[]{:S(2)}) collective-permute-start(bf16[1088,256]{1,0:T(8,128)(2,1)S(1)} %get-tuple-element.40.refs_0_.refs_4_), channel_id=1, source_target_pairs={{0,1},{1,0},{2,3},{3,2},{4,5},{5,4},{6,7},{7,6},{8,9},{9,8},{10,11... | collective-permute-start | bytes 1671176 | tf_op jit(solution)/shard_map/ppermute | solution.py:510
  4.8 1.5 %collective-permute-start.1 = (bf16[1088,256]{1,0:T(8,128)(2,1)S(1)}, bf16[1088,256]{1,0:T(8,128)(2,1)S(1)}, u32[]{:S(2)}, u32[]{:S(2)}) collective-permute-start(bf16[1088,256]{1,0:T(8,128)(2,1)S(1)} %get-tuple-element.40.refs_0_.refs_4_), channel_id=1, source_target_pairs={{0,16},{1,17},{2,18},{3,19},{4,20},{5,21},{6,22},{7,23},{8,24},{9,... | collective-permute-start | bytes 1671176 | tf_op jit(solution)/shard_map/ppermute | solution.py:510
  6.3 1.6 %collective-permute-start.2 = (bf16[16,256]{1,0:T(8,128)(2,1)S(1)}, bf16[16,256]{1,0:T(8,128)(2,1)S(1)}, u32[]{:S(2)}, u32[]{:S(2)}) collective-permute-start(bf16[16,256]{1,0:T(8,128)(2,1)S(1)} %get-tuple-element.38.refs_1_), channel_id=1, source_target_pairs={{0,2},{1,3},{2,0},{3,1},{4,6},{5,7},{6,4},{7,5},{8,10},{9,11},{10,... | collective-permute-start | bytes 24584 | tf_op jit(solution)/shard_map/ppermute | solution.py:510
  7.9 2.6 %collective-permute-start.3 = (bf16[16,256]{1,0:T(8,128)(2,1)S(1)}, bf16[16,256]{1,0:T(8,128)(2,1)S(1)}, u32[]{:S(2)}, u32[]{:S(2)}) collective-permute-start(bf16[16,256]{1,0:T(8,128)(2,1)S(1)} %get-tuple-element.38.refs_1_), channel_id=1, source_target_pairs={{0,4},{1,5},{2,6},{3,7},{4,0},{5,1},{6,2},{7,3},{8,12},{9,13},{10,... | collective-permute-start | bytes 24584 | tf_op jit(solution)/shard_map/ppermute | solution.py:510
  10.5 0.2 collective-permute-start.4
  10.7 0.0 collective-permute-done.2
  10.7 1.7 %collective-permute-done.3 = bf16[16,256]{1,0:T(8,128)(2,1)S(1)} collective-permute-done((bf16[16,256]{1,0:T(8,128)(2,1)S(1)}, bf16[16,256]{1,0:T(8,128)(2,1)S(1)}, u32[]{:S(2)}, u32[]{:S(2)}) %collective-permute-start.3) | collective-permute-done | bytes 8224 | tf_op jit(solution)/shard_map/ppermute | solution.py:510
  12.4 3.5 %collective-permute-done.4 = bf16[16,256]{1,0:T(8,128)(2,1)S(1)} collective-permute-done((bf16[16,256]{1,0:T(8,128)(2,1)S(1)}, bf16[16,256]{1,0:T(8,128)(2,1)S(1)}, u32[]{:S(2)}, u32[]{:S(2)}) %collective-permute-start.4) | collective-permute-done | bytes 8224 | tf_op jit(solution)/shard_map/ppermute | solution.py:510
  15.9 0.0 collective-permute-start.5
  15.9 1.4 %product.6 = (bf16[1024,64]{1,0:T(8,128)(2,1)S(1)}, f32[1024,256]{1,0:T(8,128)S(1)}) custom-call(bf16[1088,256]{1,0:T(8,128)(2,1)S(1)} %get-tuple-element.40.refs_0_.refs_4_, bf16[16,1024]{1,0:T(8,128)(2,1)S(1)} %constant_dynamic-update-slice_fusion.refs_1_), custom_call_target="tpu_custom_call" | custom-call | tf_op jit(solution)/shard_map/product/pallas_call | solution.py:183
  17.4 0.0 copy-start
  17.4 1.0 %copy-done = f32[1024,256]{1,0:T(8,128)} copy-done((f32[1024,256]{1,0:T(8,128)}, f32[1024,256]{1,0:T(8,128)S(1)}, u32[]{:S(2)}) %copy-start) | copy-done | bytes 1048600
  18.4 0.0 collective-permute-done.5.refs_1_
  18.4 1.4 %product.7 = (bf16[1024,64]{1,0:T(8,128)(2,1)S(1)}, f32[1024,256]{1,0:T(8,128)S(1)}) custom-call(bf16[1088,256]{1,0:T(8,128)(2,1)S(1)} %get-tuple-element.40.refs_0_.refs_4_, bf16[16,1024]{1,0:T(8,128)(2,1)S(1)} %collective-permute-done.5.refs_1_), custom_call_target="tpu_custom_call" | custom-call | tf_op jit(solution)/shard_map/product/pallas_call | solution.py:183
  19.8 0.0 copy-start.2
  19.8 1.0 %copy-done.2 = f32[1024,256]{1,0:T(8,128)} copy-done((f32[1024,256]{1,0:T(8,128)}, f32[1024,256]{1,0:T(8,128)S(1)}, u32[]{:S(2)}) %copy-start.2) | copy-done | bytes 1048600
  20.8 0.0 collective-permute-done.refs_0_
  20.8 0.0 collective-permute-done.1.refs_0_
  20.8 0.6 collective-permute-start.6
  21.4 0.0 copy-start.7
  21.4 0.6 collective-permute-start.7
  22.0 0.0 copy-start.4
  22.0 0.0 copy-start.5
  22.0 0.0 copy-start.6
  22.0 0.1 pad_add_fusion.refs_0_
  22.1 0.0 copy-done.7
  22.1 0.6 copy-done.4
  22.7 0.0 copy-done.5
  22.7 0.0 copy-done.6
  22.7 1.1 %skeletons.1 = (bf16[5,64,128]{2,1,0:T(8,128)(2,1)S(1)}, bf16[192,768]{1,0:T(8,128)(2,1)S(1)}, bf16[16,64]{1,0:T(8,128)(2,1)S(1)}) custom-call(s32[4]{0:T(128)S(1)} %pad_add_fusion.refs_0_, bf16[16,256]{1,0:T(8,128)(2,1)S(1)} %get-tuple-element.38.refs_1_, s32[2,64]{1,0:T(2,128)S(1)} %copy-done.5, s32[1,64]{1,0:T(1,128)S(1)} %copy-done.7, ...), custom_call_target="tpu_custom_call" | custom-call | tf_op jit(solution)/shard_map/skeletons/pallas_call | solution.py:458
  23.8 0.0 copy-start.1
  23.8 1.2 %copy-done.1 = f32[1024,256]{1,0:T(8,128)S(1)} copy-done((f32[1024,256]{1,0:T(8,128)S(1)}, f32[1024,256]{1,0:T(8,128)}, u32[]{:S(2)}) %copy-start.1) | copy-done | bytes 1048600
  25.1 0.0 copy-start.3
  25.1 1.2 %copy-done.3 = f32[1024,256]{1,0:T(8,128)S(1)} copy-done((f32[1024,256]{1,0:T(8,128)S(1)}, f32[1024,256]{1,0:T(8,128)}, u32[]{:S(2)}) %copy-start.3) | copy-done | bytes 1048600
  26.3 2.5 %product.8 = (f32[1024,256]{1,0:T(8,128)S(1)}, f32[1024,256]{1,0:T(8,128)S(1)}) custom-call(bf16[1088,256]{1,0:T(8,128)(2,1)S(1)} %collective-permute-done.refs_0_, bf16[1024,64]{1,0:T(8,128)(2,1)S(1)} %get-tuple-element.44.refs_1_.refs_2_, bf16[1024,64]{1,0:T(8,128)(2,1)S(1)} %get-tuple-element.45.refs_2_, f32[1024,256]{1,0:T(8,128)S(1)} %copy-done.1, ...), custom_call_target="tpu_custom_call" | custom-call | tf_op jit(solution)/shard_map/product/pallas_call | solution.py:183
  28.8 2.5 %product.9 = (f32[1024,256]{1,0:T(8,128)S(1)}, f32[1024,256]{1,0:T(8,128)S(1)}) custom-call(bf16[1088,256]{1,0:T(8,128)(2,1)S(1)} %collective-permute-done.1.refs_0_, bf16[1024,64]{1,0:T(8,128)(2,1)S(1)} %get-tuple-element.44.refs_1_.refs_2_, bf16[1024,64]{1,0:T(8,128)(2,1)S(1)} %get-tuple-element.45.refs_2_, f32[1024,256]{1,0:T(8,128)S(1)} %get-tuple-element.49.refs_3_, ...), custom_call_target="tpu_custom_call" | custom-call | tf_op jit(solution)/shard_map/product/pallas_call | solution.py:183
  31.2 0.0 collective-permute-done.6.refs_0_
  31.2 0.0 collective-permute-done.7.refs_1_
  31.2 1.4 %product.11 = f32[1024,256]{1,0:T(8,128)S(1)} custom-call(bf16[544,256]{1,0:T(8,128)(2,1)S(1)} %collective-permute-done.6.refs_0_, bf16[544,256]{1,0:T(8,128)(2,1)S(1)} %collective-permute-done.7.refs_1_, bf16[1024,64]{1,0:T(8,128)(2,1)S(1)} %get-tuple-element.45.refs_2_, f32[1024,256]{1,0:T(8,128)S(1)} %get-tuple-element.55.refs_3_), custom_call_target="tpu_custom_call" | custom-call | tf_op jit(solution)/shard_map/product/pallas_call | solution.py:183
  32.7 0.1 collective-permute-start.8
  32.7 1.4 %product.10.refs_0_ = f32[1024,256]{1,0:T(8,128)S(1)} custom-call(bf16[544,256]{1,0:T(8,128)(2,1)S(1)} %collective-permute-done.6.refs_0_, bf16[544,256]{1,0:T(8,128)(2,1)S(1)} %collective-permute-done.7.refs_1_, bf16[1024,64]{1,0:T(8,128)(2,1)S(1)} %get-tuple-element.44.refs_1_.refs_2_, f32[1024,256]{1,0:T(8,128)S(1)} %get-tuple-element.54.refs_3_), custom_call_target="tpu_custom_call" | custom-call | tf_op jit(solution)/shard_map/product/pallas_call | solution.py:183
  34.2 1.2 %collective-permute-done.8.refs_1_ = f32[1024,256]{1,0:T(8,128)S(1)} collective-permute-done((f32[1024,256]{1,0:T(8,128)S(1)}, f32[1024,256]{1,0:T(8,128)S(1)}, u32[]{:S(2)}, u32[]{:S(2)}) %collective-permute-start.8) | collective-permute-done | bytes 1048608 | tf_op jit(solution)/shard_map/ppermute | solution.py:510
  35.4 0.1 combine.1
  35.5 1.7 %collective-permute-start.10 = (bf16[256,256]{1,0:T(8,128)(2,1)S(1)}, bf16[256,256]{1,0:T(8,128)(2,1)S(1)}, u32[]{:S(2)}, u32[]{:S(2)}) collective-permute-start(bf16[256,256]{1,0:T(8,128)(2,1)S(1)} %get-tuple-element.59), channel_id=1, source_target_pairs={{0,4},{1,5},{2,6},{3,7},{4,0},{5,1},{6,2},{7,3},{8,12},{9,13},{10,... | collective-permute-start | bytes 393224 | tf_op jit(solution)/shard_map/ppermute | solution.py:510
  37.2 1.4 %collective-permute-start.11 = (bf16[256,256]{1,0:T(8,128)(2,1)S(1)}, bf16[256,256]{1,0:T(8,128)(2,1)S(1)}, u32[]{:S(2)}, u32[]{:S(2)}) collective-permute-start(bf16[256,256]{1,0:T(8,128)(2,1)S(1)} %get-tuple-element.60), channel_id=1, source_target_pairs={{0,6},{1,7},{2,4},{3,5},{4,2},{5,3},{6,0},{7,1},{8,14},{9,15},{10,... | collective-permute-start | bytes 393224 | tf_op jit(solution)/shard_map/ppermute | solution.py:510
  38.6 0.5 collective-permute-start.9
  39.1 1.5 %collective-permute-start.12 = (bf16[16,64]{1,0:T(8,128)(2,1)S(1)}, bf16[16,64]{1,0:T(8,128)(2,1)S(1)}, u32[]{:S(2)}, u32[]{:S(2)}) collective-permute-start(bf16[16,64]{1,0:T(8,128)(2,1)S(1)} %get-tuple-element.63.refs_1_), channel_id=1, source_target_pairs={{0,1},{1,0},{2,3},{3,2},{4,5},{5,4},{6,7},{7,6},{8,9},{9,8},{10,11... | collective-permute-start | bytes 6152 | tf_op jit(solution)/shard_map/ppermute | solution.py:510
  40.6 2.1 %collective-permute-done.12.refs_2_ = bf16[16,64]{1,0:T(8,128)(2,1)S(1)} collective-permute-done((bf16[16,64]{1,0:T(8,128)(2,1)S(1)}, bf16[16,64]{1,0:T(8,128)(2,1)S(1)}, u32[]{:S(2)}, u32[]{:S(2)}) %collective-permute-start.12) | collective-permute-done | bytes 2080 | tf_op jit(solution)/shard_map/ppermute | solution.py:510
  42.7 1.0 %couplings.2 = (bf16[192,768]{1,0:T(8,128)(2,1)S(1)}, bf16[16,64]{1,0:T(8,128)(2,1)S(1)}) custom-call(s32[4]{0:T(128)S(1)} %pad_add_fusion.refs_0_, bf16[16,64]{1,0:T(8,128)(2,1)S(1)} %get-tuple-element.63.refs_1_, bf16[16,64]{1,0:T(8,128)(2,1)S(1)} %collective-permute-done.12.refs_2_, bf16[5,64,128]{2,1,0:T(8,128)(2,1)S(1)} %get-tuple-element.61.refs_3_.refs_5_), custom_call_target="tpu_custom_call" | custom-call | tf_op jit(solution)/shard_map/couplings/pallas_call | solution.py:486
  43.6 1.6 %collective-permute-start.13 = (bf16[16,64]{1,0:T(8,128)(2,1)S(1)}, bf16[16,64]{1,0:T(8,128)(2,1)S(1)}, u32[]{:S(2)}, u32[]{:S(2)}) collective-permute-start(bf16[16,64]{1,0:T(8,128)(2,1)S(1)} %get-tuple-element.65.refs_1_), channel_id=1, source_target_pairs={{0,2},{1,3},{2,0},{3,1},{4,6},{5,7},{6,4},{7,5},{8,10},{9,11},{10,... | collective-permute-start | bytes 6152 | tf_op jit(solution)/shard_map/ppermute | solution.py:510
  45.3 3.8 %collective-permute-done.13.refs_2_ = bf16[16,64]{1,0:T(8,128)(2,1)S(1)} collective-permute-done((bf16[16,64]{1,0:T(8,128)(2,1)S(1)}, bf16[16,64]{1,0:T(8,128)(2,1)S(1)}, u32[]{:S(2)}, u32[]{:S(2)}) %collective-permute-start.13) | collective-permute-done | bytes 2080 | tf_op jit(solution)/shard_map/ppermute | solution.py:510
  49.1 1.0 %couplings.3.refs_8_.refs_4_ = bf16[192,768]{1,0:T(8,128)(2,1)S(1)} custom-call(s32[4]{0:T(128)S(1)} %pad_add_fusion.refs_0_, bf16[16,64]{1,0:T(8,128)(2,1)S(1)} %get-tuple-element.65.refs_1_, bf16[16,64]{1,0:T(8,128)(2,1)S(1)} %collective-permute-done.13.refs_2_, bf16[5,64,128]{2,1,0:T(8,128)(2,1)S(1)} %get-tuple-element.61.refs_3_.refs_5_), custom_call_target="tpu_custom_call" | custom-call | tf_op jit(solution)/shard_map/couplings/pallas_call | solution.py:486
  50.1 0.0 collective-permute-done.10.refs_2_
  50.1 0.0 collective-permute-done.11.refs_3_
  50.1 0.0 collective-permute-done.9.refs_1_
  50.1 5.8 %leaves.1 = (f32[2,64,128]{2,1,0:T(8,128)}, f32[64,128]{1,0:T(8,128)S(1)}, f32[128,256]{1,0:T(8,128)S(1)}) custom-call(f32[256,256]{1,0:T(8,128)S(1)} %get-tuple-element.57.refs_0_, bf16[256,256]{1,0:T(8,128)(2,1)S(1)} %collective-permute-done.9.refs_1_, bf16[256,256]{1,0:T(8,128)(2,1)S(1)} %collective-permute-done.10.refs_2_, ...), custom_call_target="tpu_custom_call" | custom-call | tf_op jit(solution)/shard_map/leaves/pallas_call | solution.py:327
  55.9 1.6 %collective-permute-start.14 = (f32[128,256]{1,0:T(8,128)S(1)}, f32[128,256]{1,0:T(8,128)S(1)}, u32[]{:S(2)}, u32[]{:S(2)}) collective-permute-start(f32[128,256]{1,0:T(8,128)S(1)} %get-tuple-element.67.refs_1_), channel_id=1, source_target_pairs={{0,1},{1,0},{2,3},{3,2},{4,5},{5,4},{6,7},{7,6},{8,9},{9,8},{10,11... | collective-permute-start | bytes 393224 | tf_op jit(solution)/shard_map/ppermute | solution.py:510
  57.5 3.5 %collective-permute-done.14.refs_2_ = f32[128,256]{1,0:T(8,128)S(1)} collective-permute-done((f32[128,256]{1,0:T(8,128)S(1)}, f32[128,256]{1,0:T(8,128)S(1)}, u32[]{:S(2)}, u32[]{:S(2)}) %collective-permute-start.14) | collective-permute-done | bytes 131104 | tf_op jit(solution)/shard_map/ppermute | solution.py:510
  60.9 3.1 %level.2 = (f32[64,128]{1,0:T(8,128)S(1)}, f32[128,256]{1,0:T(8,128)S(1)}) custom-call(s32[4]{0:T(128)S(1)} %pad_add_fusion.refs_0_, f32[128,256]{1,0:T(8,128)S(1)} %get-tuple-element.67.refs_1_, f32[128,256]{1,0:T(8,128)S(1)} %collective-permute-done.14.refs_2_, bf16[5,64,128]{2,1,0:T(8,128)(2,1)S(1)} %get-tuple-element.61.refs_3_.refs_5_, ...), custom_call_target="tpu_custom_call" | custom-call | tf_op jit(solution)/shard_map/level/pallas_call | solution.py:404
  64.0 1.3 %collective-permute-start.15 = (f32[128,256]{1,0:T(8,128)S(1)}, f32[128,256]{1,0:T(8,128)S(1)}, u32[]{:S(2)}, u32[]{:S(2)}) collective-permute-start(f32[128,256]{1,0:T(8,128)S(1)} %get-tuple-element.68.refs_1_), channel_id=1, source_target_pairs={{0,2},{1,3},{2,0},{3,1},{4,6},{5,7},{6,4},{7,5},{8,10},{9,11},{10,... | collective-permute-start | bytes 393224 | tf_op jit(solution)/shard_map/ppermute | solution.py:510
  65.4 3.7 %collective-permute-done.15.refs_2_ = f32[128,256]{1,0:T(8,128)S(1)} collective-permute-done((f32[128,256]{1,0:T(8,128)S(1)}, f32[128,256]{1,0:T(8,128)S(1)}, u32[]{:S(2)}, u32[]{:S(2)}) %collective-permute-start.15) | collective-permute-done | bytes 131104 | tf_op jit(solution)/shard_map/ppermute | solution.py:510
  69.0 3.8 %level.3 = (f32[3,1,64,128]{3,2,1,0:T(8,128)}, f32[2,1,64,256]{3,2,1,0:T(8,128)}) custom-call(s32[4]{0:T(128)S(1)} %pad_add_fusion.refs_0_, f32[128,256]{1,0:T(8,128)S(1)} %get-tuple-element.68.refs_1_, f32[128,256]{1,0:T(8,128)S(1)} %collective-permute-done.15.refs_2_, bf16[5,64,128]{2,1,0:T(8,128)(2,1)S(1)} %get-tuple-element.61.refs_3_.refs_5_, ...), custom_call_target="tpu_custom_call" | custom-call | tf_op jit(solution)/shard_map/level/pallas_call | solution.py:404
  (6 shorter events, 0.0 us)
Async XLA Ops:
  1.8 19.0 %collective-permute-start = (bf16[1088,256]{1,0:T(8,128)(2,1)S(1)}, bf16[1088,256]{1,0:T(8,128)(2,1)S(1)}, u32[]{:S(2)}, u32[]{:S(2)}) collective-permute-start(bf16[1088,256]{1,0:T(8,128)(2,1)S(1)} %get-tuple-element.40.refs_0_.refs_4_), channel_id=1, source_target_pairs={{0,1},{1,0},{2,3},{3,2},{4,5},{5,4},{6,7},{7,6},{8,9},{9,8},{10,11... | collective-permute-start | bytes 1671176 | tf_op jit(solution)/shard_map/ppermute | solution.py:510
  4.8 16.0 %collective-permute-start.1 = (bf16[1088,256]{1,0:T(8,128)(2,1)S(1)}, bf16[1088,256]{1,0:T(8,128)(2,1)S(1)}, u32[]{:S(2)}, u32[]{:S(2)}) collective-permute-start(bf16[1088,256]{1,0:T(8,128)(2,1)S(1)} %get-tuple-element.40.refs_0_.refs_4_), channel_id=1, source_target_pairs={{0,16},{1,17},{2,18},{3,19},{4,20},{5,21},{6,22},{7,23},{8,24},{9,... | collective-permute-start | bytes 1671176 | tf_op jit(solution)/shard_map/ppermute | solution.py:510
  6.3 4.4 %collective-permute-start.2 = (bf16[16,256]{1,0:T(8,128)(2,1)S(1)}, bf16[16,256]{1,0:T(8,128)(2,1)S(1)}, u32[]{:S(2)}, u32[]{:S(2)}) collective-permute-start(bf16[16,256]{1,0:T(8,128)(2,1)S(1)} %get-tuple-element.38.refs_1_), channel_id=1, source_target_pairs={{0,2},{1,3},{2,0},{3,1},{4,6},{5,7},{6,4},{7,5},{8,10},{9,11},{10,... | collective-permute-start | bytes 24584 | tf_op jit(solution)/shard_map/ppermute | solution.py:510
  7.9 4.5 %collective-permute-start.3 = (bf16[16,256]{1,0:T(8,128)(2,1)S(1)}, bf16[16,256]{1,0:T(8,128)(2,1)S(1)}, u32[]{:S(2)}, u32[]{:S(2)}) collective-permute-start(bf16[16,256]{1,0:T(8,128)(2,1)S(1)} %get-tuple-element.38.refs_1_), channel_id=1, source_target_pairs={{0,4},{1,5},{2,6},{3,7},{4,0},{5,1},{6,2},{7,3},{8,12},{9,13},{10,... | collective-permute-start | bytes 24584 | tf_op jit(solution)/shard_map/ppermute | solution.py:510
  10.5 5.4 %collective-permute-start.4 = (bf16[16,256]{1,0:T(8,128)(2,1)S(1)}, bf16[16,256]{1,0:T(8,128)(2,1)S(1)}, u32[]{:S(2)}, u32[]{:S(2)}) collective-permute-start(bf16[16,256]{1,0:T(8,128)(2,1)S(1)} %get-tuple-element.38.refs_1_), channel_id=1, source_target_pairs={{0,6},{1,7},{2,4},{3,5},{4,2},{5,3},{6,0},{7,1},{8,14},{9,15},{10,... | collective-permute-start | bytes 24584 | tf_op jit(solution)/shard_map/ppermute | solution.py:510
  15.9 2.4 %collective-permute-start.5 = (bf16[16,1024]{1,0:T(8,128)(2,1)S(1)}, bf16[16,1024]{1,0:T(8,128)(2,1)S(1)}, u32[]{:S(2)}, u32[]{:S(2)}) collective-permute-start(bf16[16,1024]{1,0:T(8,128)(2,1)S(1)} %constant_dynamic-update-slice_fusion.refs_1_), channel_id=1, source_target_pairs={{0,8},{1,9},{2,10},{3,11},{4,12},{5,13},{6,14},{7,15},{8,0},{9,1},... | collective-permute-start | bytes 98312 | tf_op jit(solution)/shard_map/ppermute | solution.py:510
  17.4 1.0 %copy-start = (f32[1024,256]{1,0:T(8,128)}, f32[1024,256]{1,0:T(8,128)S(1)}, u32[]{:S(2)}) copy-start(f32[1024,256]{1,0:T(8,128)S(1)} %get-tuple-element.47.refs_3_) | copy-start | bytes 3145732
  19.8 1.0 %copy-start.2 = (f32[1024,256]{1,0:T(8,128)}, f32[1024,256]{1,0:T(8,128)S(1)}, u32[]{:S(2)}) copy-start(f32[1024,256]{1,0:T(8,128)S(1)} %get-tuple-element.48.refs_4_) | copy-start | bytes 3145732
  20.8 10.4 %collective-permute-start.6 = (bf16[544,256]{1,0:T(8,128)(2,1)S(1)}, bf16[544,256]{1,0:T(8,128)(2,1)S(1)}, u32[]{:S(2)}, u32[]{:S(2)}) collective-permute-start(bf16[544,256]{1,0:T(8,128)(2,1)S(1)} %slice.6), channel_id=1, source_target_pairs={{0,16},{1,17},{2,18},{3,19},{4,20},{5,21},{6,22},{7,23},{8,24},{9,... | collective-permute-start | bytes 835592 | tf_op jit(solution)/shard_map/ppermute | solution.py:510
  21.4 0.7 copy-start.7
  21.4 9.8 %collective-permute-start.7 = (bf16[544,256]{1,0:T(8,128)(2,1)S(1)}, bf16[544,256]{1,0:T(8,128)(2,1)S(1)}, u32[]{:S(2)}, u32[]{:S(2)}) collective-permute-start(bf16[544,256]{1,0:T(8,128)(2,1)S(1)} %slice.7), channel_id=1, source_target_pairs={{0,1},{1,0},{2,3},{3,2},{4,5},{5,4},{6,7},{7,6},{8,9},{9,8},{10,11... | collective-permute-start | bytes 835592 | tf_op jit(solution)/shard_map/ppermute | solution.py:510
  22.0 0.7 copy-start.4
  22.0 0.7 copy-start.5
  22.0 0.7 copy-start.6
  23.8 1.2 %copy-start.1 = (f32[1024,256]{1,0:T(8,128)S(1)}, f32[1024,256]{1,0:T(8,128)}, u32[]{:S(2)}) copy-start(f32[1024,256]{1,0:T(8,128)} %copy-done) | copy-start | bytes 3145732
  25.1 1.2 %copy-start.3 = (f32[1024,256]{1,0:T(8,128)S(1)}, f32[1024,256]{1,0:T(8,128)}, u32[]{:S(2)}) copy-start(f32[1024,256]{1,0:T(8,128)} %copy-done.2) | copy-start | bytes 3145732
  32.7 2.7 %collective-permute-start.8 = (f32[1024,256]{1,0:T(8,128)S(1)}, f32[1024,256]{1,0:T(8,128)S(1)}, u32[]{:S(2)}, u32[]{:S(2)}) collective-permute-start(f32[1024,256]{1,0:T(8,128)S(1)} %product.11), channel_id=1, source_target_pairs={{0,8},{1,9},{2,10},{3,11},{4,12},{5,13},{6,14},{7,15},{8,0},{9,1},... | collective-permute-start | bytes 3145736 | tf_op jit(solution)/shard_map/ppermute | solution.py:510
  35.5 14.6 %collective-permute-start.10 = (bf16[256,256]{1,0:T(8,128)(2,1)S(1)}, bf16[256,256]{1,0:T(8,128)(2,1)S(1)}, u32[]{:S(2)}, u32[]{:S(2)}) collective-permute-start(bf16[256,256]{1,0:T(8,128)(2,1)S(1)} %get-tuple-element.59), channel_id=1, source_target_pairs={{0,4},{1,5},{2,6},{3,7},{4,0},{5,1},{6,2},{7,3},{8,12},{9,13},{10,... | collective-permute-start | bytes 393224 | tf_op jit(solution)/shard_map/ppermute | solution.py:510
  37.2 12.8 %collective-permute-start.11 = (bf16[256,256]{1,0:T(8,128)(2,1)S(1)}, bf16[256,256]{1,0:T(8,128)(2,1)S(1)}, u32[]{:S(2)}, u32[]{:S(2)}) collective-permute-start(bf16[256,256]{1,0:T(8,128)(2,1)S(1)} %get-tuple-element.60), channel_id=1, source_target_pairs={{0,6},{1,7},{2,4},{3,5},{4,2},{5,3},{6,0},{7,1},{8,14},{9,15},{10,... | collective-permute-start | bytes 393224 | tf_op jit(solution)/shard_map/ppermute | solution.py:510
  38.6 11.5 %collective-permute-start.9 = (bf16[256,256]{1,0:T(8,128)(2,1)S(1)}, bf16[256,256]{1,0:T(8,128)(2,1)S(1)}, u32[]{:S(2)}, u32[]{:S(2)}) collective-permute-start(bf16[256,256]{1,0:T(8,128)(2,1)S(1)} %get-tuple-element.58), channel_id=1, source_target_pairs={{0,2},{1,3},{2,0},{3,1},{4,6},{5,7},{6,4},{7,5},{8,10},{9,11},{10,... | collective-permute-start | bytes 393224 | tf_op jit(solution)/shard_map/ppermute | solution.py:510
  39.1 3.6 %collective-permute-start.12 = (bf16[16,64]{1,0:T(8,128)(2,1)S(1)}, bf16[16,64]{1,0:T(8,128)(2,1)S(1)}, u32[]{:S(2)}, u32[]{:S(2)}) collective-permute-start(bf16[16,64]{1,0:T(8,128)(2,1)S(1)} %get-tuple-element.63.refs_1_), channel_id=1, source_target_pairs={{0,1},{1,0},{2,3},{3,2},{4,5},{5,4},{6,7},{7,6},{8,9},{9,8},{10,11... | collective-permute-start | bytes 6152 | tf_op jit(solution)/shard_map/ppermute | solution.py:510
  43.6 5.5 %collective-permute-start.13 = (bf16[16,64]{1,0:T(8,128)(2,1)S(1)}, bf16[16,64]{1,0:T(8,128)(2,1)S(1)}, u32[]{:S(2)}, u32[]{:S(2)}) collective-permute-start(bf16[16,64]{1,0:T(8,128)(2,1)S(1)} %get-tuple-element.65.refs_1_), channel_id=1, source_target_pairs={{0,2},{1,3},{2,0},{3,1},{4,6},{5,7},{6,4},{7,5},{8,10},{9,11},{10,... | collective-permute-start | bytes 6152 | tf_op jit(solution)/shard_map/ppermute | solution.py:510
  55.9 5.0 %collective-permute-start.14 = (f32[128,256]{1,0:T(8,128)S(1)}, f32[128,256]{1,0:T(8,128)S(1)}, u32[]{:S(2)}, u32[]{:S(2)}) collective-permute-start(f32[128,256]{1,0:T(8,128)S(1)} %get-tuple-element.67.refs_1_), channel_id=1, source_target_pairs={{0,1},{1,0},{2,3},{3,2},{4,5},{5,4},{6,7},{7,6},{8,9},{9,8},{10,11... | collective-permute-start | bytes 393224 | tf_op jit(solution)/shard_map/ppermute | solution.py:510
  64.0 5.0 %collective-permute-start.15 = (f32[128,256]{1,0:T(8,128)S(1)}, f32[128,256]{1,0:T(8,128)S(1)}, u32[]{:S(2)}, u32[]{:S(2)}) collective-permute-start(f32[128,256]{1,0:T(8,128)S(1)} %get-tuple-element.68.refs_1_), channel_id=1, source_target_pairs={{0,2},{1,3},{2,0},{3,1},{4,6},{5,7},{6,4},{7,5},{8,10},{9,11},{10,... | collective-permute-start | bytes 393224 | tf_op jit(solution)/shard_map/ppermute | solution.py:510

commit v3 on v2

--- a/solution.py
+++ b/solution.py
@@ -12,7 +12,6 @@
 BF16 = jnp.bfloat16
 DOUBLINGS = 9
 VMEM = pl.BlockSpec(memory_space=pltpu.VMEM)
-SMEM = pl.BlockSpec(memory_space=pltpu.SMEM)
 
 
 def vmem(shape, kind=F32):
@@ -20,6 +19,7 @@
 
 
 COST = pl.CostEstimate(flops=0, bytes_accessed=0, transcendentals=0)
+LONG = pl.CostEstimate(flops=10**10, bytes_accessed=0, transcendentals=0)
 PARAMS = pltpu.CompilerParams(vmem_limit_bytes=16 << 20)
 
 
@@ -76,18 +76,26 @@
     return jnp.concatenate([feats, feats, feats, norm_rows(norm, 3, width)], axis=0).astype(BF16)
 
 
-def pack_body(probes_ref, points_ref, packed_ref, own_ref, held_ref, sem):
+def pack_body(*refs):
+    probes_ref, points_ref, *table_refs = refs[:6]
+    packed_ref, own_ref, held_ref, rows_ref, *held_tables, sem = refs[6:]
     quarters, span, _ = probes_ref.shape
     half = quarters // 2
     rows = half * (span + 16)
-    copies = [pltpu.make_async_copy(points_ref, held_ref, sem.at[quarters])]
+    pairs = [(points_ref, held_ref), *zip(table_refs, held_tables)]
+    small = len(pairs)
     for quarter in range(quarters):
         start = quarter // half * rows + quarter % half * span
-        target = packed_ref.at[pl.ds(start, span)]
-        copies.append(pltpu.make_async_copy(probes_ref.at[quarter], target, sem.at[quarter]))
+        pairs.append((probes_ref.at[quarter], packed_ref.at[pl.ds(start, span)]))
+    copies = [
+        pltpu.make_async_copy(source, target, sem.at[pos])
+        for pos, (source, target) in enumerate(pairs)
+    ]
     for copy in copies:
         copy.start()
-    copies[0].wait()
+    rows_ref[...] = jnp.zeros_like(rows_ref)
+    for copy in copies[:small]:
+        copy.wait()
     points = held_ref[...].astype(F32)
     for quarter in range(quarters):
         feats = points[:, quarter, :].astype(BF16)
@@ -95,27 +103,37 @@
         packed_ref[pl.ds(start, 16), :] = feats
         if quarter == 0:
             own_ref[...] = feats
-    for copy in copies[1:]:
+    start = 0
+    for table in held_tables:
+        count, rank = table.shape
+        rows_ref[pl.ds(start, count), pl.ds(0, rank)] = table[...].astype(F32)
+        start += count
+    packed_ref[pl.ds(2 * rows, rows_ref.shape[0]), :] = rows_ref[...].astype(BF16)
+    for copy in copies[small:]:
         copy.wait()
 
 
-def pack(probes, points):
+def pack(probes, points, tables):
     quarters, span, samples = probes.shape
+    table_rows = -(-sum(table.shape[0] for table in tables) // 16) * 16
+    inputs = (probes, points, *tables)
     return pl.pallas_call(
         pack_body,
         out_shape=(
-            vmem((quarters * (span + 16), samples), BF16),
+            vmem((quarters * (span + 16) + table_rows, samples), BF16),
             vmem((16, span), BF16),
         ),
-        in_specs=[pl.BlockSpec(memory_space=pltpu.HBM)] * 2,
+        in_specs=[pl.BlockSpec(memory_space=pltpu.HBM)] * len(inputs),
         scratch_shapes=[
             pltpu.VMEM(points.shape, BF16),
-            pltpu.SemaphoreType.DMA((quarters + 1,)),
+            pltpu.VMEM((table_rows, samples), F32),
+            *[pltpu.VMEM(table.shape, jnp.int32) for table in tables],
+            pltpu.SemaphoreType.DMA((quarters + 1 + len(tables),)),
         ],
         cost_estimate=COST,
         compiler_params=PARAMS,
         name="pack",
-    )(*(pltpu.with_memory_space_constraint(value, pltpu.HBM) for value in (probes, points)))
+    )(*(pltpu.with_memory_space_constraint(value, pltpu.HBM) for value in inputs))
 
 
 def masked(entries):
@@ -127,87 +145,114 @@
 
 def add_source(source_ref, row_refs, cols_ref, put, span, own):
     size = 2 * (span + 16)
-    parts = range(0, source_ref.shape[0], size)
+    parts = range(0, source_ref.shape[0] // size * size, size)
     for number, part in enumerate(parts):
         for quarter in range(2):
             feats = source_ref[pl.ds(part + 2 * span + 16 * quarter, 16), :]
             cols_ref[:, pl.ds((2 * number + quarter) * span, span)] = col_features(feats)
     columns = 2 * span * len(parts)
-    for half, rows_ref in enumerate(row_refs):
+    for group, rows_ref in enumerate(row_refs):
         for start in range(0, rows_ref.shape[0], span):
             feats = rows_ref[pl.ds(start, span), :]
             entries = jnp.exp2(over(feats, cols_ref[:, :columns], 1, 0))
-            if own and half == 0 and start == 0:
+            if own and group == 0 and start == 0:
                 entries = jnp.concatenate([masked(entries[:, :span]), entries[:, span:]], axis=1)
             randoms = [source_ref[pl.ds(part, 2 * span), :] for part in parts]
-            put(half, start, over(entries.astype(BF16), jnp.concatenate(randoms, axis=0), 1, 0))
-
-
-def product_body(gain, span, first, own, source_count, half_count, *refs):
-    refs = list(refs)
-    cols_ref = refs.pop()
-    take = lambda count: [refs.pop(0) for _ in range(count)]
-    sources = take(source_count)
-    if first:
-        point_refs, row_refs = take(half_count), take(half_count)
-        for points_ref, rows_ref in zip(point_refs, row_refs):
-            for start in range(0, points_ref.shape[1], span):
-                feats = points_ref[:, pl.ds(start, span)]
-                rows_ref[pl.ds(start, span), :] = row_features(feats, gain).T.astype(BF16)
-    else:
-        row_refs, old_refs = take(half_count), take(half_count)
-    total_refs = take(half_count)
+            put(group, start, over(entries.astype(BF16), jnp.concatenate(randoms, axis=0), 1, 0))
+
+
+def first_product_body(gain, span, own, groups, point_count, *refs):
+    source_ref, *point_refs = refs[: point_count + 1]
+    row_refs = refs[point_count + 1 : point_count + 1 + len(groups)]
+    total_refs, cols_ref = refs[point_count + 1 + len(groups) : -1], refs[-1]
+    for rows_ref, places in zip(row_refs, groups):
+        for pos, (array, start) in enumerate(places):
+            feats = point_refs[array][:, pl.ds(start, span)]
+            rows_ref[pl.ds(pos * span, span), :] = row_features(feats, gain).T.astype(BF16)
+
+    def put(group, start, value):
+        total_refs[group][pl.ds(start, span), :] = value
+
+    add_source(source_ref, row_refs, cols_ref, put, span, own)
+
+
+def first_product(source, points, groups, span, gain, own):
+    samples = source.shape[1]
+    rows = [len(places) * span for places in groups]
+    out = pl.pallas_call(
+        lambda *refs: first_product_body(gain, span, own, groups, len(points), *refs),
+        out_shape=[vmem((count, 64), BF16) for count in rows]
+        + [vmem((count, samples), F32) for count in rows],
+        scratch_shapes=[pltpu.VMEM((64, 4 * span), BF16)],
+        cost_estimate=COST,
+        compiler_params=PARAMS,
+        name="first_product",
+    )(source, *points)
+    return out[: len(groups)], out[len(groups) :]
+
+
+def product_body(span, source_count, count, *refs):
+    sources, refs = refs[:source_count], refs[source_count:]
+    row_refs, old_refs, total_refs = refs[:count], refs[count : 2 * count], refs[2 * count : -1]
+    cols_ref = refs[-1]
     for number, source in enumerate(sources):
 
-        def put(half, start, value):
+        def put(group, start, value):
             place = pl.ds(start, span)
-            if number > 0:
-                total_refs[half][place, :] += value
-            elif first:
-                total_refs[half][place, :] = value
-            else:
-                total_refs[half][place, :] = old_refs[half][place, :] + value
-
-        add_source(source, row_refs, cols_ref, put, span, first and own and number == 0)
-
-
-def product(sources, rows, span, totals=None, gain=None, own=True):
-    samples = sources[0].shape[1]
-    first = totals is None
-    count = len(rows)
-    counts = [half.shape[1] if first else half.shape[0] for half in rows]
-    columns = max(s.shape[0] // (span + 16) * span for s in sources)
-    out = [vmem((count, samples), F32) for count in counts]
-    if first:
-        out = [vmem((count, 64), BF16) for count in counts] + out
-    out = pl.pallas_call(
-        lambda *refs: product_body(gain, span, first, own, len(sources), count, *refs),
-        out_shape=out,
-        scratch_shapes=[pltpu.VMEM((64, columns), BF16)],
+            base = old_refs if number == 0 else total_refs
+            total_refs[group][place, :] = base[group][place, :] + value
+
+        add_source(source, row_refs, cols_ref, put, span, False)
+
+
+def product(sources, rows, totals, span):
+    return pl.pallas_call(
+        lambda *refs: product_body(span, len(sources), len(rows), *refs),
+        out_shape=[vmem(total.shape, F32) for total in totals],
+        scratch_shapes=[pltpu.VMEM((64, 4 * span), BF16)],
         cost_estimate=COST,
         compiler_params=PARAMS,
         name="product",
-    )(*sources, *rows, *([] if first else totals))
-    return (out[:count], out[count:]) if first else out
-
-
-def combine_body(span, mine_ref, theirs_ref, own_ref, *sent_refs):
-    own_ref[...] = mine_ref[pl.ds(0, span), :] + theirs_ref[pl.ds(0, span), :]
-    for number, sent_ref in enumerate(sent_refs):
-        place = pl.ds((number + 1) * span, span)
-        sent_ref[...] = (mine_ref[place, :] + theirs_ref[place, :]).astype(BF16)
-
-
-def combine(mine, theirs, span):
-    rows, samples = mine.shape
-    return pl.pallas_call(
-        lambda *refs: combine_body(span, *refs),
-        out_shape=[vmem((span, samples), F32)]
-        + [vmem((span, samples), BF16)] * (rows // span - 1),
-        cost_estimate=COST,
-        compiler_params=PARAMS,
-        name="combine",
-    )(mine, theirs)
+    )(*sources, *rows, *totals)
+
+
+def halves_body(first_ref, second_ref, first_half, second_half):
+    rows = first_half.shape[0]
+    first_half[...] = first_ref[pl.ds(0, rows), :]
+    second_half[...] = second_ref[pl.ds(rows, rows), :]
+
+
+def halves(first, second, rows):
+    return pl.pallas_call(
+        halves_body,
+        out_shape=[vmem((rows, first.shape[1]), BF16)] * 2,
+        cost_estimate=COST,
+        compiler_params=PARAMS,
+        name="halves",
+    )(first, second)
+
+
+def add_up_body(span, kept, sent, mine_ref, theirs_ref, *refs):
+    kept_ref, sent_ref = refs[-2:]
+    for chunks, out_ref in ((kept, kept_ref), (sent, sent_ref)):
+        for pos, chunk in enumerate(chunks):
+            place = pl.ds(chunk * span, span)
+            value = mine_ref[place, :] + theirs_ref[place, :].astype(F32)
+            out_ref[pl.ds(pos * span, span), :] = value.astype(out_ref.dtype)
+
+
+def add_up(mine, theirs, kept, sent, span, after=(), cost=COST):
+    samples = mine.shape[1]
+    return pl.pallas_call(
+        lambda *refs: add_up_body(span, kept, sent, *refs),
+        out_shape=(
+            vmem((len(kept) * span, samples), F32),
+            vmem((len(sent) * span, samples), BF16),
+        ),
+        cost_estimate=cost,
+        compiler_params=PARAMS,
+        name="add_up",
+    )(mine, theirs, *after)
 
 
 def wide_product(first, second, second_dim):
@@ -321,7 +366,7 @@
     copy.wait()
 
 
-def leaves(own, others, source, picks, couplings, upper_couplings, leaf_count):
+def leaves(own, others, source, picks, couplings, later, leaf_count):
     samples = own.shape[1]
     rank, pool = picks.shape[1:]
     return pl.pallas_call(
@@ -336,10 +381,14 @@
         cost_estimate=COST,
         compiler_params=PARAMS,
         name="leaves",
-    )(own, *others, source, picks, couplings, *upper_couplings)
-
-
-def level_body(number, place_ref, mine_ref, theirs_ref, picks_ref, couplings_ref, *refs):
+    )(own, *others, source, picks, couplings, later)
+
+
+def first_of_pair(number):
+    return (lax.axis_index("col") >> (number - 2)) % 2 == 0
+
+
+def level_body(number, mine_ref, theirs_ref, picks_ref, couplings_ref, *refs):
     rank = picks_ref.shape[1]
     if number == 2:
         upper_ref, state_ref = refs
@@ -364,7 +413,7 @@
         if number > 2:
             copies[2].start()
 
-    mine_first = place_ref[number - 2] == 0
+    mine_first = first_of_pair(number)
     mine, theirs = mine_ref[...], theirs_ref[...]
     first = jnp.where(mine_first, mine, theirs)
     second = jnp.where(mine_first, theirs, mine)
@@ -384,7 +433,7 @@
             copy.wait()
 
 
-def level(number, place, mine, theirs, picks, couplings, below=()):
+def level(number, mine, theirs, picks, couplings, below=()):
     rank, pool = picks.shape[1:]
     samples = mine.shape[1]
     out_shape = (
@@ -404,21 +453,21 @@
     return pl.pallas_call(
         lambda *refs: level_body(number, *refs),
         out_shape=out_shape,
-        in_specs=[SMEM] + [VMEM] * (4 + len(below)),
+        in_specs=[VMEM] * (4 + len(below)),
         out_specs=out_specs,
         scratch_shapes=scratch,
         cost_estimate=COST,
         compiler_params=PARAMS,
         name="level",
-    )(place, mine, theirs, picks, couplings, *below)
+    )(mine, theirs, picks, couplings, *below)
 
 
 def one_hot(chosen, pool):
     place = lax.broadcasted_iota(jnp.int32, (pool, chosen.shape[1]), 0)
-    return jnp.where(place == chosen, 1.0, 0.0).astype(F32)
-
-
-def couple(first, second, picks, gain, couplings_ref, points_ref):
+    return jnp.where(place.astype(F32) == chosen, 1.0, 0.0).astype(F32)
+
+
+def couple(first, second, picks, gain, couplings_ref):
     rank = first.shape[1]
     points = jnp.concatenate([first, second], axis=1)
     entries = jnp.exp2(over(row_features(points, gain).astype(BF16), col_features(points), 0, 0))
@@ -428,78 +477,88 @@
     chosen = select_rows(picks.T.astype(BF16), entries)
     high, middle, low = split(jnp.concatenate([entries, chosen], axis=0))
     couplings_ref[...] = jnp.concatenate([high, high, middle, middle, low, high], axis=1)
-    if points_ref is not None:
-        points_ref[...] = over(points, picks, 1, 0).astype(BF16)
 
 
 def coupling_shape(rank):
     return vmem((3 * rank, 12 * rank), BF16)
 
 
-def skeletons_body(gain, place_ref, own_ref, leaf_ref, one_ref, two_ref, three_ref, *refs):
-    picks_ref, couplings_ref, points_ref = refs
-    count, rank = leaf_ref.shape
-    rows = [leaf_ref[leaf : leaf + 1, :] for leaf in range(count)]
-    rows.append(one_ref[...])
-    rows.append(two_ref[pl.ds(place_ref[2], 1), :])
-    rows.append(three_ref[pl.ds(place_ref[3], 1), :])
-    hots = [one_hot(row, picks_ref.shape[2]) for row in rows]
-    for number, hot in enumerate(hots):
-        picks_ref[number] = hot.T.astype(BF16)
-    children = [
-        over(own_ref[:, pl.ds(leaf * LEAF, LEAF)], hots[leaf].astype(BF16), 1, 0)
-        for leaf in range(count)
-    ]
-    couple(*children, hots[count], gain, couplings_ref, points_ref)
-
-
-def skeletons(place, own_points, tables, gain):
+def skeletons_body(gain, span, counts, mine_ref, beside_ref, *refs):
+    picks_ref, one_ref, two_ref, points_ref = refs
+    rank, pool = picks_ref.shape[1:]
+    leaf_count = counts[0]
+    tables = 4 * (span + 16)
+    nodes = []
+    for source_ref in (mine_ref, beside_ref):
+        rows = source_ref[pl.ds(tables, source_ref.shape[0] - tables), :rank].astype(F32)
+        hots = [one_hot(rows[pos : pos + 1], pool) for pos in range(leaf_count + 1)]
+        children = []
+        for leaf in range(leaf_count):
+            feats = source_ref[pl.ds(2 * span, 16), pl.ds(leaf * LEAF, LEAF)]
+            children.append(over(feats, hots[leaf].astype(BF16), 1, 0))
+        points = jnp.concatenate(children, axis=1)
+        nodes.append(over(points, hots[leaf_count], 1, 0))
+        if source_ref is mine_ref:
+            couple(*children, hots[leaf_count], gain, one_ref)
+            table, start = rows, leaf_count + counts[1]
+            for number, count in enumerate(counts[2:]):
+                wanted = start + (lax.axis_index("col") >> (number + 1))
+                place = lax.broadcasted_iota(jnp.int32, table.shape, 0)
+                row = jnp.sum(jnp.where(place == wanted, table, 0.0), axis=0, keepdims=True)
+                hots.append(one_hot(row, pool))
+                start += count
+            for number, hot in enumerate(hots):
+                picks_ref[number] = hot.T.astype(BF16)
+            upper = hots[leaf_count + 1]
+    mine, theirs = nodes
+    mine_first = first_of_pair(2)
+    first = jnp.where(mine_first, mine, theirs)
+    second = jnp.where(mine_first, theirs, mine)
+    couple(first, second, upper, gain, two_ref)
+    points_ref[...] = over(jnp.concatenate([first, second], axis=1), upper, 1, 0).astype(BF16)
+
+
+def skeletons(packed, beside, tables, span, gain):
     leaf_count, rank = tables[0].shape
-    return pl.pallas_call(
-        lambda *refs: skeletons_body(gain, *refs),
+    counts = [table.shape[0] for table in tables]
+    return pl.pallas_call(
+        lambda *refs: skeletons_body(gain, span, counts, *refs),
         out_shape=(
             vmem((leaf_count + 3, rank, LEAF), BF16),
             coupling_shape(rank),
+            coupling_shape(rank),
             vmem((16, rank), BF16),
         ),
-        in_specs=[SMEM] + [VMEM] * 5,
         cost_estimate=COST,
         compiler_params=PARAMS,
         name="skeletons",
-    )(place, own_points, *tables)
-
-
-def couplings_body(gain, number, place_ref, mine_ref, theirs_ref, picks_ref, couplings_ref, *refs):
-    mine_first = place_ref[number - 2] == 0
+    )(packed, beside)
+
+
+def top_couplings_body(gain, mine_ref, theirs_ref, picks_ref, couplings_ref):
+    mine_first = first_of_pair(3)
     mine, theirs = mine_ref[...].astype(F32), theirs_ref[...].astype(F32)
     first = jnp.where(mine_first, mine, theirs)
     second = jnp.where(mine_first, theirs, mine)
-    picks = picks_ref[picks_ref.shape[0] + number - 4].astype(F32).T
-    couple(first, second, picks, gain, couplings_ref, refs[0] if refs else None)
-
-
-def couplings(number, place, mine, theirs, picks, gain):
-    rank = picks.shape[1]
-    out_shape = [coupling_shape(rank)]
-    if number == 2:
-        out_shape.append(vmem(mine.shape, BF16))
-    return pl.pallas_call(
-        lambda *refs: couplings_body(gain, number, *refs),
-        out_shape=out_shape,
-        in_specs=[SMEM] + [VMEM] * 3,
-        cost_estimate=COST,
-        compiler_params=PARAMS,
-        name="couplings",
-    )(place, mine, theirs, picks)
+    picks = picks_ref[picks_ref.shape[0] - 1].astype(F32).T
+    couple(first, second, picks, gain, couplings_ref)
+
+
+def top_couplings(mine, theirs, picks, gain):
+    return pl.pallas_call(
+        lambda *refs: top_couplings_body(gain, *refs),
+        out_shape=coupling_shape(picks.shape[1]),
+        cost_estimate=COST,
+        compiler_params=PARAMS,
+        name="top_couplings",
+    )(mine, theirs, picks)
 
 
 def local(probes, points, leaf_skeleton, skeleton_one, skeleton_two, skeleton_three):
     span = probes.shape[1]
     row_count = lax.axis_size("row")
     col_count = lax.axis_size("col")
-    col_pos = lax.axis_index("col")
     gain = 16.0 / math.sqrt(4 * span * row_count * col_count)
-    place = jnp.stack([col_pos & 1, col_pos >> 1 & 1, col_pos >> 1, col_pos >> 2])
 
     def swap(value, row_bits, col_bits):
         pairs = [
@@ -509,57 +568,78 @@
         ]
         return lax.ppermute(value, ("row", "col"), pairs)
 
-    packed, own_points = pack(probes, points)
+    tables = (leaf_skeleton, skeleton_one, skeleton_two, skeleton_three)
+    packed, own_points = pack(probes, points, tables)
     beside = swap(packed, 0, 1)
     across = swap(packed, 2, 0)
-    line_points = [own_points]
-    for offset in range(1, col_count // 2):
-        line_points.append(swap(own_points, 0, 2 * offset))
-    line_points = jnp.concatenate(line_points, axis=1)
-    row_points = [line_points, swap(line_points, 1, 0)]
-
-    row_feats, totals = product([packed], row_points[:1], span, gain=gain)
-    more_feats, more_totals = product([packed], row_points[1:], span, gain=gain, own=False)
-    row_feats, totals = row_feats + more_feats, totals + more_totals
+    line = col_count // 2
+    line_points = [own_points] + [swap(own_points, 0, 2 * chunk) for chunk in range(1, line)]
+    sibling_points = swap(jnp.concatenate(line_points, axis=1), 1, 0)
+    near, far = range(2), range(2, line)
+    feats, totals = first_product(
+        packed,
+        line_points,
+        [[(chunk, 0) for chunk in group] for group in (near, far)],
+        span,
+        gain,
+        True,
+    )
+    more = first_product(
+        packed,
+        [sibling_points],
+        [[(0, chunk * span) for chunk in group] for group in (near, far)],
+        span,
+        gain,
+        False,
+    )
+    feats, totals = [*feats, *more[0]], [*totals, *more[1]]
     beside, across, *totals = lax.optimization_barrier((beside, across, *totals))
     pieces = [packed, beside, across]
-    half = packed.shape[0] // 2
-    diagonal = [swap(beside[:half], 2, 0), swap(across[half:], 0, 1)]
-    totals = product([beside], row_feats, span, totals)
-    totals = product([across], row_feats, span, totals)
-    tables = (leaf_skeleton, skeleton_one, skeleton_two, skeleton_three)
-    picks, couplings_one, points_one = skeletons(place, own_points, tables, gain)
-    points_one, *totals = lax.optimization_barrier((points_one, *totals))
+    relayed = halves(beside, across, 2 * (span + 16))
+    diagonal = [swap(relayed[0], 2, 0), swap(relayed[1], 0, 1)]
+    picks, couplings_one, couplings_two, points_two = skeletons(packed, beside, tables, span, gain)
+    totals = product([beside], feats, totals, span)
+    totals = product([across], feats, totals, span)
+    points_two, *totals = lax.optimization_barrier((points_two, *totals))
     pieces += diagonal
     for bit in range(2, row_count.bit_length() - 1):
         more = [swap(value, 1 << bit, 0) for value in pieces]
-        totals = product(more, row_feats, span, totals)
+        totals = product(more, feats, totals, span)
         pieces += more
-    (theirs,) = product(diagonal, row_feats[1:], span, totals[1:])
+    (theirs,) = product(diagonal, feats[3:], totals[3:], span)
     from_sibling = swap(theirs, 1, 0)
-    (mine,) = product(diagonal, row_feats[:1], span, totals[:1])
-    kept, *sent = combine(mine, from_sibling, span)
-    received = [swap(value, 0, 2 * (number + 1)) for number, value in enumerate(sent)]
-
-    points_one, kept = lax.optimization_barrier((points_one, kept))
-    couplings_two, points_two = couplings(
-        2, place, points_one, swap(points_one, 0, 1), picks, gain
-    )
-    (couplings_three,) = couplings(3, place, points_two, swap(points_two, 0, 2), picks, gain)
-
-    leaf_count = leaf_skeleton.shape[0]
+    (mine,) = product(diagonal, feats[1:2], totals[1:2], span)
+    kept, sent = add_up(mine, from_sibling, range(0, line - 2, 2), range(1, line - 2, 2), span)
+    sent, total = lax.optimization_barrier((sent, totals[2]))
+    arrived = swap(sent, 0, 2)
+    (theirs,) = product(diagonal, feats[2:3], [total], span)
+    from_sibling = swap(theirs, 1, 0)
+    (mine,) = product(diagonal, feats[:1], totals[:1], span)
+    received = []
+    beside_two = swap(points_two, 0, 2)
+    chunks = list(range(2, line, 2))
+    bit = 2
+    while chunks:
+        sent_places = [pos for pos, chunk in enumerate(chunks) if chunk & bit]
+        kept_places = [pos for pos, chunk in enumerate(chunks) if not chunk & bit]
+        kept, sent = add_up(
+            kept, arrived, kept_places or sent_places, sent_places, span, (beside_two,), LONG
+        )
+        arrived = swap(sent, 0, 2 * bit)
+        received.append(arrived[:span] if len(sent_places) > 1 else arrived)
+        arrived = arrived[span:]
+        chunks = [chunks[pos] for pos in kept_places]
+        bit *= 2
+    own_sum, near_sent = add_up(mine, from_sibling, [0], [1], span, (sent,))
+    received.append(swap(near_sent, 0, 2))
+
+    couplings_three = top_couplings(points_two, beside_two, picks, gain)
     leaf_interp, interp_one, state = leaves(
-        kept, received, packed, picks, couplings_one, (couplings_two, couplings_three), leaf_count
-    )
-    interp_two, state_two = level(2, place, state, swap(state, 0, 1), picks, couplings_two)
+        own_sum, received, packed, picks, couplings_one, couplings_three, leaf_skeleton.shape[0]
+    )
+    interp_two, state_two = level(2, state, swap(state, 0, 1), picks, couplings_two)
     upper_interp, top_state = level(
-        3,
-        place,
-        state_two,
-        swap(state_two, 0, 2),
-        picks,
-        couplings_three,
-        (interp_one, interp_two),
+        3, state_two, swap(state_two, 0, 2), picks, couplings_three, (interp_one, interp_two)
     )
     return jnp.swapaxes(leaf_interp, 1, 2), jnp.swapaxes(upper_interp, 2, 3), top_state
 

time: 73.2 us -> 67.4 us (0.921)
  local copies, waits for them, and re-layouts: 5.07 us -> 0 us
  Pallas kernels: 27.6 us -> 26.5 us
    unnamed x19 -> x0, local copies, waits for them, and re-layouts: 5.03 us -> none
    pallas_call x2, Pallas kernels: 6.84 us -> 5.75 us  [level(): pl.pallas_call(lambda *refs: level_body(number, *refs), out_shape=out_sha...]
    pallas_call x11 -> x15, Pallas kernels: 14.9 us -> 15.2 us  [the longest x6 8.53 us: product(): pl.pallas_call(lambda *refs: product_body(span, len(sources), len(rows),...]
  transfers between devices with their start and end apart: 16 -> 16, of which waited for: 7 -> 10; matrix products, arithmetic and copies ran while one was open for 0% -> 0% of each run, Pallas kernels for 17% -> 19%
where the time goes in v3:
time: 67.4 us; the launch traced here: 67.3 us
  Pallas kernels  26.5 us (39%)
  waiting for transfers between devices  20.1 us (30%)
  starting transfers between devices  19.7 us (29%)
  between operations  0.94 us (1%)
    ppermute x16, waiting for transfers between devices, swap(): return lax.ppermute(value, ('row', 'col'), pairs)  20.1 us
    ppermute x16, starting transfers between devices, swap(): return lax.ppermute(value, ('row', 'col'), pairs)  19.7 us
    pallas_call x6, Pallas kernels, product(): pl.pallas_call(lambda *refs: product_body(span, len(sources), len(rows),...  8.53 us
    pallas_call x2, Pallas kernels, level(): pl.pallas_call(lambda *refs: level_body(number, *refs), out_shape=out_sha...  5.75 us
    pallas_call x1, Pallas kernels, leaves(): pl.pallas_call(lambda *refs: leaves_body(len(others), *refs), out_shape=(...  5.59 us
    pallas_call x2, Pallas kernels, first_product(): pl.pallas_call(lambda *refs: first_product_body(gain, span, own, groups,...  2.91 us
  transfers between devices with their start and end apart: 16, of which 10 were waited for; matrix products, arithmetic and copies ran while one was open for 0% of the time, Pallas kernels for 19%

profile of v3, /device:TPU:0, one launch (start us, length us, event | category | flops | bytes accessed | tf_op | source)
XLA Modules:
  0.0 67.3 jit_solution(10410247809452405707)
XLA Ops:
  0.6 1.3 %pack.1 = (bf16[1104,256]{1,0:T(8,128)(2,1)S(1)}, bf16[16,256]{1,0:T(8,128)(2,1)S(1)}) custom-call(bf16[4,256,256]{2,1,0:T(8,128)(2,1)} %refs_0_.1, bf16[16,4,256]{2,1,0:T(4,128)(2,1)} %refs_1_.1, s32[2,64]{1,0:T(2,128)} %refs_2_.1, s32[1,64]{1,0:T(1,128)} %refs_3_.1, s32[4,64]{1,0:T(4,128)} %refs_4_.1, s32[2,64]{1,0:T(2,128)} %refs_5_.1), custom_call_target="tpu_custom_call" | custom-call | tf_op jit(solution)/shard_map/pack/pallas_call | solution.py:120
  1.9 3.0 %collective-permute-start.1 = (bf16[1104,256]{1,0:T(8,128)(2,1)S(1)}, bf16[1104,256]{1,0:T(8,128)(2,1)S(1)}, u32[]{:S(2)}, u32[]{:S(2)}) collective-permute-start(bf16[1104,256]{1,0:T(8,128)(2,1)S(1)} %get-tuple-element.52.refs_0_.refs_3_), channel_id=1, source_target_pairs={{0,16},{1,17},{2,18},{3,19},{4,20},{5,21},{6,22},{7,23},{8,24},{9,... | collective-permute-start | bytes 1695752 | tf_op jit(solution)/shard_map/ppermute | solution.py:569
  4.9 1.5 %collective-permute-start = (bf16[1104,256]{1,0:T(8,128)(2,1)S(1)}, bf16[1104,256]{1,0:T(8,128)(2,1)S(1)}, u32[]{:S(2)}, u32[]{:S(2)}) collective-permute-start(bf16[1104,256]{1,0:T(8,128)(2,1)S(1)} %get-tuple-element.52.refs_0_.refs_3_), channel_id=1, source_target_pairs={{0,1},{1,0},{2,3},{3,2},{4,5},{5,4},{6,7},{7,6},{8,9},{9,8},{10,11... | collective-permute-start | bytes 1695752 | tf_op jit(solution)/shard_map/ppermute | solution.py:569
  6.4 3.6 %collective-permute-start.4 = (bf16[16,256]{1,0:T(8,128)(2,1)S(1)}, bf16[16,256]{1,0:T(8,128)(2,1)S(1)}, u32[]{:S(2)}, u32[]{:S(2)}) collective-permute-start(bf16[16,256]{1,0:T(8,128)(2,1)S(1)} %get-tuple-element.53.refs_1_), channel_id=1, source_target_pairs={{0,6},{1,7},{2,4},{3,5},{4,2},{5,3},{6,0},{7,1},{8,14},{9,15},{10,... | collective-permute-start | bytes 24584 | tf_op jit(solution)/shard_map/ppermute | solution.py:569
  10.0 0.0 collective-permute-start.3
  10.0 0.8 %collective-permute-start.2 = (bf16[16,256]{1,0:T(8,128)(2,1)S(1)}, bf16[16,256]{1,0:T(8,128)(2,1)S(1)}, u32[]{:S(2)}, u32[]{:S(2)}) collective-permute-start(bf16[16,256]{1,0:T(8,128)(2,1)S(1)} %get-tuple-element.53.refs_1_), channel_id=1, source_target_pairs={{0,2},{1,3},{2,0},{3,1},{4,6},{5,7},{6,4},{7,5},{8,10},{9,11},{10,... | collective-permute-start | bytes 24584 | tf_op jit(solution)/shard_map/ppermute | solution.py:569
  10.8 1.1 %collective-permute-done.4.refs_4_ = bf16[16,256]{1,0:T(8,128)(2,1)S(1)} collective-permute-done((bf16[16,256]{1,0:T(8,128)(2,1)S(1)}, bf16[16,256]{1,0:T(8,128)(2,1)S(1)}, u32[]{:S(2)}, u32[]{:S(2)}) %collective-permute-start.4) | collective-permute-done | bytes 8224 | tf_op jit(solution)/shard_map/ppermute | solution.py:569
  11.9 2.7 %collective-permute-done.3.refs_3_ = bf16[16,256]{1,0:T(8,128)(2,1)S(1)} collective-permute-done((bf16[16,256]{1,0:T(8,128)(2,1)S(1)}, bf16[16,256]{1,0:T(8,128)(2,1)S(1)}, u32[]{:S(2)}, u32[]{:S(2)}) %collective-permute-start.3) | collective-permute-done | bytes 8224 | tf_op jit(solution)/shard_map/ppermute | solution.py:569
  14.6 0.0 collective-permute-done.2.refs_2_
  14.6 0.0 collective-permute-start.5
  14.6 1.5 %first_product.2 = (bf16[512,64]{1,0:T(8,128)(2,1)S(1)}, bf16[512,64]{1,0:T(8,128)(2,1)S(1)}, f32[512,256]{1,0:T(8,128)S(1)}, f32[512,256]{1,0:T(8,128)S(1)}) custom-call(bf16[1104,256]{1,0:T(8,128)(2,1)S(1)} %get-tuple-element.52.refs_0_.refs_3_, bf16[16,256]{1,0:T(8,128)(2,1)S(1)} %get-tuple-element.53.refs_1_, ...), custom_call_target="tpu_custom_call" | custom-call | tf_op jit(solution)/shard_map/first_product/pallas_call | solution.py:182
  16.0 0.0 collective-permute-done.5.refs_1_
  16.1 1.5 %first_product.3 = (bf16[512,64]{1,0:T(8,128)(2,1)S(1)}, bf16[512,64]{1,0:T(8,128)(2,1)S(1)}, f32[512,256]{1,0:T(8,128)S(1)}, f32[512,256]{1,0:T(8,128)S(1)}) custom-call(bf16[1104,256]{1,0:T(8,128)(2,1)S(1)} %get-tuple-element.52.refs_0_.refs_3_, bf16[16,1024]{1,0:T(8,128)(2,1)S(1)} %collective-permute-done.5.refs_1_), custom_call_target="tpu_custom_call" | custom-call | tf_op jit(solution)/shard_map/first_product/pallas_call | solution.py:182
  17.5 0.2 collective-permute-done.1.second_ref.refs_0_
  17.7 1.5 %collective-permute-done.first_ref.refs_1_.refs_0_ = bf16[1104,256]{1,0:T(8,128)(2,1)S(1)} collective-permute-done((bf16[1104,256]{1,0:T(8,128)(2,1)S(1)}, bf16[1104,256]{1,0:T(8,128)(2,1)S(1)}, u32[]{:S(2)}, u32[]{:S(2)}) %collective-permute-start) | collective-permute-done | bytes 565280 | tf_op jit(solution)/shard_map/ppermute | solution.py:569
  19.2 0.4 collective-permute-start.6
  19.7 1.6 %collective-permute-start.7 = (bf16[544,256]{1,0:T(8,128)(2,1)S(1)}, bf16[544,256]{1,0:T(8,128)(2,1)S(1)}, u32[]{:S(2)}, u32[]{:S(2)}) collective-permute-start(bf16[544,256]{1,0:T(8,128)(2,1)S(1)} %get-tuple-element.61), channel_id=1, source_target_pairs={{0,1},{1,0},{2,3},{3,2},{4,5},{5,4},{6,7},{7,6},{8,9},{9,8},{10,11... | collective-permute-start | bytes 835592 | tf_op jit(solution)/shard_map/ppermute | solution.py:569
  21.3 1.2 %skeletons.1 = (bf16[5,64,128]{2,1,0:T(8,128)(2,1)S(1)}, bf16[192,768]{1,0:T(8,128)(2,1)S(1)}, bf16[192,768]{1,0:T(8,128)(2,1)S(1)}, bf16[16,64]{1,0:T(8,128)(2,1)S(1)}) custom-call(bf16[1104,256]{1,0:T(8,128)(2,1)S(1)} %get-tuple-element.52.refs_0_.refs_3_, bf16[1104,256]{1,0:T(8,128)(2,1)S(1)} %collective-permute-done.first_ref.refs_1_.refs_0_), custom_call_target="tpu_custom_call" | custom-call | tf_op jit(solution)/shard_map/skeletons/pallas_call | solution.py:524
  22.5 2.5 %product.6 = (f32[512,256]{1,0:T(8,128)S(1)}, f32[512,256]{1,0:T(8,128)S(1)}, f32[512,256]{1,0:T(8,128)S(1)}, f32[512,256]{1,0:T(8,128)S(1)}) custom-call(bf16[1104,256]{1,0:T(8,128)(2,1)S(1)} %collective-permute-done.first_ref.refs_1_.refs_0_, bf16[512,64]{1,0:T(8,128)(2,1)S(1)} %get-tuple-element.62.refs_1_.refs_2_, ...), custom_call_target="tpu_custom_call" | custom-call | tf_op jit(solution)/shard_map/product/pallas_call | solution.py:209
  24.9 2.5 %product.7 = (f32[512,256]{1,0:T(8,128)S(1)}, f32[512,256]{1,0:T(8,128)S(1)}, f32[512,256]{1,0:T(8,128)S(1)}, f32[512,256]{1,0:T(8,128)S(1)}) custom-call(bf16[1104,256]{1,0:T(8,128)(2,1)S(1)} %collective-permute-done.1.second_ref.refs_0_, bf16[512,64]{1,0:T(8,128)(2,1)S(1)} %get-tuple-element.62.refs_1_.refs_2_, ...), custom_call_target="tpu_custom_call" | custom-call | tf_op jit(solution)/shard_map/product/pallas_call | solution.py:209
  27.5 0.0 collective-permute-done.6.refs_0_
  27.5 0.0 collective-permute-done.7.refs_1_
  27.5 0.9 %product.10 = f32[512,256]{1,0:T(8,128)S(1)} custom-call(bf16[544,256]{1,0:T(8,128)(2,1)S(1)} %collective-permute-done.6.refs_0_, bf16[544,256]{1,0:T(8,128)(2,1)S(1)} %collective-permute-done.7.refs_1_, bf16[512,64]{1,0:T(8,128)(2,1)S(1)} %get-tuple-element.66.refs_4_.refs_2_, f32[512,256]{1,0:T(8,128)S(1)} %get-tuple-element.81.refs_3_), custom_call_target="tpu_custom_call" | custom-call | tf_op jit(solution)/shard_map/product/pallas_call | solution.py:209
  28.4 0.1 collective-permute-start.8
  28.5 0.9 %product.9.refs_0_ = f32[512,256]{1,0:T(8,128)S(1)} custom-call(bf16[544,256]{1,0:T(8,128)(2,1)S(1)} %collective-permute-done.6.refs_0_, bf16[544,256]{1,0:T(8,128)(2,1)S(1)} %collective-permute-done.7.refs_1_, bf16[512,64]{1,0:T(8,128)(2,1)S(1)} %get-tuple-element.64.refs_2_, f32[512,256]{1,0:T(8,128)S(1)} %get-tuple-element.80.refs_3_), custom_call_target="tpu_custom_call" | custom-call | tf_op jit(solution)/shard_map/product/pallas_call | solution.py:209
  29.3 1.0 %collective-permute-done.8.refs_1_ = f32[512,256]{1,0:T(8,128)S(1)} collective-permute-done((f32[512,256]{1,0:T(8,128)S(1)}, f32[512,256]{1,0:T(8,128)S(1)}, u32[]{:S(2)}, u32[]{:S(2)}) %collective-permute-start.8) | collective-permute-done | bytes 524320 | tf_op jit(solution)/shard_map/ppermute | solution.py:569
  30.4 0.1 add_up.3
  30.4 1.6 %collective-permute-start.10 = (bf16[256,256]{1,0:T(8,128)(2,1)S(1)}, bf16[256,256]{1,0:T(8,128)(2,1)S(1)}, u32[]{:S(2)}, u32[]{:S(2)}) collective-permute-start(bf16[256,256]{1,0:T(8,128)(2,1)S(1)} %get-tuple-element.86), channel_id=1, source_target_pairs={{0,2},{1,3},{2,0},{3,1},{4,6},{5,7},{6,4},{7,5},{8,10},{9,11},{10,... | collective-permute-start | bytes 393224 | tf_op jit(solution)/shard_map/ppermute | solution.py:569
  32.0 0.4 collective-permute-start.11
  32.5 0.9 %product.8.refs_0_ = f32[512,256]{1,0:T(8,128)S(1)} custom-call(bf16[544,256]{1,0:T(8,128)(2,1)S(1)} %collective-permute-done.6.refs_0_, bf16[544,256]{1,0:T(8,128)(2,1)S(1)} %collective-permute-done.7.refs_1_, bf16[512,64]{1,0:T(8,128)(2,1)S(1)} %get-tuple-element.62.refs_1_.refs_2_, f32[512,256]{1,0:T(8,128)S(1)} %get-tuple-element.79.refs_3_), custom_call_target="tpu_custom_call" | custom-call | tf_op jit(solution)/shard_map/product/pallas_call | solution.py:209
  33.4 0.9 %product.11 = f32[512,256]{1,0:T(8,128)S(1)} custom-call(bf16[544,256]{1,0:T(8,128)(2,1)S(1)} %collective-permute-done.6.refs_0_, bf16[544,256]{1,0:T(8,128)(2,1)S(1)} %collective-permute-done.7.refs_1_, bf16[512,64]{1,0:T(8,128)(2,1)S(1)} %get-tuple-element.65.refs_3_.refs_2_, f32[512,256]{1,0:T(8,128)S(1)} %get-tuple-element.84.refs_3_), custom_call_target="tpu_custom_call" | custom-call | tf_op jit(solution)/shard_map/product/pallas_call | solution.py:209
  34.3 0.1 collective-permute-start.9
  34.4 1.7 %collective-permute-done.11.refs_2_.refs_1_ = bf16[16,64]{1,0:T(8,128)(2,1)S(1)} collective-permute-done((bf16[16,64]{1,0:T(8,128)(2,1)S(1)}, bf16[16,64]{1,0:T(8,128)(2,1)S(1)}, u32[]{:S(2)}, u32[]{:S(2)}) %collective-permute-start.11) | collective-permute-done | bytes 2080 | tf_op jit(solution)/shard_map/ppermute | solution.py:569
  36.1 0.0 collective-permute-done.10.refs_1_
  36.1 0.8 %add_up.4 = (f32[256,256]{1,0:T(8,128)}, bf16[256,256]{1,0:T(8,128)(2,1)S(1)}) custom-call(f32[256,256]{1,0:T(8,128)S(1)} %get-tuple-element.85.refs_0_, bf16[256,256]{1,0:T(8,128)(2,1)S(1)} %collective-permute-done.10.refs_1_, bf16[16,64]{1,0:T(8,128)(2,1)S(1)} %collective-permute-done.11.refs_2_.refs_1_), custom_call_target="tpu_custom_call" | custom-call | flops 10000000000 | tf_op jit(solution)/shard_map/add_up/pallas_call | solution.py:246
  36.9 2.6 %collective-permute-start.12 = (bf16[256,256]{1,0:T(8,128)(2,1)S(1)}, bf16[256,256]{1,0:T(8,128)(2,1)S(1)}, u32[]{:S(2)}, u32[]{:S(2)}) collective-permute-start(bf16[256,256]{1,0:T(8,128)(2,1)S(1)} %get-tuple-element.88.refs_2_), channel_id=1, source_target_pairs={{0,4},{1,5},{2,6},{3,7},{4,0},{5,1},{6,2},{7,3},{8,12},{9,13},{10,... | collective-permute-start | bytes 393224 | tf_op jit(solution)/shard_map/ppermute | solution.py:569
  39.4 0.0 collective-permute-done.9.refs_1_
  39.4 0.1 add_up.5
  39.5 1.6 %collective-permute-start.13 = (bf16[256,256]{1,0:T(8,128)(2,1)S(1)}, bf16[256,256]{1,0:T(8,128)(2,1)S(1)}, u32[]{:S(2)}, u32[]{:S(2)}) collective-permute-start(bf16[256,256]{1,0:T(8,128)(2,1)S(1)} %get-tuple-element.90), channel_id=1, source_target_pairs={{0,2},{1,3},{2,0},{3,1},{4,6},{5,7},{6,4},{7,5},{8,10},{9,11},{10,... | collective-permute-start | bytes 393224 | tf_op jit(solution)/shard_map/ppermute | solution.py:569
  41.1 0.4 top_couplings.1.refs_6_.refs_3_
  41.6 3.7 %collective-permute-done.12.refs_1_ = bf16[256,256]{1,0:T(8,128)(2,1)S(1)} collective-permute-done((bf16[256,256]{1,0:T(8,128)(2,1)S(1)}, bf16[256,256]{1,0:T(8,128)(2,1)S(1)}, u32[]{:S(2)}, u32[]{:S(2)}) %collective-permute-start.12) | collective-permute-done | bytes 131104 | tf_op jit(solution)/shard_map/ppermute | solution.py:569
  45.3 0.4 collective-permute-done.13.refs_2_
  45.7 5.6 %leaves.1 = (f32[2,64,128]{2,1,0:T(8,128)}, f32[64,128]{1,0:T(8,128)S(1)}, f32[128,256]{1,0:T(8,128)S(1)}) custom-call(f32[256,256]{1,0:T(8,128)S(1)} %get-tuple-element.89.refs_0_, bf16[256,256]{1,0:T(8,128)(2,1)S(1)} %collective-permute-done.12.refs_1_, bf16[256,256]{1,0:T(8,128)(2,1)S(1)} %collective-permute-done.13.refs_2_, ...), custom_call_target="tpu_custom_call" | custom-call | tf_op jit(solution)/shard_map/leaves/pallas_call | solution.py:372
  51.3 0.9 %collective-permute-start.14 = (f32[128,256]{1,0:T(8,128)S(1)}, f32[128,256]{1,0:T(8,128)S(1)}, u32[]{:S(2)}, u32[]{:S(2)}) collective-permute-start(f32[128,256]{1,0:T(8,128)S(1)} %get-tuple-element.94.refs_0_), channel_id=1, source_target_pairs={{0,1},{1,0},{2,3},{3,2},{4,5},{5,4},{6,7},{7,6},{8,9},{9,8},{10,11... | collective-permute-start | bytes 393224 | tf_op jit(solution)/shard_map/ppermute | solution.py:569
  52.2 4.1 %collective-permute-done.14.refs_1_ = f32[128,256]{1,0:T(8,128)S(1)} collective-permute-done((f32[128,256]{1,0:T(8,128)S(1)}, f32[128,256]{1,0:T(8,128)S(1)}, u32[]{:S(2)}, u32[]{:S(2)}) %collective-permute-start.14) | collective-permute-done | bytes 131104 | tf_op jit(solution)/shard_map/ppermute | solution.py:569
  56.3 2.5 %level.2 = (f32[64,128]{1,0:T(8,128)S(1)}, f32[128,256]{1,0:T(8,128)S(1)}) custom-call(f32[128,256]{1,0:T(8,128)S(1)} %get-tuple-element.94.refs_0_, f32[128,256]{1,0:T(8,128)S(1)} %collective-permute-done.14.refs_1_, bf16[5,64,128]{2,1,0:T(8,128)(2,1)S(1)} %get-tuple-element.91.refs_2_.refs_4_, bf16[192,768]{1,0:T(8,128)(2,1)S(1)} %get-tuple-element.95.refs_3_), custom_call_target="tpu_custom_call" | custom-call | tf_op jit(solution)/shard_map/level/pallas_call | solution.py:453
  58.9 1.3 %collective-permute-start.15 = (f32[128,256]{1,0:T(8,128)S(1)}, f32[128,256]{1,0:T(8,128)S(1)}, u32[]{:S(2)}, u32[]{:S(2)}) collective-permute-start(f32[128,256]{1,0:T(8,128)S(1)} %get-tuple-element.96.refs_0_), channel_id=1, source_target_pairs={{0,2},{1,3},{2,0},{3,1},{4,6},{5,7},{6,4},{7,5},{8,10},{9,11},{10,... | collective-permute-start | bytes 393224 | tf_op jit(solution)/shard_map/ppermute | solution.py:569
  60.2 3.7 %collective-permute-done.15.refs_1_ = f32[128,256]{1,0:T(8,128)S(1)} collective-permute-done((f32[128,256]{1,0:T(8,128)S(1)}, f32[128,256]{1,0:T(8,128)S(1)}, u32[]{:S(2)}, u32[]{:S(2)}) %collective-permute-start.15) | collective-permute-done | bytes 131104 | tf_op jit(solution)/shard_map/ppermute | solution.py:569
  63.9 3.2 %level.3 = (f32[3,1,64,128]{3,2,1,0:T(8,128)}, f32[2,1,64,256]{3,2,1,0:T(8,128)}) custom-call(f32[128,256]{1,0:T(8,128)S(1)} %get-tuple-element.96.refs_0_, f32[128,256]{1,0:T(8,128)S(1)} %collective-permute-done.15.refs_1_, bf16[5,64,128]{2,1,0:T(8,128)(2,1)S(1)} %get-tuple-element.91.refs_2_.refs_4_, bf16[192,768]{1,0:T(8,128)(2,1)S(1)} %top_couplings.1.refs_6_.refs_3_, ...), custom_call_target="tpu_custom_call" | custom-call | tf_op jit(solution)/shard_map/level/pallas_call | solution.py:453
  (2 shorter events, 0.0 us)
Async XLA Ops:
  1.9 15.8 %collective-permute-start.1 = (bf16[1104,256]{1,0:T(8,128)(2,1)S(1)}, bf16[1104,256]{1,0:T(8,128)(2,1)S(1)}, u32[]{:S(2)}, u32[]{:S(2)}) collective-permute-start(bf16[1104,256]{1,0:T(8,128)(2,1)S(1)} %get-tuple-element.52.refs_0_.refs_3_), channel_id=1, source_target_pairs={{0,16},{1,17},{2,18},{3,19},{4,20},{5,21},{6,22},{7,23},{8,24},{9,... | collective-permute-start | bytes 1695752 | tf_op jit(solution)/shard_map/ppermute | solution.py:569
  4.9 14.3 %collective-permute-start = (bf16[1104,256]{1,0:T(8,128)(2,1)S(1)}, bf16[1104,256]{1,0:T(8,128)(2,1)S(1)}, u32[]{:S(2)}, u32[]{:S(2)}) collective-permute-start(bf16[1104,256]{1,0:T(8,128)(2,1)S(1)} %get-tuple-element.52.refs_0_.refs_3_), channel_id=1, source_target_pairs={{0,1},{1,0},{2,3},{3,2},{4,5},{5,4},{6,7},{7,6},{8,9},{9,8},{10,11... | collective-permute-start | bytes 1695752 | tf_op jit(solution)/shard_map/ppermute | solution.py:569
  6.4 5.4 %collective-permute-start.4 = (bf16[16,256]{1,0:T(8,128)(2,1)S(1)}, bf16[16,256]{1,0:T(8,128)(2,1)S(1)}, u32[]{:S(2)}, u32[]{:S(2)}) collective-permute-start(bf16[16,256]{1,0:T(8,128)(2,1)S(1)} %get-tuple-element.53.refs_1_), channel_id=1, source_target_pairs={{0,6},{1,7},{2,4},{3,5},{4,2},{5,3},{6,0},{7,1},{8,14},{9,15},{10,... | collective-permute-start | bytes 24584 | tf_op jit(solution)/shard_map/ppermute | solution.py:569
  10.0 4.5 %collective-permute-start.3 = (bf16[16,256]{1,0:T(8,128)(2,1)S(1)}, bf16[16,256]{1,0:T(8,128)(2,1)S(1)}, u32[]{:S(2)}, u32[]{:S(2)}) collective-permute-start(bf16[16,256]{1,0:T(8,128)(2,1)S(1)} %get-tuple-element.53.refs_1_), channel_id=1, source_target_pairs={{0,4},{1,5},{2,6},{3,7},{4,0},{5,1},{6,2},{7,3},{8,12},{9,13},{10,... | collective-permute-start | bytes 24584 | tf_op jit(solution)/shard_map/ppermute | solution.py:569
  10.0 4.5 %collective-permute-start.2 = (bf16[16,256]{1,0:T(8,128)(2,1)S(1)}, bf16[16,256]{1,0:T(8,128)(2,1)S(1)}, u32[]{:S(2)}, u32[]{:S(2)}) collective-permute-start(bf16[16,256]{1,0:T(8,128)(2,1)S(1)} %get-tuple-element.53.refs_1_), channel_id=1, source_target_pairs={{0,2},{1,3},{2,0},{3,1},{4,6},{5,7},{6,4},{7,5},{8,10},{9,11},{10,... | collective-permute-start | bytes 24584 | tf_op jit(solution)/shard_map/ppermute | solution.py:569
  14.6 1.5 %collective-permute-start.5 = (bf16[16,1024]{1,0:T(8,128)(2,1)S(1)}, bf16[16,1024]{1,0:T(8,128)(2,1)S(1)}, u32[]{:S(2)}, u32[]{:S(2)}) collective-permute-start(bf16[16,1024]{1,0:T(8,128)(2,1)S(1)} %pad_maximum_fusion), channel_id=1, source_target_pairs={{0,8},{1,9},{2,10},{3,11},{4,12},{5,13},{6,14},{7,15},{8,0},{9,1},... | collective-permute-start | bytes 98312 | tf_op jit(solution)/shard_map/ppermute | solution.py:569
  19.2 8.2 %collective-permute-start.6 = (bf16[544,256]{1,0:T(8,128)(2,1)S(1)}, bf16[544,256]{1,0:T(8,128)(2,1)S(1)}, u32[]{:S(2)}, u32[]{:S(2)}) collective-permute-start(bf16[544,256]{1,0:T(8,128)(2,1)S(1)} %get-tuple-element.60), channel_id=1, source_target_pairs={{0,16},{1,17},{2,18},{3,19},{4,20},{5,21},{6,22},{7,23},{8,24},{9,... | collective-permute-start | bytes 835592 | tf_op jit(solution)/shard_map/ppermute | solution.py:569
  19.7 7.8 %collective-permute-start.7 = (bf16[544,256]{1,0:T(8,128)(2,1)S(1)}, bf16[544,256]{1,0:T(8,128)(2,1)S(1)}, u32[]{:S(2)}, u32[]{:S(2)}) collective-permute-start(bf16[544,256]{1,0:T(8,128)(2,1)S(1)} %get-tuple-element.61), channel_id=1, source_target_pairs={{0,1},{1,0},{2,3},{3,2},{4,5},{5,4},{6,7},{7,6},{8,9},{9,8},{10,11... | collective-permute-start | bytes 835592 | tf_op jit(solution)/shard_map/ppermute | solution.py:569
  28.4 2.0 %collective-permute-start.8 = (f32[512,256]{1,0:T(8,128)S(1)}, f32[512,256]{1,0:T(8,128)S(1)}, u32[]{:S(2)}, u32[]{:S(2)}) collective-permute-start(f32[512,256]{1,0:T(8,128)S(1)} %product.10), channel_id=1, source_target_pairs={{0,8},{1,9},{2,10},{3,11},{4,12},{5,13},{6,14},{7,15},{8,0},{9,1},... | collective-permute-start | bytes 1572872 | tf_op jit(solution)/shard_map/ppermute | solution.py:569
  30.4 5.7 %collective-permute-start.10 = (bf16[256,256]{1,0:T(8,128)(2,1)S(1)}, bf16[256,256]{1,0:T(8,128)(2,1)S(1)}, u32[]{:S(2)}, u32[]{:S(2)}) collective-permute-start(bf16[256,256]{1,0:T(8,128)(2,1)S(1)} %get-tuple-element.86), channel_id=1, source_target_pairs={{0,2},{1,3},{2,0},{3,1},{4,6},{5,7},{6,4},{7,5},{8,10},{9,11},{10,... | collective-permute-start | bytes 393224 | tf_op jit(solution)/shard_map/ppermute | solution.py:569
  32.0 4.0 %collective-permute-start.11 = (bf16[16,64]{1,0:T(8,128)(2,1)S(1)}, bf16[16,64]{1,0:T(8,128)(2,1)S(1)}, u32[]{:S(2)}, u32[]{:S(2)}) collective-permute-start(bf16[16,64]{1,0:T(8,128)(2,1)S(1)} %get-tuple-element.87.refs_0_), channel_id=1, source_target_pairs={{0,2},{1,3},{2,0},{3,1},{4,6},{5,7},{6,4},{7,5},{8,10},{9,11},{10,... | collective-permute-start | bytes 6152 | tf_op jit(solution)/shard_map/ppermute | solution.py:569
  34.3 5.2 %collective-permute-start.9 = (f32[512,256]{1,0:T(8,128)S(1)}, f32[512,256]{1,0:T(8,128)S(1)}, u32[]{:S(2)}, u32[]{:S(2)}) collective-permute-start(f32[512,256]{1,0:T(8,128)S(1)} %product.11), channel_id=1, source_target_pairs={{0,8},{1,9},{2,10},{3,11},{4,12},{5,13},{6,14},{7,15},{8,0},{9,1},... | collective-permute-start | bytes 1572872 | tf_op jit(solution)/shard_map/ppermute | solution.py:569
  36.9 8.5 %collective-permute-start.12 = (bf16[256,256]{1,0:T(8,128)(2,1)S(1)}, bf16[256,256]{1,0:T(8,128)(2,1)S(1)}, u32[]{:S(2)}, u32[]{:S(2)}) collective-permute-start(bf16[256,256]{1,0:T(8,128)(2,1)S(1)} %get-tuple-element.88.refs_2_), channel_id=1, source_target_pairs={{0,4},{1,5},{2,6},{3,7},{4,0},{5,1},{6,2},{7,3},{8,12},{9,13},{10,... | collective-permute-start | bytes 393224 | tf_op jit(solution)/shard_map/ppermute | solution.py:569
  39.5 6.2 %collective-permute-start.13 = (bf16[256,256]{1,0:T(8,128)(2,1)S(1)}, bf16[256,256]{1,0:T(8,128)(2,1)S(1)}, u32[]{:S(2)}, u32[]{:S(2)}) collective-permute-start(bf16[256,256]{1,0:T(8,128)(2,1)S(1)} %get-tuple-element.90), channel_id=1, source_target_pairs={{0,2},{1,3},{2,0},{3,1},{4,6},{5,7},{6,4},{7,5},{8,10},{9,11},{10,... | collective-permute-start | bytes 393224 | tf_op jit(solution)/shard_map/ppermute | solution.py:569
  51.3 5.0 %collective-permute-start.14 = (f32[128,256]{1,0:T(8,128)S(1)}, f32[128,256]{1,0:T(8,128)S(1)}, u32[]{:S(2)}, u32[]{:S(2)}) collective-permute-start(f32[128,256]{1,0:T(8,128)S(1)} %get-tuple-element.94.refs_0_), channel_id=1, source_target_pairs={{0,1},{1,0},{2,3},{3,2},{4,5},{5,4},{6,7},{7,6},{8,9},{9,8},{10,11... | collective-permute-start | bytes 393224 | tf_op jit(solution)/shard_map/ppermute | solution.py:569
  58.9 5.0 %collective-permute-start.15 = (f32[128,256]{1,0:T(8,128)S(1)}, f32[128,256]{1,0:T(8,128)S(1)}, u32[]{:S(2)}, u32[]{:S(2)}) collective-permute-start(f32[128,256]{1,0:T(8,128)S(1)} %get-tuple-element.96.refs_0_), channel_id=1, source_target_pairs={{0,2},{1,3},{2,0},{3,1},{4,6},{5,7},{6,4},{7,5},{8,10},{9,11},{10,... | collective-permute-start | bytes 393224 | tf_op jit(solution)/shard_map/ppermute | solution.py:569

commit v4 on v3

--- a/solution.py
+++ b/solution.py
@@ -232,23 +232,19 @@
     )(first, second)
 
 
-def add_up_body(span, kept, sent, mine_ref, theirs_ref, *refs):
-    kept_ref, sent_ref = refs[-2:]
-    for chunks, out_ref in ((kept, kept_ref), (sent, sent_ref)):
+def add_up_body(span, outs, mine_ref, theirs_ref, *refs):
+    for (chunks, _), out_ref in zip(outs, refs[-len(outs) :]):
         for pos, chunk in enumerate(chunks):
             place = pl.ds(chunk * span, span)
             value = mine_ref[place, :] + theirs_ref[place, :].astype(F32)
             out_ref[pl.ds(pos * span, span), :] = value.astype(out_ref.dtype)
 
 
-def add_up(mine, theirs, kept, sent, span, after=(), cost=COST):
+def add_up(mine, theirs, outs, span, after=(), cost=COST):
     samples = mine.shape[1]
     return pl.pallas_call(
-        lambda *refs: add_up_body(span, kept, sent, *refs),
-        out_shape=(
-            vmem((len(kept) * span, samples), F32),
-            vmem((len(sent) * span, samples), BF16),
-        ),
+        lambda *refs: add_up_body(span, outs, *refs),
+        out_shape=[vmem((len(chunks) * span, samples), kind) for chunks, kind in outs],
         cost_estimate=cost,
         compiler_params=PARAMS,
         name="add_up",
@@ -323,25 +319,29 @@
     return [solved * (inverse * FRONT) for solved, _, inverse in states]
 
 
-def merge(samples, reduced, coupling, picks, early=None):
-    pool = samples.shape[0]
-    high, middle, low = split(reduced)
-    coupled = over(
-        coupling, jnp.concatenate([high, middle, high, middle, high, low], axis=0), 1, 0
-    )
-    stacked = samples - coupled[:pool]
-    skeleton = select_rows(picks, samples) - coupled[pool:]
+def merge(nodes, early=None):
+    stacks, skeletons = [], []
+    for samples, reduced, coupling, picks in nodes:
+        pool = samples.shape[0]
+        high, middle, low = split(reduced)
+        coupled = over(
+            coupling, jnp.concatenate([high, middle, high, middle, high, low], axis=0), 1, 0
+        )
+        stacks.append(samples - coupled[:pool])
+        skeletons.append(select_rows(picks, samples) - coupled[pool:])
     if early is not None:
-        early(skeleton)
-    (interp,) = interpolate([stacked], [skeleton])
-    return interp, skeleton, wide_product(interp, reduced, 0)
+        early(skeletons[0])
+    interps = interpolate(stacks, skeletons)
+    return [
+        (interp, skeleton, wide_product(interp, node[1], 0))
+        for interp, skeleton, node in zip(interps, skeletons, nodes)
+    ]
 
 
 def leaves_body(received, *refs):
     own_ref, *others = refs[: received + 1]
     source_ref, picks_ref, couplings_ref = refs[received + 1 : received + 4]
-    leaf_ref, upper_ref, state_ref, held_ref, sem = refs[-5:]
-    rank = picks_ref.shape[1]
+    leaf_ref, upper_ref, skeleton_ref, reduced_ref, sent_ref, held_ref, sem = refs[-7:]
     total = own_ref[...]
     for other in others:
         total = total + other[...].astype(F32)
@@ -354,15 +354,18 @@
         reduced.append(exact_product(interp, source_ref[pl.ds(leaf * LEAF, LEAF), :]))
     copy = pltpu.make_async_copy(held_ref, leaf_ref, sem)
     copy.start()
-    interp, skeleton, reduced = merge(
+    node = (
         jnp.concatenate(skeletons, axis=0),
         jnp.concatenate(reduced, axis=0),
         couplings_ref[...],
         picks_ref[count],
     )
+    ((interp, skeleton, reduced),) = merge([node])
     upper_ref[...] = interp
-    state_ref[pl.ds(0, rank), :] = skeleton
-    state_ref[pl.ds(rank, rank), :] = reduced
+    skeleton_ref[...] = skeleton
+    reduced_ref[...] = reduced
+    for pos, part in enumerate((*split(skeleton)[:2], reduced.astype(BF16))):
+        sent_ref[pl.ds(pos * skeleton.shape[0], skeleton.shape[0]), :] = part
     copy.wait()
 
 
@@ -374,92 +377,93 @@
         out_shape=(
             jax.ShapeDtypeStruct((leaf_count, rank, LEAF), F32),
             vmem((rank, pool), F32),
-            vmem((2 * rank, samples), F32),
+            vmem((rank, samples), F32),
+            vmem((rank, samples), F32),
+            vmem((3 * rank, samples), BF16),
         ),
-        out_specs=(pl.BlockSpec(memory_space=pl.ANY), VMEM, VMEM),
+        out_specs=(pl.BlockSpec(memory_space=pl.ANY), VMEM, VMEM, VMEM, VMEM),
         scratch_shapes=[pltpu.VMEM((leaf_count, rank, LEAF), F32), pltpu.SemaphoreType.DMA],
         cost_estimate=COST,
         compiler_params=PARAMS,
         name="leaves",
-    )(own, *others, source, picks, couplings, later)
+    )(own, *others, source, picks, couplings, *later)
 
 
 def first_of_pair(number):
     return (lax.axis_index("col") >> (number - 2)) % 2 == 0
 
 
-def level_body(number, mine_ref, theirs_ref, picks_ref, couplings_ref, *refs):
-    rank = picks_ref.shape[1]
-    if number == 2:
-        upper_ref, state_ref = refs
-    else:
-        one_ref, two_ref, upper_out, top_out, upper_ref, state_ref, sem = refs
-        places = [
-            (one_ref, upper_out.at[0, 0]),
-            (two_ref, upper_out.at[1, 0]),
-            (state_ref.at[pl.ds(0, rank)], top_out.at[0, 0]),
-            (state_ref.at[pl.ds(rank, rank)], top_out.at[1, 0]),
-            (upper_ref, upper_out.at[2, 0]),
-        ]
-        copies = [
-            pltpu.make_async_copy(source, target, sem.at[pos])
-            for pos, (source, target) in enumerate(places)
-        ]
-        copies[0].start()
-        copies[1].start()
-
-    def early(skeleton):
-        state_ref[pl.ds(0, rank), :] = skeleton
-        if number > 2:
-            copies[2].start()
-
-    mine_first = first_of_pair(number)
-    mine, theirs = mine_ref[...], theirs_ref[...]
+def pair(mine, theirs, mine_first):
     first = jnp.where(mine_first, mine, theirs)
     second = jnp.where(mine_first, theirs, mine)
-    interp, _, reduced = merge(
-        jnp.concatenate([first[:rank], second[:rank]], axis=0),
-        jnp.concatenate([first[rank:], second[rank:]], axis=0),
-        couplings_ref[...],
-        picks_ref[picks_ref.shape[0] + number - 4],
-        early,
-    )
-    upper_ref[...] = interp
-    state_ref[pl.ds(rank, rank), :] = reduced
-    if number > 2:
+    return jnp.concatenate([first, second], axis=0)
+
+
+def upper_body(picks_count, *refs):
+    states = [(refs[0][...], refs[1][...])]
+    rank = refs[0].shape[0]
+    for got_ref in refs[2:5]:
+        high, middle, reduced = (got_ref[pl.ds(pos * rank, rank), :] for pos in range(3))
+        states.append((high.astype(F32) + middle.astype(F32), reduced.astype(F32)))
+    picks_ref, two_ref, other_ref, three_ref, one_ref, upper_out, top_out = refs[5:12]
+    upper_ref, state_ref, sem = refs[12:]
+    places = [
+        (one_ref, upper_out.at[0, 0]),
+        (upper_ref.at[0], upper_out.at[1, 0]),
+        (upper_ref.at[1], upper_out.at[2, 0]),
+        (state_ref.at[0], top_out.at[0, 0]),
+        (state_ref.at[1], top_out.at[1, 0]),
+    ]
+    copies = [
+        pltpu.make_async_copy(source, target, sem.at[pos])
+        for pos, (source, target) in enumerate(places)
+    ]
+    copies[0].start()
+    mine_first = first_of_pair(2)
+    nodes = []
+    for number, coupling_ref in enumerate((two_ref, other_ref)):
+        mine, theirs = states[2 * number : 2 * number + 2]
+        picks = picks_ref[picks_count - 3 + number]
+        stacks = [pair(*parts, mine_first) for parts in zip(mine, theirs)]
+        nodes.append((*stacks, coupling_ref[...], picks))
+    mine, theirs = merge(nodes)
+    upper_ref[0] = mine[0]
+    copies[1].start()
+
+    def early(skeleton):
+        state_ref[0] = skeleton
         copies[3].start()
-        copies[4].start()
-        for copy in copies:
-            copy.wait()
-
-
-def level(number, mine, theirs, picks, couplings, below=()):
+
+    mine_first = first_of_pair(3)
+    stacks = [pair(*parts, mine_first) for parts in zip(mine[1:], theirs[1:])]
+    ((interp, _, reduced),) = merge([(*stacks, three_ref[...], picks_ref[picks_count - 1])], early)
+    upper_ref[1] = interp
+    copies[2].start()
+    state_ref[1] = reduced
+    copies[4].start()
+    for copy in copies:
+        copy.wait()
+
+
+def upper_levels(skeleton, reduced, got, picks, couplings, interp_one):
     rank, pool = picks.shape[1:]
-    samples = mine.shape[1]
-    out_shape = (
-        vmem((rank, pool), F32),
-        vmem(mine.shape, F32),
-    )
-    out_specs = (VMEM, VMEM)
-    scratch = []
-    if below:
-        scratch = [pltpu.VMEM(out.shape, F32) for out in out_shape]
-        scratch.append(pltpu.SemaphoreType.DMA((5,)))
-        out_shape = (
+    samples = skeleton.shape[1]
+    return pl.pallas_call(
+        lambda *refs: upper_body(picks.shape[0], *refs),
+        out_shape=(
             jax.ShapeDtypeStruct((3, 1, rank, pool), F32),
             jax.ShapeDtypeStruct((2, 1, rank, samples), F32),
-        )
-        out_specs = (pl.BlockSpec(memory_space=pl.ANY),) * 2
-    return pl.pallas_call(
-        lambda *refs: level_body(number, *refs),
-        out_shape=out_shape,
-        in_specs=[VMEM] * (4 + len(below)),
-        out_specs=out_specs,
-        scratch_shapes=scratch,
-        cost_estimate=COST,
-        compiler_params=PARAMS,
-        name="level",
-    )(mine, theirs, picks, couplings, *below)
+        ),
+        out_specs=(pl.BlockSpec(memory_space=pl.ANY),) * 2,
+        scratch_shapes=[
+            pltpu.VMEM((2, rank, pool), F32),
+            pltpu.VMEM((2, rank, samples), F32),
+            pltpu.SemaphoreType.DMA((5,)),
+        ],
+        cost_estimate=COST,
+        compiler_params=PARAMS,
+        name="upper_levels",
+    )(skeleton, reduced, *got, picks, *couplings, interp_one)
 
 
 def one_hot(chosen, pool):
@@ -500,13 +504,13 @@
         nodes.append(over(points, hots[leaf_count], 1, 0))
         if source_ref is mine_ref:
             couple(*children, hots[leaf_count], gain, one_ref)
-            table, start = rows, leaf_count + counts[1]
-            for number, count in enumerate(counts[2:]):
-                wanted = start + (lax.axis_index("col") >> (number + 1))
-                place = lax.broadcasted_iota(jnp.int32, table.shape, 0)
-                row = jnp.sum(jnp.where(place == wanted, table, 0.0), axis=0, keepdims=True)
-                hots.append(one_hot(row, pool))
-                start += count
+            start = leaf_count + counts[1]
+            level_two = lax.axis_index("col") // 2
+            wanted = [level_two, level_two + 1 - 2 * (level_two % 2), counts[2] + level_two // 2]
+            for row in wanted:
+                place = lax.broadcasted_iota(jnp.int32, rows.shape, 0)
+                named = jnp.where(place == start + row, rows, 0.0)
+                hots.append(one_hot(jnp.sum(named, axis=0, keepdims=True), pool))
             for number, hot in enumerate(hots):
                 picks_ref[number] = hot.T.astype(BF16)
             upper = hots[leaf_count + 1]
@@ -515,7 +519,7 @@
     first = jnp.where(mine_first, mine, theirs)
     second = jnp.where(mine_first, theirs, mine)
     couple(first, second, upper, gain, two_ref)
-    points_ref[...] = over(jnp.concatenate([first, second], axis=1), upper, 1, 0).astype(BF16)
+    points_ref[...] = jnp.concatenate([first, second], axis=1).astype(BF16)
 
 
 def skeletons(packed, beside, tables, span, gain):
@@ -524,10 +528,10 @@
     return pl.pallas_call(
         lambda *refs: skeletons_body(gain, span, counts, *refs),
         out_shape=(
-            vmem((leaf_count + 3, rank, LEAF), BF16),
+            vmem((leaf_count + 4, rank, LEAF), BF16),
             coupling_shape(rank),
             coupling_shape(rank),
-            vmem((16, rank), BF16),
+            vmem((16, 2 * rank), BF16),
         ),
         cost_estimate=COST,
         compiler_params=PARAMS,
@@ -535,19 +539,22 @@
     )(packed, beside)
 
 
-def top_couplings_body(gain, mine_ref, theirs_ref, picks_ref, couplings_ref):
+def top_couplings_body(gain, mine_ref, theirs_ref, picks_ref, other_ref, three_ref):
+    count, rank, _ = picks_ref.shape
+    picks = [picks_ref[count - pos].astype(F32).T for pos in (3, 2, 1)]
+    mine, theirs = mine_ref[...].astype(F32), theirs_ref[...].astype(F32)
+    couple(theirs[:, :rank], theirs[:, rank:], picks[1], gain, other_ref)
+    mine, theirs = over(mine, picks[0], 1, 0), over(theirs, picks[1], 1, 0)
     mine_first = first_of_pair(3)
-    mine, theirs = mine_ref[...].astype(F32), theirs_ref[...].astype(F32)
     first = jnp.where(mine_first, mine, theirs)
     second = jnp.where(mine_first, theirs, mine)
-    picks = picks_ref[picks_ref.shape[0] - 1].astype(F32).T
-    couple(first, second, picks, gain, couplings_ref)
+    couple(first, second, picks[2], gain, three_ref)
 
 
 def top_couplings(mine, theirs, picks, gain):
     return pl.pallas_call(
         lambda *refs: top_couplings_body(gain, *refs),
-        out_shape=coupling_shape(picks.shape[1]),
+        out_shape=[coupling_shape(picks.shape[1])] * 2,
         cost_estimate=COST,
         compiler_params=PARAMS,
         name="top_couplings",
@@ -609,37 +616,39 @@
     (theirs,) = product(diagonal, feats[3:], totals[3:], span)
     from_sibling = swap(theirs, 1, 0)
     (mine,) = product(diagonal, feats[1:2], totals[1:2], span)
-    kept, sent = add_up(mine, from_sibling, range(0, line - 2, 2), range(1, line - 2, 2), span)
+    outs = [(range(0, line - 2, 2), F32), (range(1, line - 2, 2), BF16)]
+    kept, sent = add_up(mine, from_sibling, outs, span)
     sent, total = lax.optimization_barrier((sent, totals[2]))
     arrived = swap(sent, 0, 2)
     (theirs,) = product(diagonal, feats[2:3], [total], span)
     from_sibling = swap(theirs, 1, 0)
     (mine,) = product(diagonal, feats[:1], totals[:1], span)
+    other_points = swap(points_two, 0, 2)
     received = []
-    beside_two = swap(points_two, 0, 2)
     chunks = list(range(2, line, 2))
     bit = 2
     while chunks:
         sent_places = [pos for pos, chunk in enumerate(chunks) if chunk & bit]
         kept_places = [pos for pos, chunk in enumerate(chunks) if not chunk & bit]
-        kept, sent = add_up(
-            kept, arrived, kept_places or sent_places, sent_places, span, (beside_two,), LONG
-        )
+        outs = [(sent_places, BF16)] + [(kept_places, F32)] * (len(kept_places) > 0)
+        sent, *kept = add_up(kept, arrived, outs, span, (other_points,), LONG)
         arrived = swap(sent, 0, 2 * bit)
         received.append(arrived[:span] if len(sent_places) > 1 else arrived)
-        arrived = arrived[span:]
+        if kept:
+            (kept,) = kept
+            arrived = arrived[span:]
         chunks = [chunks[pos] for pos in kept_places]
         bit *= 2
-    own_sum, near_sent = add_up(mine, from_sibling, [0], [1], span, (sent,))
+    own_sum, near_sent = add_up(mine, from_sibling, [([0], F32), ([1], BF16)], span, (sent,))
     received.append(swap(near_sent, 0, 2))
-
-    couplings_three = top_couplings(points_two, beside_two, picks, gain)
-    leaf_interp, interp_one, state = leaves(
-        own_sum, received, packed, picks, couplings_one, couplings_three, leaf_skeleton.shape[0]
-    )
-    interp_two, state_two = level(2, state, swap(state, 0, 1), picks, couplings_two)
-    upper_interp, top_state = level(
-        3, state_two, swap(state_two, 0, 2), picks, couplings_three, (interp_one, interp_two)
+    later = top_couplings(points_two, other_points, picks, gain)
+
+    leaf_interp, interp_one, skeleton, reduced, sent = leaves(
+        own_sum, received, packed, picks, couplings_one, later, leaf_skeleton.shape[0]
+    )
+    got = [swap(sent, 0, bits) for bits in (1, 2, 3)]
+    upper_interp, top_state = upper_levels(
+        skeleton, reduced, got, picks, (couplings_two, *later), interp_one
     )
     return jnp.swapaxes(leaf_interp, 1, 2), jnp.swapaxes(upper_interp, 2, 3), top_state
 

time: 67.4 us -> 64 us (0.950)
  waiting for transfers between devices: 20.1 us -> 15.4 us
  starting transfers between devices: 19.7 us -> 21.2 us
    ppermute x16 -> x17, waiting for transfers between devices: 20.1 us -> 15.4 us  [swap(): return lax.ppermute(value, ('row', 'col'), pairs)]
    ppermute x16 -> x17, starting transfers between devices: 19.7 us -> 21.2 us  [swap(): return lax.ppermute(value, ('row', 'col'), pairs)]
    pallas_call x6 -> x5, Pallas kernels: 7.03 us -> 6.85 us  [the longest x1 5.94 us: upper_levels(): pl.pallas_call(lambda *refs: upper_body(picks.shape[0], *refs), out_shape...]
  transfers between devices with their start and end apart: 16 -> 17, of which waited for: 10 -> 11; matrix products, arithmetic and copies ran while one was open for 0% -> 0% of each run, Pallas kernels for 19% -> 20%
where the time goes in v4:
time: 64 us; the launch traced here: 63.9 us
  Pallas kernels  26.3 us (41%)
  starting transfers between devices  21.2 us (33%)
  waiting for transfers between devices  15.4 us (24%)
  between operations  0.94 us (1%)
    ppermute x17, starting transfers between devices, swap(): return lax.ppermute(value, ('row', 'col'), pairs)  21.2 us
    ppermute x17, waiting for transfers between devices, swap(): return lax.ppermute(value, ('row', 'col'), pairs)  15.4 us
    pallas_call x6, Pallas kernels, product(): pl.pallas_call(lambda *refs: product_body(span, len(sources), len(rows),...  8.53 us
    pallas_call x1, Pallas kernels, upper_levels(): pl.pallas_call(lambda *refs: upper_body(picks.shape[0], *refs), out_shape...  5.94 us
    pallas_call x1, Pallas kernels, leaves(): pl.pallas_call(lambda *refs: leaves_body(len(others), *refs), out_shape=(...  5.59 us
    pallas_call x2, Pallas kernels, first_product(): pl.pallas_call(lambda *refs: first_product_body(gain, span, own, groups,...  2.91 us
  transfers between devices with their start and end apart: 17, of which 11 were waited for; matrix products, arithmetic and copies ran while one was open for 0% of the time, Pallas kernels for 20%

profile of v4, /device:TPU:0, one launch (start us, length us, event | category | flops | bytes accessed | tf_op | source)
XLA Modules:
  0.0 63.9 jit_solution(10259646500859331076)
XLA Ops:
  0.6 1.3 %pack.1 = (bf16[1104,256]{1,0:T(8,128)(2,1)S(1)}, bf16[16,256]{1,0:T(8,128)(2,1)S(1)}) custom-call(bf16[4,256,256]{2,1,0:T(8,128)(2,1)} %refs_0_.1, bf16[16,4,256]{2,1,0:T(4,128)(2,1)} %refs_1_.1, s32[2,64]{1,0:T(2,128)} %refs_2_.1, s32[1,64]{1,0:T(1,128)} %refs_3_.1, s32[4,64]{1,0:T(4,128)} %refs_4_.1, s32[2,64]{1,0:T(2,128)} %refs_5_.1), custom_call_target="tpu_custom_call" | custom-call | tf_op jit(solution)/shard_map/pack/pallas_call | solution.py:120
  1.9 3.0 %collective-permute-start.1 = (bf16[1104,256]{1,0:T(8,128)(2,1)S(1)}, bf16[1104,256]{1,0:T(8,128)(2,1)S(1)}, u32[]{:S(2)}, u32[]{:S(2)}) collective-permute-start(bf16[1104,256]{1,0:T(8,128)(2,1)S(1)} %get-tuple-element.53.refs_0_.refs_3_), channel_id=1, source_target_pairs={{0,16},{1,17},{2,18},{3,19},{4,20},{5,21},{6,22},{7,23},{8,24},{9,... | collective-permute-start | bytes 1695752 | tf_op jit(solution)/shard_map/ppermute | solution.py:576
  4.9 1.5 %collective-permute-start = (bf16[1104,256]{1,0:T(8,128)(2,1)S(1)}, bf16[1104,256]{1,0:T(8,128)(2,1)S(1)}, u32[]{:S(2)}, u32[]{:S(2)}) collective-permute-start(bf16[1104,256]{1,0:T(8,128)(2,1)S(1)} %get-tuple-element.53.refs_0_.refs_3_), channel_id=1, source_target_pairs={{0,1},{1,0},{2,3},{3,2},{4,5},{5,4},{6,7},{7,6},{8,9},{9,8},{10,11... | collective-permute-start | bytes 1695752 | tf_op jit(solution)/shard_map/ppermute | solution.py:576
  6.4 3.6 %collective-permute-start.4 = (bf16[16,256]{1,0:T(8,128)(2,1)S(1)}, bf16[16,256]{1,0:T(8,128)(2,1)S(1)}, u32[]{:S(2)}, u32[]{:S(2)}) collective-permute-start(bf16[16,256]{1,0:T(8,128)(2,1)S(1)} %get-tuple-element.54.refs_1_), channel_id=1, source_target_pairs={{0,6},{1,7},{2,4},{3,5},{4,2},{5,3},{6,0},{7,1},{8,14},{9,15},{10,... | collective-permute-start | bytes 24584 | tf_op jit(solution)/shard_map/ppermute | solution.py:576
  10.0 0.0 collective-permute-start.3
  10.0 0.8 %collective-permute-start.2 = (bf16[16,256]{1,0:T(8,128)(2,1)S(1)}, bf16[16,256]{1,0:T(8,128)(2,1)S(1)}, u32[]{:S(2)}, u32[]{:S(2)}) collective-permute-start(bf16[16,256]{1,0:T(8,128)(2,1)S(1)} %get-tuple-element.54.refs_1_), channel_id=1, source_target_pairs={{0,2},{1,3},{2,0},{3,1},{4,6},{5,7},{6,4},{7,5},{8,10},{9,11},{10,... | collective-permute-start | bytes 24584 | tf_op jit(solution)/shard_map/ppermute | solution.py:576
  10.8 1.1 %collective-permute-done.4.refs_4_ = bf16[16,256]{1,0:T(8,128)(2,1)S(1)} collective-permute-done((bf16[16,256]{1,0:T(8,128)(2,1)S(1)}, bf16[16,256]{1,0:T(8,128)(2,1)S(1)}, u32[]{:S(2)}, u32[]{:S(2)}) %collective-permute-start.4) | collective-permute-done | bytes 8224 | tf_op jit(solution)/shard_map/ppermute | solution.py:576
  11.9 2.7 %collective-permute-done.3.refs_3_ = bf16[16,256]{1,0:T(8,128)(2,1)S(1)} collective-permute-done((bf16[16,256]{1,0:T(8,128)(2,1)S(1)}, bf16[16,256]{1,0:T(8,128)(2,1)S(1)}, u32[]{:S(2)}, u32[]{:S(2)}) %collective-permute-start.3) | collective-permute-done | bytes 8224 | tf_op jit(solution)/shard_map/ppermute | solution.py:576
  14.6 0.0 collective-permute-done.2.refs_2_
  14.6 0.0 collective-permute-start.5
  14.6 1.5 %first_product.2 = (bf16[512,64]{1,0:T(8,128)(2,1)S(1)}, bf16[512,64]{1,0:T(8,128)(2,1)S(1)}, f32[512,256]{1,0:T(8,128)S(1)}, f32[512,256]{1,0:T(8,128)S(1)}) custom-call(bf16[1104,256]{1,0:T(8,128)(2,1)S(1)} %get-tuple-element.53.refs_0_.refs_3_, bf16[16,256]{1,0:T(8,128)(2,1)S(1)} %get-tuple-element.54.refs_1_, ...), custom_call_target="tpu_custom_call" | custom-call | tf_op jit(solution)/shard_map/first_product/pallas_call | solution.py:182
  16.0 0.0 collective-permute-done.5.refs_1_
  16.1 1.5 %first_product.3 = (bf16[512,64]{1,0:T(8,128)(2,1)S(1)}, bf16[512,64]{1,0:T(8,128)(2,1)S(1)}, f32[512,256]{1,0:T(8,128)S(1)}, f32[512,256]{1,0:T(8,128)S(1)}) custom-call(bf16[1104,256]{1,0:T(8,128)(2,1)S(1)} %get-tuple-element.53.refs_0_.refs_3_, bf16[16,1024]{1,0:T(8,128)(2,1)S(1)} %collective-permute-done.5.refs_1_), custom_call_target="tpu_custom_call" | custom-call | tf_op jit(solution)/shard_map/first_product/pallas_call | solution.py:182
  17.5 0.2 collective-permute-done.1.second_ref.refs_0_
  17.7 1.5 %collective-permute-done.first_ref.refs_1_.refs_0_ = bf16[1104,256]{1,0:T(8,128)(2,1)S(1)} collective-permute-done((bf16[1104,256]{1,0:T(8,128)(2,1)S(1)}, bf16[1104,256]{1,0:T(8,128)(2,1)S(1)}, u32[]{:S(2)}, u32[]{:S(2)}) %collective-permute-start) | collective-permute-done | bytes 565280 | tf_op jit(solution)/shard_map/ppermute | solution.py:576
  19.2 0.4 collective-permute-start.6
  19.7 1.6 %collective-permute-start.7 = (bf16[544,256]{1,0:T(8,128)(2,1)S(1)}, bf16[544,256]{1,0:T(8,128)(2,1)S(1)}, u32[]{:S(2)}, u32[]{:S(2)}) collective-permute-start(bf16[544,256]{1,0:T(8,128)(2,1)S(1)} %get-tuple-element.62), channel_id=1, source_target_pairs={{0,1},{1,0},{2,3},{3,2},{4,5},{5,4},{6,7},{7,6},{8,9},{9,8},{10,11... | collective-permute-start | bytes 835592 | tf_op jit(solution)/shard_map/ppermute | solution.py:576
  21.3 1.2 %skeletons.1 = (bf16[6,64,128]{2,1,0:T(8,128)(2,1)S(1)}, bf16[192,768]{1,0:T(8,128)(2,1)S(1)}, bf16[192,768]{1,0:T(8,128)(2,1)S(1)}, bf16[16,128]{1,0:T(8,128)(2,1)S(1)}) custom-call(bf16[1104,256]{1,0:T(8,128)(2,1)S(1)} %get-tuple-element.53.refs_0_.refs_3_, bf16[1104,256]{1,0:T(8,128)(2,1)S(1)} %collective-permute-done.first_ref.refs_1_.refs_0_), custom_call_target="tpu_custom_call" | custom-call | tf_op jit(solution)/shard_map/skeletons/pallas_call | solution.py:528
  22.5 2.5 %product.6 = (f32[512,256]{1,0:T(8,128)S(1)}, f32[512,256]{1,0:T(8,128)S(1)}, f32[512,256]{1,0:T(8,128)S(1)}, f32[512,256]{1,0:T(8,128)S(1)}) custom-call(bf16[1104,256]{1,0:T(8,128)(2,1)S(1)} %collective-permute-done.first_ref.refs_1_.refs_0_, bf16[512,64]{1,0:T(8,128)(2,1)S(1)} %get-tuple-element.63.refs_1_.refs_2_, ...), custom_call_target="tpu_custom_call" | custom-call | tf_op jit(solution)/shard_map/product/pallas_call | solution.py:209
  24.9 2.5 %product.7 = (f32[512,256]{1,0:T(8,128)S(1)}, f32[512,256]{1,0:T(8,128)S(1)}, f32[512,256]{1,0:T(8,128)S(1)}, f32[512,256]{1,0:T(8,128)S(1)}) custom-call(bf16[1104,256]{1,0:T(8,128)(2,1)S(1)} %collective-permute-done.1.second_ref.refs_0_, bf16[512,64]{1,0:T(8,128)(2,1)S(1)} %get-tuple-element.63.refs_1_.refs_2_, ...), custom_call_target="tpu_custom_call" | custom-call | tf_op jit(solution)/shard_map/product/pallas_call | solution.py:209
  27.5 0.0 collective-permute-done.6.refs_0_
  27.5 0.0 collective-permute-done.7.refs_1_
  27.5 0.9 %product.10 = f32[512,256]{1,0:T(8,128)S(1)} custom-call(bf16[544,256]{1,0:T(8,128)(2,1)S(1)} %collective-permute-done.6.refs_0_, bf16[544,256]{1,0:T(8,128)(2,1)S(1)} %collective-permute-done.7.refs_1_, bf16[512,64]{1,0:T(8,128)(2,1)S(1)} %get-tuple-element.67.refs_4_.refs_2_, f32[512,256]{1,0:T(8,128)S(1)} %get-tuple-element.82.refs_3_), custom_call_target="tpu_custom_call" | custom-call | tf_op jit(solution)/shard_map/product/pallas_call | solution.py:209
  28.4 0.1 collective-permute-start.8
  28.5 0.9 %product.9.refs_0_ = f32[512,256]{1,0:T(8,128)S(1)} custom-call(bf16[544,256]{1,0:T(8,128)(2,1)S(1)} %collective-permute-done.6.refs_0_, bf16[544,256]{1,0:T(8,128)(2,1)S(1)} %collective-permute-done.7.refs_1_, bf16[512,64]{1,0:T(8,128)(2,1)S(1)} %get-tuple-element.65.refs_2_, f32[512,256]{1,0:T(8,128)S(1)} %get-tuple-element.81.refs_3_), custom_call_target="tpu_custom_call" | custom-call | tf_op jit(solution)/shard_map/product/pallas_call | solution.py:209
  29.4 1.0 %collective-permute-done.8.refs_1_ = f32[512,256]{1,0:T(8,128)S(1)} collective-permute-done((f32[512,256]{1,0:T(8,128)S(1)}, f32[512,256]{1,0:T(8,128)S(1)}, u32[]{:S(2)}, u32[]{:S(2)}) %collective-permute-start.8) | collective-permute-done | bytes 524320 | tf_op jit(solution)/shard_map/ppermute | solution.py:576
  30.3 0.1 add_up.3
  30.4 1.6 %collective-permute-start.10 = (bf16[256,256]{1,0:T(8,128)(2,1)S(1)}, bf16[256,256]{1,0:T(8,128)(2,1)S(1)}, u32[]{:S(2)}, u32[]{:S(2)}) collective-permute-start(bf16[256,256]{1,0:T(8,128)(2,1)S(1)} %get-tuple-element.87), channel_id=1, source_target_pairs={{0,2},{1,3},{2,0},{3,1},{4,6},{5,7},{6,4},{7,5},{8,10},{9,11},{10,... | collective-permute-start | bytes 393224 | tf_op jit(solution)/shard_map/ppermute | solution.py:576
  32.0 0.5 collective-permute-start.11
  32.5 0.9 %product.8.refs_0_ = f32[512,256]{1,0:T(8,128)S(1)} custom-call(bf16[544,256]{1,0:T(8,128)(2,1)S(1)} %collective-permute-done.6.refs_0_, bf16[544,256]{1,0:T(8,128)(2,1)S(1)} %collective-permute-done.7.refs_1_, bf16[512,64]{1,0:T(8,128)(2,1)S(1)} %get-tuple-element.63.refs_1_.refs_2_, f32[512,256]{1,0:T(8,128)S(1)} %get-tuple-element.80.refs_3_), custom_call_target="tpu_custom_call" | custom-call | tf_op jit(solution)/shard_map/product/pallas_call | solution.py:209
  33.4 0.9 %product.11 = f32[512,256]{1,0:T(8,128)S(1)} custom-call(bf16[544,256]{1,0:T(8,128)(2,1)S(1)} %collective-permute-done.6.refs_0_, bf16[544,256]{1,0:T(8,128)(2,1)S(1)} %collective-permute-done.7.refs_1_, bf16[512,64]{1,0:T(8,128)(2,1)S(1)} %get-tuple-element.66.refs_3_.refs_2_, f32[512,256]{1,0:T(8,128)S(1)} %get-tuple-element.85.refs_3_), custom_call_target="tpu_custom_call" | custom-call | tf_op jit(solution)/shard_map/product/pallas_call | solution.py:209
  34.3 0.1 collective-permute-start.9
  34.4 1.7 %collective-permute-done.11.refs_2_.refs_1_ = bf16[16,128]{1,0:T(8,128)(2,1)S(1)} collective-permute-done((bf16[16,128]{1,0:T(8,128)(2,1)S(1)}, bf16[16,128]{1,0:T(8,128)(2,1)S(1)}, u32[]{:S(2)}, u32[]{:S(2)}) %collective-permute-start.11) | collective-permute-done | bytes 4128 | tf_op jit(solution)/shard_map/ppermute | solution.py:576
  36.1 0.0 collective-permute-done.10.refs_1_
  36.1 2.8 %collective-permute-start.12 = (bf16[256,256]{1,0:T(8,128)(2,1)S(1)}, bf16[256,256]{1,0:T(8,128)(2,1)S(1)}, u32[]{:S(2)}, u32[]{:S(2)}) collective-permute-start(bf16[256,256]{1,0:T(8,128)(2,1)S(1)} %add_up.4.refs_2_), channel_id=1, source_target_pairs={{0,4},{1,5},{2,6},{3,7},{4,0},{5,1},{6,2},{7,3},{8,12},{9,13},{10,... | collective-permute-start | bytes 393224 | tf_op jit(solution)/shard_map/ppermute | solution.py:576
  39.0 0.0 collective-permute-done.9.refs_1_
  39.0 0.1 add_up.5
  39.0 1.6 %collective-permute-start.13 = (bf16[256,256]{1,0:T(8,128)(2,1)S(1)}, bf16[256,256]{1,0:T(8,128)(2,1)S(1)}, u32[]{:S(2)}, u32[]{:S(2)}) collective-permute-start(bf16[256,256]{1,0:T(8,128)(2,1)S(1)} %get-tuple-element.90), channel_id=1, source_target_pairs={{0,2},{1,3},{2,0},{3,1},{4,6},{5,7},{6,4},{7,5},{8,10},{9,11},{10,... | collective-permute-start | bytes 393224 | tf_op jit(solution)/shard_map/ppermute | solution.py:576
  40.7 0.8 %top_couplings.1 = (bf16[192,768]{1,0:T(8,128)(2,1)S(1)}, bf16[192,768]{1,0:T(8,128)(2,1)S(1)}) custom-call(bf16[16,128]{1,0:T(8,128)(2,1)S(1)} %get-tuple-element.88.refs_0_, bf16[16,128]{1,0:T(8,128)(2,1)S(1)} %collective-permute-done.11.refs_2_.refs_1_, bf16[6,64,128]{2,1,0:T(8,128)(2,1)S(1)} %get-tuple-element.91.refs_2_.refs_4_.refs_5_), custom_call_target="tpu_custom_call" | custom-call | tf_op jit(solution)/shard_map/top_couplings/pallas_call | solution.py:555
  41.4 3.4 %collective-permute-done.12.refs_1_ = bf16[256,256]{1,0:T(8,128)(2,1)S(1)} collective-permute-done((bf16[256,256]{1,0:T(8,128)(2,1)S(1)}, bf16[256,256]{1,0:T(8,128)(2,1)S(1)}, u32[]{:S(2)}, u32[]{:S(2)}) %collective-permute-start.12) | collective-permute-done | bytes 131104 | tf_op jit(solution)/shard_map/ppermute | solution.py:576
  44.8 0.4 collective-permute-done.13.refs_2_
  45.2 5.6 %leaves.1 = (f32[2,64,128]{2,1,0:T(8,128)}, f32[64,128]{1,0:T(8,128)S(1)}, f32[64,256]{1,0:T(8,128)S(1)}, f32[64,256]{1,0:T(8,128)S(1)}, bf16[192,256]{1,0:T(8,128)(2,1)S(1)}) custom-call(f32[256,256]{1,0:T(8,128)S(1)} %get-tuple-element.89.refs_0_, bf16[256,256]{1,0:T(8,128)(2,1)S(1)} %collective-permute-done.12.refs_1_, ...), custom_call_target="tpu_custom_call" | custom-call | tf_op jit(solution)/shard_map/leaves/pallas_call | solution.py:375
  50.8 1.6 %collective-permute-start.16 = (bf16[192,256]{1,0:T(8,128)(2,1)S(1)}, bf16[192,256]{1,0:T(8,128)(2,1)S(1)}, u32[]{:S(2)}, u32[]{:S(2)}) collective-permute-start(bf16[192,256]{1,0:T(8,128)(2,1)S(1)} %get-tuple-element.98), channel_id=1, source_target_pairs={{0,3},{1,2},{2,1},{3,0},{4,7},{5,6},{6,5},{7,4},{8,11},{9,10},{10,... | collective-permute-start | bytes 294920 | tf_op jit(solution)/shard_map/ppermute | solution.py:576
  52.4 0.7 %collective-permute-start.15 = (bf16[192,256]{1,0:T(8,128)(2,1)S(1)}, bf16[192,256]{1,0:T(8,128)(2,1)S(1)}, u32[]{:S(2)}, u32[]{:S(2)}) collective-permute-start(bf16[192,256]{1,0:T(8,128)(2,1)S(1)} %get-tuple-element.98), channel_id=1, source_target_pairs={{0,2},{1,3},{2,0},{3,1},{4,6},{5,7},{6,4},{7,5},{8,10},{9,11},{10,... | collective-permute-start | bytes 294920 | tf_op jit(solution)/shard_map/ppermute | solution.py:576
  53.2 1.2 %collective-permute-start.14 = (bf16[192,256]{1,0:T(8,128)(2,1)S(1)}, bf16[192,256]{1,0:T(8,128)(2,1)S(1)}, u32[]{:S(2)}, u32[]{:S(2)}) collective-permute-start(bf16[192,256]{1,0:T(8,128)(2,1)S(1)} %get-tuple-element.98), channel_id=1, source_target_pairs={{0,1},{1,0},{2,3},{3,2},{4,5},{5,4},{6,7},{7,6},{8,9},{9,8},{10,11... | collective-permute-start | bytes 294920 | tf_op jit(solution)/shard_map/ppermute | solution.py:576
  54.4 2.0 %collective-permute-done.16.refs_4_ = bf16[192,256]{1,0:T(8,128)(2,1)S(1)} collective-permute-done((bf16[192,256]{1,0:T(8,128)(2,1)S(1)}, bf16[192,256]{1,0:T(8,128)(2,1)S(1)}, u32[]{:S(2)}, u32[]{:S(2)}) %collective-permute-start.16) | collective-permute-done | bytes 98336 | tf_op jit(solution)/shard_map/ppermute | solution.py:576
  56.4 0.7 %collective-permute-done.15.refs_3_ = bf16[192,256]{1,0:T(8,128)(2,1)S(1)} collective-permute-done((bf16[192,256]{1,0:T(8,128)(2,1)S(1)}, bf16[192,256]{1,0:T(8,128)(2,1)S(1)}, u32[]{:S(2)}, u32[]{:S(2)}) %collective-permute-start.15) | collective-permute-done | bytes 98336 | tf_op jit(solution)/shard_map/ppermute | solution.py:576
  57.1 0.7 %collective-permute-done.14.refs_2_ = bf16[192,256]{1,0:T(8,128)(2,1)S(1)} collective-permute-done((bf16[192,256]{1,0:T(8,128)(2,1)S(1)}, bf16[192,256]{1,0:T(8,128)(2,1)S(1)}, u32[]{:S(2)}, u32[]{:S(2)}) %collective-permute-start.14) | collective-permute-done | bytes 98336 | tf_op jit(solution)/shard_map/ppermute | solution.py:576
  57.8 5.9 %upper_levels.1 = (f32[3,1,64,128]{3,2,1,0:T(8,128)}, f32[2,1,64,256]{3,2,1,0:T(8,128)}) custom-call(f32[64,256]{1,0:T(8,128)S(1)} %get-tuple-element.96.refs_0_, f32[64,256]{1,0:T(8,128)S(1)} %get-tuple-element.97.refs_1_, bf16[192,256]{1,0:T(8,128)(2,1)S(1)} %collective-permute-done.14.refs_2_, bf16[192,256]{1,0:T(8,128)(2,1)S(1)} %collective-permute-done.15.refs_3_, ...), custom_call_target="tpu_custom_call" | custom-call | tf_op jit(solution)/shard_map/upper_levels/pallas_call | solution.py:451
  (3 shorter events, 0.1 us)
Async XLA Ops:
  1.9 15.8 %collective-permute-start.1 = (bf16[1104,256]{1,0:T(8,128)(2,1)S(1)}, bf16[1104,256]{1,0:T(8,128)(2,1)S(1)}, u32[]{:S(2)}, u32[]{:S(2)}) collective-permute-start(bf16[1104,256]{1,0:T(8,128)(2,1)S(1)} %get-tuple-element.53.refs_0_.refs_3_), channel_id=1, source_target_pairs={{0,16},{1,17},{2,18},{3,19},{4,20},{5,21},{6,22},{7,23},{8,24},{9,... | collective-permute-start | bytes 1695752 | tf_op jit(solution)/shard_map/ppermute | solution.py:576
  4.9 14.3 %collective-permute-start = (bf16[1104,256]{1,0:T(8,128)(2,1)S(1)}, bf16[1104,256]{1,0:T(8,128)(2,1)S(1)}, u32[]{:S(2)}, u32[]{:S(2)}) collective-permute-start(bf16[1104,256]{1,0:T(8,128)(2,1)S(1)} %get-tuple-element.53.refs_0_.refs_3_), channel_id=1, source_target_pairs={{0,1},{1,0},{2,3},{3,2},{4,5},{5,4},{6,7},{7,6},{8,9},{9,8},{10,11... | collective-permute-start | bytes 1695752 | tf_op jit(solution)/shard_map/ppermute | solution.py:576
  6.4 5.4 %collective-permute-start.4 = (bf16[16,256]{1,0:T(8,128)(2,1)S(1)}, bf16[16,256]{1,0:T(8,128)(2,1)S(1)}, u32[]{:S(2)}, u32[]{:S(2)}) collective-permute-start(bf16[16,256]{1,0:T(8,128)(2,1)S(1)} %get-tuple-element.54.refs_1_), channel_id=1, source_target_pairs={{0,6},{1,7},{2,4},{3,5},{4,2},{5,3},{6,0},{7,1},{8,14},{9,15},{10,... | collective-permute-start | bytes 24584 | tf_op jit(solution)/shard_map/ppermute | solution.py:576
  10.0 4.5 %collective-permute-start.3 = (bf16[16,256]{1,0:T(8,128)(2,1)S(1)}, bf16[16,256]{1,0:T(8,128)(2,1)S(1)}, u32[]{:S(2)}, u32[]{:S(2)}) collective-permute-start(bf16[16,256]{1,0:T(8,128)(2,1)S(1)} %get-tuple-element.54.refs_1_), channel_id=1, source_target_pairs={{0,4},{1,5},{2,6},{3,7},{4,0},{5,1},{6,2},{7,3},{8,12},{9,13},{10,... | collective-permute-start | bytes 24584 | tf_op jit(solution)/shard_map/ppermute | solution.py:576
  10.0 4.5 %collective-permute-start.2 = (bf16[16,256]{1,0:T(8,128)(2,1)S(1)}, bf16[16,256]{1,0:T(8,128)(2,1)S(1)}, u32[]{:S(2)}, u32[]{:S(2)}) collective-permute-start(bf16[16,256]{1,0:T(8,128)(2,1)S(1)} %get-tuple-element.54.refs_1_), channel_id=1, source_target_pairs={{0,2},{1,3},{2,0},{3,1},{4,6},{5,7},{6,4},{7,5},{8,10},{9,11},{10,... | collective-permute-start | bytes 24584 | tf_op jit(solution)/shard_map/ppermute | solution.py:576
  14.6 1.5 %collective-permute-start.5 = (bf16[16,1024]{1,0:T(8,128)(2,1)S(1)}, bf16[16,1024]{1,0:T(8,128)(2,1)S(1)}, u32[]{:S(2)}, u32[]{:S(2)}) collective-permute-start(bf16[16,1024]{1,0:T(8,128)(2,1)S(1)} %pad_maximum_fusion), channel_id=1, source_target_pairs={{0,8},{1,9},{2,10},{3,11},{4,12},{5,13},{6,14},{7,15},{8,0},{9,1},... | collective-permute-start | bytes 98312 | tf_op jit(solution)/shard_map/ppermute | solution.py:576
  19.2 8.2 %collective-permute-start.6 = (bf16[544,256]{1,0:T(8,128)(2,1)S(1)}, bf16[544,256]{1,0:T(8,128)(2,1)S(1)}, u32[]{:S(2)}, u32[]{:S(2)}) collective-permute-start(bf16[544,256]{1,0:T(8,128)(2,1)S(1)} %get-tuple-element.61), channel_id=1, source_target_pairs={{0,16},{1,17},{2,18},{3,19},{4,20},{5,21},{6,22},{7,23},{8,24},{9,... | collective-permute-start | bytes 835592 | tf_op jit(solution)/shard_map/ppermute | solution.py:576
  19.7 7.8 %collective-permute-start.7 = (bf16[544,256]{1,0:T(8,128)(2,1)S(1)}, bf16[544,256]{1,0:T(8,128)(2,1)S(1)}, u32[]{:S(2)}, u32[]{:S(2)}) collective-permute-start(bf16[544,256]{1,0:T(8,128)(2,1)S(1)} %get-tuple-element.62), channel_id=1, source_target_pairs={{0,1},{1,0},{2,3},{3,2},{4,5},{5,4},{6,7},{7,6},{8,9},{9,8},{10,11... | collective-permute-start | bytes 835592 | tf_op jit(solution)/shard_map/ppermute | solution.py:576
  28.4 2.0 %collective-permute-start.8 = (f32[512,256]{1,0:T(8,128)S(1)}, f32[512,256]{1,0:T(8,128)S(1)}, u32[]{:S(2)}, u32[]{:S(2)}) collective-permute-start(f32[512,256]{1,0:T(8,128)S(1)} %product.10), channel_id=1, source_target_pairs={{0,8},{1,9},{2,10},{3,11},{4,12},{5,13},{6,14},{7,15},{8,0},{9,1},... | collective-permute-start | bytes 1572872 | tf_op jit(solution)/shard_map/ppermute | solution.py:576
  30.4 5.7 %collective-permute-start.10 = (bf16[256,256]{1,0:T(8,128)(2,1)S(1)}, bf16[256,256]{1,0:T(8,128)(2,1)S(1)}, u32[]{:S(2)}, u32[]{:S(2)}) collective-permute-start(bf16[256,256]{1,0:T(8,128)(2,1)S(1)} %get-tuple-element.87), channel_id=1, source_target_pairs={{0,2},{1,3},{2,0},{3,1},{4,6},{5,7},{6,4},{7,5},{8,10},{9,11},{10,... | collective-permute-start | bytes 393224 | tf_op jit(solution)/shard_map/ppermute | solution.py:576
  32.0 4.1 %collective-permute-start.11 = (bf16[16,128]{1,0:T(8,128)(2,1)S(1)}, bf16[16,128]{1,0:T(8,128)(2,1)S(1)}, u32[]{:S(2)}, u32[]{:S(2)}) collective-permute-start(bf16[16,128]{1,0:T(8,128)(2,1)S(1)} %get-tuple-element.88.refs_0_), channel_id=1, source_target_pairs={{0,2},{1,3},{2,0},{3,1},{4,6},{5,7},{6,4},{7,5},{8,10},{9,11},{10,... | collective-permute-start | bytes 12296 | tf_op jit(solution)/shard_map/ppermute | solution.py:576
  34.3 4.7 %collective-permute-start.9 = (f32[512,256]{1,0:T(8,128)S(1)}, f32[512,256]{1,0:T(8,128)S(1)}, u32[]{:S(2)}, u32[]{:S(2)}) collective-permute-start(f32[512,256]{1,0:T(8,128)S(1)} %product.11), channel_id=1, source_target_pairs={{0,8},{1,9},{2,10},{3,11},{4,12},{5,13},{6,14},{7,15},{8,0},{9,1},... | collective-permute-start | bytes 1572872 | tf_op jit(solution)/shard_map/ppermute | solution.py:576
  36.1 8.7 %collective-permute-start.12 = (bf16[256,256]{1,0:T(8,128)(2,1)S(1)}, bf16[256,256]{1,0:T(8,128)(2,1)S(1)}, u32[]{:S(2)}, u32[]{:S(2)}) collective-permute-start(bf16[256,256]{1,0:T(8,128)(2,1)S(1)} %add_up.4.refs_2_), channel_id=1, source_target_pairs={{0,4},{1,5},{2,6},{3,7},{4,0},{5,1},{6,2},{7,3},{8,12},{9,13},{10,... | collective-permute-start | bytes 393224 | tf_op jit(solution)/shard_map/ppermute | solution.py:576
  39.0 6.2 %collective-permute-start.13 = (bf16[256,256]{1,0:T(8,128)(2,1)S(1)}, bf16[256,256]{1,0:T(8,128)(2,1)S(1)}, u32[]{:S(2)}, u32[]{:S(2)}) collective-permute-start(bf16[256,256]{1,0:T(8,128)(2,1)S(1)} %get-tuple-element.90), channel_id=1, source_target_pairs={{0,2},{1,3},{2,0},{3,1},{4,6},{5,7},{6,4},{7,5},{8,10},{9,11},{10,... | collective-permute-start | bytes 393224 | tf_op jit(solution)/shard_map/ppermute | solution.py:576
  50.8 5.6 %collective-permute-start.16 = (bf16[192,256]{1,0:T(8,128)(2,1)S(1)}, bf16[192,256]{1,0:T(8,128)(2,1)S(1)}, u32[]{:S(2)}, u32[]{:S(2)}) collective-permute-start(bf16[192,256]{1,0:T(8,128)(2,1)S(1)} %get-tuple-element.98), channel_id=1, source_target_pairs={{0,3},{1,2},{2,1},{3,0},{4,7},{5,6},{6,5},{7,4},{8,11},{9,10},{10,... | collective-permute-start | bytes 294920 | tf_op jit(solution)/shard_map/ppermute | solution.py:576
  52.4 4.6 %collective-permute-start.15 = (bf16[192,256]{1,0:T(8,128)(2,1)S(1)}, bf16[192,256]{1,0:T(8,128)(2,1)S(1)}, u32[]{:S(2)}, u32[]{:S(2)}) collective-permute-start(bf16[192,256]{1,0:T(8,128)(2,1)S(1)} %get-tuple-element.98), channel_id=1, source_target_pairs={{0,2},{1,3},{2,0},{3,1},{4,6},{5,7},{6,4},{7,5},{8,10},{9,11},{10,... | collective-permute-start | bytes 294920 | tf_op jit(solution)/shard_map/ppermute | solution.py:576
  53.2 4.6 %collective-permute-start.14 = (bf16[192,256]{1,0:T(8,128)(2,1)S(1)}, bf16[192,256]{1,0:T(8,128)(2,1)S(1)}, u32[]{:S(2)}, u32[]{:S(2)}) collective-permute-start(bf16[192,256]{1,0:T(8,128)(2,1)S(1)} %get-tuple-element.98), channel_id=1, source_target_pairs={{0,1},{1,0},{2,3},{3,2},{4,5},{5,4},{6,7},{7,6},{8,9},{9,8},{10,11... | collective-permute-start | bytes 294920 | tf_op jit(solution)/shard_map/ppermute | solution.py:576

commit v5 on v4

--- a/solution.py
+++ b/solution.py
@@ -18,7 +18,7 @@
     return pltpu.VMEM(tuple(shape), kind)
 
 
-COST = pl.CostEstimate(flops=0, bytes_accessed=0, transcendentals=0)
+COST = pl.CostEstimate(flops=10**9, bytes_accessed=0, transcendentals=0)
 LONG = pl.CostEstimate(flops=10**10, bytes_accessed=0, transcendentals=0)
 PARAMS = pltpu.CompilerParams(vmem_limit_bytes=16 << 20)
 
@@ -78,15 +78,13 @@
 
 def pack_body(*refs):
     probes_ref, points_ref, *table_refs = refs[:6]
-    packed_ref, own_ref, held_ref, rows_ref, *held_tables, sem = refs[6:]
-    quarters, span, _ = probes_ref.shape
-    half = quarters // 2
-    rows = half * (span + 16)
+    first_ref, second_ref, own_ref, held_ref, rows_ref, *held_tables, sem = refs[6:]
+    span = probes_ref.shape[1]
     pairs = [(points_ref, held_ref), *zip(table_refs, held_tables)]
     small = len(pairs)
-    for quarter in range(quarters):
-        start = quarter // half * rows + quarter % half * span
-        pairs.append((probes_ref.at[quarter], packed_ref.at[pl.ds(start, span)]))
+    for quarter in range(4):
+        target = (first_ref, second_ref)[quarter // 2].at[pl.ds(quarter % 2 * span, span)]
+        pairs.append((probes_ref.at[quarter], target))
     copies = [
         pltpu.make_async_copy(source, target, sem.at[pos])
         for pos, (source, target) in enumerate(pairs)
@@ -97,10 +95,10 @@
     for copy in copies[:small]:
         copy.wait()
     points = held_ref[...].astype(F32)
-    for quarter in range(quarters):
+    for quarter in range(4):
         feats = points[:, quarter, :].astype(BF16)
-        start = quarter // half * rows + half * span + quarter % half * 16
-        packed_ref[pl.ds(start, 16), :] = feats
+        half_ref = (first_ref, second_ref)[quarter // 2]
+        half_ref[pl.ds(2 * span + quarter % 2 * 16, 16), :] = feats
         if quarter == 0:
             own_ref[...] = feats
     start = 0
@@ -108,19 +106,20 @@
         count, rank = table.shape
         rows_ref[pl.ds(start, count), pl.ds(0, rank)] = table[...].astype(F32)
         start += count
-    packed_ref[pl.ds(2 * rows, rows_ref.shape[0]), :] = rows_ref[...].astype(BF16)
+    first_ref[pl.ds(second_ref.shape[0], rows_ref.shape[0]), :] = rows_ref[...].astype(BF16)
     for copy in copies[small:]:
         copy.wait()
 
 
 def pack(probes, points, tables):
-    quarters, span, samples = probes.shape
+    _, span, samples = probes.shape
     table_rows = -(-sum(table.shape[0] for table in tables) // 16) * 16
     inputs = (probes, points, *tables)
     return pl.pallas_call(
         pack_body,
         out_shape=(
-            vmem((quarters * (span + 16) + table_rows, samples), BF16),
+            vmem((2 * (span + 16) + table_rows, samples), BF16),
+            vmem((2 * (span + 16), samples), BF16),
             vmem((16, span), BF16),
         ),
         in_specs=[pl.BlockSpec(memory_space=pltpu.HBM)] * len(inputs),
@@ -128,7 +127,7 @@
             pltpu.VMEM(points.shape, BF16),
             pltpu.VMEM((table_rows, samples), F32),
             *[pltpu.VMEM(table.shape, jnp.int32) for table in tables],
-            pltpu.SemaphoreType.DMA((quarters + 1 + len(tables),)),
+            pltpu.SemaphoreType.DMA((5 + len(tables),)),
         ],
         cost_estimate=COST,
         compiler_params=PARAMS,
@@ -143,28 +142,26 @@
     return jnp.where(row_leaf == col_leaf, 0.0, entries)
 
 
-def add_source(source_ref, row_refs, cols_ref, put, span, own):
-    size = 2 * (span + 16)
-    parts = range(0, source_ref.shape[0] // size * size, size)
-    for number, part in enumerate(parts):
+def add_halves(half_refs, row_refs, cols_ref, put, span, own):
+    for number, half_ref in enumerate(half_refs):
         for quarter in range(2):
-            feats = source_ref[pl.ds(part + 2 * span + 16 * quarter, 16), :]
+            feats = half_ref[pl.ds(2 * span + 16 * quarter, 16), :]
             cols_ref[:, pl.ds((2 * number + quarter) * span, span)] = col_features(feats)
-    columns = 2 * span * len(parts)
+    columns = 2 * span * len(half_refs)
     for group, rows_ref in enumerate(row_refs):
         for start in range(0, rows_ref.shape[0], span):
             feats = rows_ref[pl.ds(start, span), :]
             entries = jnp.exp2(over(feats, cols_ref[:, :columns], 1, 0))
             if own and group == 0 and start == 0:
                 entries = jnp.concatenate([masked(entries[:, :span]), entries[:, span:]], axis=1)
-            randoms = [source_ref[pl.ds(part, 2 * span), :] for part in parts]
+            randoms = [half_ref[pl.ds(0, 2 * span), :] for half_ref in half_refs]
             put(group, start, over(entries.astype(BF16), jnp.concatenate(randoms, axis=0), 1, 0))
 
 
-def first_product_body(gain, span, own, groups, point_count, *refs):
-    source_ref, *point_refs = refs[: point_count + 1]
-    row_refs = refs[point_count + 1 : point_count + 1 + len(groups)]
-    total_refs, cols_ref = refs[point_count + 1 + len(groups) : -1], refs[-1]
+def first_product_body(gain, span, groups, point_count, *refs):
+    half_refs, point_refs = refs[:2], refs[2 : point_count + 2]
+    row_refs = refs[point_count + 2 : point_count + 2 + len(groups)]
+    total_refs, cols_ref = refs[point_count + 2 + len(groups) : -1], refs[-1]
     for rows_ref, places in zip(row_refs, groups):
         for pos, (array, start) in enumerate(places):
             feats = point_refs[array][:, pl.ds(start, span)]
@@ -173,63 +170,47 @@
     def put(group, start, value):
         total_refs[group][pl.ds(start, span), :] = value
 
-    add_source(source_ref, row_refs, cols_ref, put, span, own)
-
-
-def first_product(source, points, groups, span, gain, own):
-    samples = source.shape[1]
+    add_halves(half_refs, row_refs, cols_ref, put, span, True)
+
+
+def first_product(halves, points, groups, span, gain):
+    samples = halves[0].shape[1]
     rows = [len(places) * span for places in groups]
     out = pl.pallas_call(
-        lambda *refs: first_product_body(gain, span, own, groups, len(points), *refs),
+        lambda *refs: first_product_body(gain, span, groups, len(points), *refs),
         out_shape=[vmem((count, 64), BF16) for count in rows]
         + [vmem((count, samples), F32) for count in rows],
         scratch_shapes=[pltpu.VMEM((64, 4 * span), BF16)],
         cost_estimate=COST,
         compiler_params=PARAMS,
         name="first_product",
-    )(source, *points)
+    )(*halves, *points)
     return out[: len(groups)], out[len(groups) :]
 
 
-def product_body(span, source_count, count, *refs):
-    sources, refs = refs[:source_count], refs[source_count:]
+def product_body(span, half_count, count, *refs):
+    half_refs, refs = refs[:half_count], refs[half_count:]
     row_refs, old_refs, total_refs = refs[:count], refs[count : 2 * count], refs[2 * count : -1]
     cols_ref = refs[-1]
-    for number, source in enumerate(sources):
+    for number in range(0, half_count, 2):
 
         def put(group, start, value):
             place = pl.ds(start, span)
             base = old_refs if number == 0 else total_refs
             total_refs[group][place, :] = base[group][place, :] + value
 
-        add_source(source, row_refs, cols_ref, put, span, False)
-
-
-def product(sources, rows, totals, span):
+        add_halves(half_refs[number : number + 2], row_refs, cols_ref, put, span, False)
+
+
+def product(halves, rows, totals, span):
     return pl.pallas_call(
-        lambda *refs: product_body(span, len(sources), len(rows), *refs),
+        lambda *refs: product_body(span, len(halves), len(rows), *refs),
         out_shape=[vmem(total.shape, F32) for total in totals],
         scratch_shapes=[pltpu.VMEM((64, 4 * span), BF16)],
         cost_estimate=COST,
         compiler_params=PARAMS,
         name="product",
-    )(*sources, *rows, *totals)
-
-
-def halves_body(first_ref, second_ref, first_half, second_half):
-    rows = first_half.shape[0]
-    first_half[...] = first_ref[pl.ds(0, rows), :]
-    second_half[...] = second_ref[pl.ds(rows, rows), :]
-
-
-def halves(first, second, rows):
-    return pl.pallas_call(
-        halves_body,
-        out_shape=[vmem((rows, first.shape[1]), BF16)] * 2,
-        cost_estimate=COST,
-        compiler_params=PARAMS,
-        name="halves",
-    )(first, second)
+    )(*halves, *rows, *totals)
 
 
 def add_up_body(span, outs, mine_ref, theirs_ref, *refs):
@@ -491,7 +472,7 @@
     picks_ref, one_ref, two_ref, points_ref = refs
     rank, pool = picks_ref.shape[1:]
     leaf_count = counts[0]
-    tables = 4 * (span + 16)
+    tables = 2 * (span + 16)
     nodes = []
     for source_ref in (mine_ref, beside_ref):
         rows = source_ref[pl.ds(tables, source_ref.shape[0] - tables), :rank].astype(F32)
@@ -576,39 +557,34 @@
         return lax.ppermute(value, ("row", "col"), pairs)
 
     tables = (leaf_skeleton, skeleton_one, skeleton_two, skeleton_three)
-    packed, own_points = pack(probes, points, tables)
-    beside = swap(packed, 0, 1)
-    across = swap(packed, 2, 0)
+    first, second, own_points = pack(probes, points, tables)
+    beside_first, across_second = swap(first, 0, 1), swap(second, 2, 0)
     line = col_count // 2
-    line_points = [own_points] + [swap(own_points, 0, 2 * chunk) for chunk in range(1, line)]
-    sibling_points = swap(jnp.concatenate(line_points, axis=1), 1, 0)
+    line_points = own_points
+    for bit in range(1, col_count.bit_length() - 1):
+        line_points = jnp.concatenate([line_points, swap(line_points, 0, 1 << bit)], axis=1)
+        if bit == 1:
+            line_points, *late = lax.optimization_barrier((line_points, first, second))
+    beside_second, across_first = swap(late[1], 0, 1), swap(late[0], 2, 0)
+    line_points = [line_points, swap(line_points, 1, 0)]
     near, far = range(2), range(2, line)
-    feats, totals = first_product(
-        packed,
-        line_points,
-        [[(chunk, 0) for chunk in group] for group in (near, far)],
-        span,
-        gain,
-        True,
-    )
-    more = first_product(
-        packed,
-        [sibling_points],
-        [[(0, chunk * span) for chunk in group] for group in (near, far)],
-        span,
-        gain,
-        False,
-    )
-    feats, totals = [*feats, *more[0]], [*totals, *more[1]]
-    beside, across, *totals = lax.optimization_barrier((beside, across, *totals))
-    pieces = [packed, beside, across]
-    relayed = halves(beside, across, 2 * (span + 16))
-    diagonal = [swap(relayed[0], 2, 0), swap(relayed[1], 0, 1)]
-    picks, couplings_one, couplings_two, points_two = skeletons(packed, beside, tables, span, gain)
-    totals = product([beside], feats, totals, span)
-    totals = product([across], feats, totals, span)
-    points_two, *totals = lax.optimization_barrier((points_two, *totals))
-    pieces += diagonal
+    groups = [
+        [(core, chunk * span) for chunk in group] for core in range(2) for group in (near, far)
+    ]
+    feats, totals = first_product((first, second), line_points, groups, span, gain)
+    beside_first, across_second, *totals = lax.optimization_barrier(
+        (beside_first, across_second, *totals)
+    )
+    diagonal = [swap(beside_first, 2, 0), swap(across_second, 0, 1)]
+    picks, couplings_one, couplings_two, points_two = skeletons(
+        first, beside_first, tables, span, gain
+    )
+    beside_second, across_first, points_two, *totals = lax.optimization_barrier(
+        (beside_second, across_first, points_two, *totals)
+    )
+    totals = product([beside_first, beside_second], feats, totals, span)
+    totals = product([across_first, across_second], feats, totals, span)
+    pieces = [first, second, beside_first, beside_second, across_first, across_second, *diagonal]
     for bit in range(2, row_count.bit_length() - 1):
         more = [swap(value, 1 << bit, 0) for value in pieces]
         totals = product(more, feats, totals, span)
@@ -618,7 +594,7 @@
     (mine,) = product(diagonal, feats[1:2], totals[1:2], span)
     outs = [(range(0, line - 2, 2), F32), (range(1, line - 2, 2), BF16)]
     kept, sent = add_up(mine, from_sibling, outs, span)
-    sent, total = lax.optimization_barrier((sent, totals[2]))
+    sent, total, points_two = lax.optimization_barrier((sent, totals[2], points_two))
     arrived = swap(sent, 0, 2)
     (theirs,) = product(diagonal, feats[2:3], [total], span)
     from_sibling = swap(theirs, 1, 0)
@@ -644,7 +620,7 @@
     later = top_couplings(points_two, other_points, picks, gain)
 
     leaf_interp, interp_one, skeleton, reduced, sent = leaves(
-        own_sum, received, packed, picks, couplings_one, later, leaf_skeleton.shape[0]
+        own_sum, received, first, picks, couplings_one, later, leaf_skeleton.shape[0]
     )
     got = [swap(sent, 0, bits) for bits in (1, 2, 3)]
     upper_interp, top_state = upper_levels(

time: 64 us -> 64.1 us (level)
  starting transfers between devices: 21.2 us -> 22.3 us
    ppermute x17 -> x18, starting transfers between devices: 21.2 us -> 22.3 us  [swap(): return lax.ppermute(value, ('row', 'col'), pairs)]
    pallas_call x10 -> x8, Pallas kernels: 12.7 us -> 12 us  [the longest x6 8.22 us: product(): pl.pallas_call(lambda *refs: product_body(span, len(halves), len(rows), *...]
    ppermute x17 -> x18, waiting for transfers between devices: 15.4 us -> 15 us  [swap(): return lax.ppermute(value, ('row', 'col'), pairs)]
  transfers between devices with their start and end apart: 17 -> 18, of which waited for: 11 -> 8; matrix products, arithmetic and copies ran while one was open for 0% -> 0% of each run, Pallas kernels for 20% -> 19%
where the time goes in v5:
time: 64.1 us; the launch traced here: 64 us
  Pallas kernels  25.7 us (40%)
  starting transfers between devices  22.3 us (35%)
  waiting for transfers between devices  15 us (23%)
  between operations  0.95 us (1%)
    ppermute x18, starting transfers between devices, swap(): return lax.ppermute(value, ('row', 'col'), pairs)  22.3 us
    ppermute x18, waiting for transfers between devices, swap(): return lax.ppermute(value, ('row', 'col'), pairs)  15 us
    pallas_call x6, Pallas kernels, product(): pl.pallas_call(lambda *refs: product_body(span, len(halves), len(rows), *...  8.22 us
    pallas_call x1, Pallas kernels, upper_levels(): pl.pallas_call(lambda *refs: upper_body(picks.shape[0], *refs), out_shape...  5.94 us
    pallas_call x1, Pallas kernels, leaves(): pl.pallas_call(lambda *refs: leaves_body(len(others), *refs), out_shape=(...  5.59 us
    pallas_call x1, Pallas kernels, first_product(): pl.pallas_call(lambda *refs: first_product_body(gain, span, groups, len(p...  2.53 us
  transfers between devices with their start and end apart: 18, of which 8 were waited for; matrix products, arithmetic and copies ran while one was open for 0% of the time, Pallas kernels for 19%

profile of v5, /device:TPU:0, one launch (start us, length us, event | category | flops | bytes accessed | tf_op | source)
XLA Modules:
  0.0 64.0 jit_solution(13725010760707278533)
XLA Ops:
  0.6 1.3 %pack.1 = (bf16[560,256]{1,0:T(8,128)(2,1)S(1)}, bf16[544,256]{1,0:T(8,128)(2,1)S(1)}, bf16[16,256]{1,0:T(8,128)(2,1)S(1)}) custom-call(bf16[4,256,256]{2,1,0:T(8,128)(2,1)} %refs_0_.1, bf16[16,4,256]{2,1,0:T(4,128)(2,1)} %refs_1_.1, s32[2,64]{1,0:T(2,128)} %refs_2_.1, s32[1,64]{1,0:T(1,128)} %refs_3_.1, s32[4,64]{1,0:T(4,128)} %refs_4_.1, s32[2,64]{1,0:T(2,128)} %refs_5_.1), custom_call_target="tpu_custom_call" | custom-call | flops 1000000000 | tf_op jit(solution)/shard_map/pack/pallas_call | solution.py:118
  1.9 3.1 %collective-permute-start.2 = (bf16[16,256]{1,0:T(8,128)(2,1)S(1)}, bf16[16,256]{1,0:T(8,128)(2,1)S(1)}, u32[]{:S(2)}, u32[]{:S(2)}) collective-permute-start(bf16[16,256]{1,0:T(8,128)(2,1)S(1)} %get-tuple-element.60), channel_id=1, source_target_pairs={{0,2},{1,3},{2,0},{3,1},{4,6},{5,7},{6,4},{7,5},{8,10},{9,11},{10,... | collective-permute-start | bytes 24584 | tf_op jit(solution)/shard_map/ppermute | solution.py:557
  5.0 1.5 %collective-permute-start = (bf16[560,256]{1,0:T(8,128)(2,1)S(1)}, bf16[560,256]{1,0:T(8,128)(2,1)S(1)}, u32[]{:S(2)}, u32[]{:S(2)}) collective-permute-start(bf16[560,256]{1,0:T(8,128)(2,1)S(1)} %get-tuple-element.70.refs_0_.refs_3_), channel_id=1, source_target_pairs={{0,1},{1,0},{2,3},{3,2},{4,5},{5,4},{6,7},{7,6},{8,9},{9,8},{10,11... | collective-permute-start | bytes 860168 | tf_op jit(solution)/shard_map/ppermute | solution.py:557
  6.5 1.5 %collective-permute-start.1 = (bf16[544,256]{1,0:T(8,128)(2,1)S(1)}, bf16[544,256]{1,0:T(8,128)(2,1)S(1)}, u32[]{:S(2)}, u32[]{:S(2)}) collective-permute-start(bf16[544,256]{1,0:T(8,128)(2,1)S(1)} %get-tuple-element.69.refs_1_), channel_id=1, source_target_pairs={{0,16},{1,17},{2,18},{3,19},{4,20},{5,21},{6,22},{7,23},{8,24},{9,... | collective-permute-start | bytes 835592 | tf_op jit(solution)/shard_map/ppermute | solution.py:557
  8.0 0.0 collective-permute-done.2
  8.0 2.6 %collective-permute-start.3 = (bf16[16,512]{1,0:T(8,128)(2,1)S(1)}, bf16[16,512]{1,0:T(8,128)(2,1)S(1)}, u32[]{:S(2)}, u32[]{:S(2)}) collective-permute-start(bf16[16,512]{1,0:T(8,128)(2,1)S(1)} %pad_maximum_fusion), channel_id=1, source_target_pairs={{0,4},{1,5},{2,6},{3,7},{4,0},{5,1},{6,2},{7,3},{8,12},{9,13},{10,... | collective-permute-start | bytes 49160 | tf_op jit(solution)/shard_map/ppermute | solution.py:557
  10.6 0.6 collective-permute-start.8
  11.2 1.5 %collective-permute-start.7 = (bf16[544,256]{1,0:T(8,128)(2,1)S(1)}, bf16[544,256]{1,0:T(8,128)(2,1)S(1)}, u32[]{:S(2)}, u32[]{:S(2)}) collective-permute-start(bf16[544,256]{1,0:T(8,128)(2,1)S(1)} %get-tuple-element.69.refs_1_), channel_id=1, source_target_pairs={{0,1},{1,0},{2,3},{3,2},{4,5},{5,4},{6,7},{7,6},{8,9},{9,8},{10,11... | collective-permute-start | bytes 835592 | tf_op jit(solution)/shard_map/ppermute | solution.py:557
  12.7 0.0 collective-permute-done.3
  12.7 0.0 collective-permute-start.4
  12.7 1.2 %collective-permute-done.4.refs_3_ = bf16[16,1024]{1,0:T(8,128)(2,1)S(1)} collective-permute-done((bf16[16,1024]{1,0:T(8,128)(2,1)S(1)}, bf16[16,1024]{1,0:T(8,128)(2,1)S(1)}, u32[]{:S(2)}, u32[]{:S(2)}) %collective-permute-start.4) | collective-permute-done | bytes 32800 | tf_op jit(solution)/shard_map/ppermute | solution.py:557
  13.9 2.5 %first_product.1 = (bf16[512,64]{1,0:T(8,128)(2,1)S(1)}, bf16[512,64]{1,0:T(8,128)(2,1)S(1)}, bf16[512,64]{1,0:T(8,128)(2,1)S(1)}, bf16[512,64]{1,0:T(8,128)(2,1...) custom-call(bf16[560,256]{1,0:T(8,128)(2,1)S(1)} %get-tuple-element.70, ...), custom_call_target="tpu_custom_call" | custom-call | flops 1000000000 | tf_op jit(solution)/shard_map/first_product/pallas_call | solution.py:179
  16.4 0.0 collective-permute-done.1.refs_1_
  16.4 0.0 collective-permute-done.refs_1_.refs_0_
  16.4 1.2 %collective-permute-start.5 = (bf16[560,256]{1,0:T(8,128)(2,1)S(1)}, bf16[560,256]{1,0:T(8,128)(2,1)S(1)}, u32[]{:S(2)}, u32[]{:S(2)}) collective-permute-start(bf16[560,256]{1,0:T(8,128)(2,1)S(1)} %collective-permute-done.refs_1_.refs_0_), channel_id=1, source_target_pairs={{0,16},{1,17},{2,18},{3,19},{4,20},{5,21},{6,22},{7,23},{8,24},{9,... | collective-permute-start | bytes 860168 | tf_op jit(solution)/shard_map/ppermute | solution.py:557
  17.6 0.9 %collective-permute-start.6 = (bf16[544,256]{1,0:T(8,128)(2,1)S(1)}, bf16[544,256]{1,0:T(8,128)(2,1)S(1)}, u32[]{:S(2)}, u32[]{:S(2)}) collective-permute-start(bf16[544,256]{1,0:T(8,128)(2,1)S(1)} %collective-permute-done.1.refs_1_), channel_id=1, source_target_pairs={{0,1},{1,0},{2,3},{3,2},{4,5},{5,4},{6,7},{7,6},{8,9},{9,8},{10,11... | collective-permute-start | bytes 835592 | tf_op jit(solution)/shard_map/ppermute | solution.py:557
  18.5 1.2 %skeletons.1 = (bf16[6,64,128]{2,1,0:T(8,128)(2,1)S(1)}, bf16[192,768]{1,0:T(8,128)(2,1)S(1)}, bf16[192,768]{1,0:T(8,128)(2,1)S(1)}, bf16[16,128]{1,0:T(8,128)(2,1)S(1)}) custom-call(bf16[560,256]{1,0:T(8,128)(2,1)S(1)} %get-tuple-element.70.refs_0_.refs_3_, bf16[560,256]{1,0:T(8,128)(2,1)S(1)} %collective-permute-done.refs_1_.refs_0_), custom_call_target="tpu_custom_call" | custom-call | flops 1000000000 | tf_op jit(solution)/shard_map/skeletons/pallas_call | solution.py:509
  19.7 0.0 collective-permute-done.7.refs_1_
  19.7 1.9 %collective-permute-done.8.refs_0_ = bf16[560,256]{1,0:T(8,128)(2,1)S(1)} collective-permute-done((bf16[560,256]{1,0:T(8,128)(2,1)S(1)}, bf16[560,256]{1,0:T(8,128)(2,1)S(1)}, u32[]{:S(2)}, u32[]{:S(2)}) %collective-permute-start.8) | collective-permute-done | bytes 286752 | tf_op jit(solution)/shard_map/ppermute | solution.py:557
  21.6 2.5 %product.6 = (f32[512,256]{1,0:T(8,128)S(1)}, f32[512,256]{1,0:T(8,128)S(1)}, f32[512,256]{1,0:T(8,128)S(1)}, f32[512,256]{1,0:T(8,128)S(1)}) custom-call(bf16[560,256]{1,0:T(8,128)(2,1)S(1)} %collective-permute-done.refs_1_.refs_0_, bf16[544,256]{1,0:T(8,128)(2,1)S(1)} %collective-permute-done.7.refs_1_, bf16[512,64]{1,0:T(8,128)(2,1)S(1)} %get-tuple-element.68.refs_2_, ...), custom_call_target="tpu_custom_call" | custom-call | flops 1000000000 | tf_op jit(solution)/shard_map/product/pallas_call | solution.py:206
  24.1 2.5 %product.7 = (f32[512,256]{1,0:T(8,128)S(1)}, f32[512,256]{1,0:T(8,128)S(1)}, f32[512,256]{1,0:T(8,128)S(1)}, f32[512,256]{1,0:T(8,128)S(1)}) custom-call(bf16[560,256]{1,0:T(8,128)(2,1)S(1)} %collective-permute-done.8.refs_0_, bf16[544,256]{1,0:T(8,128)(2,1)S(1)} %collective-permute-done.1.refs_1_, bf16[512,64]{1,0:T(8,128)(2,1)S(1)} %get-tuple-element.68.refs_2_, ...), custom_call_target="tpu_custom_call" | custom-call | flops 1000000000 | tf_op jit(solution)/shard_map/product/pallas_call | solution.py:206
  26.5 0.0 collective-permute-done.6.refs_1_
  26.6 0.0 collective-permute-done.5.refs_0_
  26.6 0.8 %product.10 = f32[512,256]{1,0:T(8,128)S(1)} custom-call(bf16[560,256]{1,0:T(8,128)(2,1)S(1)} %collective-permute-done.5.refs_0_, bf16[544,256]{1,0:T(8,128)(2,1)S(1)} %collective-permute-done.6.refs_1_, bf16[512,64]{1,0:T(8,128)(2,1)S(1)} %get-tuple-element.79.refs_5_.refs_2_, f32[512,256]{1,0:T(8,128)S(1)} %get-tuple-element.91.refs_3_), custom_call_target="tpu_custom_call" | custom-call | flops 1000000000 | tf_op jit(solution)/shard_map/product/pallas_call | solution.py:206
  27.4 0.1 collective-permute-start.9
  27.5 0.8 %product.9.refs_0_ = f32[512,256]{1,0:T(8,128)S(1)} custom-call(bf16[560,256]{1,0:T(8,128)(2,1)S(1)} %collective-permute-done.5.refs_0_, bf16[544,256]{1,0:T(8,128)(2,1)S(1)} %collective-permute-done.6.refs_1_, bf16[512,64]{1,0:T(8,128)(2,1)S(1)} %get-tuple-element.77.refs_3_.refs_2_, f32[512,256]{1,0:T(8,128)S(1)} %get-tuple-element.90.refs_3_), custom_call_target="tpu_custom_call" | custom-call | flops 1000000000 | tf_op jit(solution)/shard_map/product/pallas_call | solution.py:206
  28.3 1.1 %collective-permute-done.9.refs_1_ = f32[512,256]{1,0:T(8,128)S(1)} collective-permute-done((f32[512,256]{1,0:T(8,128)S(1)}, f32[512,256]{1,0:T(8,128)S(1)}, u32[]{:S(2)}, u32[]{:S(2)}) %collective-permute-start.9) | collective-permute-done | bytes 524320 | tf_op jit(solution)/shard_map/ppermute | solution.py:557
  29.4 0.1 add_up.3
  29.5 0.5 collective-permute-start.11
  30.0 0.8 %product.8.refs_0_ = f32[512,256]{1,0:T(8,128)S(1)} custom-call(bf16[560,256]{1,0:T(8,128)(2,1)S(1)} %collective-permute-done.5.refs_0_, bf16[544,256]{1,0:T(8,128)(2,1)S(1)} %collective-permute-done.6.refs_1_, bf16[512,64]{1,0:T(8,128)(2,1)S(1)} %get-tuple-element.68.refs_2_, f32[512,256]{1,0:T(8,128)S(1)} %get-tuple-element.89.refs_3_), custom_call_target="tpu_custom_call" | custom-call | flops 1000000000 | tf_op jit(solution)/shard_map/product/pallas_call | solution.py:206
  30.8 1.6 %collective-permute-start.12 = (bf16[16,128]{1,0:T(8,128)(2,1)S(1)}, bf16[16,128]{1,0:T(8,128)(2,1)S(1)}, u32[]{:S(2)}, u32[]{:S(2)}) collective-permute-start(bf16[16,128]{1,0:T(8,128)(2,1)S(1)} %get-tuple-element.98.refs_0_), channel_id=1, source_target_pairs={{0,2},{1,3},{2,0},{3,1},{4,6},{5,7},{6,4},{7,5},{8,10},{9,11},{10,... | collective-permute-start | bytes 12296 | tf_op jit(solution)/shard_map/ppermute | solution.py:557
  32.4 0.8 %product.11 = f32[512,256]{1,0:T(8,128)S(1)} custom-call(bf16[560,256]{1,0:T(8,128)(2,1)S(1)} %collective-permute-done.5.refs_0_, bf16[544,256]{1,0:T(8,128)(2,1)S(1)} %collective-permute-done.6.refs_1_, bf16[512,64]{1,0:T(8,128)(2,1)S(1)} %get-tuple-element.78.refs_4_.refs_2_, f32[512,256]{1,0:T(8,128)S(1)} %get-tuple-element.95.refs_3_), custom_call_target="tpu_custom_call" | custom-call | flops 1000000000 | tf_op jit(solution)/shard_map/product/pallas_call | solution.py:206
  33.3 0.1 collective-permute-start.10
  33.3 1.8 %collective-permute-done.12.refs_2_.refs_1_ = bf16[16,128]{1,0:T(8,128)(2,1)S(1)} collective-permute-done((bf16[16,128]{1,0:T(8,128)(2,1)S(1)}, bf16[16,128]{1,0:T(8,128)(2,1)S(1)}, u32[]{:S(2)}, u32[]{:S(2)}) %collective-permute-start.12) | collective-permute-done | bytes 4128 | tf_op jit(solution)/shard_map/ppermute | solution.py:557
  35.1 0.0 collective-permute-done.11.refs_1_
  35.2 2.7 %collective-permute-start.13 = (bf16[256,256]{1,0:T(8,128)(2,1)S(1)}, bf16[256,256]{1,0:T(8,128)(2,1)S(1)}, u32[]{:S(2)}, u32[]{:S(2)}) collective-permute-start(bf16[256,256]{1,0:T(8,128)(2,1)S(1)} %add_up.4.refs_2_), channel_id=1, source_target_pairs={{0,4},{1,5},{2,6},{3,7},{4,0},{5,1},{6,2},{7,3},{8,12},{9,13},{10,... | collective-permute-start | bytes 393224 | tf_op jit(solution)/shard_map/ppermute | solution.py:557
  37.8 0.0 collective-permute-done.10.refs_1_
  37.9 0.1 add_up.5
  37.9 1.0 %collective-permute-start.14 = (bf16[256,256]{1,0:T(8,128)(2,1)S(1)}, bf16[256,256]{1,0:T(8,128)(2,1)S(1)}, u32[]{:S(2)}, u32[]{:S(2)}) collective-permute-start(bf16[256,256]{1,0:T(8,128)(2,1)S(1)} %get-tuple-element.100), channel_id=1, source_target_pairs={{0,2},{1,3},{2,0},{3,1},{4,6},{5,7},{6,4},{7,5},{8,10},{9,11},{10,... | collective-permute-start | bytes 393224 | tf_op jit(solution)/shard_map/ppermute | solution.py:557
  38.9 0.9 %top_couplings.1 = (bf16[192,768]{1,0:T(8,128)(2,1)S(1)}, bf16[192,768]{1,0:T(8,128)(2,1)S(1)}) custom-call(bf16[16,128]{1,0:T(8,128)(2,1)S(1)} %get-tuple-element.98.refs_0_, bf16[16,128]{1,0:T(8,128)(2,1)S(1)} %collective-permute-done.12.refs_2_.refs_1_, bf16[6,64,128]{2,1,0:T(8,128)(2,1)S(1)} %get-tuple-element.101.refs_2_.refs_4_.refs_5_), custom_call_target="tpu_custom_call" | custom-call | flops 1000000000 | tf_op jit(solution)/shard_map/top_couplings/pallas_call | solution.py:536
  39.7 4.0 %collective-permute-done.13.refs_1_ = bf16[256,256]{1,0:T(8,128)(2,1)S(1)} collective-permute-done((bf16[256,256]{1,0:T(8,128)(2,1)S(1)}, bf16[256,256]{1,0:T(8,128)(2,1)S(1)}, u32[]{:S(2)}, u32[]{:S(2)}) %collective-permute-start.13) | collective-permute-done | bytes 131104 | tf_op jit(solution)/shard_map/ppermute | solution.py:557
  43.7 1.3 %collective-permute-done.14.refs_2_ = bf16[256,256]{1,0:T(8,128)(2,1)S(1)} collective-permute-done((bf16[256,256]{1,0:T(8,128)(2,1)S(1)}, bf16[256,256]{1,0:T(8,128)(2,1)S(1)}, u32[]{:S(2)}, u32[]{:S(2)}) %collective-permute-start.14) | collective-permute-done | bytes 131104 | tf_op jit(solution)/shard_map/ppermute | solution.py:557
  45.0 5.6 %leaves.1 = (f32[2,64,128]{2,1,0:T(8,128)}, f32[64,128]{1,0:T(8,128)S(1)}, f32[64,256]{1,0:T(8,128)S(1)}, f32[64,256]{1,0:T(8,128)S(1)}, bf16[192,256]{1,0:T(8,128)(2,1)S(1)}) custom-call(f32[256,256]{1,0:T(8,128)S(1)} %get-tuple-element.99.refs_0_, bf16[256,256]{1,0:T(8,128)(2,1)S(1)} %collective-permute-done.13.refs_1_, ...), custom_call_target="tpu_custom_call" | custom-call | flops 1000000000 | tf_op jit(solution)/shard_map/leaves/pallas_call | solution.py:356
  50.6 0.1 collective-permute-start.15
  50.7 1.1 %collective-permute-start.16 = (bf16[192,256]{1,0:T(8,128)(2,1)S(1)}, bf16[192,256]{1,0:T(8,128)(2,1)S(1)}, u32[]{:S(2)}, u32[]{:S(2)}) collective-permute-start(bf16[192,256]{1,0:T(8,128)(2,1)S(1)} %get-tuple-element.108), channel_id=1, source_target_pairs={{0,2},{1,3},{2,0},{3,1},{4,6},{5,7},{6,4},{7,5},{8,10},{9,11},{10,... | collective-permute-start | bytes 294920 | tf_op jit(solution)/shard_map/ppermute | solution.py:557
  51.8 2.4 %collective-permute-start.17 = (bf16[192,256]{1,0:T(8,128)(2,1)S(1)}, bf16[192,256]{1,0:T(8,128)(2,1)S(1)}, u32[]{:S(2)}, u32[]{:S(2)}) collective-permute-start(bf16[192,256]{1,0:T(8,128)(2,1)S(1)} %get-tuple-element.108), channel_id=1, source_target_pairs={{0,3},{1,2},{2,1},{3,0},{4,7},{5,6},{6,5},{7,4},{8,11},{9,10},{10,... | collective-permute-start | bytes 294920 | tf_op jit(solution)/shard_map/ppermute | solution.py:557
  54.1 2.2 %collective-permute-done.15.refs_2_ = bf16[192,256]{1,0:T(8,128)(2,1)S(1)} collective-permute-done((bf16[192,256]{1,0:T(8,128)(2,1)S(1)}, bf16[192,256]{1,0:T(8,128)(2,1)S(1)}, u32[]{:S(2)}, u32[]{:S(2)}) %collective-permute-start.15) | collective-permute-done | bytes 98336 | tf_op jit(solution)/shard_map/ppermute | solution.py:557
  56.3 0.0 collective-permute-done.16.refs_3_
  56.3 1.5 %collective-permute-done.17.refs_4_ = bf16[192,256]{1,0:T(8,128)(2,1)S(1)} collective-permute-done((bf16[192,256]{1,0:T(8,128)(2,1)S(1)}, bf16[192,256]{1,0:T(8,128)(2,1)S(1)}, u32[]{:S(2)}, u32[]{:S(2)}) %collective-permute-start.17) | collective-permute-done | bytes 98336 | tf_op jit(solution)/shard_map/ppermute | solution.py:557
  57.9 5.9 %upper_levels.1 = (f32[3,1,64,128]{3,2,1,0:T(8,128)}, f32[2,1,64,256]{3,2,1,0:T(8,128)}) custom-call(f32[64,256]{1,0:T(8,128)S(1)} %get-tuple-element.106.refs_0_, f32[64,256]{1,0:T(8,128)S(1)} %get-tuple-element.107.refs_1_, bf16[192,256]{1,0:T(8,128)(2,1)S(1)} %collective-permute-done.15.refs_2_, bf16[192,256]{1,0:T(8,128)(2,1)S(1)} %collective-permute-done.16.refs_3_, ...), custom_call_target="tpu_custom_call" | custom-call | flops 1000000000 | tf_op jit(solution)/shard_map/upper_levels/pallas_call | solution.py:432
  (4 shorter events, 0.0 us)
Async XLA Ops:
  1.9 6.1 %collective-permute-start.2 = (bf16[16,256]{1,0:T(8,128)(2,1)S(1)}, bf16[16,256]{1,0:T(8,128)(2,1)S(1)}, u32[]{:S(2)}, u32[]{:S(2)}) collective-permute-start(bf16[16,256]{1,0:T(8,128)(2,1)S(1)} %get-tuple-element.60), channel_id=1, source_target_pairs={{0,2},{1,3},{2,0},{3,1},{4,6},{5,7},{6,4},{7,5},{8,10},{9,11},{10,... | collective-permute-start | bytes 24584 | tf_op jit(solution)/shard_map/ppermute | solution.py:557
  5.0 11.4 %collective-permute-start = (bf16[560,256]{1,0:T(8,128)(2,1)S(1)}, bf16[560,256]{1,0:T(8,128)(2,1)S(1)}, u32[]{:S(2)}, u32[]{:S(2)}) collective-permute-start(bf16[560,256]{1,0:T(8,128)(2,1)S(1)} %get-tuple-element.70.refs_0_.refs_3_), channel_id=1, source_target_pairs={{0,1},{1,0},{2,3},{3,2},{4,5},{5,4},{6,7},{7,6},{8,9},{9,8},{10,11... | collective-permute-start | bytes 860168 | tf_op jit(solution)/shard_map/ppermute | solution.py:557
  6.5 9.9 %collective-permute-start.1 = (bf16[544,256]{1,0:T(8,128)(2,1)S(1)}, bf16[544,256]{1,0:T(8,128)(2,1)S(1)}, u32[]{:S(2)}, u32[]{:S(2)}) collective-permute-start(bf16[544,256]{1,0:T(8,128)(2,1)S(1)} %get-tuple-element.69.refs_1_), channel_id=1, source_target_pairs={{0,16},{1,17},{2,18},{3,19},{4,20},{5,21},{6,22},{7,23},{8,24},{9,... | collective-permute-start | bytes 835592 | tf_op jit(solution)/shard_map/ppermute | solution.py:557
  8.0 4.7 %collective-permute-start.3 = (bf16[16,512]{1,0:T(8,128)(2,1)S(1)}, bf16[16,512]{1,0:T(8,128)(2,1)S(1)}, u32[]{:S(2)}, u32[]{:S(2)}) collective-permute-start(bf16[16,512]{1,0:T(8,128)(2,1)S(1)} %pad_maximum_fusion), channel_id=1, source_target_pairs={{0,4},{1,5},{2,6},{3,7},{4,0},{5,1},{6,2},{7,3},{8,12},{9,13},{10,... | collective-permute-start | bytes 49160 | tf_op jit(solution)/shard_map/ppermute | solution.py:557
  10.6 11.0 %collective-permute-start.8 = (bf16[560,256]{1,0:T(8,128)(2,1)S(1)}, bf16[560,256]{1,0:T(8,128)(2,1)S(1)}, u32[]{:S(2)}, u32[]{:S(2)}) collective-permute-start(bf16[560,256]{1,0:T(8,128)(2,1)S(1)} %get-tuple-element.70.refs_0_.refs_3_), channel_id=1, source_target_pairs={{0,16},{1,17},{2,18},{3,19},{4,20},{5,21},{6,22},{7,23},{8,24},{9,... | collective-permute-start | bytes 860168 | tf_op jit(solution)/shard_map/ppermute | solution.py:557
  11.2 8.5 %collective-permute-start.7 = (bf16[544,256]{1,0:T(8,128)(2,1)S(1)}, bf16[544,256]{1,0:T(8,128)(2,1)S(1)}, u32[]{:S(2)}, u32[]{:S(2)}) collective-permute-start(bf16[544,256]{1,0:T(8,128)(2,1)S(1)} %get-tuple-element.69.refs_1_), channel_id=1, source_target_pairs={{0,1},{1,0},{2,3},{3,2},{4,5},{5,4},{6,7},{7,6},{8,9},{9,8},{10,11... | collective-permute-start | bytes 835592 | tf_op jit(solution)/shard_map/ppermute | solution.py:557
  12.7 1.2 %collective-permute-start.4 = (bf16[16,1024]{1,0:T(8,128)(2,1)S(1)}, bf16[16,1024]{1,0:T(8,128)(2,1)S(1)}, u32[]{:S(2)}, u32[]{:S(2)}) collective-permute-start(bf16[16,1024]{1,0:T(8,128)(2,1)S(1)} %constant_dynamic-update-slice_fusion.refs_2_), channel_id=1, source_target_pairs={{0,8},{1,9},{2,10},{3,11},{4,12},{5,13},{6,14},{7,15},{8,0},{9,1},... | collective-permute-start | bytes 98312 | tf_op jit(solution)/shard_map/ppermute | solution.py:557
  16.4 10.2 %collective-permute-start.5 = (bf16[560,256]{1,0:T(8,128)(2,1)S(1)}, bf16[560,256]{1,0:T(8,128)(2,1)S(1)}, u32[]{:S(2)}, u32[]{:S(2)}) collective-permute-start(bf16[560,256]{1,0:T(8,128)(2,1)S(1)} %collective-permute-done.refs_1_.refs_0_), channel_id=1, source_target_pairs={{0,16},{1,17},{2,18},{3,19},{4,20},{5,21},{6,22},{7,23},{8,24},{9,... | collective-permute-start | bytes 860168 | tf_op jit(solution)/shard_map/ppermute | solution.py:557
  17.6 8.9 %collective-permute-start.6 = (bf16[544,256]{1,0:T(8,128)(2,1)S(1)}, bf16[544,256]{1,0:T(8,128)(2,1)S(1)}, u32[]{:S(2)}, u32[]{:S(2)}) collective-permute-start(bf16[544,256]{1,0:T(8,128)(2,1)S(1)} %collective-permute-done.1.refs_1_), channel_id=1, source_target_pairs={{0,1},{1,0},{2,3},{3,2},{4,5},{5,4},{6,7},{7,6},{8,9},{9,8},{10,11... | collective-permute-start | bytes 835592 | tf_op jit(solution)/shard_map/ppermute | solution.py:557
  27.4 2.0 %collective-permute-start.9 = (f32[512,256]{1,0:T(8,128)S(1)}, f32[512,256]{1,0:T(8,128)S(1)}, u32[]{:S(2)}, u32[]{:S(2)}) collective-permute-start(f32[512,256]{1,0:T(8,128)S(1)} %product.10), channel_id=1, source_target_pairs={{0,8},{1,9},{2,10},{3,11},{4,12},{5,13},{6,14},{7,15},{8,0},{9,1},... | collective-permute-start | bytes 1572872 | tf_op jit(solution)/shard_map/ppermute | solution.py:557
  29.5 5.7 %collective-permute-start.11 = (bf16[256,256]{1,0:T(8,128)(2,1)S(1)}, bf16[256,256]{1,0:T(8,128)(2,1)S(1)}, u32[]{:S(2)}, u32[]{:S(2)}) collective-permute-start(bf16[256,256]{1,0:T(8,128)(2,1)S(1)} %get-tuple-element.97), channel_id=1, source_target_pairs={{0,2},{1,3},{2,0},{3,1},{4,6},{5,7},{6,4},{7,5},{8,10},{9,11},{10,... | collective-permute-start | bytes 393224 | tf_op jit(solution)/shard_map/ppermute | solution.py:557
  30.8 4.3 %collective-permute-start.12 = (bf16[16,128]{1,0:T(8,128)(2,1)S(1)}, bf16[16,128]{1,0:T(8,128)(2,1)S(1)}, u32[]{:S(2)}, u32[]{:S(2)}) collective-permute-start(bf16[16,128]{1,0:T(8,128)(2,1)S(1)} %get-tuple-element.98.refs_0_), channel_id=1, source_target_pairs={{0,2},{1,3},{2,0},{3,1},{4,6},{5,7},{6,4},{7,5},{8,10},{9,11},{10,... | collective-permute-start | bytes 12296 | tf_op jit(solution)/shard_map/ppermute | solution.py:557
  33.3 4.6 %collective-permute-start.10 = (f32[512,256]{1,0:T(8,128)S(1)}, f32[512,256]{1,0:T(8,128)S(1)}, u32[]{:S(2)}, u32[]{:S(2)}) collective-permute-start(f32[512,256]{1,0:T(8,128)S(1)} %product.11), channel_id=1, source_target_pairs={{0,8},{1,9},{2,10},{3,11},{4,12},{5,13},{6,14},{7,15},{8,0},{9,1},... | collective-permute-start | bytes 1572872 | tf_op jit(solution)/shard_map/ppermute | solution.py:557
  35.2 8.5 %collective-permute-start.13 = (bf16[256,256]{1,0:T(8,128)(2,1)S(1)}, bf16[256,256]{1,0:T(8,128)(2,1)S(1)}, u32[]{:S(2)}, u32[]{:S(2)}) collective-permute-start(bf16[256,256]{1,0:T(8,128)(2,1)S(1)} %add_up.4.refs_2_), channel_id=1, source_target_pairs={{0,4},{1,5},{2,6},{3,7},{4,0},{5,1},{6,2},{7,3},{8,12},{9,13},{10,... | collective-permute-start | bytes 393224 | tf_op jit(solution)/shard_map/ppermute | solution.py:557
  37.9 7.1 %collective-permute-start.14 = (bf16[256,256]{1,0:T(8,128)(2,1)S(1)}, bf16[256,256]{1,0:T(8,128)(2,1)S(1)}, u32[]{:S(2)}, u32[]{:S(2)}) collective-permute-start(bf16[256,256]{1,0:T(8,128)(2,1)S(1)} %get-tuple-element.100), channel_id=1, source_target_pairs={{0,2},{1,3},{2,0},{3,1},{4,6},{5,7},{6,4},{7,5},{8,10},{9,11},{10,... | collective-permute-start | bytes 393224 | tf_op jit(solution)/shard_map/ppermute | solution.py:557
  50.6 5.7 %collective-permute-start.15 = (bf16[192,256]{1,0:T(8,128)(2,1)S(1)}, bf16[192,256]{1,0:T(8,128)(2,1)S(1)}, u32[]{:S(2)}, u32[]{:S(2)}) collective-permute-start(bf16[192,256]{1,0:T(8,128)(2,1)S(1)} %get-tuple-element.108), channel_id=1, source_target_pairs={{0,1},{1,0},{2,3},{3,2},{4,5},{5,4},{6,7},{7,6},{8,9},{9,8},{10,11... | collective-permute-start | bytes 294920 | tf_op jit(solution)/shard_map/ppermute | solution.py:557
  50.7 5.7 %collective-permute-start.16 = (bf16[192,256]{1,0:T(8,128)(2,1)S(1)}, bf16[192,256]{1,0:T(8,128)(2,1)S(1)}, u32[]{:S(2)}, u32[]{:S(2)}) collective-permute-start(bf16[192,256]{1,0:T(8,128)(2,1)S(1)} %get-tuple-element.108), channel_id=1, source_target_pairs={{0,2},{1,3},{2,0},{3,1},{4,6},{5,7},{6,4},{7,5},{8,10},{9,11},{10,... | collective-permute-start | bytes 294920 | tf_op jit(solution)/shard_map/ppermute | solution.py:557
  51.8 6.1 %collective-permute-start.17 = (bf16[192,256]{1,0:T(8,128)(2,1)S(1)}, bf16[192,256]{1,0:T(8,128)(2,1)S(1)}, u32[]{:S(2)}, u32[]{:S(2)}) collective-permute-start(bf16[192,256]{1,0:T(8,128)(2,1)S(1)} %get-tuple-element.108), channel_id=1, source_target_pairs={{0,3},{1,2},{2,1},{3,0},{4,7},{5,6},{6,5},{7,4},{8,11},{9,10},{10,... | collective-permute-start | bytes 294920 | tf_op jit(solution)/shard_map/ppermute | solution.py:557

commit v6 on v5

--- a/solution.py
+++ b/solution.py
@@ -589,17 +589,18 @@
         more = [swap(value, 1 << bit, 0) for value in pieces]
         totals = product(more, feats, totals, span)
         pieces += more
+    other_points = swap(points_two, 0, 2)
+    other_points, *totals = lax.optimization_barrier((other_points, *totals))
     (theirs,) = product(diagonal, feats[3:], totals[3:], span)
     from_sibling = swap(theirs, 1, 0)
     (mine,) = product(diagonal, feats[1:2], totals[1:2], span)
     outs = [(range(0, line - 2, 2), F32), (range(1, line - 2, 2), BF16)]
     kept, sent = add_up(mine, from_sibling, outs, span)
-    sent, total, points_two = lax.optimization_barrier((sent, totals[2], points_two))
+    sent, total = lax.optimization_barrier((sent, totals[2]))
     arrived = swap(sent, 0, 2)
     (theirs,) = product(diagonal, feats[2:3], [total], span)
     from_sibling = swap(theirs, 1, 0)
     (mine,) = product(diagonal, feats[:1], totals[:1], span)
-    other_points = swap(points_two, 0, 2)
     received = []
     chunks = list(range(2, line, 2))
     bit = 2
@@ -607,7 +608,7 @@
         sent_places = [pos for pos, chunk in enumerate(chunks) if chunk & bit]
         kept_places = [pos for pos, chunk in enumerate(chunks) if not chunk & bit]
         outs = [(sent_places, BF16)] + [(kept_places, F32)] * (len(kept_places) > 0)
-        sent, *kept = add_up(kept, arrived, outs, span, (other_points,), LONG)
+        sent, *kept = add_up(kept, arrived, outs, span, cost=LONG)
         arrived = swap(sent, 0, 2 * bit)
         received.append(arrived[:span] if len(sent_places) > 1 else arrived)
         if kept:

time: 64.1 us -> 63.9 us (level)
  waiting for transfers between devices: 15 us -> 13.9 us
  starting transfers between devices: 22.3 us -> 23.1 us
    ppermute x18, waiting for transfers between devices: 15 us -> 13.9 us  [swap(): return lax.ppermute(value, ('row', 'col'), pairs)]
    ppermute x18, starting transfers between devices: 22.3 us -> 23.1 us  [swap(): return lax.ppermute(value, ('row', 'col'), pairs)]
where the time goes in v6:
time: 63.9 us; the launch traced here: 63.7 us
  Pallas kernels  25.7 us (40%)
  starting transfers between devices  23.1 us (36%)
  waiting for transfers between devices  13.9 us (22%)
  between operations  0.94 us (1%)
    ppermute x18, starting transfers between devices, swap(): return lax.ppermute(value, ('row', 'col'), pairs)  23.1 us
    ppermute x18, waiting for transfers between devices, swap(): return lax.ppermute(value, ('row', 'col'), pairs)  13.9 us
    pallas_call x6, Pallas kernels, product(): pl.pallas_call(lambda *refs: product_body(span, len(halves), len(rows), *...  8.23 us
    pallas_call x1, Pallas kernels, upper_levels(): pl.pallas_call(lambda *refs: upper_body(picks.shape[0], *refs), out_shape...  5.94 us
    pallas_call x1, Pallas kernels, leaves(): pl.pallas_call(lambda *refs: leaves_body(len(others), *refs), out_shape=(...  5.59 us
    pallas_call x1, Pallas kernels, first_product(): pl.pallas_call(lambda *refs: first_product_body(gain, span, groups, len(p...  2.53 us
  transfers between devices with their start and end apart: 18, of which 8 were waited for; matrix products, arithmetic and copies ran while one was open for 0% of the time, Pallas kernels for 19%

profile of v6, /device:TPU:0, one launch (start us, length us, event | category | flops | bytes accessed | tf_op | source)
XLA Modules:
  0.0 63.7 jit_solution(1104410653708642055)
XLA Ops:
  0.6 1.3 %pack.1 = (bf16[560,256]{1,0:T(8,128)(2,1)S(1)}, bf16[544,256]{1,0:T(8,128)(2,1)S(1)}, bf16[16,256]{1,0:T(8,128)(2,1)S(1)}) custom-call(bf16[4,256,256]{2,1,0:T(8,128)(2,1)} %refs_0_.1, bf16[16,4,256]{2,1,0:T(4,128)(2,1)} %refs_1_.1, s32[2,64]{1,0:T(2,128)} %refs_2_.1, s32[1,64]{1,0:T(1,128)} %refs_3_.1, s32[4,64]{1,0:T(4,128)} %refs_4_.1, s32[2,64]{1,0:T(2,128)} %refs_5_.1), custom_call_target="tpu_custom_call" | custom-call | flops 1000000000 | tf_op jit(solution)/shard_map/pack/pallas_call | solution.py:118
  1.9 3.1 %collective-permute-start.2 = (bf16[16,256]{1,0:T(8,128)(2,1)S(1)}, bf16[16,256]{1,0:T(8,128)(2,1)S(1)}, u32[]{:S(2)}, u32[]{:S(2)}) collective-permute-start(bf16[16,256]{1,0:T(8,128)(2,1)S(1)} %get-tuple-element.64), channel_id=1, source_target_pairs={{0,2},{1,3},{2,0},{3,1},{4,6},{5,7},{6,4},{7,5},{8,10},{9,11},{10,... | collective-permute-start | bytes 24584 | tf_op jit(solution)/shard_map/ppermute | solution.py:557
  5.0 1.5 %collective-permute-start = (bf16[560,256]{1,0:T(8,128)(2,1)S(1)}, bf16[560,256]{1,0:T(8,128)(2,1)S(1)}, u32[]{:S(2)}, u32[]{:S(2)}) collective-permute-start(bf16[560,256]{1,0:T(8,128)(2,1)S(1)} %get-tuple-element.74.refs_0_.refs_3_), channel_id=1, source_target_pairs={{0,1},{1,0},{2,3},{3,2},{4,5},{5,4},{6,7},{7,6},{8,9},{9,8},{10,11... | collective-permute-start | bytes 860168 | tf_op jit(solution)/shard_map/ppermute | solution.py:557
  6.5 1.5 %collective-permute-start.1 = (bf16[544,256]{1,0:T(8,128)(2,1)S(1)}, bf16[544,256]{1,0:T(8,128)(2,1)S(1)}, u32[]{:S(2)}, u32[]{:S(2)}) collective-permute-start(bf16[544,256]{1,0:T(8,128)(2,1)S(1)} %get-tuple-element.73.refs_1_), channel_id=1, source_target_pairs={{0,16},{1,17},{2,18},{3,19},{4,20},{5,21},{6,22},{7,23},{8,24},{9,... | collective-permute-start | bytes 835592 | tf_op jit(solution)/shard_map/ppermute | solution.py:557
  8.0 0.0 collective-permute-done.2
  8.0 2.6 %collective-permute-start.3 = (bf16[16,512]{1,0:T(8,128)(2,1)S(1)}, bf16[16,512]{1,0:T(8,128)(2,1)S(1)}, u32[]{:S(2)}, u32[]{:S(2)}) collective-permute-start(bf16[16,512]{1,0:T(8,128)(2,1)S(1)} %pad_maximum_fusion), channel_id=1, source_target_pairs={{0,4},{1,5},{2,6},{3,7},{4,0},{5,1},{6,2},{7,3},{8,12},{9,13},{10,... | collective-permute-start | bytes 49160 | tf_op jit(solution)/shard_map/ppermute | solution.py:557
  10.6 0.6 collective-permute-start.8
  11.2 1.5 %collective-permute-start.7 = (bf16[544,256]{1,0:T(8,128)(2,1)S(1)}, bf16[544,256]{1,0:T(8,128)(2,1)S(1)}, u32[]{:S(2)}, u32[]{:S(2)}) collective-permute-start(bf16[544,256]{1,0:T(8,128)(2,1)S(1)} %get-tuple-element.73.refs_1_), channel_id=1, source_target_pairs={{0,1},{1,0},{2,3},{3,2},{4,5},{5,4},{6,7},{7,6},{8,9},{9,8},{10,11... | collective-permute-start | bytes 835592 | tf_op jit(solution)/shard_map/ppermute | solution.py:557
  12.7 0.0 collective-permute-done.3
  12.7 0.0 collective-permute-start.4
  12.7 1.2 %collective-permute-done.4.refs_3_ = bf16[16,1024]{1,0:T(8,128)(2,1)S(1)} collective-permute-done((bf16[16,1024]{1,0:T(8,128)(2,1)S(1)}, bf16[16,1024]{1,0:T(8,128)(2,1)S(1)}, u32[]{:S(2)}, u32[]{:S(2)}) %collective-permute-start.4) | collective-permute-done | bytes 32800 | tf_op jit(solution)/shard_map/ppermute | solution.py:557
  13.9 2.5 %first_product.1 = (bf16[512,64]{1,0:T(8,128)(2,1)S(1)}, bf16[512,64]{1,0:T(8,128)(2,1)S(1)}, bf16[512,64]{1,0:T(8,128)(2,1)S(1)}, bf16[512,64]{1,0:T(8,128)(2,1...) custom-call(bf16[560,256]{1,0:T(8,128)(2,1)S(1)} %get-tuple-element.74, ...), custom_call_target="tpu_custom_call" | custom-call | flops 1000000000 | tf_op jit(solution)/shard_map/first_product/pallas_call | solution.py:179
  16.4 0.0 collective-permute-done.1.refs_1_
  16.4 0.0 collective-permute-done.refs_1_.refs_0_
  16.4 1.2 %collective-permute-start.5 = (bf16[560,256]{1,0:T(8,128)(2,1)S(1)}, bf16[560,256]{1,0:T(8,128)(2,1)S(1)}, u32[]{:S(2)}, u32[]{:S(2)}) collective-permute-start(bf16[560,256]{1,0:T(8,128)(2,1)S(1)} %collective-permute-done.refs_1_.refs_0_), channel_id=1, source_target_pairs={{0,16},{1,17},{2,18},{3,19},{4,20},{5,21},{6,22},{7,23},{8,24},{9,... | collective-permute-start | bytes 860168 | tf_op jit(solution)/shard_map/ppermute | solution.py:557
  17.6 0.9 %collective-permute-start.6 = (bf16[544,256]{1,0:T(8,128)(2,1)S(1)}, bf16[544,256]{1,0:T(8,128)(2,1)S(1)}, u32[]{:S(2)}, u32[]{:S(2)}) collective-permute-start(bf16[544,256]{1,0:T(8,128)(2,1)S(1)} %collective-permute-done.1.refs_1_), channel_id=1, source_target_pairs={{0,1},{1,0},{2,3},{3,2},{4,5},{5,4},{6,7},{7,6},{8,9},{9,8},{10,11... | collective-permute-start | bytes 835592 | tf_op jit(solution)/shard_map/ppermute | solution.py:557
  18.5 1.2 %skeletons.1 = (bf16[6,64,128]{2,1,0:T(8,128)(2,1)S(1)}, bf16[192,768]{1,0:T(8,128)(2,1)S(1)}, bf16[192,768]{1,0:T(8,128)(2,1)S(1)}, bf16[16,128]{1,0:T(8,128)(2,1)S(1)}) custom-call(bf16[560,256]{1,0:T(8,128)(2,1)S(1)} %get-tuple-element.74.refs_0_.refs_3_, bf16[560,256]{1,0:T(8,128)(2,1)S(1)} %collective-permute-done.refs_1_.refs_0_), custom_call_target="tpu_custom_call" | custom-call | flops 1000000000 | tf_op jit(solution)/shard_map/skeletons/pallas_call | solution.py:509
  19.7 0.0 collective-permute-done.7.refs_1_
  19.7 1.9 %collective-permute-done.8.refs_0_ = bf16[560,256]{1,0:T(8,128)(2,1)S(1)} collective-permute-done((bf16[560,256]{1,0:T(8,128)(2,1)S(1)}, bf16[560,256]{1,0:T(8,128)(2,1)S(1)}, u32[]{:S(2)}, u32[]{:S(2)}) %collective-permute-start.8) | collective-permute-done | bytes 286752 | tf_op jit(solution)/shard_map/ppermute | solution.py:557
  21.6 0.0 collective-permute-start.9
  21.6 2.5 %product.6 = (f32[512,256]{1,0:T(8,128)S(1)}, f32[512,256]{1,0:T(8,128)S(1)}, f32[512,256]{1,0:T(8,128)S(1)}, f32[512,256]{1,0:T(8,128)S(1)}) custom-call(bf16[560,256]{1,0:T(8,128)(2,1)S(1)} %collective-permute-done.refs_1_.refs_0_, bf16[544,256]{1,0:T(8,128)(2,1)S(1)} %collective-permute-done.7.refs_1_, bf16[512,64]{1,0:T(8,128)(2,1)S(1)} %get-tuple-element.72.refs_2_, ...), custom_call_target="tpu_custom_call" | custom-call | flops 1000000000 | tf_op jit(solution)/shard_map/product/pallas_call | solution.py:206
  24.1 2.5 %product.7 = (f32[512,256]{1,0:T(8,128)S(1)}, f32[512,256]{1,0:T(8,128)S(1)}, f32[512,256]{1,0:T(8,128)S(1)}, f32[512,256]{1,0:T(8,128)S(1)}) custom-call(bf16[560,256]{1,0:T(8,128)(2,1)S(1)} %collective-permute-done.8.refs_0_, bf16[544,256]{1,0:T(8,128)(2,1)S(1)} %collective-permute-done.1.refs_1_, bf16[512,64]{1,0:T(8,128)(2,1)S(1)} %get-tuple-element.72.refs_2_, ...), custom_call_target="tpu_custom_call" | custom-call | flops 1000000000 | tf_op jit(solution)/shard_map/product/pallas_call | solution.py:206
  26.6 0.0 collective-permute-done.9.refs_1_
  26.6 0.0 collective-permute-done.6.refs_1_
  26.6 0.0 collective-permute-done.5.refs_0_
  26.6 0.8 %product.10 = f32[512,256]{1,0:T(8,128)S(1)} custom-call(bf16[560,256]{1,0:T(8,128)(2,1)S(1)} %collective-permute-done.5.refs_0_, bf16[544,256]{1,0:T(8,128)(2,1)S(1)} %collective-permute-done.6.refs_1_, bf16[512,64]{1,0:T(8,128)(2,1)S(1)} %get-tuple-element.84.refs_5_.refs_2_, f32[512,256]{1,0:T(8,128)S(1)} %get-tuple-element.100.refs_3_), custom_call_target="tpu_custom_call" | custom-call | flops 1000000000 | tf_op jit(solution)/shard_map/product/pallas_call | solution.py:206
  27.4 0.1 collective-permute-start.10
  27.5 0.8 %product.9.refs_0_ = f32[512,256]{1,0:T(8,128)S(1)} custom-call(bf16[560,256]{1,0:T(8,128)(2,1)S(1)} %collective-permute-done.5.refs_0_, bf16[544,256]{1,0:T(8,128)(2,1)S(1)} %collective-permute-done.6.refs_1_, bf16[512,64]{1,0:T(8,128)(2,1)S(1)} %get-tuple-element.82.refs_3_.refs_2_, f32[512,256]{1,0:T(8,128)S(1)} %get-tuple-element.99.refs_3_), custom_call_target="tpu_custom_call" | custom-call | flops 1000000000 | tf_op jit(solution)/shard_map/product/pallas_call | solution.py:206
  28.3 1.1 %collective-permute-done.10.refs_1_ = f32[512,256]{1,0:T(8,128)S(1)} collective-permute-done((f32[512,256]{1,0:T(8,128)S(1)}, f32[512,256]{1,0:T(8,128)S(1)}, u32[]{:S(2)}, u32[]{:S(2)}) %collective-permute-start.10) | collective-permute-done | bytes 524320 | tf_op jit(solution)/shard_map/ppermute | solution.py:557
  29.4 0.1 add_up.3
  29.5 2.1 %collective-permute-start.12 = (bf16[256,256]{1,0:T(8,128)(2,1)S(1)}, bf16[256,256]{1,0:T(8,128)(2,1)S(1)}, u32[]{:S(2)}, u32[]{:S(2)}) collective-permute-start(bf16[256,256]{1,0:T(8,128)(2,1)S(1)} %get-tuple-element.105), channel_id=1, source_target_pairs={{0,2},{1,3},{2,0},{3,1},{4,6},{5,7},{6,4},{7,5},{8,10},{9,11},{10,... | collective-permute-start | bytes 393224 | tf_op jit(solution)/shard_map/ppermute | solution.py:557
  31.5 0.8 %product.8.refs_0_ = f32[512,256]{1,0:T(8,128)S(1)} custom-call(bf16[560,256]{1,0:T(8,128)(2,1)S(1)} %collective-permute-done.5.refs_0_, bf16[544,256]{1,0:T(8,128)(2,1)S(1)} %collective-permute-done.6.refs_1_, bf16[512,64]{1,0:T(8,128)(2,1)S(1)} %get-tuple-element.72.refs_2_, f32[512,256]{1,0:T(8,128)S(1)} %get-tuple-element.98.refs_3_), custom_call_target="tpu_custom_call" | custom-call | flops 1000000000 | tf_op jit(solution)/shard_map/product/pallas_call | solution.py:206
  32.4 0.8 %product.11 = f32[512,256]{1,0:T(8,128)S(1)} custom-call(bf16[560,256]{1,0:T(8,128)(2,1)S(1)} %collective-permute-done.5.refs_0_, bf16[544,256]{1,0:T(8,128)(2,1)S(1)} %collective-permute-done.6.refs_1_, bf16[512,64]{1,0:T(8,128)(2,1)S(1)} %get-tuple-element.83.refs_4_.refs_2_, f32[512,256]{1,0:T(8,128)S(1)} %get-tuple-element.103.refs_3_), custom_call_target="tpu_custom_call" | custom-call | flops 1000000000 | tf_op jit(solution)/shard_map/product/pallas_call | solution.py:206
  33.2 0.1 collective-permute-start.11
  33.3 2.1 %collective-permute-done.12.refs_1_ = bf16[256,256]{1,0:T(8,128)(2,1)S(1)} collective-permute-done((bf16[256,256]{1,0:T(8,128)(2,1)S(1)}, bf16[256,256]{1,0:T(8,128)(2,1)S(1)}, u32[]{:S(2)}, u32[]{:S(2)}) %collective-permute-start.12) | collective-permute-done | bytes 131104 | tf_op jit(solution)/shard_map/ppermute | solution.py:557
  35.4 2.7 %collective-permute-start.13 = (bf16[256,256]{1,0:T(8,128)(2,1)S(1)}, bf16[256,256]{1,0:T(8,128)(2,1)S(1)}, u32[]{:S(2)}, u32[]{:S(2)}) collective-permute-start(bf16[256,256]{1,0:T(8,128)(2,1)S(1)} %add_up.4.refs_2_), channel_id=1, source_target_pairs={{0,4},{1,5},{2,6},{3,7},{4,0},{5,1},{6,2},{7,3},{8,12},{9,13},{10,... | collective-permute-start | bytes 393224 | tf_op jit(solution)/shard_map/ppermute | solution.py:557
  38.1 0.0 collective-permute-done.11.refs_1_
  38.1 0.1 add_up.5
  38.1 1.8 %collective-permute-start.14 = (bf16[256,256]{1,0:T(8,128)(2,1)S(1)}, bf16[256,256]{1,0:T(8,128)(2,1)S(1)}, u32[]{:S(2)}, u32[]{:S(2)}) collective-permute-start(bf16[256,256]{1,0:T(8,128)(2,1)S(1)} %get-tuple-element.107), channel_id=1, source_target_pairs={{0,2},{1,3},{2,0},{3,1},{4,6},{5,7},{6,4},{7,5},{8,10},{9,11},{10,... | collective-permute-start | bytes 393224 | tf_op jit(solution)/shard_map/ppermute | solution.py:557
  39.9 0.9 %top_couplings.1 = (bf16[192,768]{1,0:T(8,128)(2,1)S(1)}, bf16[192,768]{1,0:T(8,128)(2,1)S(1)}) custom-call(bf16[16,128]{1,0:T(8,128)(2,1)S(1)} %get-tuple-element.80.refs_0_, bf16[16,128]{1,0:T(8,128)(2,1)S(1)} %collective-permute-done.9.refs_1_, bf16[6,64,128]{2,1,0:T(8,128)(2,1)S(1)} %get-tuple-element.108.refs_2_.refs_4_.refs_5_), custom_call_target="tpu_custom_call" | custom-call | flops 1000000000 | tf_op jit(solution)/shard_map/top_couplings/pallas_call | solution.py:536
  40.8 3.4 %collective-permute-done.13.refs_1_ = bf16[256,256]{1,0:T(8,128)(2,1)S(1)} collective-permute-done((bf16[256,256]{1,0:T(8,128)(2,1)S(1)}, bf16[256,256]{1,0:T(8,128)(2,1)S(1)}, u32[]{:S(2)}, u32[]{:S(2)}) %collective-permute-start.13) | collective-permute-done | bytes 131104 | tf_op jit(solution)/shard_map/ppermute | solution.py:557
  44.2 0.3 collective-permute-done.14.refs_2_
  44.5 5.6 %leaves.1 = (f32[2,64,128]{2,1,0:T(8,128)}, f32[64,128]{1,0:T(8,128)S(1)}, f32[64,256]{1,0:T(8,128)S(1)}, f32[64,256]{1,0:T(8,128)S(1)}, bf16[192,256]{1,0:T(8,128)(2,1)S(1)}) custom-call(f32[256,256]{1,0:T(8,128)S(1)} %get-tuple-element.106.refs_0_, bf16[256,256]{1,0:T(8,128)(2,1)S(1)} %collective-permute-done.13.refs_1_, ...), custom_call_target="tpu_custom_call" | custom-call | flops 1000000000 | tf_op jit(solution)/shard_map/leaves/pallas_call | solution.py:356
  50.1 0.9 %collective-permute-start.15 = (bf16[192,256]{1,0:T(8,128)(2,1)S(1)}, bf16[192,256]{1,0:T(8,128)(2,1)S(1)}, u32[]{:S(2)}, u32[]{:S(2)}) collective-permute-start(bf16[192,256]{1,0:T(8,128)(2,1)S(1)} %get-tuple-element.116), channel_id=1, source_target_pairs={{0,1},{1,0},{2,3},{3,2},{4,5},{5,4},{6,7},{7,6},{8,9},{9,8},{10,11... | collective-permute-start | bytes 294920 | tf_op jit(solution)/shard_map/ppermute | solution.py:557
  51.0 1.2 %collective-permute-start.16 = (bf16[192,256]{1,0:T(8,128)(2,1)S(1)}, bf16[192,256]{1,0:T(8,128)(2,1)S(1)}, u32[]{:S(2)}, u32[]{:S(2)}) collective-permute-start(bf16[192,256]{1,0:T(8,128)(2,1)S(1)} %get-tuple-element.116), channel_id=1, source_target_pairs={{0,2},{1,3},{2,0},{3,1},{4,6},{5,7},{6,4},{7,5},{8,10},{9,11},{10,... | collective-permute-start | bytes 294920 | tf_op jit(solution)/shard_map/ppermute | solution.py:557
  52.1 1.5 %collective-permute-start.17 = (bf16[192,256]{1,0:T(8,128)(2,1)S(1)}, bf16[192,256]{1,0:T(8,128)(2,1)S(1)}, u32[]{:S(2)}, u32[]{:S(2)}) collective-permute-start(bf16[192,256]{1,0:T(8,128)(2,1)S(1)} %get-tuple-element.116), channel_id=1, source_target_pairs={{0,3},{1,2},{2,1},{3,0},{4,7},{5,6},{6,5},{7,4},{8,11},{9,10},{10,... | collective-permute-start | bytes 294920 | tf_op jit(solution)/shard_map/ppermute | solution.py:557
  53.6 2.2 %collective-permute-done.15.refs_2_ = bf16[192,256]{1,0:T(8,128)(2,1)S(1)} collective-permute-done((bf16[192,256]{1,0:T(8,128)(2,1)S(1)}, bf16[192,256]{1,0:T(8,128)(2,1)S(1)}, u32[]{:S(2)}, u32[]{:S(2)}) %collective-permute-start.15) | collective-permute-done | bytes 98336 | tf_op jit(solution)/shard_map/ppermute | solution.py:557
  55.8 0.0 collective-permute-done.16.refs_3_
  55.8 1.8 %collective-permute-done.17.refs_4_ = bf16[192,256]{1,0:T(8,128)(2,1)S(1)} collective-permute-done((bf16[192,256]{1,0:T(8,128)(2,1)S(1)}, bf16[192,256]{1,0:T(8,128)(2,1)S(1)}, u32[]{:S(2)}, u32[]{:S(2)}) %collective-permute-start.17) | collective-permute-done | bytes 98336 | tf_op jit(solution)/shard_map/ppermute | solution.py:557
  57.6 5.9 %upper_levels.1 = (f32[3,1,64,128]{3,2,1,0:T(8,128)}, f32[2,1,64,256]{3,2,1,0:T(8,128)}) custom-call(f32[64,256]{1,0:T(8,128)S(1)} %get-tuple-element.114.refs_0_, f32[64,256]{1,0:T(8,128)S(1)} %get-tuple-element.115.refs_1_, bf16[192,256]{1,0:T(8,128)(2,1)S(1)} %collective-permute-done.15.refs_2_, bf16[192,256]{1,0:T(8,128)(2,1)S(1)} %collective-permute-done.16.refs_3_, ...), custom_call_target="tpu_custom_call" | custom-call | flops 1000000000 | tf_op jit(solution)/shard_map/upper_levels/pallas_call | solution.py:432
  (4 shorter events, 0.0 us)
Async XLA Ops:
  1.9 6.1 %collective-permute-start.2 = (bf16[16,256]{1,0:T(8,128)(2,1)S(1)}, bf16[16,256]{1,0:T(8,128)(2,1)S(1)}, u32[]{:S(2)}, u32[]{:S(2)}) collective-permute-start(bf16[16,256]{1,0:T(8,128)(2,1)S(1)} %get-tuple-element.64), channel_id=1, source_target_pairs={{0,2},{1,3},{2,0},{3,1},{4,6},{5,7},{6,4},{7,5},{8,10},{9,11},{10,... | collective-permute-start | bytes 24584 | tf_op jit(solution)/shard_map/ppermute | solution.py:557
  5.0 11.4 %collective-permute-start = (bf16[560,256]{1,0:T(8,128)(2,1)S(1)}, bf16[560,256]{1,0:T(8,128)(2,1)S(1)}, u32[]{:S(2)}, u32[]{:S(2)}) collective-permute-start(bf16[560,256]{1,0:T(8,128)(2,1)S(1)} %get-tuple-element.74.refs_0_.refs_3_), channel_id=1, source_target_pairs={{0,1},{1,0},{2,3},{3,2},{4,5},{5,4},{6,7},{7,6},{8,9},{9,8},{10,11... | collective-permute-start | bytes 860168 | tf_op jit(solution)/shard_map/ppermute | solution.py:557
  6.5 9.9 %collective-permute-start.1 = (bf16[544,256]{1,0:T(8,128)(2,1)S(1)}, bf16[544,256]{1,0:T(8,128)(2,1)S(1)}, u32[]{:S(2)}, u32[]{:S(2)}) collective-permute-start(bf16[544,256]{1,0:T(8,128)(2,1)S(1)} %get-tuple-element.73.refs_1_), channel_id=1, source_target_pairs={{0,16},{1,17},{2,18},{3,19},{4,20},{5,21},{6,22},{7,23},{8,24},{9,... | collective-permute-start | bytes 835592 | tf_op jit(solution)/shard_map/ppermute | solution.py:557
  8.0 4.7 %collective-permute-start.3 = (bf16[16,512]{1,0:T(8,128)(2,1)S(1)}, bf16[16,512]{1,0:T(8,128)(2,1)S(1)}, u32[]{:S(2)}, u32[]{:S(2)}) collective-permute-start(bf16[16,512]{1,0:T(8,128)(2,1)S(1)} %pad_maximum_fusion), channel_id=1, source_target_pairs={{0,4},{1,5},{2,6},{3,7},{4,0},{5,1},{6,2},{7,3},{8,12},{9,13},{10,... | collective-permute-start | bytes 49160 | tf_op jit(solution)/shard_map/ppermute | solution.py:557
  10.6 11.0 %collective-permute-start.8 = (bf16[560,256]{1,0:T(8,128)(2,1)S(1)}, bf16[560,256]{1,0:T(8,128)(2,1)S(1)}, u32[]{:S(2)}, u32[]{:S(2)}) collective-permute-start(bf16[560,256]{1,0:T(8,128)(2,1)S(1)} %get-tuple-element.74.refs_0_.refs_3_), channel_id=1, source_target_pairs={{0,16},{1,17},{2,18},{3,19},{4,20},{5,21},{6,22},{7,23},{8,24},{9,... | collective-permute-start | bytes 860168 | tf_op jit(solution)/shard_map/ppermute | solution.py:557
  11.2 8.5 %collective-permute-start.7 = (bf16[544,256]{1,0:T(8,128)(2,1)S(1)}, bf16[544,256]{1,0:T(8,128)(2,1)S(1)}, u32[]{:S(2)}, u32[]{:S(2)}) collective-permute-start(bf16[544,256]{1,0:T(8,128)(2,1)S(1)} %get-tuple-element.73.refs_1_), channel_id=1, source_target_pairs={{0,1},{1,0},{2,3},{3,2},{4,5},{5,4},{6,7},{7,6},{8,9},{9,8},{10,11... | collective-permute-start | bytes 835592 | tf_op jit(solution)/shard_map/ppermute | solution.py:557
  12.7 1.2 %collective-permute-start.4 = (bf16[16,1024]{1,0:T(8,128)(2,1)S(1)}, bf16[16,1024]{1,0:T(8,128)(2,1)S(1)}, u32[]{:S(2)}, u32[]{:S(2)}) collective-permute-start(bf16[16,1024]{1,0:T(8,128)(2,1)S(1)} %constant_dynamic-update-slice_fusion.refs_2_), channel_id=1, source_target_pairs={{0,8},{1,9},{2,10},{3,11},{4,12},{5,13},{6,14},{7,15},{8,0},{9,1},... | collective-permute-start | bytes 98312 | tf_op jit(solution)/shard_map/ppermute | solution.py:557
  16.4 10.2 %collective-permute-start.5 = (bf16[560,256]{1,0:T(8,128)(2,1)S(1)}, bf16[560,256]{1,0:T(8,128)(2,1)S(1)}, u32[]{:S(2)}, u32[]{:S(2)}) collective-permute-start(bf16[560,256]{1,0:T(8,128)(2,1)S(1)} %collective-permute-done.refs_1_.refs_0_), channel_id=1, source_target_pairs={{0,16},{1,17},{2,18},{3,19},{4,20},{5,21},{6,22},{7,23},{8,24},{9,... | collective-permute-start | bytes 860168 | tf_op jit(solution)/shard_map/ppermute | solution.py:557
  17.6 9.0 %collective-permute-start.6 = (bf16[544,256]{1,0:T(8,128)(2,1)S(1)}, bf16[544,256]{1,0:T(8,128)(2,1)S(1)}, u32[]{:S(2)}, u32[]{:S(2)}) collective-permute-start(bf16[544,256]{1,0:T(8,128)(2,1)S(1)} %collective-permute-done.1.refs_1_), channel_id=1, source_target_pairs={{0,1},{1,0},{2,3},{3,2},{4,5},{5,4},{6,7},{7,6},{8,9},{9,8},{10,11... | collective-permute-start | bytes 835592 | tf_op jit(solution)/shard_map/ppermute | solution.py:557
  21.6 5.0 %collective-permute-start.9 = (bf16[16,128]{1,0:T(8,128)(2,1)S(1)}, bf16[16,128]{1,0:T(8,128)(2,1)S(1)}, u32[]{:S(2)}, u32[]{:S(2)}) collective-permute-start(bf16[16,128]{1,0:T(8,128)(2,1)S(1)} %get-tuple-element.80.refs_0_), channel_id=1, source_target_pairs={{0,2},{1,3},{2,0},{3,1},{4,6},{5,7},{6,4},{7,5},{8,10},{9,11},{10,... | collective-permute-start | bytes 12296 | tf_op jit(solution)/shard_map/ppermute | solution.py:557
  27.4 2.0 %collective-permute-start.10 = (f32[512,256]{1,0:T(8,128)S(1)}, f32[512,256]{1,0:T(8,128)S(1)}, u32[]{:S(2)}, u32[]{:S(2)}) collective-permute-start(f32[512,256]{1,0:T(8,128)S(1)} %product.10), channel_id=1, source_target_pairs={{0,8},{1,9},{2,10},{3,11},{4,12},{5,13},{6,14},{7,15},{8,0},{9,1},... | collective-permute-start | bytes 1572872 | tf_op jit(solution)/shard_map/ppermute | solution.py:557
  29.5 5.9 %collective-permute-start.12 = (bf16[256,256]{1,0:T(8,128)(2,1)S(1)}, bf16[256,256]{1,0:T(8,128)(2,1)S(1)}, u32[]{:S(2)}, u32[]{:S(2)}) collective-permute-start(bf16[256,256]{1,0:T(8,128)(2,1)S(1)} %get-tuple-element.105), channel_id=1, source_target_pairs={{0,2},{1,3},{2,0},{3,1},{4,6},{5,7},{6,4},{7,5},{8,10},{9,11},{10,... | collective-permute-start | bytes 393224 | tf_op jit(solution)/shard_map/ppermute | solution.py:557
  33.2 4.9 %collective-permute-start.11 = (f32[512,256]{1,0:T(8,128)S(1)}, f32[512,256]{1,0:T(8,128)S(1)}, u32[]{:S(2)}, u32[]{:S(2)}) collective-permute-start(f32[512,256]{1,0:T(8,128)S(1)} %product.11), channel_id=1, source_target_pairs={{0,8},{1,9},{2,10},{3,11},{4,12},{5,13},{6,14},{7,15},{8,0},{9,1},... | collective-permute-start | bytes 1572872 | tf_op jit(solution)/shard_map/ppermute | solution.py:557
  35.4 8.8 %collective-permute-start.13 = (bf16[256,256]{1,0:T(8,128)(2,1)S(1)}, bf16[256,256]{1,0:T(8,128)(2,1)S(1)}, u32[]{:S(2)}, u32[]{:S(2)}) collective-permute-start(bf16[256,256]{1,0:T(8,128)(2,1)S(1)} %add_up.4.refs_2_), channel_id=1, source_target_pairs={{0,4},{1,5},{2,6},{3,7},{4,0},{5,1},{6,2},{7,3},{8,12},{9,13},{10,... | collective-permute-start | bytes 393224 | tf_op jit(solution)/shard_map/ppermute | solution.py:557
  38.1 6.3 %collective-permute-start.14 = (bf16[256,256]{1,0:T(8,128)(2,1)S(1)}, bf16[256,256]{1,0:T(8,128)(2,1)S(1)}, u32[]{:S(2)}, u32[]{:S(2)}) collective-permute-start(bf16[256,256]{1,0:T(8,128)(2,1)S(1)} %get-tuple-element.107), channel_id=1, source_target_pairs={{0,2},{1,3},{2,0},{3,1},{4,6},{5,7},{6,4},{7,5},{8,10},{9,11},{10,... | collective-permute-start | bytes 393224 | tf_op jit(solution)/shard_map/ppermute | solution.py:557
  50.1 5.7 %collective-permute-start.15 = (bf16[192,256]{1,0:T(8,128)(2,1)S(1)}, bf16[192,256]{1,0:T(8,128)(2,1)S(1)}, u32[]{:S(2)}, u32[]{:S(2)}) collective-permute-start(bf16[192,256]{1,0:T(8,128)(2,1)S(1)} %get-tuple-element.116), channel_id=1, source_target_pairs={{0,1},{1,0},{2,3},{3,2},{4,5},{5,4},{6,7},{7,6},{8,9},{9,8},{10,11... | collective-permute-start | bytes 294920 | tf_op jit(solution)/shard_map/ppermute | solution.py:557
  51.0 4.9 %collective-permute-start.16 = (bf16[192,256]{1,0:T(8,128)(2,1)S(1)}, bf16[192,256]{1,0:T(8,128)(2,1)S(1)}, u32[]{:S(2)}, u32[]{:S(2)}) collective-permute-start(bf16[192,256]{1,0:T(8,128)(2,1)S(1)} %get-tuple-element.116), channel_id=1, source_target_pairs={{0,2},{1,3},{2,0},{3,1},{4,6},{5,7},{6,4},{7,5},{8,10},{9,11},{10,... | collective-permute-start | bytes 294920 | tf_op jit(solution)/shard_map/ppermute | solution.py:557
  52.1 5.5 %collective-permute-start.17 = (bf16[192,256]{1,0:T(8,128)(2,1)S(1)}, bf16[192,256]{1,0:T(8,128)(2,1)S(1)}, u32[]{:S(2)}, u32[]{:S(2)}) collective-permute-start(bf16[192,256]{1,0:T(8,128)(2,1)S(1)} %get-tuple-element.116), channel_id=1, source_target_pairs={{0,3},{1,2},{2,1},{3,0},{4,7},{5,6},{6,5},{7,4},{8,11},{9,10},{10,... | collective-permute-start | bytes 294920 | tf_op jit(solution)/shard_map/ppermute | solution.py:557

commit v7 on v6

--- a/solution.py
+++ b/solution.py
@@ -589,8 +589,6 @@
         more = [swap(value, 1 << bit, 0) for value in pieces]
         totals = product(more, feats, totals, span)
         pieces += more
-    other_points = swap(points_two, 0, 2)
-    other_points, *totals = lax.optimization_barrier((other_points, *totals))
     (theirs,) = product(diagonal, feats[3:], totals[3:], span)
     from_sibling = swap(theirs, 1, 0)
     (mine,) = product(diagonal, feats[1:2], totals[1:2], span)
@@ -618,6 +616,8 @@
         bit *= 2
     own_sum, near_sent = add_up(mine, from_sibling, [([0], F32), ([1], BF16)], span, (sent,))
     received.append(swap(near_sent, 0, 2))
+    points_two, near_sent = lax.optimization_barrier((points_two, near_sent))
+    other_points = swap(points_two, 0, 2)
     later = top_couplings(points_two, other_points, picks, gain)
 
     leaf_interp, interp_one, skeleton, reduced, sent = leaves(

time: 63.9 us -> 65 us (1.017)
  waiting for transfers between devices: 13.9 us -> 16.3 us
  starting transfers between devices: 23.1 us -> 21.8 us
    ppermute x18, waiting for transfers between devices: 13.9 us -> 16.3 us  [swap(): return lax.ppermute(value, ('row', 'col'), pairs)]
    ppermute x18, starting transfers between devices: 23.1 us -> 21.8 us  [swap(): return lax.ppermute(value, ('row', 'col'), pairs)]
  transfers between devices with their start and end apart: 18 -> 18, of which waited for: 8 -> 7; matrix products, arithmetic and copies ran while one was open for 0% -> 0% of each run, Pallas kernels for 19% -> 19%
where the time goes in v7:
time: 65 us; the launch traced here: 64.8 us
  Pallas kernels  25.7 us (40%)
  starting transfers between devices  21.8 us (34%)
  waiting for transfers between devices  16.3 us (25%)
  between operations  0.96 us (1%)
    ppermute x18, starting transfers between devices, swap(): return lax.ppermute(value, ('row', 'col'), pairs)  21.8 us
    ppermute x18, waiting for transfers between devices, swap(): return lax.ppermute(value, ('row', 'col'), pairs)  16.3 us
    pallas_call x6, Pallas kernels, product(): pl.pallas_call(lambda *refs: product_body(span, len(halves), len(rows), *...  8.22 us
    pallas_call x1, Pallas kernels, upper_levels(): pl.pallas_call(lambda *refs: upper_body(picks.shape[0], *refs), out_shape...  5.94 us
    pallas_call x1, Pallas kernels, leaves(): pl.pallas_call(lambda *refs: leaves_body(len(others), *refs), out_shape=(...  5.6 us
    pallas_call x1, Pallas kernels, first_product(): pl.pallas_call(lambda *refs: first_product_body(gain, span, groups, len(p...  2.53 us
  transfers between devices with their start and end apart: 18, of which 7 were waited for; matrix products, arithmetic and copies ran while one was open for 0% of the time, Pallas kernels for 19%

profile of v7, /device:TPU:0, one launch (start us, length us, event | category | flops | bytes accessed | tf_op | source)
XLA Modules:
  0.0 64.8 jit_solution(13159538639807848992)
XLA Ops:
  0.6 1.3 %pack.1 = (bf16[560,256]{1,0:T(8,128)(2,1)S(1)}, bf16[544,256]{1,0:T(8,128)(2,1)S(1)}, bf16[16,256]{1,0:T(8,128)(2,1)S(1)}) custom-call(bf16[4,256,256]{2,1,0:T(8,128)(2,1)} %refs_0_.1, bf16[16,4,256]{2,1,0:T(4,128)(2,1)} %refs_1_.1, s32[2,64]{1,0:T(2,128)} %refs_2_.1, s32[1,64]{1,0:T(1,128)} %refs_3_.1, s32[4,64]{1,0:T(4,128)} %refs_4_.1, s32[2,64]{1,0:T(2,128)} %refs_5_.1), custom_call_target="tpu_custom_call" | custom-call | flops 1000000000 | tf_op jit(solution)/shard_map/pack/pallas_call | solution.py:118
  1.9 3.1 %collective-permute-start.2 = (bf16[16,256]{1,0:T(8,128)(2,1)S(1)}, bf16[16,256]{1,0:T(8,128)(2,1)S(1)}, u32[]{:S(2)}, u32[]{:S(2)}) collective-permute-start(bf16[16,256]{1,0:T(8,128)(2,1)S(1)} %get-tuple-element.60), channel_id=1, source_target_pairs={{0,2},{1,3},{2,0},{3,1},{4,6},{5,7},{6,4},{7,5},{8,10},{9,11},{10,... | collective-permute-start | bytes 24584 | tf_op jit(solution)/shard_map/ppermute | solution.py:557
  5.0 1.5 %collective-permute-start = (bf16[560,256]{1,0:T(8,128)(2,1)S(1)}, bf16[560,256]{1,0:T(8,128)(2,1)S(1)}, u32[]{:S(2)}, u32[]{:S(2)}) collective-permute-start(bf16[560,256]{1,0:T(8,128)(2,1)S(1)} %get-tuple-element.70.refs_0_.refs_3_), channel_id=1, source_target_pairs={{0,1},{1,0},{2,3},{3,2},{4,5},{5,4},{6,7},{7,6},{8,9},{9,8},{10,11... | collective-permute-start | bytes 860168 | tf_op jit(solution)/shard_map/ppermute | solution.py:557
  6.5 1.5 %collective-permute-start.1 = (bf16[544,256]{1,0:T(8,128)(2,1)S(1)}, bf16[544,256]{1,0:T(8,128)(2,1)S(1)}, u32[]{:S(2)}, u32[]{:S(2)}) collective-permute-start(bf16[544,256]{1,0:T(8,128)(2,1)S(1)} %get-tuple-element.69.refs_1_), channel_id=1, source_target_pairs={{0,16},{1,17},{2,18},{3,19},{4,20},{5,21},{6,22},{7,23},{8,24},{9,... | collective-permute-start | bytes 835592 | tf_op jit(solution)/shard_map/ppermute | solution.py:557
  8.0 0.0 collective-permute-done.2
  8.0 2.6 %collective-permute-start.3 = (bf16[16,512]{1,0:T(8,128)(2,1)S(1)}, bf16[16,512]{1,0:T(8,128)(2,1)S(1)}, u32[]{:S(2)}, u32[]{:S(2)}) collective-permute-start(bf16[16,512]{1,0:T(8,128)(2,1)S(1)} %pad_maximum_fusion), channel_id=1, source_target_pairs={{0,4},{1,5},{2,6},{3,7},{4,0},{5,1},{6,2},{7,3},{8,12},{9,13},{10,... | collective-permute-start | bytes 49160 | tf_op jit(solution)/shard_map/ppermute | solution.py:557
  10.6 0.6 collective-permute-start.8
  11.2 1.5 %collective-permute-start.7 = (bf16[544,256]{1,0:T(8,128)(2,1)S(1)}, bf16[544,256]{1,0:T(8,128)(2,1)S(1)}, u32[]{:S(2)}, u32[]{:S(2)}) collective-permute-start(bf16[544,256]{1,0:T(8,128)(2,1)S(1)} %get-tuple-element.69.refs_1_), channel_id=1, source_target_pairs={{0,1},{1,0},{2,3},{3,2},{4,5},{5,4},{6,7},{7,6},{8,9},{9,8},{10,11... | collective-permute-start | bytes 835592 | tf_op jit(solution)/shard_map/ppermute | solution.py:557
  12.7 0.0 collective-permute-done.3
  12.7 0.0 collective-permute-start.4
  12.7 1.2 %collective-permute-done.4.refs_3_ = bf16[16,1024]{1,0:T(8,128)(2,1)S(1)} collective-permute-done((bf16[16,1024]{1,0:T(8,128)(2,1)S(1)}, bf16[16,1024]{1,0:T(8,128)(2,1)S(1)}, u32[]{:S(2)}, u32[]{:S(2)}) %collective-permute-start.4) | collective-permute-done | bytes 32800 | tf_op jit(solution)/shard_map/ppermute | solution.py:557
  13.9 2.5 %first_product.1 = (bf16[512,64]{1,0:T(8,128)(2,1)S(1)}, bf16[512,64]{1,0:T(8,128)(2,1)S(1)}, bf16[512,64]{1,0:T(8,128)(2,1)S(1)}, bf16[512,64]{1,0:T(8,128)(2,1...) custom-call(bf16[560,256]{1,0:T(8,128)(2,1)S(1)} %get-tuple-element.70, ...), custom_call_target="tpu_custom_call" | custom-call | flops 1000000000 | tf_op jit(solution)/shard_map/first_product/pallas_call | solution.py:179
  16.4 0.0 collective-permute-done.1.refs_1_
  16.4 0.0 collective-permute-done.refs_1_.refs_0_
  16.4 1.2 %collective-permute-start.5 = (bf16[560,256]{1,0:T(8,128)(2,1)S(1)}, bf16[560,256]{1,0:T(8,128)(2,1)S(1)}, u32[]{:S(2)}, u32[]{:S(2)}) collective-permute-start(bf16[560,256]{1,0:T(8,128)(2,1)S(1)} %collective-permute-done.refs_1_.refs_0_), channel_id=1, source_target_pairs={{0,16},{1,17},{2,18},{3,19},{4,20},{5,21},{6,22},{7,23},{8,24},{9,... | collective-permute-start | bytes 860168 | tf_op jit(solution)/shard_map/ppermute | solution.py:557
  17.6 0.9 %collective-permute-start.6 = (bf16[544,256]{1,0:T(8,128)(2,1)S(1)}, bf16[544,256]{1,0:T(8,128)(2,1)S(1)}, u32[]{:S(2)}, u32[]{:S(2)}) collective-permute-start(bf16[544,256]{1,0:T(8,128)(2,1)S(1)} %collective-permute-done.1.refs_1_), channel_id=1, source_target_pairs={{0,1},{1,0},{2,3},{3,2},{4,5},{5,4},{6,7},{7,6},{8,9},{9,8},{10,11... | collective-permute-start | bytes 835592 | tf_op jit(solution)/shard_map/ppermute | solution.py:557
  18.5 1.2 %skeletons.1 = (bf16[6,64,128]{2,1,0:T(8,128)(2,1)S(1)}, bf16[192,768]{1,0:T(8,128)(2,1)S(1)}, bf16[192,768]{1,0:T(8,128)(2,1)S(1)}, bf16[16,128]{1,0:T(8,128)(2,1)S(1)}) custom-call(bf16[560,256]{1,0:T(8,128)(2,1)S(1)} %get-tuple-element.70.refs_0_.refs_3_, bf16[560,256]{1,0:T(8,128)(2,1)S(1)} %collective-permute-done.refs_1_.refs_0_), custom_call_target="tpu_custom_call" | custom-call | flops 1000000000 | tf_op jit(solution)/shard_map/skeletons/pallas_call | solution.py:509
  19.7 0.0 collective-permute-done.7.refs_1_
  19.7 1.9 %collective-permute-done.8.refs_0_ = bf16[560,256]{1,0:T(8,128)(2,1)S(1)} collective-permute-done((bf16[560,256]{1,0:T(8,128)(2,1)S(1)}, bf16[560,256]{1,0:T(8,128)(2,1)S(1)}, u32[]{:S(2)}, u32[]{:S(2)}) %collective-permute-start.8) | collective-permute-done | bytes 286752 | tf_op jit(solution)/shard_map/ppermute | solution.py:557
  21.6 2.5 %product.6 = (f32[512,256]{1,0:T(8,128)S(1)}, f32[512,256]{1,0:T(8,128)S(1)}, f32[512,256]{1,0:T(8,128)S(1)}, f32[512,256]{1,0:T(8,128)S(1)}) custom-call(bf16[560,256]{1,0:T(8,128)(2,1)S(1)} %collective-permute-done.refs_1_.refs_0_, bf16[544,256]{1,0:T(8,128)(2,1)S(1)} %collective-permute-done.7.refs_1_, bf16[512,64]{1,0:T(8,128)(2,1)S(1)} %get-tuple-element.68.refs_2_, ...), custom_call_target="tpu_custom_call" | custom-call | flops 1000000000 | tf_op jit(solution)/shard_map/product/pallas_call | solution.py:206
  24.1 2.5 %product.7 = (f32[512,256]{1,0:T(8,128)S(1)}, f32[512,256]{1,0:T(8,128)S(1)}, f32[512,256]{1,0:T(8,128)S(1)}, f32[512,256]{1,0:T(8,128)S(1)}) custom-call(bf16[560,256]{1,0:T(8,128)(2,1)S(1)} %collective-permute-done.8.refs_0_, bf16[544,256]{1,0:T(8,128)(2,1)S(1)} %collective-permute-done.1.refs_1_, bf16[512,64]{1,0:T(8,128)(2,1)S(1)} %get-tuple-element.68.refs_2_, ...), custom_call_target="tpu_custom_call" | custom-call | flops 1000000000 | tf_op jit(solution)/shard_map/product/pallas_call | solution.py:206
  26.5 0.0 collective-permute-done.6.refs_1_
  26.6 0.0 collective-permute-done.5.refs_0_
  26.6 0.8 %product.10 = f32[512,256]{1,0:T(8,128)S(1)} custom-call(bf16[560,256]{1,0:T(8,128)(2,1)S(1)} %collective-permute-done.5.refs_0_, bf16[544,256]{1,0:T(8,128)(2,1)S(1)} %collective-permute-done.6.refs_1_, bf16[512,64]{1,0:T(8,128)(2,1)S(1)} %get-tuple-element.79.refs_5_.refs_2_, f32[512,256]{1,0:T(8,128)S(1)} %get-tuple-element.91.refs_3_), custom_call_target="tpu_custom_call" | custom-call | flops 1000000000 | tf_op jit(solution)/shard_map/product/pallas_call | solution.py:206
  27.4 0.1 collective-permute-start.9
  27.5 0.8 %product.9.refs_0_ = f32[512,256]{1,0:T(8,128)S(1)} custom-call(bf16[560,256]{1,0:T(8,128)(2,1)S(1)} %collective-permute-done.5.refs_0_, bf16[544,256]{1,0:T(8,128)(2,1)S(1)} %collective-permute-done.6.refs_1_, bf16[512,64]{1,0:T(8,128)(2,1)S(1)} %get-tuple-element.77.refs_3_.refs_2_, f32[512,256]{1,0:T(8,128)S(1)} %get-tuple-element.90.refs_3_), custom_call_target="tpu_custom_call" | custom-call | flops 1000000000 | tf_op jit(solution)/shard_map/product/pallas_call | solution.py:206
  28.3 1.1 %collective-permute-done.9.refs_1_ = f32[512,256]{1,0:T(8,128)S(1)} collective-permute-done((f32[512,256]{1,0:T(8,128)S(1)}, f32[512,256]{1,0:T(8,128)S(1)}, u32[]{:S(2)}, u32[]{:S(2)}) %collective-permute-start.9) | collective-permute-done | bytes 524320 | tf_op jit(solution)/shard_map/ppermute | solution.py:557
  29.4 0.1 add_up.3
  29.5 0.5 collective-permute-start.11
  30.0 0.8 %product.8.refs_0_ = f32[512,256]{1,0:T(8,128)S(1)} custom-call(bf16[560,256]{1,0:T(8,128)(2,1)S(1)} %collective-permute-done.5.refs_0_, bf16[544,256]{1,0:T(8,128)(2,1)S(1)} %collective-permute-done.6.refs_1_, bf16[512,64]{1,0:T(8,128)(2,1)S(1)} %get-tuple-element.68.refs_2_, f32[512,256]{1,0:T(8,128)S(1)} %get-tuple-element.89.refs_3_), custom_call_target="tpu_custom_call" | custom-call | flops 1000000000 | tf_op jit(solution)/shard_map/product/pallas_call | solution.py:206
  30.8 0.8 %product.11 = f32[512,256]{1,0:T(8,128)S(1)} custom-call(bf16[560,256]{1,0:T(8,128)(2,1)S(1)} %collective-permute-done.5.refs_0_, bf16[544,256]{1,0:T(8,128)(2,1)S(1)} %collective-permute-done.6.refs_1_, bf16[512,64]{1,0:T(8,128)(2,1)S(1)} %get-tuple-element.78.refs_4_.refs_2_, f32[512,256]{1,0:T(8,128)S(1)} %get-tuple-element.94.refs_3_), custom_call_target="tpu_custom_call" | custom-call | flops 1000000000 | tf_op jit(solution)/shard_map/product/pallas_call | solution.py:206
  31.7 0.1 collective-permute-start.10
  31.7 3.3 %collective-permute-done.11.refs_1_ = bf16[256,256]{1,0:T(8,128)(2,1)S(1)} collective-permute-done((bf16[256,256]{1,0:T(8,128)(2,1)S(1)}, bf16[256,256]{1,0:T(8,128)(2,1)S(1)}, u32[]{:S(2)}, u32[]{:S(2)}) %collective-permute-start.11) | collective-permute-done | bytes 131104 | tf_op jit(solution)/shard_map/ppermute | solution.py:557
  35.1 2.7 %collective-permute-start.12 = (bf16[256,256]{1,0:T(8,128)(2,1)S(1)}, bf16[256,256]{1,0:T(8,128)(2,1)S(1)}, u32[]{:S(2)}, u32[]{:S(2)}) collective-permute-start(bf16[256,256]{1,0:T(8,128)(2,1)S(1)} %add_up.4.refs_2_), channel_id=1, source_target_pairs={{0,4},{1,5},{2,6},{3,7},{4,0},{5,1},{6,2},{7,3},{8,12},{9,13},{10,... | collective-permute-start | bytes 393224 | tf_op jit(solution)/shard_map/ppermute | solution.py:557
  37.8 0.0 collective-permute-done.10.refs_1_
  37.8 0.1 add_up.5
  37.8 0.6 collective-permute-start.13
  38.4 1.5 %collective-permute-start.14 = (bf16[16,128]{1,0:T(8,128)(2,1)S(1)}, bf16[16,128]{1,0:T(8,128)(2,1)S(1)}, u32[]{:S(2)}, u32[]{:S(2)}) collective-permute-start(bf16[16,128]{1,0:T(8,128)(2,1)S(1)} %get-tuple-element.102.refs_0_), channel_id=1, source_target_pairs={{0,2},{1,3},{2,0},{3,1},{4,6},{5,7},{6,4},{7,5},{8,10},{9,11},{10,... | collective-permute-start | bytes 12296 | tf_op jit(solution)/shard_map/ppermute | solution.py:557
  39.9 5.1 %collective-permute-done.14.refs_1_ = bf16[16,128]{1,0:T(8,128)(2,1)S(1)} collective-permute-done((bf16[16,128]{1,0:T(8,128)(2,1)S(1)}, bf16[16,128]{1,0:T(8,128)(2,1)S(1)}, u32[]{:S(2)}, u32[]{:S(2)}) %collective-permute-start.14) | collective-permute-done | bytes 4128 | tf_op jit(solution)/shard_map/ppermute | solution.py:557
  45.0 0.8 %top_couplings.1 = (bf16[192,768]{1,0:T(8,128)(2,1)S(1)}, bf16[192,768]{1,0:T(8,128)(2,1)S(1)}) custom-call(bf16[16,128]{1,0:T(8,128)(2,1)S(1)} %get-tuple-element.102.refs_0_, bf16[16,128]{1,0:T(8,128)(2,1)S(1)} %collective-permute-done.14.refs_1_, bf16[6,64,128]{2,1,0:T(8,128)(2,1)S(1)} %get-tuple-element.99.refs_2_.refs_4_.refs_5_), custom_call_target="tpu_custom_call" | custom-call | flops 1000000000 | tf_op jit(solution)/shard_map/top_couplings/pallas_call | solution.py:536
  45.9 0.0 collective-permute-done.12.refs_1_
  45.9 0.0 collective-permute-done.13.refs_2_
  45.9 5.6 %leaves.1 = (f32[2,64,128]{2,1,0:T(8,128)}, f32[64,128]{1,0:T(8,128)S(1)}, f32[64,256]{1,0:T(8,128)S(1)}, f32[64,256]{1,0:T(8,128)S(1)}, bf16[192,256]{1,0:T(8,128)(2,1)S(1)}) custom-call(f32[256,256]{1,0:T(8,128)S(1)} %get-tuple-element.97.refs_0_, bf16[256,256]{1,0:T(8,128)(2,1)S(1)} %collective-permute-done.12.refs_1_, ...), custom_call_target="tpu_custom_call" | custom-call | flops 1000000000 | tf_op jit(solution)/shard_map/leaves/pallas_call | solution.py:356
  51.5 0.1 collective-permute-start.15
  51.6 0.9 %collective-permute-start.16 = (bf16[192,256]{1,0:T(8,128)(2,1)S(1)}, bf16[192,256]{1,0:T(8,128)(2,1)S(1)}, u32[]{:S(2)}, u32[]{:S(2)}) collective-permute-start(bf16[192,256]{1,0:T(8,128)(2,1)S(1)} %get-tuple-element.108), channel_id=1, source_target_pairs={{0,2},{1,3},{2,0},{3,1},{4,6},{5,7},{6,4},{7,5},{8,10},{9,11},{10,... | collective-permute-start | bytes 294920 | tf_op jit(solution)/shard_map/ppermute | solution.py:557
  52.5 2.6 %collective-permute-start.17 = (bf16[192,256]{1,0:T(8,128)(2,1)S(1)}, bf16[192,256]{1,0:T(8,128)(2,1)S(1)}, u32[]{:S(2)}, u32[]{:S(2)}) collective-permute-start(bf16[192,256]{1,0:T(8,128)(2,1)S(1)} %get-tuple-element.108), channel_id=1, source_target_pairs={{0,3},{1,2},{2,1},{3,0},{4,7},{5,6},{6,5},{7,4},{8,11},{9,10},{10,... | collective-permute-start | bytes 294920 | tf_op jit(solution)/shard_map/ppermute | solution.py:557
  55.0 2.2 %collective-permute-done.15.refs_2_ = bf16[192,256]{1,0:T(8,128)(2,1)S(1)} collective-permute-done((bf16[192,256]{1,0:T(8,128)(2,1)S(1)}, bf16[192,256]{1,0:T(8,128)(2,1)S(1)}, u32[]{:S(2)}, u32[]{:S(2)}) %collective-permute-start.15) | collective-permute-done | bytes 98336 | tf_op jit(solution)/shard_map/ppermute | solution.py:557
  57.2 0.0 collective-permute-done.16.refs_3_
  57.2 1.5 %collective-permute-done.17.refs_4_ = bf16[192,256]{1,0:T(8,128)(2,1)S(1)} collective-permute-done((bf16[192,256]{1,0:T(8,128)(2,1)S(1)}, bf16[192,256]{1,0:T(8,128)(2,1)S(1)}, u32[]{:S(2)}, u32[]{:S(2)}) %collective-permute-start.17) | collective-permute-done | bytes 98336 | tf_op jit(solution)/shard_map/ppermute | solution.py:557
  58.7 5.9 %upper_levels.1 = (f32[3,1,64,128]{3,2,1,0:T(8,128)}, f32[2,1,64,256]{3,2,1,0:T(8,128)}) custom-call(f32[64,256]{1,0:T(8,128)S(1)} %get-tuple-element.106.refs_0_, f32[64,256]{1,0:T(8,128)S(1)} %get-tuple-element.107.refs_1_, bf16[192,256]{1,0:T(8,128)(2,1)S(1)} %collective-permute-done.15.refs_2_, bf16[192,256]{1,0:T(8,128)(2,1)S(1)} %collective-permute-done.16.refs_3_, ...), custom_call_target="tpu_custom_call" | custom-call | flops 1000000000 | tf_op jit(solution)/shard_map/upper_levels/pallas_call | solution.py:432
  (4 shorter events, 0.0 us)
Async XLA Ops:
  1.9 6.1 %collective-permute-start.2 = (bf16[16,256]{1,0:T(8,128)(2,1)S(1)}, bf16[16,256]{1,0:T(8,128)(2,1)S(1)}, u32[]{:S(2)}, u32[]{:S(2)}) collective-permute-start(bf16[16,256]{1,0:T(8,128)(2,1)S(1)} %get-tuple-element.60), channel_id=1, source_target_pairs={{0,2},{1,3},{2,0},{3,1},{4,6},{5,7},{6,4},{7,5},{8,10},{9,11},{10,... | collective-permute-start | bytes 24584 | tf_op jit(solution)/shard_map/ppermute | solution.py:557
  5.0 11.4 %collective-permute-start = (bf16[560,256]{1,0:T(8,128)(2,1)S(1)}, bf16[560,256]{1,0:T(8,128)(2,1)S(1)}, u32[]{:S(2)}, u32[]{:S(2)}) collective-permute-start(bf16[560,256]{1,0:T(8,128)(2,1)S(1)} %get-tuple-element.70.refs_0_.refs_3_), channel_id=1, source_target_pairs={{0,1},{1,0},{2,3},{3,2},{4,5},{5,4},{6,7},{7,6},{8,9},{9,8},{10,11... | collective-permute-start | bytes 860168 | tf_op jit(solution)/shard_map/ppermute | solution.py:557
  6.5 9.9 %collective-permute-start.1 = (bf16[544,256]{1,0:T(8,128)(2,1)S(1)}, bf16[544,256]{1,0:T(8,128)(2,1)S(1)}, u32[]{:S(2)}, u32[]{:S(2)}) collective-permute-start(bf16[544,256]{1,0:T(8,128)(2,1)S(1)} %get-tuple-element.69.refs_1_), channel_id=1, source_target_pairs={{0,16},{1,17},{2,18},{3,19},{4,20},{5,21},{6,22},{7,23},{8,24},{9,... | collective-permute-start | bytes 835592 | tf_op jit(solution)/shard_map/ppermute | solution.py:557
  8.0 4.7 %collective-permute-start.3 = (bf16[16,512]{1,0:T(8,128)(2,1)S(1)}, bf16[16,512]{1,0:T(8,128)(2,1)S(1)}, u32[]{:S(2)}, u32[]{:S(2)}) collective-permute-start(bf16[16,512]{1,0:T(8,128)(2,1)S(1)} %pad_maximum_fusion), channel_id=1, source_target_pairs={{0,4},{1,5},{2,6},{3,7},{4,0},{5,1},{6,2},{7,3},{8,12},{9,13},{10,... | collective-permute-start | bytes 49160 | tf_op jit(solution)/shard_map/ppermute | solution.py:557
  10.6 11.0 %collective-permute-start.8 = (bf16[560,256]{1,0:T(8,128)(2,1)S(1)}, bf16[560,256]{1,0:T(8,128)(2,1)S(1)}, u32[]{:S(2)}, u32[]{:S(2)}) collective-permute-start(bf16[560,256]{1,0:T(8,128)(2,1)S(1)} %get-tuple-element.70.refs_0_.refs_3_), channel_id=1, source_target_pairs={{0,16},{1,17},{2,18},{3,19},{4,20},{5,21},{6,22},{7,23},{8,24},{9,... | collective-permute-start | bytes 860168 | tf_op jit(solution)/shard_map/ppermute | solution.py:557
  11.2 8.5 %collective-permute-start.7 = (bf16[544,256]{1,0:T(8,128)(2,1)S(1)}, bf16[544,256]{1,0:T(8,128)(2,1)S(1)}, u32[]{:S(2)}, u32[]{:S(2)}) collective-permute-start(bf16[544,256]{1,0:T(8,128)(2,1)S(1)} %get-tuple-element.69.refs_1_), channel_id=1, source_target_pairs={{0,1},{1,0},{2,3},{3,2},{4,5},{5,4},{6,7},{7,6},{8,9},{9,8},{10,11... | collective-permute-start | bytes 835592 | tf_op jit(solution)/shard_map/ppermute | solution.py:557
  12.7 1.2 %collective-permute-start.4 = (bf16[16,1024]{1,0:T(8,128)(2,1)S(1)}, bf16[16,1024]{1,0:T(8,128)(2,1)S(1)}, u32[]{:S(2)}, u32[]{:S(2)}) collective-permute-start(bf16[16,1024]{1,0:T(8,128)(2,1)S(1)} %constant_dynamic-update-slice_fusion.refs_2_), channel_id=1, source_target_pairs={{0,8},{1,9},{2,10},{3,11},{4,12},{5,13},{6,14},{7,15},{8,0},{9,1},... | collective-permute-start | bytes 98312 | tf_op jit(solution)/shard_map/ppermute | solution.py:557
  16.4 10.2 %collective-permute-start.5 = (bf16[560,256]{1,0:T(8,128)(2,1)S(1)}, bf16[560,256]{1,0:T(8,128)(2,1)S(1)}, u32[]{:S(2)}, u32[]{:S(2)}) collective-permute-start(bf16[560,256]{1,0:T(8,128)(2,1)S(1)} %collective-permute-done.refs_1_.refs_0_), channel_id=1, source_target_pairs={{0,16},{1,17},{2,18},{3,19},{4,20},{5,21},{6,22},{7,23},{8,24},{9,... | collective-permute-start | bytes 860168 | tf_op jit(solution)/shard_map/ppermute | solution.py:557
  17.6 8.9 %collective-permute-start.6 = (bf16[544,256]{1,0:T(8,128)(2,1)S(1)}, bf16[544,256]{1,0:T(8,128)(2,1)S(1)}, u32[]{:S(2)}, u32[]{:S(2)}) collective-permute-start(bf16[544,256]{1,0:T(8,128)(2,1)S(1)} %collective-permute-done.1.refs_1_), channel_id=1, source_target_pairs={{0,1},{1,0},{2,3},{3,2},{4,5},{5,4},{6,7},{7,6},{8,9},{9,8},{10,11... | collective-permute-start | bytes 835592 | tf_op jit(solution)/shard_map/ppermute | solution.py:557
  27.4 2.0 %collective-permute-start.9 = (f32[512,256]{1,0:T(8,128)S(1)}, f32[512,256]{1,0:T(8,128)S(1)}, u32[]{:S(2)}, u32[]{:S(2)}) collective-permute-start(f32[512,256]{1,0:T(8,128)S(1)} %product.10), channel_id=1, source_target_pairs={{0,8},{1,9},{2,10},{3,11},{4,12},{5,13},{6,14},{7,15},{8,0},{9,1},... | collective-permute-start | bytes 1572872 | tf_op jit(solution)/shard_map/ppermute | solution.py:557
  29.5 5.6 %collective-permute-start.11 = (bf16[256,256]{1,0:T(8,128)(2,1)S(1)}, bf16[256,256]{1,0:T(8,128)(2,1)S(1)}, u32[]{:S(2)}, u32[]{:S(2)}) collective-permute-start(bf16[256,256]{1,0:T(8,128)(2,1)S(1)} %get-tuple-element.96), channel_id=1, source_target_pairs={{0,2},{1,3},{2,0},{3,1},{4,6},{5,7},{6,4},{7,5},{8,10},{9,11},{10,... | collective-permute-start | bytes 393224 | tf_op jit(solution)/shard_map/ppermute | solution.py:557
  31.7 6.1 %collective-permute-start.10 = (f32[512,256]{1,0:T(8,128)S(1)}, f32[512,256]{1,0:T(8,128)S(1)}, u32[]{:S(2)}, u32[]{:S(2)}) collective-permute-start(f32[512,256]{1,0:T(8,128)S(1)} %product.11), channel_id=1, source_target_pairs={{0,8},{1,9},{2,10},{3,11},{4,12},{5,13},{6,14},{7,15},{8,0},{9,1},... | collective-permute-start | bytes 1572872 | tf_op jit(solution)/shard_map/ppermute | solution.py:557
  35.1 10.8 %collective-permute-start.12 = (bf16[256,256]{1,0:T(8,128)(2,1)S(1)}, bf16[256,256]{1,0:T(8,128)(2,1)S(1)}, u32[]{:S(2)}, u32[]{:S(2)}) collective-permute-start(bf16[256,256]{1,0:T(8,128)(2,1)S(1)} %add_up.4.refs_2_), channel_id=1, source_target_pairs={{0,4},{1,5},{2,6},{3,7},{4,0},{5,1},{6,2},{7,3},{8,12},{9,13},{10,... | collective-permute-start | bytes 393224 | tf_op jit(solution)/shard_map/ppermute | solution.py:557
  37.8 8.1 %collective-permute-start.13 = (bf16[256,256]{1,0:T(8,128)(2,1)S(1)}, bf16[256,256]{1,0:T(8,128)(2,1)S(1)}, u32[]{:S(2)}, u32[]{:S(2)}) collective-permute-start(bf16[256,256]{1,0:T(8,128)(2,1)S(1)} %get-tuple-element.98), channel_id=1, source_target_pairs={{0,2},{1,3},{2,0},{3,1},{4,6},{5,7},{6,4},{7,5},{8,10},{9,11},{10,... | collective-permute-start | bytes 393224 | tf_op jit(solution)/shard_map/ppermute | solution.py:557
  38.4 6.6 %collective-permute-start.14 = (bf16[16,128]{1,0:T(8,128)(2,1)S(1)}, bf16[16,128]{1,0:T(8,128)(2,1)S(1)}, u32[]{:S(2)}, u32[]{:S(2)}) collective-permute-start(bf16[16,128]{1,0:T(8,128)(2,1)S(1)} %get-tuple-element.102.refs_0_), channel_id=1, source_target_pairs={{0,2},{1,3},{2,0},{3,1},{4,6},{5,7},{6,4},{7,5},{8,10},{9,11},{10,... | collective-permute-start | bytes 12296 | tf_op jit(solution)/shard_map/ppermute | solution.py:557
  51.5 5.7 %collective-permute-start.15 = (bf16[192,256]{1,0:T(8,128)(2,1)S(1)}, bf16[192,256]{1,0:T(8,128)(2,1)S(1)}, u32[]{:S(2)}, u32[]{:S(2)}) collective-permute-start(bf16[192,256]{1,0:T(8,128)(2,1)S(1)} %get-tuple-element.108), channel_id=1, source_target_pairs={{0,1},{1,0},{2,3},{3,2},{4,5},{5,4},{6,7},{7,6},{8,9},{9,8},{10,11... | collective-permute-start | bytes 294920 | tf_op jit(solution)/shard_map/ppermute | solution.py:557
  51.6 5.7 %collective-permute-start.16 = (bf16[192,256]{1,0:T(8,128)(2,1)S(1)}, bf16[192,256]{1,0:T(8,128)(2,1)S(1)}, u32[]{:S(2)}, u32[]{:S(2)}) collective-permute-start(bf16[192,256]{1,0:T(8,128)(2,1)S(1)} %get-tuple-element.108), channel_id=1, source_target_pairs={{0,2},{1,3},{2,0},{3,1},{4,6},{5,7},{6,4},{7,5},{8,10},{9,11},{10,... | collective-permute-start | bytes 294920 | tf_op jit(solution)/shard_map/ppermute | solution.py:557
  52.5 6.3 %collective-permute-start.17 = (bf16[192,256]{1,0:T(8,128)(2,1)S(1)}, bf16[192,256]{1,0:T(8,128)(2,1)S(1)}, u32[]{:S(2)}, u32[]{:S(2)}) collective-permute-start(bf16[192,256]{1,0:T(8,128)(2,1)S(1)} %get-tuple-element.108), channel_id=1, source_target_pairs={{0,3},{1,2},{2,1},{3,0},{4,7},{5,6},{6,5},{7,4},{8,11},{9,10},{10,... | collective-permute-start | bytes 294920 | tf_op jit(solution)/shard_map/ppermute | solution.py:557

commit v8 on v7

--- a/solution.py
+++ b/solution.py
@@ -536,7 +536,7 @@
     return pl.pallas_call(
         lambda *refs: top_couplings_body(gain, *refs),
         out_shape=[coupling_shape(picks.shape[1])] * 2,
-        cost_estimate=COST,
+        cost_estimate=LONG,
         compiler_params=PARAMS,
         name="top_couplings",
     )(mine, theirs, picks)
@@ -594,7 +594,7 @@
     (mine,) = product(diagonal, feats[1:2], totals[1:2], span)
     outs = [(range(0, line - 2, 2), F32), (range(1, line - 2, 2), BF16)]
     kept, sent = add_up(mine, from_sibling, outs, span)
-    sent, total = lax.optimization_barrier((sent, totals[2]))
+    sent, total, points_two = lax.optimization_barrier((sent, totals[2], points_two))
     arrived = swap(sent, 0, 2)
     (theirs,) = product(diagonal, feats[2:3], [total], span)
     from_sibling = swap(theirs, 1, 0)
@@ -616,7 +616,6 @@
         bit *= 2
     own_sum, near_sent = add_up(mine, from_sibling, [([0], F32), ([1], BF16)], span, (sent,))
     received.append(swap(near_sent, 0, 2))
-    points_two, near_sent = lax.optimization_barrier((points_two, near_sent))
     other_points = swap(points_two, 0, 2)
     later = top_couplings(points_two, other_points, picks, gain)
 

time: 65 us -> 64 us (0.985)
  waiting for transfers between devices: 16.3 us -> 15.2 us
    ppermute x18, waiting for transfers between devices: 16.3 us -> 15.2 us  [swap(): return lax.ppermute(value, ('row', 'col'), pairs)]
  transfers between devices with their start and end apart: 18 -> 18, of which waited for: 7 -> 8; matrix products, arithmetic and copies ran while one was open for 0% -> 0% of each run, Pallas kernels for 19% -> 19%
where the time goes in v8:
time: 64 us; the launch traced here: 63.8 us
  Pallas kernels  25.7 us (40%)
  starting transfers between devices  22 us (34%)
  waiting for transfers between devices  15.2 us (24%)
  between operations  0.95 us (1%)
    ppermute x18, starting transfers between devices, swap(): return lax.ppermute(value, ('row', 'col'), pairs)  22 us
    ppermute x18, waiting for transfers between devices, swap(): return lax.ppermute(value, ('row', 'col'), pairs)  15.2 us
    pallas_call x6, Pallas kernels, product(): pl.pallas_call(lambda *refs: product_body(span, len(halves), len(rows), *...  8.22 us
    pallas_call x1, Pallas kernels, upper_levels(): pl.pallas_call(lambda *refs: upper_body(picks.shape[0], *refs), out_shape...  5.94 us
    pallas_call x1, Pallas kernels, leaves(): pl.pallas_call(lambda *refs: leaves_body(len(others), *refs), out_shape=(...  5.59 us
    pallas_call x1, Pallas kernels, first_product(): pl.pallas_call(lambda *refs: first_product_body(gain, span, groups, len(p...  2.53 us
  transfers between devices with their start and end apart: 18, of which 8 were waited for; matrix products, arithmetic and copies ran while one was open for 0% of the time, Pallas kernels for 19%

profile of v8, /device:TPU:0, one launch (start us, length us, event | category | flops | bytes accessed | tf_op | source)
XLA Modules:
  0.0 63.8 jit_solution(3042405245136984294)
XLA Ops:
  0.6 1.3 %pack.1 = (bf16[560,256]{1,0:T(8,128)(2,1)S(1)}, bf16[544,256]{1,0:T(8,128)(2,1)S(1)}, bf16[16,256]{1,0:T(8,128)(2,1)S(1)}) custom-call(bf16[4,256,256]{2,1,0:T(8,128)(2,1)} %refs_0_.1, bf16[16,4,256]{2,1,0:T(4,128)(2,1)} %refs_1_.1, s32[2,64]{1,0:T(2,128)} %refs_2_.1, s32[1,64]{1,0:T(1,128)} %refs_3_.1, s32[4,64]{1,0:T(4,128)} %refs_4_.1, s32[2,64]{1,0:T(2,128)} %refs_5_.1), custom_call_target="tpu_custom_call" | custom-call | flops 1000000000 | tf_op jit(solution)/shard_map/pack/pallas_call | solution.py:118
  1.9 3.1 %collective-permute-start.2 = (bf16[16,256]{1,0:T(8,128)(2,1)S(1)}, bf16[16,256]{1,0:T(8,128)(2,1)S(1)}, u32[]{:S(2)}, u32[]{:S(2)}) collective-permute-start(bf16[16,256]{1,0:T(8,128)(2,1)S(1)} %get-tuple-element.60), channel_id=1, source_target_pairs={{0,2},{1,3},{2,0},{3,1},{4,6},{5,7},{6,4},{7,5},{8,10},{9,11},{10,... | collective-permute-start | bytes 24584 | tf_op jit(solution)/shard_map/ppermute | solution.py:557
  5.0 1.5 %collective-permute-start = (bf16[560,256]{1,0:T(8,128)(2,1)S(1)}, bf16[560,256]{1,0:T(8,128)(2,1)S(1)}, u32[]{:S(2)}, u32[]{:S(2)}) collective-permute-start(bf16[560,256]{1,0:T(8,128)(2,1)S(1)} %get-tuple-element.70.refs_0_.refs_3_), channel_id=1, source_target_pairs={{0,1},{1,0},{2,3},{3,2},{4,5},{5,4},{6,7},{7,6},{8,9},{9,8},{10,11... | collective-permute-start | bytes 860168 | tf_op jit(solution)/shard_map/ppermute | solution.py:557
  6.5 1.5 %collective-permute-start.1 = (bf16[544,256]{1,0:T(8,128)(2,1)S(1)}, bf16[544,256]{1,0:T(8,128)(2,1)S(1)}, u32[]{:S(2)}, u32[]{:S(2)}) collective-permute-start(bf16[544,256]{1,0:T(8,128)(2,1)S(1)} %get-tuple-element.69.refs_1_), channel_id=1, source_target_pairs={{0,16},{1,17},{2,18},{3,19},{4,20},{5,21},{6,22},{7,23},{8,24},{9,... | collective-permute-start | bytes 835592 | tf_op jit(solution)/shard_map/ppermute | solution.py:557
  8.0 0.0 collective-permute-done.2
  8.0 2.6 %collective-permute-start.3 = (bf16[16,512]{1,0:T(8,128)(2,1)S(1)}, bf16[16,512]{1,0:T(8,128)(2,1)S(1)}, u32[]{:S(2)}, u32[]{:S(2)}) collective-permute-start(bf16[16,512]{1,0:T(8,128)(2,1)S(1)} %pad_maximum_fusion), channel_id=1, source_target_pairs={{0,4},{1,5},{2,6},{3,7},{4,0},{5,1},{6,2},{7,3},{8,12},{9,13},{10,... | collective-permute-start | bytes 49160 | tf_op jit(solution)/shard_map/ppermute | solution.py:557
  10.6 0.6 collective-permute-start.8
  11.2 1.5 %collective-permute-start.7 = (bf16[544,256]{1,0:T(8,128)(2,1)S(1)}, bf16[544,256]{1,0:T(8,128)(2,1)S(1)}, u32[]{:S(2)}, u32[]{:S(2)}) collective-permute-start(bf16[544,256]{1,0:T(8,128)(2,1)S(1)} %get-tuple-element.69.refs_1_), channel_id=1, source_target_pairs={{0,1},{1,0},{2,3},{3,2},{4,5},{5,4},{6,7},{7,6},{8,9},{9,8},{10,11... | collective-permute-start | bytes 835592 | tf_op jit(solution)/shard_map/ppermute | solution.py:557
  12.7 0.0 collective-permute-done.3
  12.7 0.0 collective-permute-start.4
  12.7 1.2 %collective-permute-done.4.refs_3_ = bf16[16,1024]{1,0:T(8,128)(2,1)S(1)} collective-permute-done((bf16[16,1024]{1,0:T(8,128)(2,1)S(1)}, bf16[16,1024]{1,0:T(8,128)(2,1)S(1)}, u32[]{:S(2)}, u32[]{:S(2)}) %collective-permute-start.4) | collective-permute-done | bytes 32800 | tf_op jit(solution)/shard_map/ppermute | solution.py:557
  13.9 2.5 %first_product.1 = (bf16[512,64]{1,0:T(8,128)(2,1)S(1)}, bf16[512,64]{1,0:T(8,128)(2,1)S(1)}, bf16[512,64]{1,0:T(8,128)(2,1)S(1)}, bf16[512,64]{1,0:T(8,128)(2,1...) custom-call(bf16[560,256]{1,0:T(8,128)(2,1)S(1)} %get-tuple-element.70, ...), custom_call_target="tpu_custom_call" | custom-call | flops 1000000000 | tf_op jit(solution)/shard_map/first_product/pallas_call | solution.py:179
  16.4 0.0 collective-permute-done.1.refs_1_
  16.4 0.0 collective-permute-done.refs_1_.refs_0_
  16.4 1.2 %collective-permute-start.5 = (bf16[560,256]{1,0:T(8,128)(2,1)S(1)}, bf16[560,256]{1,0:T(8,128)(2,1)S(1)}, u32[]{:S(2)}, u32[]{:S(2)}) collective-permute-start(bf16[560,256]{1,0:T(8,128)(2,1)S(1)} %collective-permute-done.refs_1_.refs_0_), channel_id=1, source_target_pairs={{0,16},{1,17},{2,18},{3,19},{4,20},{5,21},{6,22},{7,23},{8,24},{9,... | collective-permute-start | bytes 860168 | tf_op jit(solution)/shard_map/ppermute | solution.py:557
  17.6 0.9 %collective-permute-start.6 = (bf16[544,256]{1,0:T(8,128)(2,1)S(1)}, bf16[544,256]{1,0:T(8,128)(2,1)S(1)}, u32[]{:S(2)}, u32[]{:S(2)}) collective-permute-start(bf16[544,256]{1,0:T(8,128)(2,1)S(1)} %collective-permute-done.1.refs_1_), channel_id=1, source_target_pairs={{0,1},{1,0},{2,3},{3,2},{4,5},{5,4},{6,7},{7,6},{8,9},{9,8},{10,11... | collective-permute-start | bytes 835592 | tf_op jit(solution)/shard_map/ppermute | solution.py:557
  18.5 1.2 %skeletons.1 = (bf16[6,64,128]{2,1,0:T(8,128)(2,1)S(1)}, bf16[192,768]{1,0:T(8,128)(2,1)S(1)}, bf16[192,768]{1,0:T(8,128)(2,1)S(1)}, bf16[16,128]{1,0:T(8,128)(2,1)S(1)}) custom-call(bf16[560,256]{1,0:T(8,128)(2,1)S(1)} %get-tuple-element.70.refs_0_.refs_3_, bf16[560,256]{1,0:T(8,128)(2,1)S(1)} %collective-permute-done.refs_1_.refs_0_), custom_call_target="tpu_custom_call" | custom-call | flops 1000000000 | tf_op jit(solution)/shard_map/skeletons/pallas_call | solution.py:509
  19.7 0.0 collective-permute-done.7.refs_1_
  19.7 1.9 %collective-permute-done.8.refs_0_ = bf16[560,256]{1,0:T(8,128)(2,1)S(1)} collective-permute-done((bf16[560,256]{1,0:T(8,128)(2,1)S(1)}, bf16[560,256]{1,0:T(8,128)(2,1)S(1)}, u32[]{:S(2)}, u32[]{:S(2)}) %collective-permute-start.8) | collective-permute-done | bytes 286752 | tf_op jit(solution)/shard_map/ppermute | solution.py:557
  21.6 2.5 %product.6 = (f32[512,256]{1,0:T(8,128)S(1)}, f32[512,256]{1,0:T(8,128)S(1)}, f32[512,256]{1,0:T(8,128)S(1)}, f32[512,256]{1,0:T(8,128)S(1)}) custom-call(bf16[560,256]{1,0:T(8,128)(2,1)S(1)} %collective-permute-done.refs_1_.refs_0_, bf16[544,256]{1,0:T(8,128)(2,1)S(1)} %collective-permute-done.7.refs_1_, bf16[512,64]{1,0:T(8,128)(2,1)S(1)} %get-tuple-element.68.refs_2_, ...), custom_call_target="tpu_custom_call" | custom-call | flops 1000000000 | tf_op jit(solution)/shard_map/product/pallas_call | solution.py:206
  24.1 2.5 %product.7 = (f32[512,256]{1,0:T(8,128)S(1)}, f32[512,256]{1,0:T(8,128)S(1)}, f32[512,256]{1,0:T(8,128)S(1)}, f32[512,256]{1,0:T(8,128)S(1)}) custom-call(bf16[560,256]{1,0:T(8,128)(2,1)S(1)} %collective-permute-done.8.refs_0_, bf16[544,256]{1,0:T(8,128)(2,1)S(1)} %collective-permute-done.1.refs_1_, bf16[512,64]{1,0:T(8,128)(2,1)S(1)} %get-tuple-element.68.refs_2_, ...), custom_call_target="tpu_custom_call" | custom-call | flops 1000000000 | tf_op jit(solution)/shard_map/product/pallas_call | solution.py:206
  26.5 0.0 collective-permute-done.6.refs_1_
  26.6 0.0 collective-permute-done.5.refs_0_
  26.6 0.8 %product.10 = f32[512,256]{1,0:T(8,128)S(1)} custom-call(bf16[560,256]{1,0:T(8,128)(2,1)S(1)} %collective-permute-done.5.refs_0_, bf16[544,256]{1,0:T(8,128)(2,1)S(1)} %collective-permute-done.6.refs_1_, bf16[512,64]{1,0:T(8,128)(2,1)S(1)} %get-tuple-element.79.refs_5_.refs_2_, f32[512,256]{1,0:T(8,128)S(1)} %get-tuple-element.91.refs_3_), custom_call_target="tpu_custom_call" | custom-call | flops 1000000000 | tf_op jit(solution)/shard_map/product/pallas_call | solution.py:206
  27.4 0.1 collective-permute-start.9
  27.5 0.8 %product.9.refs_0_ = f32[512,256]{1,0:T(8,128)S(1)} custom-call(bf16[560,256]{1,0:T(8,128)(2,1)S(1)} %collective-permute-done.5.refs_0_, bf16[544,256]{1,0:T(8,128)(2,1)S(1)} %collective-permute-done.6.refs_1_, bf16[512,64]{1,0:T(8,128)(2,1)S(1)} %get-tuple-element.77.refs_3_.refs_2_, f32[512,256]{1,0:T(8,128)S(1)} %get-tuple-element.90.refs_3_), custom_call_target="tpu_custom_call" | custom-call | flops 1000000000 | tf_op jit(solution)/shard_map/product/pallas_call | solution.py:206
  28.3 1.1 %collective-permute-done.9.refs_1_ = f32[512,256]{1,0:T(8,128)S(1)} collective-permute-done((f32[512,256]{1,0:T(8,128)S(1)}, f32[512,256]{1,0:T(8,128)S(1)}, u32[]{:S(2)}, u32[]{:S(2)}) %collective-permute-start.9) | collective-permute-done | bytes 524320 | tf_op jit(solution)/shard_map/ppermute | solution.py:557
  29.4 0.1 add_up.3
  29.5 0.5 collective-permute-start.11
  30.0 0.8 %product.8.refs_0_ = f32[512,256]{1,0:T(8,128)S(1)} custom-call(bf16[560,256]{1,0:T(8,128)(2,1)S(1)} %collective-permute-done.5.refs_0_, bf16[544,256]{1,0:T(8,128)(2,1)S(1)} %collective-permute-done.6.refs_1_, bf16[512,64]{1,0:T(8,128)(2,1)S(1)} %get-tuple-element.68.refs_2_, f32[512,256]{1,0:T(8,128)S(1)} %get-tuple-element.89.refs_3_), custom_call_target="tpu_custom_call" | custom-call | flops 1000000000 | tf_op jit(solution)/shard_map/product/pallas_call | solution.py:206
  30.8 1.6 %collective-permute-start.14 = (bf16[16,128]{1,0:T(8,128)(2,1)S(1)}, bf16[16,128]{1,0:T(8,128)(2,1)S(1)}, u32[]{:S(2)}, u32[]{:S(2)}) collective-permute-start(bf16[16,128]{1,0:T(8,128)(2,1)S(1)} %get-tuple-element.102.refs_0_), channel_id=1, source_target_pairs={{0,2},{1,3},{2,0},{3,1},{4,6},{5,7},{6,4},{7,5},{8,10},{9,11},{10,... | collective-permute-start | bytes 12296 | tf_op jit(solution)/shard_map/ppermute | solution.py:557
  32.4 0.8 %product.11 = f32[512,256]{1,0:T(8,128)S(1)} custom-call(bf16[560,256]{1,0:T(8,128)(2,1)S(1)} %collective-permute-done.5.refs_0_, bf16[544,256]{1,0:T(8,128)(2,1)S(1)} %collective-permute-done.6.refs_1_, bf16[512,64]{1,0:T(8,128)(2,1)S(1)} %get-tuple-element.78.refs_4_.refs_2_, f32[512,256]{1,0:T(8,128)S(1)} %get-tuple-element.95.refs_3_), custom_call_target="tpu_custom_call" | custom-call | flops 1000000000 | tf_op jit(solution)/shard_map/product/pallas_call | solution.py:206
  33.3 0.1 collective-permute-start.10
  33.3 1.8 %collective-permute-done.11.refs_1_ = bf16[256,256]{1,0:T(8,128)(2,1)S(1)} collective-permute-done((bf16[256,256]{1,0:T(8,128)(2,1)S(1)}, bf16[256,256]{1,0:T(8,128)(2,1)S(1)}, u32[]{:S(2)}, u32[]{:S(2)}) %collective-permute-start.11) | collective-permute-done | bytes 131104 | tf_op jit(solution)/shard_map/ppermute | solution.py:557
  35.1 2.7 %collective-permute-start.12 = (bf16[256,256]{1,0:T(8,128)(2,1)S(1)}, bf16[256,256]{1,0:T(8,128)(2,1)S(1)}, u32[]{:S(2)}, u32[]{:S(2)}) collective-permute-start(bf16[256,256]{1,0:T(8,128)(2,1)S(1)} %add_up.4.refs_2_), channel_id=1, source_target_pairs={{0,4},{1,5},{2,6},{3,7},{4,0},{5,1},{6,2},{7,3},{8,12},{9,13},{10,... | collective-permute-start | bytes 393224 | tf_op jit(solution)/shard_map/ppermute | solution.py:557
  37.8 0.0 collective-permute-done.10.refs_1_
  37.8 0.1 add_up.5
  37.9 0.6 collective-permute-start.13
  38.5 0.0 collective-permute-done.14.refs_1_
  38.5 0.8 %top_couplings.1 = (bf16[192,768]{1,0:T(8,128)(2,1)S(1)}, bf16[192,768]{1,0:T(8,128)(2,1)S(1)}) custom-call(bf16[16,128]{1,0:T(8,128)(2,1)S(1)} %get-tuple-element.102.refs_0_, bf16[16,128]{1,0:T(8,128)(2,1)S(1)} %collective-permute-done.14.refs_1_, bf16[6,64,128]{2,1,0:T(8,128)(2,1)S(1)} %get-tuple-element.100.refs_2_.refs_4_.refs_5_), custom_call_target="tpu_custom_call" | custom-call | flops 10000000000 | tf_op jit(solution)/shard_map/top_couplings/pallas_call | solution.py:536
  39.3 4.2 %collective-permute-done.12.refs_1_ = bf16[256,256]{1,0:T(8,128)(2,1)S(1)} collective-permute-done((bf16[256,256]{1,0:T(8,128)(2,1)S(1)}, bf16[256,256]{1,0:T(8,128)(2,1)S(1)}, u32[]{:S(2)}, u32[]{:S(2)}) %collective-permute-start.12) | collective-permute-done | bytes 131104 | tf_op jit(solution)/shard_map/ppermute | solution.py:557
  43.6 1.3 %collective-permute-done.13.refs_2_ = bf16[256,256]{1,0:T(8,128)(2,1)S(1)} collective-permute-done((bf16[256,256]{1,0:T(8,128)(2,1)S(1)}, bf16[256,256]{1,0:T(8,128)(2,1)S(1)}, u32[]{:S(2)}, u32[]{:S(2)}) %collective-permute-start.13) | collective-permute-done | bytes 131104 | tf_op jit(solution)/shard_map/ppermute | solution.py:557
  44.9 5.6 %leaves.1 = (f32[2,64,128]{2,1,0:T(8,128)}, f32[64,128]{1,0:T(8,128)S(1)}, f32[64,256]{1,0:T(8,128)S(1)}, f32[64,256]{1,0:T(8,128)S(1)}, bf16[192,256]{1,0:T(8,128)(2,1)S(1)}) custom-call(f32[256,256]{1,0:T(8,128)S(1)} %get-tuple-element.98.refs_0_, bf16[256,256]{1,0:T(8,128)(2,1)S(1)} %collective-permute-done.12.refs_1_, ...), custom_call_target="tpu_custom_call" | custom-call | flops 1000000000 | tf_op jit(solution)/shard_map/leaves/pallas_call | solution.py:356
  50.5 0.1 collective-permute-start.15
  50.6 0.9 %collective-permute-start.16 = (bf16[192,256]{1,0:T(8,128)(2,1)S(1)}, bf16[192,256]{1,0:T(8,128)(2,1)S(1)}, u32[]{:S(2)}, u32[]{:S(2)}) collective-permute-start(bf16[192,256]{1,0:T(8,128)(2,1)S(1)} %get-tuple-element.108), channel_id=1, source_target_pairs={{0,2},{1,3},{2,0},{3,1},{4,6},{5,7},{6,4},{7,5},{8,10},{9,11},{10,... | collective-permute-start | bytes 294920 | tf_op jit(solution)/shard_map/ppermute | solution.py:557
  51.5 2.6 %collective-permute-start.17 = (bf16[192,256]{1,0:T(8,128)(2,1)S(1)}, bf16[192,256]{1,0:T(8,128)(2,1)S(1)}, u32[]{:S(2)}, u32[]{:S(2)}) collective-permute-start(bf16[192,256]{1,0:T(8,128)(2,1)S(1)} %get-tuple-element.108), channel_id=1, source_target_pairs={{0,3},{1,2},{2,1},{3,0},{4,7},{5,6},{6,5},{7,4},{8,11},{9,10},{10,... | collective-permute-start | bytes 294920 | tf_op jit(solution)/shard_map/ppermute | solution.py:557
  54.1 2.2 %collective-permute-done.15.refs_2_ = bf16[192,256]{1,0:T(8,128)(2,1)S(1)} collective-permute-done((bf16[192,256]{1,0:T(8,128)(2,1)S(1)}, bf16[192,256]{1,0:T(8,128)(2,1)S(1)}, u32[]{:S(2)}, u32[]{:S(2)}) %collective-permute-start.15) | collective-permute-done | bytes 98336 | tf_op jit(solution)/shard_map/ppermute | solution.py:557
  56.3 0.0 collective-permute-done.16.refs_3_
  56.3 1.5 %collective-permute-done.17.refs_4_ = bf16[192,256]{1,0:T(8,128)(2,1)S(1)} collective-permute-done((bf16[192,256]{1,0:T(8,128)(2,1)S(1)}, bf16[192,256]{1,0:T(8,128)(2,1)S(1)}, u32[]{:S(2)}, u32[]{:S(2)}) %collective-permute-start.17) | collective-permute-done | bytes 98336 | tf_op jit(solution)/shard_map/ppermute | solution.py:557
  57.7 5.9 %upper_levels.1 = (f32[3,1,64,128]{3,2,1,0:T(8,128)}, f32[2,1,64,256]{3,2,1,0:T(8,128)}) custom-call(f32[64,256]{1,0:T(8,128)S(1)} %get-tuple-element.106.refs_0_, f32[64,256]{1,0:T(8,128)S(1)} %get-tuple-element.107.refs_1_, bf16[192,256]{1,0:T(8,128)(2,1)S(1)} %collective-permute-done.15.refs_2_, bf16[192,256]{1,0:T(8,128)(2,1)S(1)} %collective-permute-done.16.refs_3_, ...), custom_call_target="tpu_custom_call" | custom-call | flops 1000000000 | tf_op jit(solution)/shard_map/upper_levels/pallas_call | solution.py:432
  (4 shorter events, 0.0 us)
Async XLA Ops:
  1.9 6.1 %collective-permute-start.2 = (bf16[16,256]{1,0:T(8,128)(2,1)S(1)}, bf16[16,256]{1,0:T(8,128)(2,1)S(1)}, u32[]{:S(2)}, u32[]{:S(2)}) collective-permute-start(bf16[16,256]{1,0:T(8,128)(2,1)S(1)} %get-tuple-element.60), channel_id=1, source_target_pairs={{0,2},{1,3},{2,0},{3,1},{4,6},{5,7},{6,4},{7,5},{8,10},{9,11},{10,... | collective-permute-start | bytes 24584 | tf_op jit(solution)/shard_map/ppermute | solution.py:557
  5.0 11.4 %collective-permute-start = (bf16[560,256]{1,0:T(8,128)(2,1)S(1)}, bf16[560,256]{1,0:T(8,128)(2,1)S(1)}, u32[]{:S(2)}, u32[]{:S(2)}) collective-permute-start(bf16[560,256]{1,0:T(8,128)(2,1)S(1)} %get-tuple-element.70.refs_0_.refs_3_), channel_id=1, source_target_pairs={{0,1},{1,0},{2,3},{3,2},{4,5},{5,4},{6,7},{7,6},{8,9},{9,8},{10,11... | collective-permute-start | bytes 860168 | tf_op jit(solution)/shard_map/ppermute | solution.py:557
  6.5 9.9 %collective-permute-start.1 = (bf16[544,256]{1,0:T(8,128)(2,1)S(1)}, bf16[544,256]{1,0:T(8,128)(2,1)S(1)}, u32[]{:S(2)}, u32[]{:S(2)}) collective-permute-start(bf16[544,256]{1,0:T(8,128)(2,1)S(1)} %get-tuple-element.69.refs_1_), channel_id=1, source_target_pairs={{0,16},{1,17},{2,18},{3,19},{4,20},{5,21},{6,22},{7,23},{8,24},{9,... | collective-permute-start | bytes 835592 | tf_op jit(solution)/shard_map/ppermute | solution.py:557
  8.0 4.7 %collective-permute-start.3 = (bf16[16,512]{1,0:T(8,128)(2,1)S(1)}, bf16[16,512]{1,0:T(8,128)(2,1)S(1)}, u32[]{:S(2)}, u32[]{:S(2)}) collective-permute-start(bf16[16,512]{1,0:T(8,128)(2,1)S(1)} %pad_maximum_fusion), channel_id=1, source_target_pairs={{0,4},{1,5},{2,6},{3,7},{4,0},{5,1},{6,2},{7,3},{8,12},{9,13},{10,... | collective-permute-start | bytes 49160 | tf_op jit(solution)/shard_map/ppermute | solution.py:557
  10.6 11.0 %collective-permute-start.8 = (bf16[560,256]{1,0:T(8,128)(2,1)S(1)}, bf16[560,256]{1,0:T(8,128)(2,1)S(1)}, u32[]{:S(2)}, u32[]{:S(2)}) collective-permute-start(bf16[560,256]{1,0:T(8,128)(2,1)S(1)} %get-tuple-element.70.refs_0_.refs_3_), channel_id=1, source_target_pairs={{0,16},{1,17},{2,18},{3,19},{4,20},{5,21},{6,22},{7,23},{8,24},{9,... | collective-permute-start | bytes 860168 | tf_op jit(solution)/shard_map/ppermute | solution.py:557
  11.2 8.5 %collective-permute-start.7 = (bf16[544,256]{1,0:T(8,128)(2,1)S(1)}, bf16[544,256]{1,0:T(8,128)(2,1)S(1)}, u32[]{:S(2)}, u32[]{:S(2)}) collective-permute-start(bf16[544,256]{1,0:T(8,128)(2,1)S(1)} %get-tuple-element.69.refs_1_), channel_id=1, source_target_pairs={{0,1},{1,0},{2,3},{3,2},{4,5},{5,4},{6,7},{7,6},{8,9},{9,8},{10,11... | collective-permute-start | bytes 835592 | tf_op jit(solution)/shard_map/ppermute | solution.py:557
  12.7 1.2 %collective-permute-start.4 = (bf16[16,1024]{1,0:T(8,128)(2,1)S(1)}, bf16[16,1024]{1,0:T(8,128)(2,1)S(1)}, u32[]{:S(2)}, u32[]{:S(2)}) collective-permute-start(bf16[16,1024]{1,0:T(8,128)(2,1)S(1)} %constant_dynamic-update-slice_fusion.refs_2_), channel_id=1, source_target_pairs={{0,8},{1,9},{2,10},{3,11},{4,12},{5,13},{6,14},{7,15},{8,0},{9,1},... | collective-permute-start | bytes 98312 | tf_op jit(solution)/shard_map/ppermute | solution.py:557
  16.4 10.2 %collective-permute-start.5 = (bf16[560,256]{1,0:T(8,128)(2,1)S(1)}, bf16[560,256]{1,0:T(8,128)(2,1)S(1)}, u32[]{:S(2)}, u32[]{:S(2)}) collective-permute-start(bf16[560,256]{1,0:T(8,128)(2,1)S(1)} %collective-permute-done.refs_1_.refs_0_), channel_id=1, source_target_pairs={{0,16},{1,17},{2,18},{3,19},{4,20},{5,21},{6,22},{7,23},{8,24},{9,... | collective-permute-start | bytes 860168 | tf_op jit(solution)/shard_map/ppermute | solution.py:557
  17.6 8.9 %collective-permute-start.6 = (bf16[544,256]{1,0:T(8,128)(2,1)S(1)}, bf16[544,256]{1,0:T(8,128)(2,1)S(1)}, u32[]{:S(2)}, u32[]{:S(2)}) collective-permute-start(bf16[544,256]{1,0:T(8,128)(2,1)S(1)} %collective-permute-done.1.refs_1_), channel_id=1, source_target_pairs={{0,1},{1,0},{2,3},{3,2},{4,5},{5,4},{6,7},{7,6},{8,9},{9,8},{10,11... | collective-permute-start | bytes 835592 | tf_op jit(solution)/shard_map/ppermute | solution.py:557
  27.4 2.0 %collective-permute-start.9 = (f32[512,256]{1,0:T(8,128)S(1)}, f32[512,256]{1,0:T(8,128)S(1)}, u32[]{:S(2)}, u32[]{:S(2)}) collective-permute-start(f32[512,256]{1,0:T(8,128)S(1)} %product.10), channel_id=1, source_target_pairs={{0,8},{1,9},{2,10},{3,11},{4,12},{5,13},{6,14},{7,15},{8,0},{9,1},... | collective-permute-start | bytes 1572872 | tf_op jit(solution)/shard_map/ppermute | solution.py:557
  29.5 5.6 %collective-permute-start.11 = (bf16[256,256]{1,0:T(8,128)(2,1)S(1)}, bf16[256,256]{1,0:T(8,128)(2,1)S(1)}, u32[]{:S(2)}, u32[]{:S(2)}) collective-permute-start(bf16[256,256]{1,0:T(8,128)(2,1)S(1)} %get-tuple-element.97), channel_id=1, source_target_pairs={{0,2},{1,3},{2,0},{3,1},{4,6},{5,7},{6,4},{7,5},{8,10},{9,11},{10,... | collective-permute-start | bytes 393224 | tf_op jit(solution)/shard_map/ppermute | solution.py:557
  30.8 7.6 %collective-permute-start.14 = (bf16[16,128]{1,0:T(8,128)(2,1)S(1)}, bf16[16,128]{1,0:T(8,128)(2,1)S(1)}, u32[]{:S(2)}, u32[]{:S(2)}) collective-permute-start(bf16[16,128]{1,0:T(8,128)(2,1)S(1)} %get-tuple-element.102.refs_0_), channel_id=1, source_target_pairs={{0,2},{1,3},{2,0},{3,1},{4,6},{5,7},{6,4},{7,5},{8,10},{9,11},{10,... | collective-permute-start | bytes 12296 | tf_op jit(solution)/shard_map/ppermute | solution.py:557
  33.3 4.5 %collective-permute-start.10 = (f32[512,256]{1,0:T(8,128)S(1)}, f32[512,256]{1,0:T(8,128)S(1)}, u32[]{:S(2)}, u32[]{:S(2)}) collective-permute-start(f32[512,256]{1,0:T(8,128)S(1)} %product.11), channel_id=1, source_target_pairs={{0,8},{1,9},{2,10},{3,11},{4,12},{5,13},{6,14},{7,15},{8,0},{9,1},... | collective-permute-start | bytes 1572872 | tf_op jit(solution)/shard_map/ppermute | solution.py:557
  35.1 8.4 %collective-permute-start.12 = (bf16[256,256]{1,0:T(8,128)(2,1)S(1)}, bf16[256,256]{1,0:T(8,128)(2,1)S(1)}, u32[]{:S(2)}, u32[]{:S(2)}) collective-permute-start(bf16[256,256]{1,0:T(8,128)(2,1)S(1)} %add_up.4.refs_2_), channel_id=1, source_target_pairs={{0,4},{1,5},{2,6},{3,7},{4,0},{5,1},{6,2},{7,3},{8,12},{9,13},{10,... | collective-permute-start | bytes 393224 | tf_op jit(solution)/shard_map/ppermute | solution.py:557
  37.9 7.1 %collective-permute-start.13 = (bf16[256,256]{1,0:T(8,128)(2,1)S(1)}, bf16[256,256]{1,0:T(8,128)(2,1)S(1)}, u32[]{:S(2)}, u32[]{:S(2)}) collective-permute-start(bf16[256,256]{1,0:T(8,128)(2,1)S(1)} %get-tuple-element.99), channel_id=1, source_target_pairs={{0,2},{1,3},{2,0},{3,1},{4,6},{5,7},{6,4},{7,5},{8,10},{9,11},{10,... | collective-permute-start | bytes 393224 | tf_op jit(solution)/shard_map/ppermute | solution.py:557
  50.5 5.7 %collective-permute-start.15 = (bf16[192,256]{1,0:T(8,128)(2,1)S(1)}, bf16[192,256]{1,0:T(8,128)(2,1)S(1)}, u32[]{:S(2)}, u32[]{:S(2)}) collective-permute-start(bf16[192,256]{1,0:T(8,128)(2,1)S(1)} %get-tuple-element.108), channel_id=1, source_target_pairs={{0,1},{1,0},{2,3},{3,2},{4,5},{5,4},{6,7},{7,6},{8,9},{9,8},{10,11... | collective-permute-start | bytes 294920 | tf_op jit(solution)/shard_map/ppermute | solution.py:557
  50.6 5.7 %collective-permute-start.16 = (bf16[192,256]{1,0:T(8,128)(2,1)S(1)}, bf16[192,256]{1,0:T(8,128)(2,1)S(1)}, u32[]{:S(2)}, u32[]{:S(2)}) collective-permute-start(bf16[192,256]{1,0:T(8,128)(2,1)S(1)} %get-tuple-element.108), channel_id=1, source_target_pairs={{0,2},{1,3},{2,0},{3,1},{4,6},{5,7},{6,4},{7,5},{8,10},{9,11},{10,... | collective-permute-start | bytes 294920 | tf_op jit(solution)/shard_map/ppermute | solution.py:557
  51.5 6.2 %collective-permute-start.17 = (bf16[192,256]{1,0:T(8,128)(2,1)S(1)}, bf16[192,256]{1,0:T(8,128)(2,1)S(1)}, u32[]{:S(2)}, u32[]{:S(2)}) collective-permute-start(bf16[192,256]{1,0:T(8,128)(2,1)S(1)} %get-tuple-element.108), channel_id=1, source_target_pairs={{0,3},{1,2},{2,1},{3,0},{4,7},{5,6},{6,5},{7,4},{8,11},{9,10},{10,... | collective-permute-start | bytes 294920 | tf_op jit(solution)/shard_map/ppermute | solution.py:557
